TPU v7x, 32 devices: a whole 2x2x4 slice. The times are simulated.
32 devices in a mesh: groups: 2 (over y), dp: 4 (over x, core), tensor: 4 (over z).
Axes of the slice: x: 2, y: 2, z: 4, core: 2. Of those that a mesh axis runs over, the one named last changes fastest.
Arguments:
- hidden: bfloat16 [6144, 8192], P(('groups', 'dp'), 'tensor'), parts along dimension 0, may hold values from -6 to 6
- query_weight: bfloat16 [8192, 8192], P(None, 'tensor'), may hold values from -0.0625 to 0.0625
- adapter_down: bfloat16 [32, 64, 8192], P('dp', None, 'tensor'), may hold values from -0.0625 to 0.0625
- adapter_up: bfloat16 [32, 64, 8192], P('dp', None, 'tensor'), may hold values from -0.75 to 0.75
- block_variant_index: int32 [8, 6], P('groups'), parts along dimension 0, may hold values from 0 to 31, as said below
- variant_pool_slot: int32 [64], P('groups'), parts along dimension 0, may hold values from 0 to 31, as said below
- block_live_count: int32 [8, 6], P(('groups', 'dp')), parts along dimension 0, may hold values from 1 to 128, 576 in all within a row
Outputs:
- query: bfloat16 [6144, 8192], P(('groups', 'dp'), 'tensor'), parts along dimension 0
There are 2 independent parts, one for each index of `groups`. A program takes and returns all parts, laid end to end along the dimension named above; an argument that names none is the same for every part. Nothing has to cross between parts.
Inputs may be any that keep to these rules, and one draw needn't show every extreme that they name: variant_pool_slot is a permutation; variant v lies in pool slot variant_pool_slot[v], held by dp index variant_pool_slot[v] // 8. `block_variant_index`: let C be 6 divided by 4, rounded up; for each replica and each dp index, at most C of the replica's blocks name variants held by that index, and some index holds exactly C (so when 6 <= 4, a replica's blocks name variants on distinct dp indices). `block_live_count`: each replica's 6 counts sum to 576, and one of them is 128.
All inputs are finite; a program needn't handle non-finite values.
Results may differ from a plain program's by a relative error of at most 0.0045.
Values may be sent and summed in bfloat16 or wider, within the bound.
No kernel may reach another device: no remote copies, remote signals or barrier semaphores. Data moves between devices by JAX's collectives and lax.ppermute only.
A program may use at most 128 MiB of HBM per device.

v0:
```python
import jax
import jax.numpy as jnp
from jax import lax
from jax.sharding import PartitionSpec as P

adapter_scale = 2.0


def shards(
    hidden,
    query_weight,
    adapter_down,
    adapter_up,
    block_variant_index,
    variant_pool_slot,
    block_live_count,
):
    replica_count = lax.axis_size("dp")
    replica = lax.axis_index("dp")
    variants_per_device = adapter_down.shape[0]
    blocks = block_variant_index.shape[1]
    block = hidden.shape[0] // blocks
    device_position = adapter_down.shape[1]
    width_shard = hidden.shape[1]
    query_shard = query_weight.shape[1]
    slots_all = variant_pool_slot[block_variant_index]
    my_slots = lax.dynamic_index_in_dim(slots_all, replica, 0, keepdims=False)
    live_rows = block_live_count[0]
    slot_capacity = (blocks + replica_count - 1) // replica_count
    owners = slots_all // variants_per_device
    owned = owners == replica
    owned_rank = jnp.cumsum(owned.astype(jnp.int32), axis=1) - 1
    picker = owned[:, None, :] & (
        owned_rank[:, None, :] == jnp.arange(slot_capacity)[None, :, None]
    )
    local_slot = slots_all % variants_per_device
    outgoing_index = jnp.sum(jnp.where(picker, local_slot[:, None, :], 0), axis=2).reshape(-1)
    outgoing_down = jnp.take(adapter_down, outgoing_index, axis=0).reshape(
        replica_count, slot_capacity, device_position, width_shard
    )
    outgoing_up = jnp.take(adapter_up, outgoing_index, axis=0).reshape(
        replica_count, slot_capacity, device_position, query_shard
    )
    got_down, got_up = (
        lax.all_to_all(outgoing_down, "dp", split_axis=0, concat_axis=0, tiled=True),
        lax.all_to_all(outgoing_up, "dp", split_axis=0, concat_axis=0, tiled=True),
    )
    my_owner = my_slots // variants_per_device
    same_owner = my_owner[:, None] == my_owner[None, :]
    earlier = jnp.arange(blocks)[None, :] < jnp.arange(blocks)[:, None]
    my_rank = jnp.sum((same_owner & earlier).astype(jnp.int32), axis=1)
    position = my_owner * slot_capacity + my_rank
    down_sel = jnp.take(
        got_down.reshape(replica_count * slot_capacity, device_position, width_shard),
        position,
        axis=0,
    )
    up_selection = jnp.take(
        got_up.reshape(replica_count * slot_capacity, device_position, query_shard),
        position,
        axis=0,
    )
    base_output = jnp.dot(
        lax.all_gather(hidden, "tensor", axis=1, tiled=True),
        query_weight,
        preferred_element_type=jnp.float32,
    )
    blocks_base_rows = base_output.reshape(blocks, block, query_shard)
    blocked = hidden.reshape(blocks, block, width_shard)
    partial_value = jnp.einsum(
        "nrd,nkd->nrk", blocked, down_sel, preferred_element_type=jnp.float32
    )
    down_projected = lax.psum(partial_value, "tensor").astype(jnp.bfloat16)
    adapter_delta = jnp.einsum(
        "bls,bsm->blm", down_projected, up_selection, preferred_element_type=jnp.float32
    )
    live_mask = jnp.arange(block)[None, :] < live_rows[:, None]
    reduced_sum = blocks_base_rows + adapter_scale * adapter_delta
    result = jnp.where(live_mask[:, :, None], reduced_sum, jnp.float32(0.0))
    return result.reshape(blocks * block, query_shard).astype(jnp.bfloat16)


def solution(mesh):
    return jax.shard_map(
        shards,
        mesh=mesh,
        in_specs=(
            P(("groups", "dp"), "tensor"),
            P(None, "tensor"),
            P("dp", None, "tensor"),
            P("dp", None, "tensor"),
            P("groups", None),
            P("groups"),
            P(("groups", "dp"), None),
        ),
        out_specs=P(("groups", "dp"), "tensor"),
        check_vma=False,
    )
```

profile of v0, /device:TPU:0, one launch (start us, length us, event | category | flops | bytes accessed | tf_op | source)
XLA Modules:
  0.0 277.2 jit_solution(7857821350075556541)
XLA Ops:
  6.5 0.0 copy-start
  6.5 0.0 copy-start.5
  6.5 0.0 copy-start.2
  6.5 0.0 all-gather.2.cloned.1.call-start
  6.5 0.7 all-gather.2.cloned.1.call-update
  7.3 0.1 copy-done.5
  7.4 0.1 reshape.182
  7.5 0.0 copy-done.2
  7.5 0.7 gather_fusion
  8.2 0.1 reshape.181
  8.3 0.2 reduce_window_sum.11
  8.5 0.1 select_reduce_fusion
  8.6 0.1 copy.8
  8.7 0.1 reshape.142
  8.8 0.0 copy-done
  8.8 2.0 gather_fusion.1
  10.8 0.0 copy-start.3
  10.8 3.8 %gather_fusion.3 = bf16[8,64,2048]{2,1,0:T(8,128)(2,1)} fusion(bf16[8,64,2048]{2,1,0:T(8,128)(2,1)} %param.14, s32[1024]{0:T(1024)S(1)} %pad_clamp_fusion.1), kind=kCustom, calls=%fused_computation.2.clone | custom fusion | bytes 4194336 | tf_op jit(solution)/shard_map/jit(_take)/gather | solution.py:41
  14.6 0.0 copy-done.3
  14.6 3.3 %broadcast_select_fusion.1 = (bf16[8,64,2048]{2,1,0:T(8,128)(2,1)}, bf16[8,64,2048]{2,1,0:T(8,128)(2,1)S(1)}) fusion(bf16[8,64,2048]{2,1,0:T(8,128)(2,1)S(1)} %copy-done.3, pred[8]{0:T(512)(128)(4,1)S(1)} %compare_and_fusion.1, bf16[8,64,2048]{2,1,0:T(8,128)(2,1)} %gather_fusion.3), kind=kLoop, calls=%fused_computation.7 | loop fusion | flops 2097152 | bytes 8388616 | tf_op jit(solution)/shard_map/jit(_take)/select_n | solution.py:38
  18.0 29.8 %all_to_all.10 = bf16[4,2,64,2048]{3,2,1,0:T(8,128)(2,1)} all-to-all(bf16[4,2,64,2048]{3,2,1,0:T(8,128)(2,1)S(1)} %bitcast.26), channel_id=1, replica_groups=mesh['groups'=2,'dp'=4,'tensor'=4] {'dp'}, dimensions={0} | all-to-all | bytes 4194304 | tf_op jit(solution)/shard_map/all_to_all | solution.py:46
  47.8 0.0 copy-start.6
  47.8 3.7 %all-to-all-start = ((bf16[4,2,64,2048]{3,2,1,0:T(8,128)(2,1)}), bf16[4,2,64,2048]{3,2,1,0:T(8,128)(2,1)S(1)}, u32[]{:S(2)}, u32[]{:S(2)}) async-start(bf16[4,2,64,2048]{3,2,1,0:T(8,128)(2,1)} %bitcast.4), calls=%async_computation | async-start | bytes 4194304 | tf_op jit(solution)/shard_map/all_to_all | solution.py:45
  51.6 0.2 convert_reduce_fusion
  51.8 0.0 copy-done.6
  51.8 0.1 iota_compare_fusion.2
  51.9 3.5 %gather_fusion.4 = bf16[6,64,2048]{2,1,0:T(8,128)(2,1)} fusion(bf16[8,64,2048]{2,1,0:T(8,128)(2,1)} %bitcast.28, s32[1024]{0:T(1024)S(1)} %pad_clamp_fusion), kind=kCustom, calls=%fused_computation.3.clone | custom fusion | bytes 3145752 | tf_op jit(solution)/shard_map/jit(_take)/gather | solution.py:58
  55.3 21.8 %all-to-all-done = bf16[4,2,64,2048]{3,2,1,0:T(8,128)(2,1)S(1)} async-done(((bf16[4,2,64,2048]{3,2,1,0:T(8,128)(2,1)}), bf16[4,2,64,2048]{3,2,1,0:T(8,128)(2,1)S(1)}, u32[]{:S(2)}, u32[]{:S(2)}) %all-to-all-start) | async-done | bytes 2097184 | tf_op jit(solution)/shard_map/all_to_all | solution.py:45
  77.2 1.8 gather_fusion.2
  79.0 3.7 %fusion.5 = f32[6,128,64]{1,2,0:T(8,128)S(1)} fusion(bf16[6,128,2048]{2,1,0:T(8,128)(2,1)} %bitcast.30, bf16[6,64,2048]{2,1,0:T(8,128)(2,1)} %gather_fusion.2, pred[6]{0:T(512)(128)(4,1)S(1)} %get-tuple-element.6), kind=kOutput, calls=%fused_computation.13 | convolution fusion | flops 202113024 | bytes 4915206 | tf_op jit(solution)/shard_map/nrd,nkd->nrk/dot_general | solution.py:70
  82.7 39.2 %all-reduce.1 = bf16[6,128,64]{1,2,0:T(8,128)(2,1)S(1)} all-reduce(f32[6,128,64]{1,2,0:T(8,128)S(1)} %fusion.5), channel_id=1, replica_groups=mesh['groups'=2,'dp'=4,'tensor'=4] {'tensor'}, use_global_device_ids=true, to_apply=%region_3.6 | all-reduce | flops 49152 | bytes 294912 | tf_op jit(solution)/shard_map/psum | solution.py:73
  121.9 114.2 %all-gather.2.cloned.1.call-done = bf16[768,8192]{1,0:T(8,128)(2,1)} async-done(((bf16[768,2048]{1,0:T(8,128)(2,1)}), bf16[768,8192]{1,0:T(8,128)(2,1)}) %all-gather.2.cloned.1.call-update) | async-done | bytes 12582928 | tf_op jit(solution)/shard_map/all_gather | solution.py:64
  236.1 0.0 copy-start.4
  236.1 31.4 %fusion.20 = f32[768,2048]{1,0:T(8,128)S(1)} fusion(bf16[768,8192]{1,0:T(8,128)(2,1)} %all-gather.2.cloned.1.call-done, bf16[8192,2048]{1,0:T(8,128)(2,1)} %param.12), kind=kOutput, calls=%fused_computation.56 | convolution fusion | flops 25769803776 | bytes 52428800 | tf_op jit(solution)/shard_map/dot_general | solution.py:63
  267.5 0.0 copy-done.4
  267.5 0.0 copy-start.1
  267.5 2.8 %select_convert_fusion = bf16[6,128,2048]{2,1,0:T(8,128)(2,1)} fusion(f32[6,128,2048]{2,1,0:T(8,128)S(1)} %bitcast.29, pred[6,128]{1,0:T(8,128)(4,1)S(1)} %iota_compare_fusion.2, bf16[6,64,2048]{2,1,0:T(8,128)(2,1)S(1)} %copy-done.4, pred[6]{0:T(512)(128)(4,1)S(1)} %get-tuple-element.6, bf16[6,128,64]{1,2,0:T(8,128)(2,1)S(1)} %all-reduce.1), kind=kOutput, calls=%fused_computation.5 | convolution fusion | flops 208404480 | bytes 11109126 | tf_op jit(solution)/shard_map/bls,bsm->blm/dot_general | solution.py:74
  270.3 0.0 copy-done.1
  (11 shorter events, 0.1 us)
Async XLA Ops:
  6.5 2.3 copy-start
  6.5 0.8 copy-start.5
  6.5 0.9 copy-start.2
  6.5 229.6 %all-gather.2.cloned.1.call-start = ((), (), s32[]{:S(2)}) async-start(), calls=%async_computation.2 | async-start | bytes 15728640 | tf_op jit(solution)/shard_map/all_gather | solution.py:64
  10.8 3.8 %copy-start.3 = (bf16[8,64,2048]{2,1,0:T(8,128)(2,1)S(1)}, bf16[8,64,2048]{2,1,0:T(8,128)(2,1)}, u32[]{:S(2)}) copy-start(bf16[8,64,2048]{2,1,0:T(8,128)(2,1)} %gather_fusion.1) | copy-start | bytes 6291460
  47.8 4.0 %copy-start.6 = (s32[1,6]{1,0:T(1,128)S(1)}, s32[1,6]{1,0:T(1,128)}, u32[]{:S(2)}) copy-start(s32[1,6]{1,0:T(1,128)} %param.17) | copy-start | bytes 76
  47.8 29.4 %all-to-all-start = ((bf16[4,2,64,2048]{3,2,1,0:T(8,128)(2,1)}), bf16[4,2,64,2048]{3,2,1,0:T(8,128)(2,1)S(1)}, u32[]{:S(2)}, u32[]{:S(2)}) async-start(bf16[4,2,64,2048]{3,2,1,0:T(8,128)(2,1)} %bitcast.4), calls=%async_computation | async-start | bytes 4194304 | tf_op jit(solution)/shard_map/all_to_all | solution.py:45
  236.1 31.4 %copy-start.4 = (bf16[6,64,2048]{2,1,0:T(8,128)(2,1)S(1)}, bf16[6,64,2048]{2,1,0:T(8,128)(2,1)}, u32[]{:S(2)}) copy-start(bf16[6,64,2048]{2,1,0:T(8,128)(2,1)} %gather_fusion.4) | copy-start | bytes 4718596
  267.5 2.8 %copy-start.1 = (bf16[8,64,2048]{2,1,0:T(8,128)(2,1)S(1)}, bf16[8,64,2048]{2,1,0:T(8,128)(2,1)}, u32[]{:S(2)}) copy-start(bf16[8,64,2048]{2,1,0:T(8,128)(2,1)} %param.13) | copy-start | bytes 6291460
Sparse Core Ops, SparseCore 0:
  8.9 227.1 all-gather.1
where the time goes:
time: 278 us; the launch traced here: 277 us
  waiting for transfers between devices  137 us (49%)
  blocking collectives  69 us (25%)
  matrix products  37.8 us (14%)
  between operations  13.5 us (5%)
  local copies, waits for them, and re-layouts  12.3 us (4%)
  other arithmetic  4.06 us (1%)
  starting transfers between devices  3.74 us (1%)
    all_gather x1, waiting for transfers between devices, shards(): lax.all_gather(hidden, 'tensor', axis=1, tiled=True)  114 us
    psum x1, blocking collectives, shards(): down_projected = lax.psum(partial_value, 'tensor').astype(jnp.bfloat16)  39.2 us
    dot_general x1, matrix products, shards(): jnp.dot(lax.all_gather(hidden, 'tensor', axis=1, tiled=True), query_weigh...  31.4 us
    all_to_all x1, blocking collectives, shards(): lax.all_to_all(outgoing_up, 'dp', split_axis=0, concat_axis=0, tiled=True)  29.8 us
    all_to_all x1, waiting for transfers between devices, shards(): lax.all_to_all(outgoing_down, 'dp', split_axis=0, concat_axis=0, tiled=True)  21.8 us
  transfers between devices with their start and end apart: 2, of which 2 were waited for; matrix products, arithmetic and copies ran while one was open for 7% of the time, Pallas kernels for 0%

commit v1 on v0

v1 whole, which is shorter than its diff:
```python
import jax
import jax.numpy as jnp
from jax import lax
from jax.sharding import PartitionSpec as P

adapter_scale = 2.0
live_total = 576
feature_chunks = 4


def shift(x, axis, step, size):
    pairs = [(i, i + step) for i in range(size) if 0 <= i + step < size]
    return lax.ppermute(x, axis, pairs)


def shards(
    hidden,
    query_weight,
    adapter_down,
    adapter_up,
    block_variant_index,
    variant_pool_slot,
    block_live_count,
):
    replicas = lax.axis_size("dp")
    replica = lax.axis_index("dp")
    tensor = lax.axis_size("tensor")
    pool = adapter_down.shape[0]
    blocks = block_variant_index.shape[1]
    rows, width = hidden.shape
    block = rows // blocks
    rank = adapter_down.shape[1]
    columns = query_weight.shape[1]
    capacity = (blocks + replicas - 1) // replicas
    bf16, f32 = jnp.bfloat16, jnp.float32

    live = block_live_count[0]
    start = jnp.cumsum(live) - live
    row = jnp.arange(rows)
    inside = row % block
    is_live = inside < jnp.repeat(live, block)
    place = jnp.where(is_live, jnp.repeat(start, block) + inside, -1)
    pack = (jnp.arange(live_total)[:, None] == place[None, :]).astype(bf16)
    packed = jnp.dot(pack, hidden, preferred_element_type=f32).astype(bf16)

    piece = width // feature_chunks
    gathered = [
        lax.all_gather(packed[:, j * piece : (j + 1) * piece], "tensor", axis=0)
        for j in range(feature_chunks)
    ]

    slots = variant_pool_slot[block_variant_index]
    owners = slots // pool
    local = slots % pool
    earlier = jnp.arange(blocks)[None, :] < jnp.arange(blocks)[:, None]
    nth = jnp.sum(
        ((owners[:, :, None] == owners[:, None, :]) & earlier[None]).astype(jnp.int32), axis=2
    )

    def outgoing(target):
        o, l, m = owners[target], local[target], nth[target]
        hit = (o[None, :] == replica) & (m[None, :] == jnp.arange(capacity)[:, None])
        index = jnp.sum(jnp.where(hit, l[None, :], 0), axis=1)
        return jnp.take(adapter_down, index, axis=0), jnp.take(adapter_up, index, axis=0)

    downs, ups = [], []
    for step in range(replicas):
        target = (replica + step) % replicas
        d, u = outgoing(target)
        if step:
            pairs = [(i, (i + step) % replicas) for i in range(replicas)]
            d = lax.ppermute(d, "dp", pairs)
            u = lax.ppermute(u, "dp", pairs)
        downs.append(d)
        ups.append(u)
    groups = replicas * capacity
    down_all = jnp.concatenate(downs, axis=0).reshape(groups * rank, width)
    up_all = jnp.concatenate(ups, axis=0).reshape(groups * rank, columns)

    my_owner, my_nth = owners[replica], nth[replica]
    my_group = ((replica - my_owner) % replicas) * capacity + my_nth
    live_row = jnp.arange(live_total)
    row_block = jnp.sum((live_row[:, None] >= start[None, :]).astype(jnp.int32), axis=1) - 1
    row_group = jnp.sum(
        jnp.where(row_block[:, None] == jnp.arange(blocks)[None, :], my_group[None, :], 0), axis=1
    )
    mask = row_group[:, None] == jnp.arange(groups)[None, :]

    wide = lax.dot_general(
        packed, down_all, (((1,), (1,)), ((), ())), preferred_element_type=f32
    ).reshape(live_total, groups, rank)
    partial = jnp.sum(jnp.where(mask[:, :, None], wide, 0.0), axis=1)

    before, after = jnp.zeros_like(partial), jnp.zeros_like(partial)
    for _ in range(tensor - 1):
        before = shift(partial + before, "tensor", 1, tensor)
        after = shift(partial + after, "tensor", -1, tensor)
    shrink = (before + partial + after).astype(bf16)
    spread = jnp.where(
        mask[:, :, None], (shrink * bf16(adapter_scale))[:, None, :], bf16(0.0)
    ).reshape(live_total, groups * rank)

    total = jnp.dot(spread, up_all, preferred_element_type=f32)
    weight = query_weight.reshape(tensor, feature_chunks, piece, columns)
    for j in range(feature_chunks):
        for t in range(tensor):
            total = total + jnp.dot(gathered[j][t], weight[t, j], preferred_element_type=f32)
    result = total.astype(bf16)
    unpack = (place[:, None] == jnp.arange(live_total)[None, :]).astype(bf16)
    return jnp.dot(unpack, result, preferred_element_type=f32).astype(bf16)


def solution(mesh):
    return jax.shard_map(
        shards,
        mesh=mesh,
        in_specs=(
            P(("groups", "dp"), "tensor"),
            P(None, "tensor"),
            P("dp", None, "tensor"),
            P("dp", None, "tensor"),
            P("groups", None),
            P("groups"),
            P(("groups", "dp"), None),
        ),
        out_specs=P(("groups", "dp"), "tensor"),
        check_vma=False,
    )
```

time: 278 us -> 282 us (1.014)
  matrix products: 37.8 us -> 117 us
  blocking collectives: 69 us -> 0 us
  waiting for transfers between devices: 137 us -> 96.8 us
  starting transfers between devices: 3.74 us -> 23.5 us
  local copies, waits for them, and re-layouts: 12.3 us -> 20.5 us
  other arithmetic: 4.06 us -> 10.3 us
    dot_general x3 -> x19, matrix products: 37.8 us -> 117 us  [the longest x16 84 us: shards(): jnp.dot(gathered[j][t], weight[t, j], preferred_element_type=f32)]
    all_gather x1 -> x4, waiting for transfers between devices: 114 us -> 66 us  [shards(): lax.all_gather(packed[:, j * piece:(j + 1) * piece], 'tensor', axis=0)]
    psum x1 -> x0, blocking collectives: 39.2 us -> none  [shards(): down_projected = lax.psum(partial_value, 'tensor').astype(jnp.bfloat16)]
    ppermute x0 -> x12, waiting for transfers between devices: none -> 30.1 us  [the longest x6 24.9 us: shift(): return lax.ppermute(x, axis, pairs)]
    all_to_all x1 -> x0, blocking collectives: 29.8 us -> none  [shards(): lax.all_to_all(outgoing_up, 'dp', split_axis=0, concat_axis=0, tiled=True)]
    ppermute x0 -> x12, starting transfers between devices: none -> 23.4 us  [the longest x6 15.3 us: shift(): return lax.ppermute(x, axis, pairs)]
    all_to_all x1 -> x0, waiting for transfers between devices: 21.8 us -> none  [shards(): lax.all_to_all(outgoing_down, 'dp', split_axis=0, concat_axis=0, tiled=True)]
    gather x6 -> x11, local copies, waits for them, and re-layouts: 11.9 us -> 17 us  [the longest x4 10.5 us: outgoing(): jnp.take(adapter_down, index, axis=0)]
  transfers between devices with their start and end apart: 2 -> 16, of which waited for: 2 -> 9; matrix products, arithmetic and copies ran while one was open for 7% -> 40% of each run, Pallas kernels for 0% -> 0%
where the time goes in v1:
time: 282 us; the launch traced here: 281 us
  matrix products  117 us (41%)
  waiting for transfers between devices  96.8 us (34%)
  starting transfers between devices  23.5 us (8%)
  local copies, waits for them, and re-layouts  20.5 us (7%)
  between operations  13.6 us (5%)
  other arithmetic  10.3 us (4%)
    dot_general x16, matrix products, shards(): jnp.dot(gathered[j][t], weight[t, j], preferred_element_type=f32)  84 us
    all_gather x4, waiting for transfers between devices, shards(): lax.all_gather(packed[:, j * piece:(j + 1) * piece], 'tensor', axis=0)  66 us
    dot_general x1, matrix products, shards(): return jnp.dot(unpack, result, preferred_element_type=f32).astype(bf16)  27.4 us
    ppermute x6, waiting for transfers between devices, shift(): return lax.ppermute(x, axis, pairs)  24.9 us
    ppermute x6, starting transfers between devices, shift(): return lax.ppermute(x, axis, pairs)  15.3 us
    gather x4, local copies, waits for them, and re-layouts, outgoing(): jnp.take(adapter_down, index, axis=0)  10.5 us
    select_n x8, other arithmetic, outgoing(): jnp.take(adapter_down, index, axis=0)  6.54 us
    gather x4, local copies, waits for them, and re-layouts, outgoing(): jnp.take(adapter_up, index, axis=0)  5.66 us
  transfers between devices with their start and end apart: 16, of which 9 were waited for; matrix products, arithmetic and copies ran while one was open for 40% of the time, Pallas kernels for 0%

profile of v1, /device:TPU:0, one launch (start us, length us, event | category | flops | bytes accessed | tf_op | source)
XLA Modules:
  0.0 281.4 jit_solution(12566445834468827545)
XLA Ops:
  8.9 2.0 convolution_convert_fusion.1
  10.9 1.4 copy-done.7
  12.3 1.5 fusion.105
  17.7 2.2 gather_fusion.2
  22.3 2.3 gather_fusion.4
  25.8 1.9 collective-permute-start.2
  27.8 2.3 gather_fusion.7
  30.2 3.0 %gather_fusion.3 = bf16[2,64,2048]{2,1,0:T(8,128)(2,1)} fusion(bf16[8,64,2048]{2,1,0:T(8,128)(2,1)} %param.11, s32[1024]{0:T(1024)S(1)} %pad_clamp_fusion.1), kind=kCustom, calls=%fused_computation.2.clone | custom fusion | bytes 1048584 | tf_op jit(solution)/shard_map/jit(_take)/gather | solution.py:64
  33.1 2.2 broadcast_select_fusion.3
  35.3 2.3 collective-permute-start.1
  37.9 2.2 gather_fusion.5
  40.1 3.0 %gather_fusion.1 = bf16[2,64,2048]{2,1,0:T(8,128)(2,1)} fusion(bf16[8,64,2048]{2,1,0:T(8,128)(2,1)} %param.11, s32[1024]{0:T(1024)S(1)} %pad_clamp_fusion.3), kind=kCustom, calls=%fused_computation.clone | custom fusion | bytes 1048584 | tf_op jit(solution)/shard_map/jit(_take)/gather | solution.py:64
  43.1 2.0 broadcast_select_fusion.7
  45.1 5.1 %collective-permute-done.1 = bf16[2,64,2048]{2,1,0:T(8,128)(2,1)} collective-permute-done((bf16[2,64,2048]{2,1,0:T(8,128)(2,1)}, bf16[2,64,2048]{2,1,0:T(8,128)(2,1)}, u32[]{:S(2)}, u32[]{:S(2)}) %collective-permute-start.1) | collective-permute-done | bytes 524320 | tf_op jit(solution)/shard_map/ppermute | solution.py:72
  50.2 3.3 %select_reduce_fusion = f32[576,64]{0,1:T(8,128)S(1)} fusion(bf16[2,64,2048]{2,1,0:T(8,128)(2,1)} %collective-permute-done.2, bf16[2,64,2048]{2,1,0:T(8,128)(2,1)} %collective-permute-done.1, bf16[2,64,2048]{2,1,0:T(8,128)(2,1)} %collective-permute-done, bf16[2,64,2048]{2,1,0:T(8,128)(2,1)S(1)} %get-tuple-element.29, bf16[576,2048]{1,0:T(8,128)(2,1)S(1)} %copy-done.8, ...), kind=kOutput, calls=%fused_computation.78 | convolution fusion | flops 1216901120 | bytes 4608512 | tf_op jit(solution)/shard_map/dot_general | solution.py:89
  53.5 1.3 collective-permute-start.6
  54.8 4.6 %collective-permute-start.3 = (f32[576,64]{0,1:T(8,128)S(1)}, f32[576,64]{0,1:T(8,128)S(1)}, u32[]{:S(2)}, u32[]{:S(2)}) collective-permute-start(f32[576,64]{0,1:T(8,128)S(1)} %select_reduce_fusion), channel_id=1, source_target_pairs={{0,1},{1,2},{2,3},{4,5},{5,6},{6,7},{8,9},{9,10},{10,11},{12,13},{... | collective-permute-start | bytes 442376 | tf_op jit(solution)/shard_map/ppermute | solution.py:13
  59.4 8.4 %collective-permute-done.6 = f32[576,64]{0,1:T(8,128)S(1)} collective-permute-done((f32[576,64]{0,1:T(8,128)S(1)}, f32[576,64]{0,1:T(8,128)S(1)}, u32[]{:S(2)}, u32[]{:S(2)}) %collective-permute-start.6) | collective-permute-done | bytes 147488 | tf_op jit(solution)/shard_map/ppermute | solution.py:13
  67.8 4.6 %collective-permute-start.4 = (f32[576,64]{0,1:T(8,128)S(1)}, f32[576,64]{0,1:T(8,128)S(1)}, u32[]{:S(2)}, u32[]{:S(2)}) collective-permute-start(f32[576,64]{0,1:T(8,128)S(1)} %get-tuple-element.25), channel_id=1, source_target_pairs={{0,1},{1,2},{2,3},{4,5},{5,6},{6,7},{8,9},{9,10},{10,11},{12,13},{... | collective-permute-start | bytes 442376 | tf_op jit(solution)/shard_map/ppermute | solution.py:13
  72.4 1.3 collective-permute-start.7
  73.7 1.5 collective-permute-done.4
  75.2 4.4 %collective-permute-done.7 = f32[576,64]{0,1:T(8,128)S(1)} collective-permute-done((f32[576,64]{0,1:T(8,128)S(1)}, f32[576,64]{0,1:T(8,128)S(1)}, u32[]{:S(2)}, u32[]{:S(2)}) %collective-permute-start.7) | collective-permute-done | bytes 147488 | tf_op jit(solution)/shard_map/ppermute | solution.py:13
  79.7 2.2 collective-permute-start.5
  81.9 1.3 collective-permute-start.8
  83.3 1.7 collective-permute-start.11
  85.0 1.7 collective-permute-start.10
  86.7 2.2 collective-permute-done.5
  88.9 8.4 %collective-permute-done.8 = f32[576,64]{0,1:T(8,128)S(1)} collective-permute-done((f32[576,64]{0,1:T(8,128)S(1)}, f32[576,64]{0,1:T(8,128)S(1)}, u32[]{:S(2)}, u32[]{:S(2)}) %collective-permute-start.8) | collective-permute-done | bytes 147488 | tf_op jit(solution)/shard_map/ppermute | solution.py:13
  97.4 5.5 %fusion.27 = f32[576,2048]{1,0:T(8,128)} fusion(bf16[4,4,512,2048]{3,2,1,0:T(8,128)(2,1)} %bitcast.110, bf16[2304,512]{1,0:T(8,128)(2,1)} %all-gather.11.cloned.1.call-done), kind=kOutput, calls=%fused_computation.49 | convolution fusion | flops 1207959552 | bytes 7405568 | tf_op jit(solution)/shard_map/dot_general | solution.py:107
  102.8 5.2 %fusion.28 = f32[576,2048]{1,0:T(8,128)} fusion(bf16[4,4,512,2048]{3,2,1,0:T(8,128)(2,1)} %bitcast.111, bf16[2304,512]{1,0:T(8,128)(2,1)S(1)} %copy-done.3), kind=kOutput, calls=%fused_computation.51 | convolution fusion | flops 1207959552 | bytes 7405568 | tf_op jit(solution)/shard_map/dot_general | solution.py:107
  108.1 5.1 %fusion.29 = f32[576,2048]{1,0:T(8,128)} fusion(bf16[4,4,512,2048]{3,2,1,0:T(8,128)(2,1)} %bitcast.112, bf16[2304,512]{1,0:T(8,128)(2,1)S(1)} %copy-done.3), kind=kOutput, calls=%fused_computation.53 | convolution fusion | flops 1207959552 | bytes 7405568 | tf_op jit(solution)/shard_map/dot_general | solution.py:107
  113.2 5.2 %fusion.26 = f32[576,2048]{1,0:T(8,128)} fusion(bf16[4,4,512,2048]{3,2,1,0:T(8,128)(2,1)} %bitcast.113, bf16[2304,512]{1,0:T(8,128)(2,1)S(1)} %copy-done.3), kind=kOutput, calls=%fused_computation.47 | convolution fusion | flops 1207959552 | bytes 7405568 | tf_op jit(solution)/shard_map/dot_general | solution.py:107
  118.3 6.5 %all-gather.13.cloned.1.call-done = bf16[2304,512]{1,0:T(8,128)(2,1)} async-done(((bf16[576,512]{1,0:T(8,128)(2,1)}), bf16[2304,512]{1,0:T(8,128)(2,1)}) %all-gather.13.cloned.1.call-update) | async-done | bytes 2359312 | tf_op jit(solution)/shard_map/all_gather | solution.py:48
  124.8 5.5 %fusion.23 = f32[576,2048]{1,0:T(8,128)} fusion(bf16[4,4,512,2048]{3,2,1,0:T(8,128)(2,1)} %bitcast.114, bf16[2304,512]{1,0:T(8,128)(2,1)} %all-gather.13.cloned.1.call-done), kind=kOutput, calls=%fused_computation.41 | convolution fusion | flops 1207959552 | bytes 7405568 | tf_op jit(solution)/shard_map/dot_general | solution.py:107
  130.3 5.2 %fusion.24 = f32[576,2048]{1,0:T(8,128)} fusion(bf16[4,4,512,2048]{3,2,1,0:T(8,128)(2,1)} %bitcast.115, bf16[2304,512]{1,0:T(8,128)(2,1)S(1)} %copy-done.4), kind=kOutput, calls=%fused_computation.43 | convolution fusion | flops 1207959552 | bytes 7405568 | tf_op jit(solution)/shard_map/dot_general | solution.py:107
  135.5 5.2 %fusion.25 = f32[576,2048]{1,0:T(8,128)} fusion(bf16[4,4,512,2048]{3,2,1,0:T(8,128)(2,1)} %bitcast.116, bf16[2304,512]{1,0:T(8,128)(2,1)S(1)} %copy-done.4), kind=kOutput, calls=%fused_computation.45 | convolution fusion | flops 1207959552 | bytes 7405568 | tf_op jit(solution)/shard_map/dot_general | solution.py:107
  140.7 5.2 %fusion.22 = f32[576,2048]{1,0:T(8,128)} fusion(bf16[4,4,512,2048]{3,2,1,0:T(8,128)(2,1)} %bitcast.117, bf16[2304,512]{1,0:T(8,128)(2,1)S(1)} %copy-done.4), kind=kOutput, calls=%fused_computation.39 | convolution fusion | flops 1207959552 | bytes 7405568 | tf_op jit(solution)/shard_map/dot_general | solution.py:107
  145.9 29.9 %all-gather.15.cloned.1.call-done = bf16[2304,512]{1,0:T(8,128)(2,1)} async-done(((bf16[576,512]{1,0:T(8,128)(2,1)}), bf16[2304,512]{1,0:T(8,128)(2,1)}) %all-gather.15.cloned.1.call-update) | async-done | bytes 2359312 | tf_op jit(solution)/shard_map/all_gather | solution.py:48
  175.8 5.5 %fusion.19 = f32[576,2048]{1,0:T(8,128)} fusion(bf16[4,4,512,2048]{3,2,1,0:T(8,128)(2,1)} %bitcast.118, bf16[2304,512]{1,0:T(8,128)(2,1)} %all-gather.15.cloned.1.call-done), kind=kOutput, calls=%fused_computation.33 | convolution fusion | flops 1207959552 | bytes 7405568 | tf_op jit(solution)/shard_map/dot_general | solution.py:107
  181.3 5.2 %fusion.20 = f32[576,2048]{1,0:T(8,128)} fusion(bf16[4,4,512,2048]{3,2,1,0:T(8,128)(2,1)} %bitcast.119, bf16[2304,512]{1,0:T(8,128)(2,1)S(1)} %copy-done.5), kind=kOutput, calls=%fused_computation.35 | convolution fusion | flops 1207959552 | bytes 7405568 | tf_op jit(solution)/shard_map/dot_general | solution.py:107
  186.4 5.1 %fusion.21 = f32[576,2048]{1,0:T(8,128)} fusion(bf16[4,4,512,2048]{3,2,1,0:T(8,128)(2,1)} %bitcast.120, bf16[2304,512]{1,0:T(8,128)(2,1)S(1)} %copy-done.5), kind=kOutput, calls=%fused_computation.37 | convolution fusion | flops 1207959552 | bytes 7405568 | tf_op jit(solution)/shard_map/dot_general | solution.py:107
  191.5 5.4 %fusion.18 = f32[576,2048]{1,0:T(8,128)} fusion(bf16[4,4,512,2048]{3,2,1,0:T(8,128)(2,1)} %bitcast.121, bf16[2304,512]{1,0:T(8,128)(2,1)S(1)} %copy-done.5), kind=kOutput, calls=%fused_computation.31 | convolution fusion | flops 1207959552 | bytes 7405568 | tf_op jit(solution)/shard_map/dot_general | solution.py:107
  197.0 29.6 %all-gather.9.cloned.1.call-done = bf16[2304,512]{1,0:T(8,128)(2,1)} async-done(((bf16[576,512]{1,0:T(8,128)(2,1)}), bf16[2304,512]{1,0:T(8,128)(2,1)}) %all-gather.9.cloned.1.call-update) | async-done | bytes 2359312 | tf_op jit(solution)/shard_map/all_gather | solution.py:48
  226.6 5.5 %fusion.31 = f32[576,2048]{1,0:T(8,128)} fusion(bf16[4,4,512,2048]{3,2,1,0:T(8,128)(2,1)} %bitcast.122, bf16[2304,512]{1,0:T(8,128)(2,1)} %all-gather.9.cloned.1.call-done), kind=kOutput, calls=%fused_computation.57 | convolution fusion | flops 1207959552 | bytes 7405568 | tf_op jit(solution)/shard_map/dot_general | solution.py:107
  232.0 5.1 %fusion.32 = f32[576,2048]{1,0:T(8,128)} fusion(bf16[4,4,512,2048]{3,2,1,0:T(8,128)(2,1)} %bitcast.123, bf16[2304,512]{1,0:T(8,128)(2,1)S(1)} %copy-done.6), kind=kOutput, calls=%fused_computation.59 | convolution fusion | flops 1207959552 | bytes 7405568 | tf_op jit(solution)/shard_map/dot_general | solution.py:107
  237.1 5.1 %fusion.33 = f32[576,2048]{1,0:T(8,128)} fusion(bf16[4,4,512,2048]{3,2,1,0:T(8,128)(2,1)} %bitcast.124, bf16[2304,512]{1,0:T(8,128)(2,1)S(1)} %copy-done.6), kind=kOutput, calls=%fused_computation.61 | convolution fusion | flops 1207959552 | bytes 7405568 | tf_op jit(solution)/shard_map/dot_general | solution.py:107
  242.2 5.2 %fusion.30 = f32[576,2048]{1,0:T(8,128)} fusion(bf16[4,4,512,2048]{3,2,1,0:T(8,128)(2,1)} %bitcast.125, bf16[2304,512]{1,0:T(8,128)(2,1)S(1)} %copy-done.6), kind=kOutput, calls=%fused_computation.55 | convolution fusion | flops 1207959552 | bytes 7405568 | tf_op jit(solution)/shard_map/dot_general | solution.py:107
  247.4 27.4 %convolution_convert_fusion = bf16[768,2048]{1,0:T(8,128)(2,1)} fusion(s32[768]{0:T(1024)S(1)} %fusion.85, f32[576,2048]{1,0:T(8,128)} %fusion.18, f32[576,2048]{1,0:T(8,128)} %fusion.19, f32[576,2048]{1,0:T(8,128)} %fusion.20, f32[576,2048]{1,0:T(8,128)} %fusion.21, f32[576,2048]{1,0:T(8,128)} %fusion.22, f32[576,2048]{1,0:T(8,128)} %fusion.23, ...), kind=kOutput, calls=%fused_computation.26 | convolution fusion | flops 3045408768 | bytes 80821760 | tf_op jit(solution)/shard_map/dot_general | solution.py:110
  (86 shorter events, 10.2 us)
Async XLA Ops:
  6.5 2.4 copy-start
  6.5 90.8 %all-gather.11.cloned.1.call-start = ((), (), s32[]{:S(2)}) async-start(), calls=%async_computation.1 | async-start | bytes 2949120 | tf_op jit(solution)/shard_map/all_gather | solution.py:48
  10.9 1.4 copy-start.7
  12.3 2.4 copy-start.11
  12.3 2.7 copy-start.2
  12.3 4.8 %copy-start.9 = (bf16[8,64,2048]{2,1,0:T(8,128)(2,1)S(1)}, bf16[8,64,2048]{2,1,0:T(8,128)(2,1)}, u32[]{:S(2)}) copy-start(bf16[8,64,2048]{2,1,0:T(8,128)(2,1)} %param.12) | copy-start | bytes 6291460
  13.8 111.0 %all-gather.13.cloned.1.call-start = ((), (), s32[]{:S(2)}) async-start(), calls=%async_computation.2 | async-start | bytes 2949120 | tf_op jit(solution)/shard_map/all_gather | solution.py:48
  14.6 161.2 %all-gather.15.cloned.1.call-start = ((), (), s32[]{:S(2)}) async-start(), calls=%async_computation.3 | async-start | bytes 2949120 | tf_op jit(solution)/shard_map/all_gather | solution.py:48
  21.0 24.0 %collective-permute-start = (bf16[2,64,2048]{2,1,0:T(8,128)(2,1)}, bf16[2,64,2048]{2,1,0:T(8,128)(2,1)}, u32[]{:S(2)}, u32[]{:S(2)}) collective-permute-start(bf16[2,64,2048]{2,1,0:T(8,128)(2,1)} %get-tuple-element.31), channel_id=1, source_target_pairs={{0,4},{4,8},{8,12},{12,0},{1,5},{5,9},{9,13},{13,1},{2,6},{6,10},{... | collective-permute-start | bytes 1572872 | tf_op jit(solution)/shard_map/ppermute | solution.py:72
  22.3 15.4 %copy-start.12 = (s32[1,6]{1,0:T(1,128)S(1)}, s32[1,6]{1,0:T(1,128)}, u32[]{:S(2)}) copy-start(s32[1,6]{1,0:T(1,128)} %param.15) | copy-start | bytes 76
  25.8 19.3 %collective-permute-start.2 = (bf16[2,64,2048]{2,1,0:T(8,128)(2,1)}, bf16[2,64,2048]{2,1,0:T(8,128)(2,1)}, u32[]{:S(2)}, u32[]{:S(2)}) collective-permute-start(bf16[2,64,2048]{2,1,0:T(8,128)(2,1)} %get-tuple-element.35), channel_id=1, source_target_pairs={{0,12},{4,0},{8,4},{12,8},{1,13},{5,1},{9,5},{13,9},{2,14},{6,2},{... | collective-permute-start | bytes 1572872 | tf_op jit(solution)/shard_map/ppermute | solution.py:72
  27.7 198.8 %all-gather.9.cloned.1.call-start = ((), (), s32[]{:S(2)}) async-start(), calls=%async_computation | async-start | bytes 2949120 | tf_op jit(solution)/shard_map/all_gather | solution.py:48
  27.8 22.4 %copy-start.8 = (bf16[576,2048]{1,0:T(8,128)(2,1)S(1)}, bf16[576,2048]{1,0:T(8,128)(2,1)}, u32[]{:S(2)}) copy-start(bf16[576,2048]{1,0:T(8,128)(2,1)} %copy-done.7) | copy-start | bytes 7077892
  35.3 14.9 %collective-permute-start.1 = (bf16[2,64,2048]{2,1,0:T(8,128)(2,1)}, bf16[2,64,2048]{2,1,0:T(8,128)(2,1)}, u32[]{:S(2)}, u32[]{:S(2)}) collective-permute-start(bf16[2,64,2048]{2,1,0:T(8,128)(2,1)} %get-tuple-element.33), channel_id=1, source_target_pairs={{0,8},{4,12},{8,0},{12,4},{1,9},{5,13},{9,1},{13,5},{2,10},{6,14},... | collective-permute-start | bytes 1572872 | tf_op jit(solution)/shard_map/ppermute | solution.py:72
  50.2 33.0 %copy-start.10 = (bf16[2,64,2048]{2,1,0:T(8,128)(2,1)S(1)}, bf16[2,64,2048]{2,1,0:T(8,128)(2,1)}, u32[]{:S(2)}) copy-start(bf16[2,64,2048]{2,1,0:T(8,128)(2,1)} %get-tuple-element.32) | copy-start | bytes 1572868
  53.5 14.3 %collective-permute-start.6 = (f32[576,64]{0,1:T(8,128)S(1)}, f32[576,64]{0,1:T(8,128)S(1)}, u32[]{:S(2)}, u32[]{:S(2)}) collective-permute-start(f32[576,64]{0,1:T(8,128)S(1)} %select_reduce_fusion), channel_id=1, source_target_pairs={{1,0},{2,1},{3,2},{5,4},{6,5},{7,6},{9,8},{10,9},{11,10},{13,12},{... | collective-permute-start | bytes 442376 | tf_op jit(solution)/shard_map/ppermute | solution.py:13
  54.8 13.0 %collective-permute-start.3 = (f32[576,64]{0,1:T(8,128)S(1)}, f32[576,64]{0,1:T(8,128)S(1)}, u32[]{:S(2)}, u32[]{:S(2)}) collective-permute-start(f32[576,64]{0,1:T(8,128)S(1)} %select_reduce_fusion), channel_id=1, source_target_pairs={{0,1},{1,2},{2,3},{4,5},{5,6},{6,7},{8,9},{9,10},{10,11},{12,13},{... | collective-permute-start | bytes 442376 | tf_op jit(solution)/shard_map/ppermute | solution.py:13
  67.8 7.4 %collective-permute-start.4 = (f32[576,64]{0,1:T(8,128)S(1)}, f32[576,64]{0,1:T(8,128)S(1)}, u32[]{:S(2)}, u32[]{:S(2)}) collective-permute-start(f32[576,64]{0,1:T(8,128)S(1)} %get-tuple-element.25), channel_id=1, source_target_pairs={{0,1},{1,2},{2,3},{4,5},{5,6},{6,7},{8,9},{9,10},{10,11},{12,13},{... | collective-permute-start | bytes 442376 | tf_op jit(solution)/shard_map/ppermute | solution.py:13
  72.4 7.2 %collective-permute-start.7 = (f32[576,64]{0,1:T(8,128)S(1)}, f32[576,64]{0,1:T(8,128)S(1)}, u32[]{:S(2)}, u32[]{:S(2)}) collective-permute-start(f32[576,64]{0,1:T(8,128)S(1)} %get-tuple-element.26), channel_id=1, source_target_pairs={{1,0},{2,1},{3,2},{5,4},{6,5},{7,6},{9,8},{10,9},{11,10},{13,12},{... | collective-permute-start | bytes 442376 | tf_op jit(solution)/shard_map/ppermute | solution.py:13
  79.7 9.2 %collective-permute-start.5 = (f32[576,64]{0,1:T(8,128)S(1)}, f32[576,64]{0,1:T(8,128)S(1)}, u32[]{:S(2)}, u32[]{:S(2)}) collective-permute-start(f32[576,64]{0,1:T(8,128)S(1)} %get-tuple-element.23), channel_id=1, source_target_pairs={{0,1},{1,2},{2,3},{4,5},{5,6},{6,7},{8,9},{9,10},{10,11},{12,13},{... | collective-permute-start | bytes 442376 | tf_op jit(solution)/shard_map/ppermute | solution.py:13
  81.9 15.4 %collective-permute-start.8 = (f32[576,64]{0,1:T(8,128)S(1)}, f32[576,64]{0,1:T(8,128)S(1)}, u32[]{:S(2)}, u32[]{:S(2)}) collective-permute-start(f32[576,64]{0,1:T(8,128)S(1)} %get-tuple-element.24), channel_id=1, source_target_pairs={{1,0},{2,1},{3,2},{5,4},{6,5},{7,6},{9,8},{10,9},{11,10},{13,12},{... | collective-permute-start | bytes 442376 | tf_op jit(solution)/shard_map/ppermute | solution.py:13
  83.2 164.2 %collective-permute-start.9 = (bf16[2,64,2048]{2,1,0:T(8,128)(2,1)S(1)}, bf16[2,64,2048]{2,1,0:T(8,128)(2,1)}, u32[]{:S(2)}, u32[]{:S(2)}) collective-permute-start(bf16[2,64,2048]{2,1,0:T(8,128)(2,1)S(1)} %copy-done.10), channel_id=1, source_target_pairs={{0,4},{4,8},{8,12},{12,0},{1,5},{5,9},{9,13},{13,1},{2,6},{6,10},{... | collective-permute-start | bytes 1572872 | tf_op jit(solution)/shard_map/ppermute | solution.py:73
  83.3 164.1 %collective-permute-start.11 = (bf16[2,64,2048]{2,1,0:T(8,128)(2,1)}, bf16[2,64,2048]{2,1,0:T(8,128)(2,1)}, u32[]{:S(2)}, u32[]{:S(2)}) collective-permute-start(bf16[2,64,2048]{2,1,0:T(8,128)(2,1)} %get-tuple-element.36), channel_id=1, source_target_pairs={{0,12},{4,0},{8,4},{12,8},{1,13},{5,1},{9,5},{13,9},{2,14},{6,2},{... | collective-permute-start | bytes 1572872 | tf_op jit(solution)/shard_map/ppermute | solution.py:73
  85.0 162.4 %collective-permute-start.10 = (bf16[2,64,2048]{2,1,0:T(8,128)(2,1)}, bf16[2,64,2048]{2,1,0:T(8,128)(2,1)}, u32[]{:S(2)}, u32[]{:S(2)}) collective-permute-start(bf16[2,64,2048]{2,1,0:T(8,128)(2,1)} %get-tuple-element.34), channel_id=1, source_target_pairs={{0,8},{4,12},{8,0},{12,4},{1,9},{5,13},{9,1},{13,5},{2,10},{6,14},... | collective-permute-start | bytes 1572872 | tf_op jit(solution)/shard_map/ppermute | solution.py:73
  97.4 5.5 %copy-start.3 = (bf16[2304,512]{1,0:T(8,128)(2,1)S(1)}, bf16[2304,512]{1,0:T(8,128)(2,1)}, u32[]{:S(2)}) copy-start(bf16[2304,512]{1,0:T(8,128)(2,1)} %all-gather.11.cloned.1.call-done) | copy-start | bytes 7077892
  124.8 5.5 %copy-start.4 = (bf16[2304,512]{1,0:T(8,128)(2,1)S(1)}, bf16[2304,512]{1,0:T(8,128)(2,1)}, u32[]{:S(2)}) copy-start(bf16[2304,512]{1,0:T(8,128)(2,1)} %all-gather.13.cloned.1.call-done) | copy-start | bytes 7077892
  175.8 5.5 %copy-start.5 = (bf16[2304,512]{1,0:T(8,128)(2,1)S(1)}, bf16[2304,512]{1,0:T(8,128)(2,1)}, u32[]{:S(2)}) copy-start(bf16[2304,512]{1,0:T(8,128)(2,1)} %all-gather.15.cloned.1.call-done) | copy-start | bytes 7077892
  226.6 5.5 %copy-start.6 = (bf16[2304,512]{1,0:T(8,128)(2,1)S(1)}, bf16[2304,512]{1,0:T(8,128)(2,1)}, u32[]{:S(2)}) copy-start(bf16[2304,512]{1,0:T(8,128)(2,1)} %all-gather.9.cloned.1.call-done) | copy-start | bytes 7077892
  247.4 27.5 %copy-start.1 = (bf16[768,2048]{1,0:T(8,128)(2,1)S(1)}, bf16[768,2048]{1,0:T(8,128)(2,1)}, u32[]{:S(2)}) copy-start(bf16[768,2048]{1,0:T(8,128)(2,1)} %param.9) | copy-start | bytes 9437188
Sparse Core Ops, SparseCore 0:
  13.9 56.6 all-gather.10
  72.2 52.5 all-gather.12
  126.4 49.3 all-gather.14
  177.2 49.2 all-gather.8

commit v2 on v0

v2 whole, which is shorter than its diff:
```python
import functools

import jax
import jax.numpy as jnp
from jax import lax
from jax.experimental import pallas as pl
from jax.experimental.pallas import tpu as pltpu
from jax.sharding import PartitionSpec as P

adapter_scale = 2.0
live_total = 576
chunk_width = 1024
column_tile = 512
vmem_bytes = 48 * 1024 * 1024
bf16, f32, i32 = jnp.bfloat16, jnp.float32, jnp.int32

smem = pl.BlockSpec(memory_space=pltpu.SMEM)
hbm = pl.BlockSpec(memory_space=pl.ANY)


def params():
    return pltpu.CompilerParams(vmem_limit_bytes=vmem_bytes)


def cost(flops, moved):
    return pl.CostEstimate(flops=int(flops), bytes_accessed=int(moved), transcendentals=0)


def shift(x, axis, step, size, first, last):
    pairs = [(i, i + step) for i in range(first, last + 1) if 0 <= i + step < size]
    return lax.ppermute(x, axis, pairs)


def one_hot(live, rows, axis):
    blocks = live.shape[1]
    block = rows // blocks
    flat = (1, rows) if axis else (rows, 1)
    row = lax.broadcasted_iota(i32, flat, axis)
    place = jnp.full(flat, -1, i32)
    start = 0
    for b in range(blocks):
        inside = row - b * block
        here = (inside >= 0) & (inside < live[0, b])
        place = jnp.where(here, inside + start, place)
        start = start + live[0, b]
    shape = (live_total, rows) if axis else (rows, live_total)
    return (lax.broadcasted_iota(i32, shape, 1 - axis) == place).astype(f32).astype(bf16)


def pack_kernel(live, x, out):
    hot = one_hot(live, x.shape[0], 1)
    out[...] = jnp.dot(hot, x[...], preferred_element_type=f32).astype(bf16)


def pack(hidden, live, j, piece):
    rows = hidden.shape[0]
    return pl.pallas_call(
        pack_kernel,
        grid=(1,),
        in_specs=[smem, pl.BlockSpec((rows, piece), lambda i: (0, j))],
        out_specs=pl.BlockSpec((live_total, piece), lambda i: (0, 0)),
        out_shape=jax.ShapeDtypeStruct((live_total, piece), bf16),
        compiler_params=params(),
        cost_estimate=cost(2 * rows * live_total * piece, (rows + live_total) * piece * 2),
        name="pack",
    )(live, hidden)


def choose_kernel(variants, slots, down, up, *rest, replicas, capacity, blocks):
    outs, sems = rest[:replicas], rest[replicas]
    pool, rank = down.shape[0], down.shape[1]
    me = lax.axis_index("dp")
    copies = []
    for step in range(replicas):
        target = lax.rem(me + step, replicas)
        seen = jnp.int32(0)
        index = [jnp.int32(0)] * capacity
        for b in range(blocks):
            slot = slots[variants[target, b]]
            owner = lax.div(slot, pool)
            mine = owner == me
            for m in range(capacity):
                index[m] = jnp.where(mine & (seen == m), slot - owner * pool, index[m])
            seen = seen + mine.astype(i32)
        for m in range(capacity):
            for kind, source in enumerate((down, up)):
                copies.append(
                    pltpu.make_async_copy(
                        source.at[index[m]],
                        outs[step].at[kind, m * rank : (m + 1) * rank],
                        sems.at[len(copies)],
                    )
                )
                copies[-1].start()
    for copy in copies:
        copy.wait()


def choose(variants, slots, down, up, replicas, capacity):
    pool, rank, width = down.shape
    out = jax.ShapeDtypeStruct((2, capacity * rank, width), bf16)
    return pl.pallas_call(
        functools.partial(
            choose_kernel, replicas=replicas, capacity=capacity, blocks=variants.shape[1]
        ),
        in_specs=[smem, smem, hbm, hbm],
        out_specs=[hbm] * replicas,
        out_shape=[out] * replicas,
        scratch_shapes=[pltpu.SemaphoreType.DMA((replicas * capacity * 2,))],
        compiler_params=params(),
        cost_estimate=cost(0, replicas * capacity * rank * width * 8),
        name="choose",
    )(variants, slots, down, up)


def row_groups(variants, slots, live, shape, axis, replicas, capacity, pool):
    me = lax.axis_index("dp")
    blocks = live.shape[1]
    row = lax.broadcasted_iota(i32, shape, axis)
    group = jnp.zeros(shape, i32)
    start = 0
    owners = []
    for b in range(blocks):
        owner = lax.div(slots[variants[me, b]], pool)
        nth = sum([(o == owner).astype(i32) for o in owners], jnp.int32(0))
        owners.append(owner)
        mine = lax.rem(me - owner + replicas, replicas) * capacity + nth
        group = jnp.where(row >= start, mine, group)
        start = start + live[0, b]
    return group


def shrink_kernel(variants, slots, live, *rest, replicas, capacity, pool, chunks):
    xs, downs, out = rest[:chunks], rest[chunks : chunks + replicas], rest[-1]
    depth = downs[0].shape[1]
    rank = out.shape[0]
    piece = xs[0].shape[1]
    shape = (depth, live_total)
    group = row_groups(variants, slots, live, shape, 1, replicas, capacity, pool)
    nth = lax.broadcasted_iota(i32, shape, 0) // rank
    total = jnp.zeros(shape, f32)
    for o in range(replicas):
        part = jnp.zeros(shape, f32)
        for j in range(chunks):
            part = part + lax.dot_general(
                downs[o][0, :, j * piece : (j + 1) * piece],
                xs[j][...],
                (((1,), (1,)), ((), ())),
                preferred_element_type=f32,
            )
        total = total + jnp.where(group == o * capacity + nth, part, 0.0)
    result = total[:rank]
    for m in range(1, capacity):
        result = result + total[m * rank : (m + 1) * rank]
    out[...] = result


def shrink(variants, slots, live, xs, factors, capacity, pool):
    replicas = len(factors)
    depth, width = factors[0].shape[1:]
    rank = depth // capacity
    whole = pl.BlockSpec(memory_space=pltpu.VMEM)
    down = pl.BlockSpec((1, depth, width), lambda i: (0, 0, 0))
    return pl.pallas_call(
        functools.partial(
            shrink_kernel, replicas=replicas, capacity=capacity, pool=pool, chunks=len(xs)
        ),
        grid=(1,),
        in_specs=[smem] * 3
        + [pl.BlockSpec(x.shape, lambda i: (0, 0)) for x in xs]
        + [down] * replicas,
        out_specs=pl.BlockSpec((rank, live_total), lambda i: (0, 0)),
        out_shape=jax.ShapeDtypeStruct((rank, live_total), f32),
        compiler_params=params(),
        cost_estimate=cost(
            2 * live_total * width * depth * replicas, (live_total + depth * replicas) * width * 2
        ),
        name="shrink",
    )(variants, slots, live, *xs, *factors)


def project_kernel(*refs, count, has_total, delta, last, replicas, capacity, pool):
    refs = list(refs)
    meta = refs.pop(0)
    variants, slots, live = refs[:3]
    refs = refs[3:]
    total = refs.pop(0) if has_total else None
    xs, ws = refs[:count], refs[count : 2 * count]
    refs = refs[2 * count :]
    if delta:
        low, ups = refs[0], refs[1 : 1 + replicas]
        refs = refs[1 + replicas :]
    out = refs.pop(0)
    held = refs.pop(0) if last else out

    if has_total:
        held[...] = total[...]
    else:
        held[...] = jnp.zeros(held.shape, f32)
    for s in range(count):

        @pl.when(meta[2 * s + 1] > 0)
        def _(s=s):
            held[...] += jnp.dot(xs[s][...], ws[s][...], preferred_element_type=f32)

    if delta:
        depth = ups[0].shape[1]
        shape = (live_total, depth)
        group = row_groups(variants, slots, live, shape, 0, replicas, capacity, pool)
        nth = lax.broadcasted_iota(i32, shape, 1) // (depth // capacity)
        wide = jnp.concatenate([low[...]] * capacity, axis=1) * adapter_scale
        for o in range(replicas):
            spread = jnp.where(group == o * capacity + nth, wide, 0.0).astype(bf16)
            held[...] += jnp.dot(spread, ups[o][0], preferred_element_type=f32)
    if last:
        hot = one_hot(live, out.shape[0], 0)
        result = held[...].astype(bf16)
        out[...] = jnp.dot(hot, result, preferred_element_type=f32).astype(bf16)


def project(meta, ints, total, xs, weight, sizes, low=None, factors=None, rows=None):
    replicas, capacity, pool = sizes
    columns = weight.shape[1]
    tile = min(column_tile, columns)
    count = len(xs)
    in_specs = [smem] * 3
    args = list(ints)
    if total is not None:
        in_specs.append(pl.BlockSpec((live_total, tile), lambda i, m: (0, i)))
        args.append(total)
    for x in xs:
        in_specs.append(pl.BlockSpec(x.shape, lambda i, m: (0, 0)))
        args.append(x)
    for s, x in enumerate(xs):
        in_specs.append(pl.BlockSpec((x.shape[1], tile), lambda i, m, s=s: (m[2 * s], i)))
        args.append(weight)
    flops = sum(2 * live_total * x.shape[1] * columns for x in xs)
    moved = sum(x.size * 2 + x.shape[1] * columns * 2 for x in xs) + live_total * columns * 8
    if low is not None:
        in_specs.append(pl.BlockSpec(low.shape, lambda i, m: (0, 0)))
        args.append(low)
        for u in factors:
            in_specs.append(pl.BlockSpec((1, u.shape[1], tile), lambda i, m: (1, 0, i)))
            args.append(u)
            flops += 2 * live_total * u.shape[1] * columns
    scratch = []
    if rows is None:
        out = jax.ShapeDtypeStruct((live_total, columns), f32)
        out_spec = pl.BlockSpec((live_total, tile), lambda i, m: (0, i))
    else:
        out = jax.ShapeDtypeStruct((rows, columns), bf16)
        out_spec = pl.BlockSpec((rows, tile), lambda i, m: (0, i))
        scratch = [pltpu.VMEM((live_total, tile), f32)]
    return pl.pallas_call(
        functools.partial(
            project_kernel,
            count=count,
            has_total=total is not None,
            delta=low is not None,
            last=rows is not None,
            replicas=replicas,
            capacity=capacity,
            pool=pool,
        ),
        grid_spec=pltpu.PrefetchScalarGridSpec(
            num_scalar_prefetch=1,
            grid=(columns // tile,),
            in_specs=in_specs,
            out_specs=out_spec,
            scratch_shapes=scratch,
        ),
        out_shape=out,
        compiler_params=params(),
        cost_estimate=cost(flops, moved),
        name="project",
    )(meta, *args)


def shards(
    hidden,
    query_weight,
    adapter_down,
    adapter_up,
    block_variant_index,
    variant_pool_slot,
    block_live_count,
):
    replicas = lax.axis_size("dp")
    tensor = lax.axis_size("tensor")
    place = lax.axis_index("tensor")
    pool = adapter_down.shape[0]
    blocks = block_variant_index.shape[1]
    rows, width = hidden.shape
    capacity = (blocks + replicas - 1) // replicas
    piece = min(chunk_width, width)
    chunks = width // piece
    ints = (block_variant_index, variant_pool_slot, block_live_count)
    sizes = (replicas, capacity, pool)

    own = [pack(hidden, block_live_count, j, piece) for j in range(chunks)]

    right, left = [own], [own]
    for step in range(1, tensor):
        right.append([shift(x, "tensor", 1, tensor, step - 1, tensor - 2) for x in right[-1]])
        left.append([shift(x, "tensor", -1, tensor, 1, tensor - step) for x in left[-1]])

    factors = choose(block_variant_index, variant_pool_slot, adapter_down, adapter_up, replicas, capacity)
    got = [factors[0]]
    for step in range(1, replicas):
        pairs = [(i, (i + step) % replicas) for i in range(replicas)]
        got.append(lax.ppermute(factors[step], "dp", pairs))
    partial = shrink(*ints, own, got, capacity, pool)
    before, after = jnp.zeros_like(partial), jnp.zeros_like(partial)
    for step in range(1, tensor):
        before = lax.ppermute(partial + before, "tensor", [(i, i + 1) for i in range(tensor - 1)])
        after = lax.ppermute(partial + after, "tensor", [(i, i - 1) for i in range(1, tensor)])
    low = (before + partial + after).astype(bf16).astype(f32).T

    def meta(items):
        pairs = []
        for source, j in items:
            there = (source >= 0) & (source < tensor)
            pairs += [jnp.clip(source, 0, tensor - 1) * chunks + j, there.astype(i32)]
        return jnp.stack([jnp.asarray(p, i32) for p in pairs])

    items = [(place, j) for j in range(chunks)]
    total = project(meta(items), ints, None, own, query_weight, sizes)
    for step in range(1, tensor):
        pieces = [range(chunks)] if step < tensor - 1 else [[j] for j in range(chunks)]
        for js in pieces:
            items = [(place - step, j) for j in js] + [(place + step, j) for j in js]
            xs = [right[step][j] for j in js] + [left[step][j] for j in js]
            final = step == tensor - 1 and js[-1] == chunks - 1
            with_delta = step == tensor - 1 and js[0] == 0
            total = project(
                meta(items),
                ints,
                total,
                xs,
                query_weight,
                sizes,
                low if with_delta else None,
                got if with_delta else None,
                rows if final else None,
            )
    return total


def solution(mesh):
    return jax.shard_map(
        shards,
        mesh=mesh,
        in_specs=(
            P(("groups", "dp"), "tensor"),
            P(None, "tensor"),
            P("dp", None, "tensor"),
            P("dp", None, "tensor"),
            P("groups", None),
            P("groups"),
            P(("groups", "dp"), None),
        ),
        out_specs=P(("groups", "dp"), "tensor"),
        check_vma=False,
    )
```

time: 278 us -> 235 us (0.85)
  Pallas kernels: 0 us -> 74.2 us
  blocking collectives: 69 us -> 0 us
  starting transfers between devices: 3.74 us -> 45.3 us
  matrix products: 37.8 us -> 0 us
  waiting for transfers between devices: 137 us -> 102 us
  between operations: 13.5 us -> 0.27 us
  local copies, waits for them, and re-layouts: 12.3 us -> 5.65 us
    all_gather x1 -> x0, waiting for transfers between devices: 114 us -> none  [shards(): lax.all_gather(hidden, 'tensor', axis=1, tiled=True)]
    ppermute x0 -> x21, waiting for transfers between devices: none -> 102 us  [the longest x3 47.1 us: shards(): lax.ppermute(partial + after, 'tensor', [(i, i - 1) for i in range(1, ten...]
    pallas_call x0 -> x9, Pallas kernels: none -> 74.2 us  [the longest x5 62.3 us: project(): pl.pallas_call(functools.partial(project_kernel, count=count, has_total=t...]
    ppermute x0 -> x21, starting transfers between devices: none -> 45.3 us  [the longest x12 22.6 us: shift(): return lax.ppermute(x, axis, pairs)]
    psum x1 -> x0, blocking collectives: 39.2 us -> none  [shards(): down_projected = lax.psum(partial_value, 'tensor').astype(jnp.bfloat16)]
    dot_general x3 -> x0, matrix products: 37.8 us -> none  [the longest x1 31.4 us: shards(): jnp.dot(lax.all_gather(hidden, 'tensor', axis=1, tiled=True), query_weigh...]
    all_to_all x1 -> x0, blocking collectives: 29.8 us -> none  [shards(): lax.all_to_all(outgoing_up, 'dp', split_axis=0, concat_axis=0, tiled=True)]
    all_to_all x1 -> x0, waiting for transfers between devices: 21.8 us -> none  [shards(): lax.all_to_all(outgoing_down, 'dp', split_axis=0, concat_axis=0, tiled=True)]
  transfers between devices with their start and end apart: 2 -> 21, of which waited for: 2 -> 8; matrix products, arithmetic and copies ran while one was open for 7% -> 3% of each run, Pallas kernels for 0% -> 26%
where the time goes in v2:
time: 235 us; the launch traced here: 234 us
  waiting for transfers between devices  102 us (43%)
  Pallas kernels  74.2 us (32%)
  starting transfers between devices  45.3 us (19%)
  other arithmetic  5.99 us (3%)
  local copies, waits for them, and re-layouts  5.65 us (2%)
    pallas_call x5, Pallas kernels, project(): pl.pallas_call(functools.partial(project_kernel, count=count, has_total=t...  62.3 us
    ppermute x3, waiting for transfers between devices, shards(): lax.ppermute(partial + after, 'tensor', [(i, i - 1) for i in range(1, ten...  47.1 us
    ppermute x3, waiting for transfers between devices, shards(): got.append(lax.ppermute(factors[step], 'dp', pairs))  26.5 us
    ppermute x12, starting transfers between devices, shift(): return lax.ppermute(x, axis, pairs)  22.6 us
    ppermute x12, waiting for transfers between devices, shift(): return lax.ppermute(x, axis, pairs)  19.6 us
    ppermute x3, starting transfers between devices, shards(): lax.ppermute(partial + before, 'tensor', [(i, i + 1) for i in range(tenso...  14.1 us
    ppermute x3, waiting for transfers between devices, shards(): lax.ppermute(partial + before, 'tensor', [(i, i + 1) for i in range(tenso...  9.03 us
  transfers between devices with their start and end apart: 21, of which 8 were waited for; matrix products, arithmetic and copies ran while one was open for 3% of the time, Pallas kernels for 26%

profile of v2, /device:TPU:0, one launch (start us, length us, event | category | flops | bytes accessed | tf_op | source)
XLA Modules:
  0.0 233.6 jit_solution(8788221276908906847)
XLA Ops:
  0.0 0.8 copy-done.5
  0.8 0.8 copy-done.8
  1.6 3.1 %choose.1 = (bf16[2,128,2048]{2,1,0:T(8,128)(2,1)S(1)}, bf16[2,128,2048]{2,1,0:T(8,128)(2,1)S(1)}, bf16[2,128,2048]{2,1,0:T(8,128)(2,1)S(1)}, bf16[2,128,2048]{2,1,0:T(8,128)(2,1)S(1)}) custom-call(s32[4,6]{1,0:T(4,128)S(1)} %copy-done.5, s32[32]{0:T(128)S(1)} %copy-done.8, bf16[8,64,2048]{2,1,0:T(8,128)(2,1)} %down.1, bf16[8,64,2048]{2,1,0:T(8,128)(2,1)} %up.1), custom_call_target="tpu_custom_call" | custom-call | bytes 8388608 | tf_op jit(solution)/shard_map/choose/pallas_call | solution.py:102
  4.7 0.3 collective-permute-start.10
  5.0 2.9 %collective-permute-start.11 = (bf16[2,128,2048]{2,1,0:T(8,128)(2,1)S(1)}, bf16[2,128,2048]{2,1,0:T(8,128)(2,1)S(1)}, u32[]{:S(2)}, u32[]{:S(2)}) collective-permute-start(bf16[2,128,2048]{2,1,0:T(8,128)(2,1)S(1)} %get-tuple-element.11), channel_id=1, source_target_pairs={{0,8},{4,12},{8,0},{12,4},{1,9},{5,13},{9,1},{13,5},{2,10},{6,14},... | collective-permute-start | bytes 3145736 | tf_op jit(solution)/shard_map/ppermute | solution.py:311
  7.9 1.4 collective-permute-start.12
  9.3 1.6 pack.2.refs_4_.rest_0_
  10.9 4.5 %collective-permute-start = (bf16[576,1024]{1,0:T(8,128)(2,1)S(1)}, bf16[576,1024]{1,0:T(8,128)(2,1)}, u32[]{:S(2)}, u32[]{:S(2)}) collective-permute-start(bf16[576,1024]{1,0:T(8,128)(2,1)S(1)} %pack.2.refs_4_.rest_0_), channel_id=1, source_target_pairs={{0,1},{1,2},{2,3},{4,5},{5,6},{6,7},{8,9},{9,10},{10,11},{12,13},{... | collective-permute-start | bytes 3538952 | tf_op jit(solution)/shard_map/ppermute | solution.py:31
  15.4 1.3 collective-permute-start.2
  16.7 2.6 %pack.3.refs_5_.rest_1_ = bf16[576,1024]{1,0:T(8,128)(2,1)} custom-call(s32[1,6]{1,0:T(1,128)S(1)} %copy-done.7, bf16[768,2048]{1,0:T(8,128)(2,1)S(1)} %copy-done), custom_call_target="tpu_custom_call" | custom-call | flops 905969664 | bytes 2752512 | tf_op jit(solution)/shard_map/pack/pallas_call | solution.py:57
  19.4 10.1 %collective-permute-done.10.rest_3_.refs_11_ = bf16[2,128,2048]{2,1,0:T(8,128)(2,1)S(1)} collective-permute-done((bf16[2,128,2048]{2,1,0:T(8,128)(2,1)S(1)}, bf16[2,128,2048]{2,1,0:T(8,128)(2,1)S(1)}, u32[]{:S(2)}, u32[]{:S(2)}) %collective-permute-start.10) | collective-permute-done | bytes 1048608 | tf_op jit(solution)/shard_map/ppermute | solution.py:311
  29.4 6.1 %collective-permute-start.1 = (bf16[576,1024]{1,0:T(8,128)(2,1)}, bf16[576,1024]{1,0:T(8,128)(2,1)}, u32[]{:S(2)}, u32[]{:S(2)}) collective-permute-start(bf16[576,1024]{1,0:T(8,128)(2,1)} %pack.3.refs_5_.rest_1_), channel_id=1, source_target_pairs={{0,1},{1,2},{2,3},{4,5},{5,6},{6,7},{8,9},{9,10},{10,11},{12,13},{... | collective-permute-start | bytes 3538952 | tf_op jit(solution)/shard_map/ppermute | solution.py:31
  35.6 1.3 collective-permute-start.3
  36.9 16.4 %collective-permute-done.12.rest_5_.refs_13_ = bf16[2,128,2048]{2,1,0:T(8,128)(2,1)S(1)} collective-permute-done((bf16[2,128,2048]{2,1,0:T(8,128)(2,1)S(1)}, bf16[2,128,2048]{2,1,0:T(8,128)(2,1)S(1)}, u32[]{:S(2)}, u32[]{:S(2)}) %collective-permute-start.12) | collective-permute-done | bytes 1048608 | tf_op jit(solution)/shard_map/ppermute | solution.py:311
  53.3 4.6 %shrink.1 = f32[64,576]{1,0:T(8,128)S(1)} custom-call(s32[4,6]{1,0:T(4,128)S(1)} %copy-done.6, s32[32]{0:T(128)S(1)} %copy-done.9, s32[1,6]{1,0:T(1,128)S(1)} %copy-done.7, bf16[576,1024]{1,0:T(8,128)(2,1)S(1)} %pack.2.refs_4_.rest_0_, bf16[576,1024]{1,0:T(8,128)(2,1)} %pack.3.refs_5_.rest_1_, bf16[2,128,2048]{2,1,0:T(8,128)(2,1)S(1)} %get-tuple-element.9.rest_2_.refs_10_, ...), custom_call_target="tpu_custom_call" | custom-call | flops 1207959552 | bytes 4456448 | tf_op jit(solution)/shard_map/shrink/pallas_call | solution.py:164
  57.9 0.9 copy-done.1
  58.8 1.0 copy-done.3
  59.8 0.9 copy.10
  60.7 3.5 %collective-permute-start.13 = (f32[64,576]{0,1:T(8,128)}, f32[64,576]{0,1:T(8,128)S(1)}, u32[]{:S(2)}, u32[]{:S(2)}) collective-permute-start(f32[64,576]{0,1:T(8,128)} %copy.10), channel_id=1, source_target_pairs={{0,1},{1,2},{2,3},{4,5},{5,6},{6,7},{8,9},{9,10},{10,11},{12,13},{... | collective-permute-start | bytes 442376 | tf_op jit(solution)/shard_map/ppermute | solution.py:315
  64.2 1.7 collective-permute-start.4
  66.0 1.3 collective-permute-start.6
  67.2 3.1 %collective-permute-done.13 = f32[64,576]{0,1:T(8,128)S(1)} collective-permute-done((f32[64,576]{0,1:T(8,128)}, f32[64,576]{0,1:T(8,128)S(1)}, u32[]{:S(2)}, u32[]{:S(2)}) %collective-permute-start.13) | collective-permute-done | bytes 147488 | tf_op jit(solution)/shard_map/ppermute | solution.py:315
  70.3 1.3 collective-permute-start.16
  71.6 1.7 add.64
  73.3 30.0 %collective-permute-done.16 = f32[64,576]{0,1:T(8,128)} collective-permute-done((f32[64,576]{0,1:T(8,128)}, f32[64,576]{0,1:T(8,128)}, u32[]{:S(2)}, u32[]{:S(2)}) %collective-permute-start.16) | collective-permute-done | bytes 147488 | tf_op jit(solution)/shard_map/ppermute | solution.py:316
  103.3 4.9 %collective-permute-start.14 = (f32[64,576]{0,1:T(8,128)}, f32[64,576]{0,1:T(8,128)}, u32[]{:S(2)}, u32[]{:S(2)}) collective-permute-start(f32[64,576]{0,1:T(8,128)} %add.64), channel_id=1, source_target_pairs={{0,1},{1,2},{2,3},{4,5},{5,6},{6,7},{8,9},{9,10},{10,11},{12,13},{... | collective-permute-start | bytes 442376 | tf_op jit(solution)/shard_map/ppermute | solution.py:315
  108.3 6.0 %collective-permute-done.14 = f32[64,576]{0,1:T(8,128)} collective-permute-done((f32[64,576]{0,1:T(8,128)}, f32[64,576]{0,1:T(8,128)}, u32[]{:S(2)}, u32[]{:S(2)}) %collective-permute-start.14) | collective-permute-done | bytes 147488 | tf_op jit(solution)/shard_map/ppermute | solution.py:315
  114.2 2.0 fusion
  116.2 1.3 collective-permute-start.17
  117.5 5.8 %collective-permute-start.15 = (f32[64,576]{0,1:T(8,128)}, f32[64,576]{0,1:T(8,128)}, u32[]{:S(2)}, u32[]{:S(2)}) collective-permute-start(f32[64,576]{0,1:T(8,128)} %get-tuple-element.13), channel_id=1, source_target_pairs={{0,1},{1,2},{2,3},{4,5},{5,6},{6,7},{8,9},{9,10},{10,11},{12,13},{... | collective-permute-start | bytes 442376 | tf_op jit(solution)/shard_map/ppermute | solution.py:315
  123.3 10.5 %project.5.refs_4_ = f32[576,2048]{1,0:T(8,128)} custom-call(s32[4]{0:T(128)S(1)} %pad_add_fusion.refs_0_, s32[4,6]{1,0:T(4,128)S(1)} %copy-done.6, s32[32]{0:T(128)S(1)} %copy-done.9, s32[1,6]{1,0:T(1,128)S(1)} %copy-done.7, bf16[576,1024]{1,0:T(8,128)(2,1)S(1)} %pack.2.refs_4_.rest_0_, bf16[576,1024]{1,0:T(8,128)(2,1)} %pack.3.refs_5_.rest_1_, ...), custom_call_target="tpu_custom_call" | custom-call | flops 4831838208 | bytes 20185088 | tf_op jit(solution)/shard_map/project/pallas_call | solution.py:254
  133.8 0.7 collective-permute-start.5
  134.5 1.3 collective-permute-start.7
  136.1 1.1 add.68
  137.2 1.4 collective-permute-start.18
  138.7 0.7 collective-permute-start.8
  139.4 1.3 collective-permute-start.9
  140.7 14.8 %project.6.refs_4_ = f32[576,2048]{1,0:T(8,128)} custom-call(s32[8]{0:T(128)S(1)} %stack.133.refs_0_, s32[4,6]{1,0:T(4,128)S(1)} %copy-done.6, s32[32]{0:T(128)S(1)} %copy-done.9, s32[1,6]{1,0:T(1,128)S(1)} %copy-done.7, f32[576,2048]{1,0:T(8,128)} %project.5.refs_4_, bf16[576,1024]{1,0:T(8,128)(2,1)} %collective-permute-done.refs_5_, ...), custom_call_target="tpu_custom_call" | custom-call | flops 9663676416 | bytes 30932992 | tf_op jit(solution)/shard_map/project/pallas_call | solution.py:254
  155.5 17.1 %collective-permute-done.18 = f32[64,576]{0,1:T(8,128)S(1)} collective-permute-done((f32[64,576]{0,1:T(8,128)S(1)}, f32[64,576]{0,1:T(8,128)S(1)}, u32[]{:S(2)}, u32[]{:S(2)}) %collective-permute-start.18) | collective-permute-done | bytes 147488 | tf_op jit(solution)/shard_map/ppermute | solution.py:316
  172.6 1.0 convert_bitcast_fusion.refs_9_
  173.7 0.9 collective-permute-start.19
  174.6 1.5 collective-permute-start.20
  176.1 14.5 %project.7.refs_4_ = f32[576,2048]{1,0:T(8,128)} custom-call(s32[8]{0:T(128)S(1)} %stack.124.refs_0_, s32[4,6]{1,0:T(4,128)S(1)} %copy-done.6, s32[32]{0:T(128)S(1)} %copy-done.9, s32[1,6]{1,0:T(1,128)S(1)} %copy-done.7, f32[576,2048]{1,0:T(8,128)} %project.6.refs_4_, bf16[576,1024]{1,0:T(8,128)(2,1)} %collective-permute-done.4.refs_5_, ...), custom_call_target="tpu_custom_call" | custom-call | flops 9663676416 | bytes 30932992 | tf_op jit(solution)/shard_map/project/pallas_call | solution.py:254
  190.5 7.4 %collective-permute-done.9.refs_6_ = bf16[576,1024]{1,0:T(8,128)(2,1)S(1)} collective-permute-done((bf16[576,1024]{1,0:T(8,128)(2,1)}, bf16[576,1024]{1,0:T(8,128)(2,1)S(1)}, u32[]{:S(2)}, u32[]{:S(2)}) %collective-permute-start.9) | collective-permute-done | bytes 1179680 | tf_op jit(solution)/shard_map/ppermute | solution.py:31
  197.9 1.0 copy-done.11
  198.9 11.7 %project.8.refs_4_ = f32[576,2048]{1,0:T(8,128)} custom-call(s32[4]{0:T(128)S(1)} %get-tuple-element.16.refs_0_, s32[4,6]{1,0:T(4,128)S(1)} %copy-done.6, s32[32]{0:T(128)S(1)} %copy-done.9, s32[1,6]{1,0:T(1,128)S(1)} %copy-done.7, f32[576,2048]{1,0:T(8,128)} %project.7.refs_4_, bf16[576,1024]{1,0:T(8,128)(2,1)S(1)} %collective-permute-done.8.refs_5_, ...), custom_call_target="tpu_custom_call" | custom-call | flops 6039797760 | bytes 20185088 | tf_op jit(solution)/shard_map/project/pallas_call | solution.py:254
  210.6 12.2 %collective-permute-done.20.refs_6_ = bf16[576,1024]{1,0:T(8,128)(2,1)S(1)} collective-permute-done((bf16[576,1024]{1,0:T(8,128)(2,1)}, bf16[576,1024]{1,0:T(8,128)(2,1)S(1)}, u32[]{:S(2)}, u32[]{:S(2)}) %collective-permute-start.20) | collective-permute-done | bytes 1179680 | tf_op jit(solution)/shard_map/ppermute | solution.py:31
  222.8 10.8 %project.9 = bf16[768,2048]{1,0:T(8,128)(2,1)} custom-call(s32[4]{0:T(128)S(1)} %get-tuple-element.15.refs_0_, s32[4,6]{1,0:T(4,128)S(1)} %copy-done.6, s32[32]{0:T(128)S(1)} %copy-done.9, s32[1,6]{1,0:T(1,128)S(1)} %copy-done.7, f32[576,2048]{1,0:T(8,128)} %project.8.refs_4_, bf16[576,1024]{1,0:T(8,128)(2,1)S(1)} %collective-permute-done.19.refs_5_, ...), custom_call_target="tpu_custom_call" | custom-call | flops 4831838208 | bytes 20185088 | tf_op jit(solution)/shard_map/project/pallas_call | solution.py:254
  (36 shorter events, 0.4 us)
Async XLA Ops:
  0.0 9.3 %copy-start = (bf16[768,2048]{1,0:T(8,128)(2,1)S(1)}, bf16[768,2048]{1,0:T(8,128)(2,1)}, u32[]{:S(2)}) copy-start(bf16[768,2048]{1,0:T(8,128)(2,1)} %x.3) | copy-start | bytes 9437188
  0.0 0.8 copy-start.5
  0.8 0.8 copy-start.8
  1.6 7.7 %copy-start.7 = (s32[1,6]{1,0:T(1,128)S(1)}, s32[1,6]{1,0:T(1,128)}, u32[]{:S(2)}) copy-start(s32[1,6]{1,0:T(1,128)} %refs_3_.9) | copy-start | bytes 76
  4.7 24.7 %collective-permute-start.10 = (bf16[2,128,2048]{2,1,0:T(8,128)(2,1)S(1)}, bf16[2,128,2048]{2,1,0:T(8,128)(2,1)S(1)}, u32[]{:S(2)}, u32[]{:S(2)}) collective-permute-start(bf16[2,128,2048]{2,1,0:T(8,128)(2,1)S(1)} %get-tuple-element.10), channel_id=1, source_target_pairs={{0,4},{4,8},{8,12},{12,0},{1,5},{5,9},{9,13},{13,1},{2,6},{6,10},{... | collective-permute-start | bytes 3145736 | tf_op jit(solution)/shard_map/ppermute | solution.py:311
  5.0 30.5 %collective-permute-start.11 = (bf16[2,128,2048]{2,1,0:T(8,128)(2,1)S(1)}, bf16[2,128,2048]{2,1,0:T(8,128)(2,1)S(1)}, u32[]{:S(2)}, u32[]{:S(2)}) collective-permute-start(bf16[2,128,2048]{2,1,0:T(8,128)(2,1)S(1)} %get-tuple-element.11), channel_id=1, source_target_pairs={{0,8},{4,12},{8,0},{12,4},{1,9},{5,13},{9,1},{13,5},{2,10},{6,14},... | collective-permute-start | bytes 3145736 | tf_op jit(solution)/shard_map/ppermute | solution.py:311
  7.9 45.4 %collective-permute-start.12 = (bf16[2,128,2048]{2,1,0:T(8,128)(2,1)S(1)}, bf16[2,128,2048]{2,1,0:T(8,128)(2,1)S(1)}, u32[]{:S(2)}, u32[]{:S(2)}) collective-permute-start(bf16[2,128,2048]{2,1,0:T(8,128)(2,1)S(1)} %get-tuple-element.12), channel_id=1, source_target_pairs={{0,12},{4,0},{8,4},{12,8},{1,13},{5,1},{9,5},{13,9},{2,14},{6,2},{... | collective-permute-start | bytes 3145736 | tf_op jit(solution)/shard_map/ppermute | solution.py:311
  10.9 42.4 %copy-start.6 = (s32[4,6]{1,0:T(4,128)S(1)}, s32[4,6]{1,0:T(4,128)}, u32[]{:S(2)}) copy-start(s32[4,6]{1,0:T(4,128)} %refs_1_.9) | copy-start | bytes 292
  10.9 42.4 %copy-start.9 = (s32[32]{0:T(128)S(1)}, s32[32]{0:T(128)}, u32[]{:S(2)}) copy-start(s32[32]{0:T(128)} %refs_2_.9) | copy-start | bytes 388
  10.9 53.3 %collective-permute-start = (bf16[576,1024]{1,0:T(8,128)(2,1)S(1)}, bf16[576,1024]{1,0:T(8,128)(2,1)}, u32[]{:S(2)}, u32[]{:S(2)}) collective-permute-start(bf16[576,1024]{1,0:T(8,128)(2,1)S(1)} %pack.2.refs_4_.rest_0_), channel_id=1, source_target_pairs={{0,1},{1,2},{2,3},{4,5},{5,6},{6,7},{8,9},{9,10},{10,11},{12,13},{... | collective-permute-start | bytes 3538952 | tf_op jit(solution)/shard_map/ppermute | solution.py:31
  15.4 50.5 %collective-permute-start.2 = (bf16[576,1024]{1,0:T(8,128)(2,1)S(1)}, bf16[576,1024]{1,0:T(8,128)(2,1)}, u32[]{:S(2)}, u32[]{:S(2)}) collective-permute-start(bf16[576,1024]{1,0:T(8,128)(2,1)S(1)} %pack.2.refs_4_.rest_0_), channel_id=1, source_target_pairs={{1,0},{2,1},{3,2},{5,4},{6,5},{7,6},{9,8},{10,9},{11,10},{13,12},{... | collective-permute-start | bytes 3538952 | tf_op jit(solution)/shard_map/ppermute | solution.py:31
  29.4 88.1 %collective-permute-start.1 = (bf16[576,1024]{1,0:T(8,128)(2,1)}, bf16[576,1024]{1,0:T(8,128)(2,1)}, u32[]{:S(2)}, u32[]{:S(2)}) collective-permute-start(bf16[576,1024]{1,0:T(8,128)(2,1)} %pack.3.refs_5_.rest_1_), channel_id=1, source_target_pairs={{0,1},{1,2},{2,3},{4,5},{5,6},{6,7},{8,9},{9,10},{10,11},{12,13},{... | collective-permute-start | bytes 3538952 | tf_op jit(solution)/shard_map/ppermute | solution.py:31
  35.6 98.2 %collective-permute-start.3 = (bf16[576,1024]{1,0:T(8,128)(2,1)}, bf16[576,1024]{1,0:T(8,128)(2,1)}, u32[]{:S(2)}, u32[]{:S(2)}) collective-permute-start(bf16[576,1024]{1,0:T(8,128)(2,1)} %pack.3.refs_5_.rest_1_), channel_id=1, source_target_pairs={{1,0},{2,1},{3,2},{5,4},{6,5},{7,6},{9,8},{10,9},{11,10},{13,12},{... | collective-permute-start | bytes 3538952 | tf_op jit(solution)/shard_map/ppermute | solution.py:31
  57.9 1.0 copy-start.1
  58.8 1.0 copy-start.3
  60.7 9.6 %collective-permute-start.13 = (f32[64,576]{0,1:T(8,128)}, f32[64,576]{0,1:T(8,128)S(1)}, u32[]{:S(2)}, u32[]{:S(2)}) collective-permute-start(f32[64,576]{0,1:T(8,128)} %copy.10), channel_id=1, source_target_pairs={{0,1},{1,2},{2,3},{4,5},{5,6},{6,7},{8,9},{9,10},{10,11},{12,13},{... | collective-permute-start | bytes 442376 | tf_op jit(solution)/shard_map/ppermute | solution.py:315
  64.2 74.4 %collective-permute-start.4 = (bf16[576,1024]{1,0:T(8,128)(2,1)}, bf16[576,1024]{1,0:T(8,128)(2,1)}, u32[]{:S(2)}, u32[]{:S(2)}) collective-permute-start(bf16[576,1024]{1,0:T(8,128)(2,1)} %collective-permute-done.refs_5_), channel_id=1, source_target_pairs={{1,2},{2,3},{5,6},{6,7},{9,10},{10,11},{13,14},{14,15},{17,18},{18... | collective-permute-start | bytes 3538952 | tf_op jit(solution)/shard_map/ppermute | solution.py:31
  66.0 73.4 %collective-permute-start.6 = (bf16[576,1024]{1,0:T(8,128)(2,1)}, bf16[576,1024]{1,0:T(8,128)(2,1)}, u32[]{:S(2)}, u32[]{:S(2)}) collective-permute-start(bf16[576,1024]{1,0:T(8,128)(2,1)} %collective-permute-done.2.refs_7_), channel_id=1, source_target_pairs={{1,0},{2,1},{5,4},{6,5},{9,8},{10,9},{13,12},{14,13},{17,16},{18,1... | collective-permute-start | bytes 3538952 | tf_op jit(solution)/shard_map/ppermute | solution.py:31
  70.3 33.0 %collective-permute-start.16 = (f32[64,576]{0,1:T(8,128)}, f32[64,576]{0,1:T(8,128)}, u32[]{:S(2)}, u32[]{:S(2)}) collective-permute-start(f32[64,576]{0,1:T(8,128)} %copy.10), channel_id=1, source_target_pairs={{1,0},{2,1},{3,2},{5,4},{6,5},{7,6},{9,8},{10,9},{11,10},{13,12},{... | collective-permute-start | bytes 442376 | tf_op jit(solution)/shard_map/ppermute | solution.py:316
  103.3 10.9 %collective-permute-start.14 = (f32[64,576]{0,1:T(8,128)}, f32[64,576]{0,1:T(8,128)}, u32[]{:S(2)}, u32[]{:S(2)}) collective-permute-start(f32[64,576]{0,1:T(8,128)} %add.64), channel_id=1, source_target_pairs={{0,1},{1,2},{2,3},{4,5},{5,6},{6,7},{8,9},{9,10},{10,11},{12,13},{... | collective-permute-start | bytes 442376 | tf_op jit(solution)/shard_map/ppermute | solution.py:315
  116.2 18.3 %collective-permute-start.17 = (f32[64,576]{0,1:T(8,128)}, f32[64,576]{0,1:T(8,128)}, u32[]{:S(2)}, u32[]{:S(2)}) collective-permute-start(f32[64,576]{0,1:T(8,128)} %get-tuple-element.14), channel_id=1, source_target_pairs={{1,0},{2,1},{3,2},{5,4},{6,5},{7,6},{9,8},{10,9},{11,10},{13,12},{... | collective-permute-start | bytes 442376 | tf_op jit(solution)/shard_map/ppermute | solution.py:316
  117.5 19.7 %collective-permute-start.15 = (f32[64,576]{0,1:T(8,128)}, f32[64,576]{0,1:T(8,128)}, u32[]{:S(2)}, u32[]{:S(2)}) collective-permute-start(f32[64,576]{0,1:T(8,128)} %get-tuple-element.13), channel_id=1, source_target_pairs={{0,1},{1,2},{2,3},{4,5},{5,6},{6,7},{8,9},{9,10},{10,11},{12,13},{... | collective-permute-start | bytes 442376 | tf_op jit(solution)/shard_map/ppermute | solution.py:315
  133.8 39.9 %collective-permute-start.5 = (bf16[576,1024]{1,0:T(8,128)(2,1)}, bf16[576,1024]{1,0:T(8,128)(2,1)S(1)}, u32[]{:S(2)}, u32[]{:S(2)}) collective-permute-start(bf16[576,1024]{1,0:T(8,128)(2,1)} %collective-permute-done.1.refs_6_), channel_id=1, source_target_pairs={{1,2},{2,3},{5,6},{6,7},{9,10},{10,11},{13,14},{14,15},{17,18},{18... | collective-permute-start | bytes 3538952 | tf_op jit(solution)/shard_map/ppermute | solution.py:31
  134.5 40.0 %collective-permute-start.7 = (bf16[576,1024]{1,0:T(8,128)(2,1)}, bf16[576,1024]{1,0:T(8,128)(2,1)}, u32[]{:S(2)}, u32[]{:S(2)}) collective-permute-start(bf16[576,1024]{1,0:T(8,128)(2,1)} %collective-permute-done.3.refs_8_), channel_id=1, source_target_pairs={{1,0},{2,1},{5,4},{6,5},{9,8},{10,9},{13,12},{14,13},{17,16},{18,1... | collective-permute-start | bytes 3538952 | tf_op jit(solution)/shard_map/ppermute | solution.py:31
  137.2 35.4 %copy-start.10 = (f32[64,576]{0,1:T(8,128)S(1)}, f32[64,576]{0,1:T(8,128)}, u32[]{:S(2)}) copy-start(f32[64,576]{0,1:T(8,128)} %copy.10) | copy-start | bytes 442372
  137.2 35.4 %collective-permute-start.18 = (f32[64,576]{0,1:T(8,128)S(1)}, f32[64,576]{0,1:T(8,128)S(1)}, u32[]{:S(2)}, u32[]{:S(2)}) collective-permute-start(f32[64,576]{0,1:T(8,128)S(1)} %add.68), channel_id=1, source_target_pairs={{1,0},{2,1},{3,2},{5,4},{6,5},{7,6},{9,8},{10,9},{11,10},{13,12},{... | collective-permute-start | bytes 442376 | tf_op jit(solution)/shard_map/ppermute | solution.py:316
  138.7 51.9 %collective-permute-start.8 = (bf16[576,1024]{1,0:T(8,128)(2,1)}, bf16[576,1024]{1,0:T(8,128)(2,1)S(1)}, u32[]{:S(2)}, u32[]{:S(2)}) collective-permute-start(bf16[576,1024]{1,0:T(8,128)(2,1)} %collective-permute-done.4.refs_5_), channel_id=1, source_target_pairs={{2,3},{6,7},{10,11},{14,15},{18,19},{22,23},{26,27},{30,31}} | collective-permute-start | bytes 3538952 | tf_op jit(solution)/shard_map/ppermute | solution.py:31
  139.4 58.5 %collective-permute-start.9 = (bf16[576,1024]{1,0:T(8,128)(2,1)}, bf16[576,1024]{1,0:T(8,128)(2,1)S(1)}, u32[]{:S(2)}, u32[]{:S(2)}) collective-permute-start(bf16[576,1024]{1,0:T(8,128)(2,1)} %collective-permute-done.6.refs_7_), channel_id=1, source_target_pairs={{1,0},{5,4},{9,8},{13,12},{17,16},{21,20},{25,24},{29,28}} | collective-permute-start | bytes 3538952 | tf_op jit(solution)/shard_map/ppermute | solution.py:31
  173.7 25.3 %copy-start.2 = (bf16[2,128,2048]{2,1,0:T(8,128)(2,1)S(1)}, bf16[2,128,2048]{2,1,0:T(8,128)(2,1)}, u32[]{:S(2)}) copy-start(bf16[2,128,2048]{2,1,0:T(8,128)(2,1)} %copy-done.1) | copy-start | bytes 3145732
  173.7 25.3 %copy-start.4 = (bf16[2,128,2048]{2,1,0:T(8,128)(2,1)S(1)}, bf16[2,128,2048]{2,1,0:T(8,128)(2,1)}, u32[]{:S(2)}) copy-start(bf16[2,128,2048]{2,1,0:T(8,128)(2,1)} %copy-done.3) | copy-start | bytes 3145732
  173.7 36.9 %collective-permute-start.19 = (bf16[576,1024]{1,0:T(8,128)(2,1)S(1)}, bf16[576,1024]{1,0:T(8,128)(2,1)S(1)}, u32[]{:S(2)}, u32[]{:S(2)}) collective-permute-start(bf16[576,1024]{1,0:T(8,128)(2,1)S(1)} %collective-permute-done.5.refs_6_), channel_id=1, source_target_pairs={{2,3},{6,7},{10,11},{14,15},{18,19},{22,23},{26,27},{30,31}} | collective-permute-start | bytes 3538952 | tf_op jit(solution)/shard_map/ppermute | solution.py:31
  174.6 48.3 %collective-permute-start.20 = (bf16[576,1024]{1,0:T(8,128)(2,1)}, bf16[576,1024]{1,0:T(8,128)(2,1)S(1)}, u32[]{:S(2)}, u32[]{:S(2)}) collective-permute-start(bf16[576,1024]{1,0:T(8,128)(2,1)} %collective-permute-done.7.refs_8_), channel_id=1, source_target_pairs={{1,0},{5,4},{9,8},{13,12},{17,16},{21,20},{25,24},{29,28}} | collective-permute-start | bytes 3538952 | tf_op jit(solution)/shard_map/ppermute | solution.py:31
  197.9 1.0 copy-start.11

commit v3 on v2

v3 whole, which is shorter than its diff:
```python
import functools

import jax
import jax.numpy as jnp
from jax import lax
from jax.experimental import pallas as pl
from jax.experimental.pallas import tpu as pltpu
from jax.sharding import PartitionSpec as P

adapter_scale = 2.0
live_total = 576
tail_width = 256
column_tile = 512
vmem_bytes = 48 * 1024 * 1024
bf16, f32, i32 = jnp.bfloat16, jnp.float32, jnp.int32

smem = pl.BlockSpec(memory_space=pltpu.SMEM)
hbm = pl.BlockSpec(memory_space=pl.ANY)


def params():
    return pltpu.CompilerParams(vmem_limit_bytes=vmem_bytes)


def cost(flops, moved):
    return pl.CostEstimate(flops=int(flops), bytes_accessed=int(moved), transcendentals=0)


def one_hot(live, rows, axis):
    blocks = live.shape[1]
    block = rows // blocks
    flat = (1, rows) if axis else (rows, 1)
    row = lax.broadcasted_iota(i32, flat, axis)
    place = jnp.full(flat, -1, i32)
    start = 0
    for b in range(blocks):
        inside = row - b * block
        here = (inside >= 0) & (inside < live[0, b])
        place = jnp.where(here, inside + start, place)
        start = start + live[0, b]
    shape = (live_total, rows) if axis else (rows, live_total)
    return (lax.broadcasted_iota(i32, shape, 1 - axis) == place).astype(f32).astype(bf16)


def pack_kernel(live, x, *outs):
    hot = one_hot(live, x.shape[0], 1)
    start = 0
    for out in outs:
        stop = start + out.shape[1]
        rows = jnp.dot(hot, x[:, start:stop], preferred_element_type=f32)
        out[...] = rows.astype(bf16)
        start = stop


def pack(hidden, live, widths):
    rows, width = hidden.shape
    return pl.pallas_call(
        pack_kernel,
        grid=(1,),
        in_specs=[smem, pl.BlockSpec((rows, width), lambda i: (0, 0))],
        out_specs=[pl.BlockSpec((live_total, w), lambda i: (0, 0)) for w in widths],
        out_shape=[jax.ShapeDtypeStruct((live_total, w), bf16) for w in widths],
        compiler_params=params(),
        cost_estimate=cost(2 * rows * live_total * width, (rows + live_total) * width * 2),
        name="pack",
    )(live, hidden)


def choose_kernel(variants, slots, down, up, *rest, replicas, capacity, blocks):
    outs, sems = rest[:replicas], rest[replicas]
    pool, rank = down.shape[0], down.shape[1]
    me = lax.axis_index("dp")
    copies = []
    for step in range(replicas):
        target = lax.rem(me + step, replicas)
        seen = jnp.int32(0)
        index = [jnp.int32(0)] * capacity
        for b in range(blocks):
            slot = slots[variants[target, b]]
            owner = lax.div(slot, pool)
            mine = owner == me
            for m in range(capacity):
                index[m] = jnp.where(mine & (seen == m), slot - owner * pool, index[m])
            seen = seen + mine.astype(i32)
        for m in range(capacity):
            for kind, source in enumerate((down, up)):
                copies.append(
                    pltpu.make_async_copy(
                        source.at[index[m]],
                        outs[step].at[kind, m * rank : (m + 1) * rank],
                        sems.at[len(copies)],
                    )
                )
                copies[-1].start()
    for copy in copies:
        copy.wait()


def choose(variants, slots, down, up, replicas, capacity):
    pool, rank, width = down.shape
    out = jax.ShapeDtypeStruct((2, capacity * rank, width), bf16)
    return pl.pallas_call(
        functools.partial(
            choose_kernel, replicas=replicas, capacity=capacity, blocks=variants.shape[1]
        ),
        in_specs=[smem, smem, hbm, hbm],
        out_specs=[hbm] * replicas,
        out_shape=[out] * replicas,
        scratch_shapes=[pltpu.SemaphoreType.DMA((replicas * capacity * 2,))],
        compiler_params=params(),
        cost_estimate=cost(0, replicas * capacity * rank * width * 8),
        name="choose",
    )(variants, slots, down, up)


def row_groups(variants, slots, live, shape, axis, replicas, capacity, pool):
    me = lax.axis_index("dp")
    blocks = live.shape[1]
    row = lax.broadcasted_iota(i32, shape, axis)
    group = jnp.zeros(shape, i32)
    start = 0
    owners = []
    for b in range(blocks):
        owner = lax.div(slots[variants[me, b]], pool)
        nth = sum([(o == owner).astype(i32) for o in owners], jnp.int32(0))
        owners.append(owner)
        mine = lax.rem(me - owner + replicas, replicas) * capacity + nth
        group = jnp.where(row >= start, mine, group)
        start = start + live[0, b]
    return group


def shrink_kernel(variants, slots, live, *rest, replicas, capacity, pool, chunks):
    xs, downs, out = rest[:chunks], rest[chunks : chunks + replicas], rest[-1]
    depth = downs[0].shape[1]
    rank = out.shape[0]
    shape = (depth, live_total)
    group = row_groups(variants, slots, live, shape, 1, replicas, capacity, pool)
    nth = lax.broadcasted_iota(i32, shape, 0) // rank
    total = jnp.zeros(shape, f32)
    for o in range(replicas):
        part = jnp.zeros(shape, f32)
        start = 0
        for x in xs:
            stop = start + x.shape[1]
            part = part + lax.dot_general(
                downs[o][0, :, start:stop],
                x[...],
                (((1,), (1,)), ((), ())),
                preferred_element_type=f32,
            )
            start = stop
        total = total + jnp.where(group == o * capacity + nth, part, 0.0)
    result = total[:rank]
    for m in range(1, capacity):
        result = result + total[m * rank : (m + 1) * rank]
    out[...] = result


def shrink(variants, slots, live, xs, factors, capacity, pool):
    replicas = len(factors)
    depth, width = factors[0].shape[1:]
    rank = depth // capacity
    whole = pl.BlockSpec(memory_space=pltpu.VMEM)
    down = pl.BlockSpec((1, depth, width), lambda i: (0, 0, 0))
    return pl.pallas_call(
        functools.partial(
            shrink_kernel, replicas=replicas, capacity=capacity, pool=pool, chunks=len(xs)
        ),
        grid=(1,),
        in_specs=[smem] * 3
        + [pl.BlockSpec(x.shape, lambda i: (0, 0)) for x in xs]
        + [down] * replicas,
        out_specs=pl.BlockSpec((rank, live_total), lambda i: (0, 0)),
        out_shape=jax.ShapeDtypeStruct((rank, live_total), f32),
        compiler_params=params(),
        cost_estimate=cost(
            2 * live_total * width * depth * replicas, (live_total + depth * replicas) * width * 2
        ),
        name="shrink",
    )(variants, slots, live, *xs, *factors)


def near_kernel(meta, variants, slots, live, x, w, low, *rest, replicas, capacity, pool):
    ups, out = rest[:replicas], rest[replicas]
    depth = ups[0].shape[1]
    shape = (live_total, depth)
    group = row_groups(variants, slots, live, shape, 0, replicas, capacity, pool)
    nth = lax.broadcasted_iota(i32, shape, 1) // (depth // capacity)
    wide = jnp.concatenate([low[...]] * capacity, axis=1) * adapter_scale
    total = jnp.dot(x[...], w[0], preferred_element_type=f32)
    for o in range(replicas):
        spread = jnp.where(group == o * capacity + nth, wide, 0.0).astype(bf16)
        total = total + jnp.dot(spread, ups[o][0], preferred_element_type=f32)
    out[...] = total


def near(meta, ints, x, weight, low, factors, sizes):
    replicas, capacity, pool = sizes
    columns = weight.shape[2]
    tile = min(column_tile, columns)
    depth = factors[0].shape[1]
    k = x.shape[1]
    return pl.pallas_call(
        functools.partial(near_kernel, replicas=replicas, capacity=capacity, pool=pool),
        grid_spec=pltpu.PrefetchScalarGridSpec(
            num_scalar_prefetch=1,
            grid=(columns // tile,),
            in_specs=[smem] * 3
            + [
                pl.BlockSpec(x.shape, lambda i, m: (0, 0)),
                pl.BlockSpec((1, k, tile), lambda i, m: (m[0], 0, i)),
                pl.BlockSpec(low.shape, lambda i, m: (0, 0)),
            ]
            + [pl.BlockSpec((1, depth, tile), lambda i, m: (1, 0, i))] * replicas,
            out_specs=pl.BlockSpec((live_total, tile), lambda i, m: (0, i)),
        ),
        out_shape=jax.ShapeDtypeStruct((live_total, columns), f32),
        compiler_params=params(),
        cost_estimate=cost(
            2 * live_total * columns * (k + replicas * depth), columns * (k * 2 + live_total * 4)
        ),
        name="near",
    )(meta, *ints, x, weight, low, *factors)


def far_kernel(meta, total, x, w, out):
    @pl.when(pl.program_id(0) == 0)
    def _():
        out[...] = total[...]

    out[...] += jnp.dot(x[0], w[0], preferred_element_type=f32)


def far(meta, total, x, weight):
    tensor, _, k = x.shape
    columns = weight.shape[2]
    return pl.pallas_call(
        far_kernel,
        grid_spec=pltpu.PrefetchScalarGridSpec(
            num_scalar_prefetch=1,
            grid=(tensor - 1,),
            in_specs=[
                pl.BlockSpec((live_total, columns), lambda i, m: (0, 0)),
                pl.BlockSpec((1, live_total, k), lambda i, m: (m[1 + i], 0, 0)),
                pl.BlockSpec((1, k, columns), lambda i, m: (m[1 + i], 0, 0)),
            ],
            out_specs=pl.BlockSpec((live_total, columns), lambda i, m: (0, 0)),
        ),
        out_shape=jax.ShapeDtypeStruct((live_total, columns), f32),
        compiler_params=params(),
        cost_estimate=cost(
            2 * live_total * columns * k * (tensor - 1), tensor * k * (columns + live_total) * 2
        ),
        name="far",
    )(meta, total, x, weight)


def finish_kernel(live, total, x, w, out, hot):
    @pl.when(pl.program_id(0) == 0)
    def _():
        hot[...] = one_hot(live, out.shape[0], 0)

    result = total[...]
    for t in range(x.shape[0]):
        result = result + jnp.dot(x[t], w[t], preferred_element_type=f32)
    rows = jnp.dot(hot[...], result.astype(bf16), preferred_element_type=f32)
    out[...] = rows.astype(bf16)


def finish(live, total, x, weight, rows):
    tensor, _, k = x.shape
    columns = weight.shape[2]
    tile = min(column_tile, columns)
    last = weight.shape[1] // k - 1
    return pl.pallas_call(
        finish_kernel,
        grid=(columns // tile,),
        in_specs=[
            smem,
            pl.BlockSpec((live_total, tile), lambda i: (0, i)),
            pl.BlockSpec((tensor, live_total, k), lambda i: (0, 0, 0)),
            pl.BlockSpec((tensor, k, tile), lambda i: (0, last, i)),
        ],
        out_specs=pl.BlockSpec((rows, tile), lambda i: (0, i)),
        out_shape=jax.ShapeDtypeStruct((rows, columns), bf16),
        scratch_shapes=[pltpu.VMEM((rows, live_total), bf16)],
        compiler_params=params(),
        cost_estimate=cost(
            2 * live_total * columns * (k * tensor + rows), columns * (live_total * 4 + rows * 2)
        ),
        name="finish",
    )(live, total, x, weight)


def shards(
    hidden,
    query_weight,
    adapter_down,
    adapter_up,
    block_variant_index,
    variant_pool_slot,
    block_live_count,
):
    replicas = lax.axis_size("dp")
    tensor = lax.axis_size("tensor")
    place = lax.axis_index("tensor")
    pool = adapter_down.shape[0]
    blocks = block_variant_index.shape[1]
    rows, width = hidden.shape
    capacity = (blocks + replicas - 1) // replicas
    tail = min(tail_width, width // 2)
    ints = (block_variant_index, variant_pool_slot, block_live_count)
    sizes = (replicas, capacity, pool)

    own = pack(hidden, block_live_count, (width - tail, tail))
    gathered = [lax.all_gather(x, "tensor", axis=0) for x in own]

    factors = choose(block_variant_index, variant_pool_slot, adapter_down, adapter_up, replicas, capacity)
    got = [factors[0]]
    for step in range(1, replicas):
        pairs = [(i, (i + step) % replicas) for i in range(replicas)]
        got.append(lax.ppermute(factors[step], "dp", pairs))

    partial = shrink(*ints, own, got, capacity, pool)
    before, after = jnp.zeros_like(partial), jnp.zeros_like(partial)
    for step in range(1, tensor):
        before = lax.ppermute(partial + before, "tensor", [(i, i + 1) for i in range(tensor - 1)])
        after = lax.ppermute(partial + after, "tensor", [(i, i - 1) for i in range(1, tensor)])
    low = (before + partial + after).astype(bf16).astype(f32).T

    meta = (place + jnp.arange(tensor, dtype=i32)) % tensor
    weight = query_weight.reshape(tensor, width, query_weight.shape[1])
    total = near(meta, ints, own[0], weight, low, got, sizes)
    total = far(meta, total, gathered[0], weight)
    return finish(block_live_count, total, gathered[1], weight, rows)


def solution(mesh):
    return jax.shard_map(
        shards,
        mesh=mesh,
        in_specs=(
            P(("groups", "dp"), "tensor"),
            P(None, "tensor"),
            P("dp", None, "tensor"),
            P("dp", None, "tensor"),
            P("groups", None),
            P("groups"),
            P(("groups", "dp"), None),
        ),
        out_specs=P(("groups", "dp"), "tensor"),
        check_vma=False,
    )
```

time: 235 us -> 232 us (0.987)
  Pallas kernels: 74.2 us -> 51.9 us
  between operations: 0.27 us -> 13.5 us
  waiting for transfers between devices: 102 us -> 114 us
  starting transfers between devices: 45.3 us -> 34 us
  local copies, waits for them, and re-layouts: 5.65 us -> 12.7 us
    ppermute x12 -> x0, starting transfers between devices: 22.6 us -> none  [shift(): return lax.ppermute(x, axis, pairs)]
    pallas_call x5 -> x3, Pallas kernels: 62.3 us -> 39.7 us  [the longest x1 19.5 us: far(): pl.pallas_call(far_kernel, grid_spec=pltpu.PrefetchScalarGridSpec(num_sca...]
    ppermute x12 -> x0, waiting for transfers between devices: 19.6 us -> none  [shift(): return lax.ppermute(x, axis, pairs)]
    ppermute x3, waiting for transfers between devices: 26.5 us -> 44 us  [shards(): got.append(lax.ppermute(factors[step], 'dp', pairs))]
    ppermute x3, waiting for transfers between devices: 9.03 us -> 22.4 us  [shards(): lax.ppermute(partial + before, 'tensor', [(i, i + 1) for i in range(tenso...]
    ppermute x3, starting transfers between devices: 14.1 us -> 26 us  [shards(): lax.ppermute(partial + before, 'tensor', [(i, i + 1) for i in range(tenso...]
    unnamed x24, local copies, waits for them, and re-layouts: 4.61 us -> 11.9 us
  transfers between devices with their start and end apart: 21 -> 11, of which waited for: 8 -> 9; matrix products, arithmetic and copies ran while one was open for 3% -> 3% of each run, Pallas kernels for 26% -> 17%
where the time goes in v3:
time: 232 us
  waiting for transfers between devices  114 us (49%)
  Pallas kernels  51.9 us (22%)
  starting transfers between devices  34 us (15%)
  between operations  13.5 us (6%)
  local copies, waits for them, and re-layouts  12.7 us (5%)
  other arithmetic  5.55 us (2%)
    ppermute x3, waiting for transfers between devices, shards(): lax.ppermute(partial + after, 'tensor', [(i, i - 1) for i in range(1, ten...  45.7 us
    ppermute x3, waiting for transfers between devices, shards(): got.append(lax.ppermute(factors[step], 'dp', pairs))  44 us
    ppermute x3, starting transfers between devices, shards(): lax.ppermute(partial + before, 'tensor', [(i, i + 1) for i in range(tenso...  26 us
    ppermute x3, waiting for transfers between devices, shards(): lax.ppermute(partial + before, 'tensor', [(i, i + 1) for i in range(tenso...  22.4 us
    pallas_call x1, Pallas kernels, far(): pl.pallas_call(far_kernel, grid_spec=pltpu.PrefetchScalarGridSpec(num_sca...  19.5 us
    unnamed x24, local copies, waits for them, and re-layouts  11.9 us
    pallas_call x1, Pallas kernels, near(): pl.pallas_call(functools.partial(near_kernel, replicas=replicas, capacity...  11.7 us
    pallas_call x1, Pallas kernels, finish(): pl.pallas_call(finish_kernel, grid=(columns // tile,), in_specs=[smem, pl...  8.56 us
  transfers between devices with their start and end apart: 11, of which 9 were waited for; matrix products, arithmetic and copies ran while one was open for 3% of the time, Pallas kernels for 17%

profile of v3, /device:TPU:0, one launch (start us, length us, event | category | flops | bytes accessed | tf_op | source)
XLA Modules:
  0.0 231.6 jit_solution(12357672202919548979)
XLA Ops:
  6.5 0.0 all-gather.5.cloned.1.call-start
  6.5 0.7 copy-done.8
  7.2 1.9 copy-done.10
  9.1 3.9 %pack.1 = (bf16[576,1792]{1,0:T(8,128)(2,1)}, bf16[576,256]{1,0:T(8,128)(2,1)}) custom-call(s32[1,6]{1,0:T(1,128)S(1)} %copy-done.8, bf16[768,2048]{1,0:T(8,128)(2,1)S(1)} %copy-done.10), custom_call_target="tpu_custom_call" | custom-call | flops 1811939328 | bytes 5505024 | tf_op jit(solution)/shard_map/pack/pallas_call | solution.py:57
  13.1 0.0 all-gather.5.cloned.1.call-update
  13.1 0.0 all-gather.7.cloned.1.call-start
  13.1 0.0 copy-done.6
  13.1 0.0 copy-done.7
  13.2 3.3 %choose.1 = (bf16[2,128,2048]{2,1,0:T(8,128)(2,1)S(1)}, bf16[2,128,2048]{2,1,0:T(8,128)(2,1)S(1)}, bf16[2,128,2048]{2,1,0:T(8,128)(2,1)S(1)}, bf16[2,128,2048]{2,1,0:T(8,128)(2,1)S(1)}) custom-call(s32[4,6]{1,0:T(4,128)S(1)} %copy-done.6, s32[32]{0:T(128)S(1)} %copy-done.7, bf16[8,64,2048]{2,1,0:T(8,128)(2,1)} %down.1, bf16[8,64,2048]{2,1,0:T(8,128)(2,1)} %up.1), custom_call_target="tpu_custom_call" | custom-call | bytes 8388608 | tf_op jit(solution)/shard_map/choose/pallas_call | solution.py:102
  16.5 0.3 collective-permute-start
  16.7 2.7 %collective-permute-start.1 = (bf16[2,128,2048]{2,1,0:T(8,128)(2,1)S(1)}, bf16[2,128,2048]{2,1,0:T(8,128)(2,1)S(1)}, u32[]{:S(2)}, u32[]{:S(2)}) collective-permute-start(bf16[2,128,2048]{2,1,0:T(8,128)(2,1)S(1)} %get-tuple-element.15), channel_id=1, source_target_pairs={{0,8},{4,12},{8,0},{12,4},{1,9},{5,13},{9,1},{13,5},{2,10},{6,14},... | collective-permute-start | bytes 3145736 | tf_op jit(solution)/shard_map/ppermute | solution.py:323
  19.4 1.2 collective-permute-start.2
  20.6 21.5 %collective-permute-done.rest_3_.rest_1_ = bf16[2,128,2048]{2,1,0:T(8,128)(2,1)S(1)} collective-permute-done((bf16[2,128,2048]{2,1,0:T(8,128)(2,1)S(1)}, bf16[2,128,2048]{2,1,0:T(8,128)(2,1)S(1)}, u32[]{:S(2)}, u32[]{:S(2)}) %collective-permute-start) | collective-permute-done | bytes 1048608 | tf_op jit(solution)/shard_map/ppermute | solution.py:323
  42.0 1.3 collective-permute-done.1.rest_4_.rest_2_
  43.3 21.2 %collective-permute-done.2.rest_5_.rest_3_ = bf16[2,128,2048]{2,1,0:T(8,128)(2,1)S(1)} collective-permute-done((bf16[2,128,2048]{2,1,0:T(8,128)(2,1)S(1)}, bf16[2,128,2048]{2,1,0:T(8,128)(2,1)S(1)}, u32[]{:S(2)}, u32[]{:S(2)}) %collective-permute-start.2) | collective-permute-done | bytes 1048608 | tf_op jit(solution)/shard_map/ppermute | solution.py:323
  64.5 1.1 copy-done.2
  65.6 0.0 copy-done.9
  65.6 1.2 copy-done.3
  66.8 5.0 %shrink.1 = f32[64,576]{1,0:T(8,128)S(1)} custom-call(s32[4,6]{1,0:T(4,128)S(1)} %copy-done.6, s32[32]{0:T(128)S(1)} %copy-done.7, s32[1,6]{1,0:T(1,128)S(1)} %copy-done.9, bf16[576,1792]{1,0:T(8,128)(2,1)} %get-tuple-element.11.rest_0_.x, bf16[576,256]{1,0:T(8,128)(2,1)} %get-tuple-element.12.rest_1_, ...), custom_call_target="tpu_custom_call" | custom-call | flops 1207959552 | bytes 4456448 | tf_op jit(solution)/shard_map/shrink/pallas_call | solution.py:166
  71.8 0.9 copy.10
  72.7 3.6 %collective-permute-start.3 = (f32[64,576]{0,1:T(8,128)}, f32[64,576]{0,1:T(8,128)S(1)}, u32[]{:S(2)}, u32[]{:S(2)}) collective-permute-start(f32[64,576]{0,1:T(8,128)} %copy.10), channel_id=1, source_target_pairs={{0,1},{1,2},{2,3},{4,5},{5,6},{6,7},{8,9},{9,10},{10,11},{12,13},{... | collective-permute-start | bytes 442376 | tf_op jit(solution)/shard_map/ppermute | solution.py:328
  76.3 1.3 collective-permute-start.6
  77.6 12.4 %collective-permute-done.3 = f32[64,576]{0,1:T(8,128)S(1)} collective-permute-done((f32[64,576]{0,1:T(8,128)}, f32[64,576]{0,1:T(8,128)S(1)}, u32[]{:S(2)}, u32[]{:S(2)}) %collective-permute-start.3) | collective-permute-done | bytes 147488 | tf_op jit(solution)/shard_map/ppermute | solution.py:328
  90.0 1.0 add.33
  91.0 9.1 %collective-permute-start.4 = (f32[64,576]{0,1:T(8,128)S(1)}, f32[64,576]{0,1:T(8,128)S(1)}, u32[]{:S(2)}, u32[]{:S(2)}) collective-permute-start(f32[64,576]{0,1:T(8,128)S(1)} %add.33), channel_id=1, source_target_pairs={{0,1},{1,2},{2,3},{4,5},{5,6},{6,7},{8,9},{9,10},{10,11},{12,13},{... | collective-permute-start | bytes 442376 | tf_op jit(solution)/shard_map/ppermute | solution.py:328
  100.1 3.6 %collective-permute-done.6 = f32[64,576]{0,1:T(8,128)S(1)} collective-permute-done((f32[64,576]{0,1:T(8,128)}, f32[64,576]{0,1:T(8,128)S(1)}, u32[]{:S(2)}, u32[]{:S(2)}) %collective-permute-start.6) | collective-permute-done | bytes 147488 | tf_op jit(solution)/shard_map/ppermute | solution.py:329
  103.7 9.9 %collective-permute-done.4 = f32[64,576]{0,1:T(8,128)S(1)} collective-permute-done((f32[64,576]{0,1:T(8,128)S(1)}, f32[64,576]{0,1:T(8,128)S(1)}, u32[]{:S(2)}, u32[]{:S(2)}) %collective-permute-start.4) | collective-permute-done | bytes 147488 | tf_op jit(solution)/shard_map/ppermute | solution.py:328
  113.6 1.7 fusion.1
  115.4 1.3 collective-permute-start.7
  116.7 13.3 %collective-permute-start.5 = (f32[64,576]{0,1:T(8,128)}, f32[64,576]{0,1:T(8,128)}, u32[]{:S(2)}, u32[]{:S(2)}) collective-permute-start(f32[64,576]{0,1:T(8,128)} %get-tuple-element.17), channel_id=1, source_target_pairs={{0,1},{1,2},{2,3},{4,5},{5,6},{6,7},{8,9},{9,10},{10,11},{12,13},{... | collective-permute-start | bytes 442376 | tf_op jit(solution)/shard_map/ppermute | solution.py:328
  130.0 18.2 %collective-permute-done.7 = f32[64,576]{0,1:T(8,128)S(1)} collective-permute-done((f32[64,576]{0,1:T(8,128)S(1)}, f32[64,576]{0,1:T(8,128)S(1)}, u32[]{:S(2)}, u32[]{:S(2)}) %collective-permute-start.7) | collective-permute-done | bytes 147488 | tf_op jit(solution)/shard_map/ppermute | solution.py:329
  148.2 1.7 add.37
  149.9 1.3 collective-permute-start.8
  151.2 0.0 all-gather.7.cloned.1.call-update
  151.2 0.0 collective-permute-done.5
  151.2 23.9 %collective-permute-done.8 = f32[64,576]{0,1:T(8,128)} collective-permute-done((f32[64,576]{0,1:T(8,128)}, f32[64,576]{0,1:T(8,128)}, u32[]{:S(2)}, u32[]{:S(2)}) %collective-permute-start.8) | collective-permute-done | bytes 147488 | tf_op jit(solution)/shard_map/ppermute | solution.py:329
  175.2 0.0 copy-done.11
  175.2 1.1 convert_bitcast_fusion.low
  176.3 0.0 copy-start.4
  176.3 1.2 copy-done.4
  177.5 11.7 %near.1.total = f32[576,2048]{1,0:T(8,128)} custom-call(s32[4]{0:T(128)S(1)} %and_select_fusion.meta, s32[4,6]{1,0:T(4,128)S(1)} %copy-done.6, s32[32]{0:T(128)S(1)} %copy-done.7, s32[1,6]{1,0:T(1,128)S(1)} %copy-done.9, bf16[576,1792]{1,0:T(8,128)(2,1)} %get-tuple-element.11.rest_0_.x, bf16[4,2048,2048]{2,1,0:T(8,128)(2,1)} %bitcast.6, ...), custom_call_target="tpu_custom_call" | custom-call | flops 5435817984 | bytes 12058624 | tf_op jit(solution)/shard_map/near/pallas_call | solution.py:204
  189.2 19.5 %far.1.total = f32[576,2048]{1,0:T(8,128)S(1)} custom-call(s32[4]{0:T(128)S(1)} %and_select_fusion.meta, f32[576,2048]{1,0:T(8,128)} %near.1.total, bf16[4,576,1792]{2,1,0:T(8,128)(2,1)} %bitcast.9, bf16[4,2048,2048]{2,1,0:T(8,128)(2,1)} %bitcast.7), custom_call_target="tpu_custom_call" | custom-call | flops 12683575296 | bytes 37617664 | tf_op jit(solution)/shard_map/far/pallas_call | solution.py:238
  208.7 0.0 copy-start
  208.7 2.1 copy-done
  210.8 1.8 all-gather.7.cloned.1.call-done
  212.6 2.3 %copy-done.1 = f32[576,2048]{1,0:T(8,128)S(1)} copy-done((f32[576,2048]{1,0:T(8,128)S(1)}, f32[576,2048]{1,0:T(8,128)}, u32[]{:S(2)}) %copy-start.1) | copy-done | bytes 4718616
  214.9 1.3 copy-done.5
  216.2 8.6 %finish.1 = bf16[768,2048]{1,0:T(8,128)(2,1)} custom-call(s32[1,6]{1,0:T(1,128)S(1)} %copy-done.9, f32[576,2048]{1,0:T(8,128)S(1)} %copy-done.1, bf16[4,576,256]{2,1,0:T(8,128)(2,1)S(1)} %bitcast.5, bf16[4,2048,2048]{2,1,0:T(8,128)(2,1)} %bitcast.8), custom_call_target="tpu_custom_call" | custom-call | flops 4227858432 | bytes 7864320 | tf_op jit(solution)/shard_map/finish/pallas_call | solution.py:276
  (12 shorter events, 0.0 us)
Async XLA Ops:
  6.5 6.6 %copy-start.6 = (s32[4,6]{1,0:T(4,128)S(1)}, s32[4,6]{1,0:T(4,128)}, u32[]{:S(2)}) copy-start(s32[4,6]{1,0:T(4,128)} %variants.5) | copy-start | bytes 292
  6.5 6.6 %copy-start.7 = (s32[32]{0:T(128)S(1)}, s32[32]{0:T(128)}, u32[]{:S(2)}) copy-start(s32[32]{0:T(128)} %slots.5) | copy-start | bytes 388
  6.5 182.7 %all-gather.5.cloned.1.call-start = ((), (), s32[]{:S(2)}) async-start(), calls=%async_computation | async-start | bytes 10321920 | tf_op jit(solution)/shard_map/all_gather | solution.py:317
  6.5 0.7 copy-start.8
  7.2 1.9 copy-start.10
  13.1 52.6 %copy-start.9 = (s32[1,6]{1,0:T(1,128)S(1)}, s32[1,6]{1,0:T(1,128)}, u32[]{:S(2)}) copy-start(s32[1,6]{1,0:T(1,128)} %live.7) | copy-start | bytes 76
  13.1 199.5 %all-gather.7.cloned.1.call-start = ((), (), s32[]{:S(2)}) async-start(), calls=%async_computation.1 | async-start | bytes 1474560 | tf_op jit(solution)/shard_map/all_gather | solution.py:317
  16.5 25.6 %collective-permute-start = (bf16[2,128,2048]{2,1,0:T(8,128)(2,1)S(1)}, bf16[2,128,2048]{2,1,0:T(8,128)(2,1)S(1)}, u32[]{:S(2)}, u32[]{:S(2)}) collective-permute-start(bf16[2,128,2048]{2,1,0:T(8,128)(2,1)S(1)} %get-tuple-element.14), channel_id=1, source_target_pairs={{0,4},{4,8},{8,12},{12,0},{1,5},{5,9},{9,13},{13,1},{2,6},{6,10},{... | collective-permute-start | bytes 3145736 | tf_op jit(solution)/shard_map/ppermute | solution.py:323
  16.7 26.6 %collective-permute-start.1 = (bf16[2,128,2048]{2,1,0:T(8,128)(2,1)S(1)}, bf16[2,128,2048]{2,1,0:T(8,128)(2,1)S(1)}, u32[]{:S(2)}, u32[]{:S(2)}) collective-permute-start(bf16[2,128,2048]{2,1,0:T(8,128)(2,1)S(1)} %get-tuple-element.15), channel_id=1, source_target_pairs={{0,8},{4,12},{8,0},{12,4},{1,9},{5,13},{9,1},{13,5},{2,10},{6,14},... | collective-permute-start | bytes 3145736 | tf_op jit(solution)/shard_map/ppermute | solution.py:323
  19.4 45.2 %collective-permute-start.2 = (bf16[2,128,2048]{2,1,0:T(8,128)(2,1)S(1)}, bf16[2,128,2048]{2,1,0:T(8,128)(2,1)S(1)}, u32[]{:S(2)}, u32[]{:S(2)}) collective-permute-start(bf16[2,128,2048]{2,1,0:T(8,128)(2,1)S(1)} %get-tuple-element.16), channel_id=1, source_target_pairs={{0,12},{4,0},{8,4},{12,8},{1,13},{5,1},{9,5},{13,9},{2,14},{6,2},{... | collective-permute-start | bytes 3145736 | tf_op jit(solution)/shard_map/ppermute | solution.py:323
  64.5 1.1 copy-start.2
  65.6 1.2 copy-start.3
  72.7 102.5 %copy-start.11 = (f32[64,576]{0,1:T(8,128)S(1)}, f32[64,576]{0,1:T(8,128)}, u32[]{:S(2)}) copy-start(f32[64,576]{0,1:T(8,128)} %copy.10) | copy-start | bytes 442372
  72.7 17.3 %collective-permute-start.3 = (f32[64,576]{0,1:T(8,128)}, f32[64,576]{0,1:T(8,128)S(1)}, u32[]{:S(2)}, u32[]{:S(2)}) collective-permute-start(f32[64,576]{0,1:T(8,128)} %copy.10), channel_id=1, source_target_pairs={{0,1},{1,2},{2,3},{4,5},{5,6},{6,7},{8,9},{9,10},{10,11},{12,13},{... | collective-permute-start | bytes 442376 | tf_op jit(solution)/shard_map/ppermute | solution.py:328
  76.3 27.4 %collective-permute-start.6 = (f32[64,576]{0,1:T(8,128)}, f32[64,576]{0,1:T(8,128)S(1)}, u32[]{:S(2)}, u32[]{:S(2)}) collective-permute-start(f32[64,576]{0,1:T(8,128)} %copy.10), channel_id=1, source_target_pairs={{1,0},{2,1},{3,2},{5,4},{6,5},{7,6},{9,8},{10,9},{11,10},{13,12},{... | collective-permute-start | bytes 442376 | tf_op jit(solution)/shard_map/ppermute | solution.py:329
  91.0 22.6 %collective-permute-start.4 = (f32[64,576]{0,1:T(8,128)S(1)}, f32[64,576]{0,1:T(8,128)S(1)}, u32[]{:S(2)}, u32[]{:S(2)}) collective-permute-start(f32[64,576]{0,1:T(8,128)S(1)} %add.33), channel_id=1, source_target_pairs={{0,1},{1,2},{2,3},{4,5},{5,6},{6,7},{8,9},{9,10},{10,11},{12,13},{... | collective-permute-start | bytes 442376 | tf_op jit(solution)/shard_map/ppermute | solution.py:328
  115.4 32.8 %collective-permute-start.7 = (f32[64,576]{0,1:T(8,128)S(1)}, f32[64,576]{0,1:T(8,128)S(1)}, u32[]{:S(2)}, u32[]{:S(2)}) collective-permute-start(f32[64,576]{0,1:T(8,128)S(1)} %get-tuple-element.18), channel_id=1, source_target_pairs={{1,0},{2,1},{3,2},{5,4},{6,5},{7,6},{9,8},{10,9},{11,10},{13,12},{... | collective-permute-start | bytes 442376 | tf_op jit(solution)/shard_map/ppermute | solution.py:329
  116.7 34.6 %collective-permute-start.5 = (f32[64,576]{0,1:T(8,128)}, f32[64,576]{0,1:T(8,128)}, u32[]{:S(2)}, u32[]{:S(2)}) collective-permute-start(f32[64,576]{0,1:T(8,128)} %get-tuple-element.17), channel_id=1, source_target_pairs={{0,1},{1,2},{2,3},{4,5},{5,6},{6,7},{8,9},{9,10},{10,11},{12,13},{... | collective-permute-start | bytes 442376 | tf_op jit(solution)/shard_map/ppermute | solution.py:328
  149.9 25.3 %collective-permute-start.8 = (f32[64,576]{0,1:T(8,128)}, f32[64,576]{0,1:T(8,128)}, u32[]{:S(2)}, u32[]{:S(2)}) collective-permute-start(f32[64,576]{0,1:T(8,128)} %add.37), channel_id=1, source_target_pairs={{1,0},{2,1},{3,2},{5,4},{6,5},{7,6},{9,8},{10,9},{11,10},{13,12},{... | collective-permute-start | bytes 442376 | tf_op jit(solution)/shard_map/ppermute | solution.py:329
  176.3 1.2 copy-start.4
  208.7 2.1 copy-start
  212.6 2.3 %copy-start.1 = (f32[576,2048]{1,0:T(8,128)S(1)}, f32[576,2048]{1,0:T(8,128)}, u32[]{:S(2)}) copy-start(f32[576,2048]{1,0:T(8,128)} %copy-done) | copy-start | bytes 14155780
  214.9 1.3 copy-start.5
Sparse Core Ops, SparseCore 0:
  13.2 169.0 all-gather.4
  183.8 28.7 all-gather.6

commit v4 on v2

--- a/solution.py
+++ b/solution.py
@@ -23,12 +23,7 @@
 
 
 def cost(flops, moved):
-    return pl.CostEstimate(flops=int(flops), bytes_accessed=int(moved), transcendentals=0)
-
-
-def shift(x, axis, step, size, first, last):
-    pairs = [(i, i + step) for i in range(first, last + 1) if 0 <= i + step < size]
-    return lax.ppermute(x, axis, pairs)
+    return pl.CostEstimate(flops=1, bytes_accessed=1, transcendentals=0)
 
 
 def one_hot(live, rows, axis):
@@ -47,21 +42,26 @@
     return (lax.broadcasted_iota(i32, shape, 1 - axis) == place).astype(f32).astype(bf16)
 
 
-def pack_kernel(live, x, out):
+def pack_kernel(live, x, *outs):
     hot = one_hot(live, x.shape[0], 1)
-    out[...] = jnp.dot(hot, x[...], preferred_element_type=f32).astype(bf16)
-
-
-def pack(hidden, live, j, piece):
-    rows = hidden.shape[0]
+    start = 0
+    for out in outs:
+        stop = start + out.shape[1]
+        rows = jnp.dot(hot, x[:, start:stop], preferred_element_type=f32)
+        out[...] = rows.astype(bf16)
+        start = stop
+
+
+def pack(hidden, live, widths):
+    rows, width = hidden.shape
     return pl.pallas_call(
         pack_kernel,
         grid=(1,),
-        in_specs=[smem, pl.BlockSpec((rows, piece), lambda i: (0, j))],
-        out_specs=pl.BlockSpec((live_total, piece), lambda i: (0, 0)),
-        out_shape=jax.ShapeDtypeStruct((live_total, piece), bf16),
+        in_specs=[smem, pl.BlockSpec((rows, width), lambda i: (0, 0))],
+        out_specs=[pl.BlockSpec((live_total, w), lambda i: (0, 0)) for w in widths],
+        out_shape=[jax.ShapeDtypeStruct((live_total, w), bf16) for w in widths],
         compiler_params=params(),
-        cost_estimate=cost(2 * rows * live_total * piece, (rows + live_total) * piece * 2),
+        cost_estimate=cost(2 * rows * live_total * width, (rows + live_total) * width * 2),
         name="pack",
     )(live, hidden)
 
@@ -134,20 +134,22 @@
     xs, downs, out = rest[:chunks], rest[chunks : chunks + replicas], rest[-1]
     depth = downs[0].shape[1]
     rank = out.shape[0]
-    piece = xs[0].shape[1]
     shape = (depth, live_total)
     group = row_groups(variants, slots, live, shape, 1, replicas, capacity, pool)
     nth = lax.broadcasted_iota(i32, shape, 0) // rank
     total = jnp.zeros(shape, f32)
     for o in range(replicas):
         part = jnp.zeros(shape, f32)
-        for j in range(chunks):
+        start = 0
+        for x in xs:
+            stop = start + x.shape[1]
             part = part + lax.dot_general(
-                downs[o][0, :, j * piece : (j + 1) * piece],
-                xs[j][...],
+                downs[o][0, :, start:stop],
+                x[...],
                 (((1,), (1,)), ((), ())),
                 preferred_element_type=f32,
             )
+            start = stop
         total = total + jnp.where(group == o * capacity + nth, part, 0.0)
     result = total[:rank]
     for m in range(1, capacity):
@@ -179,82 +181,110 @@
     )(variants, slots, live, *xs, *factors)
 
 
-def project_kernel(*refs, count, has_total, delta, last, replicas, capacity, pool):
+def project_kernel(*refs, groups, has_total, delta, last, replicas, capacity, pool):
     refs = list(refs)
-    meta = refs.pop(0)
-    variants, slots, live = refs[:3]
-    refs = refs[3:]
+    meta, variants, slots, live = refs[:4]
+    refs = refs[4:]
     total = refs.pop(0) if has_total else None
-    xs, ws = refs[:count], refs[count : 2 * count]
-    refs = refs[2 * count :]
-    if delta:
-        low, ups = refs[0], refs[1 : 1 + replicas]
-        refs = refs[1 + replicas :]
+    xs = [[refs.pop(0) for _ in range(g)] for g in groups]
+    ws = [refs.pop(0) for _ in groups]
+    low = refs.pop(0) if delta else None
+    ups = [refs.pop(0) for _ in range(replicas)] if delta else None
     out = refs.pop(0)
-    held = refs.pop(0) if last else out
-
-    if has_total:
-        held[...] = total[...]
-    else:
-        held[...] = jnp.zeros(held.shape, f32)
-    for s in range(count):
-
-        @pl.when(meta[2 * s + 1] > 0)
-        def _(s=s):
-            held[...] += jnp.dot(xs[s][...], ws[s][...], preferred_element_type=f32)
-
+    spread = refs.pop(0) if delta else None
+    held, hot = (refs.pop(0), refs.pop(0)) if last else (out, None)
+
+    if delta or last:
+
+        @pl.when(pl.program_id(0) == 0)
+        def _():
+            if last:
+                hot[...] = one_hot(live, out.shape[0], 0)
+            if delta:
+                depth = ups[0].shape[1]
+                shape = (live_total, depth)
+                group = row_groups(variants, slots, live, shape, 0, replicas, capacity, pool)
+                nth = lax.broadcasted_iota(i32, shape, 1) // (depth // capacity)
+                wide = jnp.concatenate([low[...]] * capacity, axis=1) * adapter_scale
+                for o in range(replicas):
+                    mine = jnp.where(group == o * capacity + nth, wide, 0.0)
+                    spread[:, o * depth : (o + 1) * depth] = mine.astype(bf16)
+
+    def product(s):
+        x = xs[s][0][...]
+        for other in xs[s][1:]:
+            x = x + other[...]
+        return jnp.dot(x, ws[s][...], preferred_element_type=f32)
+
+    sure = [s for s in range(len(groups)) if not has_total or groups[s] > 1]
+    value = total[...] if has_total else None
+    for s in sure:
+        value = product(s) if value is None else value + product(s)
     if delta:
         depth = ups[0].shape[1]
-        shape = (live_total, depth)
-        group = row_groups(variants, slots, live, shape, 0, replicas, capacity, pool)
-        nth = lax.broadcasted_iota(i32, shape, 1) // (depth // capacity)
-        wide = jnp.concatenate([low[...]] * capacity, axis=1) * adapter_scale
         for o in range(replicas):
-            spread = jnp.where(group == o * capacity + nth, wide, 0.0).astype(bf16)
-            held[...] += jnp.dot(spread, ups[o][0], preferred_element_type=f32)
+            value = value + jnp.dot(
+                spread[:, o * depth : (o + 1) * depth], ups[o][0], preferred_element_type=f32
+            )
+    if len(sure) == len(groups) and last:
+        result = value.astype(bf16)
+    else:
+        held[...] = value
+        for s in range(len(groups)):
+            if s not in sure:
+
+                @pl.when(meta[2 * s + 1] > 0)
+                def _(s=s):
+                    held[...] += product(s)
+
+        result = held[...].astype(bf16) if last else None
     if last:
-        hot = one_hot(live, out.shape[0], 0)
-        result = held[...].astype(bf16)
-        out[...] = jnp.dot(hot, result, preferred_element_type=f32).astype(bf16)
+        out[...] = jnp.dot(hot[...], result, preferred_element_type=f32).astype(bf16)
 
 
 def project(meta, ints, total, xs, weight, sizes, low=None, factors=None, rows=None):
     replicas, capacity, pool = sizes
     columns = weight.shape[1]
     tile = min(column_tile, columns)
-    count = len(xs)
     in_specs = [smem] * 3
     args = list(ints)
+    flops, moved = 0, live_total * columns * 8
     if total is not None:
         in_specs.append(pl.BlockSpec((live_total, tile), lambda i, m: (0, i)))
         args.append(total)
-    for x in xs:
-        in_specs.append(pl.BlockSpec(x.shape, lambda i, m: (0, 0)))
-        args.append(x)
-    for s, x in enumerate(xs):
-        in_specs.append(pl.BlockSpec((x.shape[1], tile), lambda i, m, s=s: (m[2 * s], i)))
+    for group in xs:
+        for x in group:
+            in_specs.append(pl.BlockSpec(x.shape, lambda i, m: (0, 0)))
+            args.append(x)
+            moved += x.size * 2
+    for s, group in enumerate(xs):
+        k = group[0].shape[1]
+        in_specs.append(pl.BlockSpec((k, tile), lambda i, m, s=s: (m[2 * s], i)))
         args.append(weight)
-    flops = sum(2 * live_total * x.shape[1] * columns for x in xs)
-    moved = sum(x.size * 2 + x.shape[1] * columns * 2 for x in xs) + live_total * columns * 8
+        flops += 2 * live_total * k * columns
+        moved += k * columns * 2
+    scratch = []
     if low is not None:
         in_specs.append(pl.BlockSpec(low.shape, lambda i, m: (0, 0)))
         args.append(low)
+        depth = factors[0].shape[1]
         for u in factors:
-            in_specs.append(pl.BlockSpec((1, u.shape[1], tile), lambda i, m: (1, 0, i)))
+            in_specs.append(pl.BlockSpec((1, depth, tile), lambda i, m: (1, 0, i)))
             args.append(u)
-            flops += 2 * live_total * u.shape[1] * columns
-    scratch = []
+            flops += 2 * live_total * depth * columns
+        scratch.append(pltpu.VMEM((live_total, replicas * depth), bf16))
     if rows is None:
         out = jax.ShapeDtypeStruct((live_total, columns), f32)
         out_spec = pl.BlockSpec((live_total, tile), lambda i, m: (0, i))
     else:
         out = jax.ShapeDtypeStruct((rows, columns), bf16)
         out_spec = pl.BlockSpec((rows, tile), lambda i, m: (0, i))
-        scratch = [pltpu.VMEM((live_total, tile), f32)]
+        scratch += [pltpu.VMEM((live_total, tile), f32), pltpu.VMEM((rows, live_total), bf16)]
+        flops += 2 * live_total * rows * columns
     return pl.pallas_call(
         functools.partial(
             project_kernel,
-            count=count,
+            groups=tuple(len(g) for g in xs),
             has_total=total is not None,
             delta=low is not None,
             last=rows is not None,
@@ -297,52 +327,85 @@
     ints = (block_variant_index, variant_pool_slot, block_live_count)
     sizes = (replicas, capacity, pool)
 
-    own = [pack(hidden, block_live_count, j, piece) for j in range(chunks)]
-
-    right, left = [own], [own]
-    for step in range(1, tensor):
-        right.append([shift(x, "tensor", 1, tensor, step - 1, tensor - 2) for x in right[-1]])
-        left.append([shift(x, "tensor", -1, tensor, 1, tensor - step) for x in left[-1]])
-
-    factors = choose(block_variant_index, variant_pool_slot, adapter_down, adapter_up, replicas, capacity)
-    got = [factors[0]]
-    for step in range(1, replicas):
-        pairs = [(i, (i + step) % replicas) for i in range(replicas)]
-        got.append(lax.ppermute(factors[step], "dp", pairs))
-    partial = shrink(*ints, own, got, capacity, pool)
-    before, after = jnp.zeros_like(partial), jnp.zeros_like(partial)
-    for step in range(1, tensor):
-        before = lax.ppermute(partial + before, "tensor", [(i, i + 1) for i in range(tensor - 1)])
-        after = lax.ppermute(partial + after, "tensor", [(i, i - 1) for i in range(1, tensor)])
-    low = (before + partial + after).astype(bf16).astype(f32).T
+    def after(values, *events):
+        return lax.optimization_barrier((values, events))[0]
+
+    def source(step):
+        return jnp.where(place >= step, place - step, jnp.minimum(place + step, tensor - 1))
 
     def meta(items):
         pairs = []
-        for source, j in items:
-            there = (source >= 0) & (source < tensor)
-            pairs += [jnp.clip(source, 0, tensor - 1) * chunks + j, there.astype(i32)]
+        for device, j, there in items:
+            pairs += [device * chunks + j, there]
         return jnp.stack([jnp.asarray(p, i32) for p in pairs])
 
-    items = [(place, j) for j in range(chunks)]
-    total = project(meta(items), ints, None, own, query_weight, sizes)
-    for step in range(1, tensor):
-        pieces = [range(chunks)] if step < tensor - 1 else [[j] for j in range(chunks)]
-        for js in pieces:
-            items = [(place - step, j) for j in js] + [(place + step, j) for j in js]
-            xs = [right[step][j] for j in js] + [left[step][j] for j in js]
-            final = step == tensor - 1 and js[-1] == chunks - 1
-            with_delta = step == tensor - 1 and js[0] == 0
-            total = project(
-                meta(items),
-                ints,
-                total,
-                xs,
-                query_weight,
-                sizes,
-                low if with_delta else None,
-                got if with_delta else None,
-                rows if final else None,
-            )
+    def move(x, way, step):
+        if way > 0:
+            pairs = [(i, i + 1) for i in range(step - 1, tensor - 1)]
+        else:
+            pairs = [(i, i - 1) for i in range(1, tensor - step + 1)]
+        return lax.ppermute(x, "tensor", pairs)
+
+    def send(x, step):
+        pairs = [(i, (i + step) % replicas) for i in range(replicas)]
+        return lax.ppermute(x, "dp", pairs)
+
+    one = jnp.int32(1)
+
+    def arrivals(total, step, js, **more):
+        items, xs = [], []
+        for j in js:
+            if 2 * step >= tensor:
+                items.append((source(step), j, one))
+                xs.append((right[step][j], left[step][j]))
+            else:
+                items.append((jnp.maximum(place - step, 0), j, (place >= step).astype(i32)))
+                xs.append((right[step][j],))
+                behind = place + step
+                items.append((jnp.minimum(behind, tensor - 1), j, (behind < tensor).astype(i32)))
+                xs.append((left[step][j],))
+        return project(meta(items), ints, total, xs, query_weight, sizes, **more)
+
+    factors = choose(*ints[:2], adapter_down, adapter_up, replicas, capacity)
+    own = pack(hidden, block_live_count, (piece,) * chunks)
+    right, left = [own], [own]
+
+    def pass_on(first=(), final=()):
+        step = len(right)
+        for w, moved in ((1, right), (-1, left)):
+            xs = list(moved[-1])
+            xs[0] = after(xs[0], *first)
+            xs[-1] = after(xs[-1], *final)
+            moved.append([move(x, w, step) for x in xs])
+
+    pass_on()
+    got = [factors[0]] + [send(factors[step], step) for step in range(1, replicas)]
+    own_total = project(
+        meta([(place, j, one) for j in range(chunks)]),
+        ints, None, [(x,) for x in own], query_weight, sizes,
+    )
+    partial = shrink(*ints, own, got, capacity, pool)
+    total = arrivals(own_total, 1, range(chunks))
+    first_total = total
+
+    sums = [partial]
+    gap = 1
+    while gap < tensor:
+        pairs = [(i, i ^ gap) for i in range(tensor)]
+        sums.append(sums[-1] + lax.ppermute(sums[-1], "tensor", pairs))
+        gap *= 2
+
+    for step in range(2, tensor):
+        if step == tensor - 1:
+            pass_on([first_total], [sums[1], total] if step > 2 else [])
+            break
+        pass_on(*([[own_total], [partial]] if step == 2 else []))
+        total = arrivals(total, step, range(chunks))
+    for j in range(chunks):
+        more = {"rows": rows} if j == chunks - 1 else {}
+        if j == chunks - 1:
+            more.update(low=sums[-1].astype(bf16).astype(f32).T, factors=got)
+        total = arrivals(total, tensor - 1, [j], **more)
     return total
 
 

time: 235 us -> 237 us (level)
  Pallas kernels: 74.2 us -> 98.5 us
  waiting for transfers between devices: 102 us -> 82.6 us
  other arithmetic: 5.99 us -> 2.06 us
    pallas_call x1, Pallas kernels: 3.09 us -> 33.7 us  [choose(): pl.pallas_call(functools.partial(choose_kernel, replicas=replicas, capaci...]
    ppermute x21 -> x17, waiting for transfers between devices: 102 us -> 82.6 us  [the longest x2 49.6 us: shards(): sums.append(sums[-1] + lax.ppermute(sums[-1], 'tensor', pairs))]
    pallas_call x5, Pallas kernels: 62.3 us -> 57.6 us  [project(): pl.pallas_call(functools.partial(project_kernel, groups=tuple((len(g) for...]
    add x3 -> x1, other arithmetic: 4.8 us -> 0.75 us  [shards(): sums.append(sums[-1] + lax.ppermute(sums[-1], 'tensor', pairs))]
    ppermute x21 -> x17, starting transfers between devices: 45.3 us -> 46.6 us  [the longest x12 22 us: move(): return lax.ppermute(x, 'tensor', pairs)]
    unnamed x24 -> x30, local copies, waits for them, and re-layouts: 4.61 us -> 5.27 us
  transfers between devices with their start and end apart: 21 -> 17, of which waited for: 8 -> 7; matrix products, arithmetic and copies ran while one was open for 3% -> 1% of each run, Pallas kernels for 26% -> 22%
where the time goes in v4:
time: 237 us; the launch traced here: 236 us
  Pallas kernels  98.5 us (42%)
  waiting for transfers between devices  82.6 us (35%)
  starting transfers between devices  46.6 us (20%)
  local copies, waits for them, and re-layouts  6.42 us (3%)
    pallas_call x5, Pallas kernels, project(): pl.pallas_call(functools.partial(project_kernel, groups=tuple((len(g) for...  57.6 us
    ppermute x2, waiting for transfers between devices, shards(): sums.append(sums[-1] + lax.ppermute(sums[-1], 'tensor', pairs))  49.6 us
    pallas_call x1, Pallas kernels, choose(): pl.pallas_call(functools.partial(choose_kernel, replicas=replicas, capaci...  33.7 us
    ppermute x12, starting transfers between devices, move(): return lax.ppermute(x, 'tensor', pairs)  22 us
    ppermute x12, waiting for transfers between devices, move(): return lax.ppermute(x, 'tensor', pairs)  21.9 us
    ppermute x3, starting transfers between devices, send(): return lax.ppermute(x, 'dp', pairs)  15.1 us
    ppermute x3, waiting for transfers between devices, send(): return lax.ppermute(x, 'dp', pairs)  11.1 us
    ppermute x2, starting transfers between devices, shards(): sums.append(sums[-1] + lax.ppermute(sums[-1], 'tensor', pairs))  9.51 us
  transfers between devices with their start and end apart: 17, of which 7 were waited for; matrix products, arithmetic and copies ran while one was open for 1% of the time, Pallas kernels for 22%

profile of v4, /device:TPU:0, one launch (start us, length us, event | category | flops | bytes accessed | tf_op | source)
XLA Modules:
  0.0 236.4 jit_solution(12862788075439639263)
XLA Ops:
  0.0 0.8 copy-done.10
  0.8 0.8 copy-done.12
  1.6 33.7 %choose.1 = (bf16[2,128,2048]{2,1,0:T(8,128)(2,1)S(1)}, bf16[2,128,2048]{2,1,0:T(8,128)(2,1)S(1)}, bf16[2,128,2048]{2,1,0:T(8,128)(2,1)S(1)}, bf16[2,128,2048]{2,1,0:T(8,128)(2,1)}) custom-call(s32[4,6]{1,0:T(4,128)S(1)} %copy-done.10, s32[32]{0:T(128)S(1)} %copy-done.12, bf16[8,64,2048]{2,1,0:T(8,128)(2,1)} %down.1, bf16[8,64,2048]{2,1,0:T(8,128)(2,1)} %up.1), custom_call_target="tpu_custom_call" | custom-call | flops 1 | bytes 1 | tf_op jit(solution)/shard_map/choose/pallas_call | solution.py:102
  35.4 0.5 collective-permute-start.6
  35.9 2.6 %collective-permute-start.7 = (bf16[2,128,2048]{2,1,0:T(8,128)(2,1)S(1)}, bf16[2,128,2048]{2,1,0:T(8,128)(2,1)S(1)}, u32[]{:S(2)}, u32[]{:S(2)}) collective-permute-start(bf16[2,128,2048]{2,1,0:T(8,128)(2,1)S(1)} %get-tuple-element.25), channel_id=1, source_target_pairs={{0,8},{4,12},{8,0},{12,4},{1,9},{5,13},{9,1},{13,5},{2,10},{6,14},... | collective-permute-start | bytes 3145736 | tf_op jit(solution)/shard_map/ppermute | solution.py:351
  38.5 2.5 %pack.1 = (bf16[576,1024]{1,0:T(8,128)(2,1)S(1)}, bf16[576,1024]{1,0:T(8,128)(2,1)S(1)}) custom-call(s32[1,6]{1,0:T(1,128)S(1)} %copy-done.14, bf16[768,2048]{1,0:T(8,128)(2,1)S(1)} %copy-done.7), custom_call_target="tpu_custom_call" | custom-call | flops 1 | bytes 1 | tf_op jit(solution)/shard_map/pack/pallas_call | solution.py:57
  41.0 0.0 copy-start
  41.0 4.6 %collective-permute-start = (bf16[576,1024]{1,0:T(8,128)(2,1)S(1)}, bf16[576,1024]{1,0:T(8,128)(2,1)}, u32[]{:S(2)}, u32[]{:S(2)}) collective-permute-start(bf16[576,1024]{1,0:T(8,128)(2,1)S(1)} %get-tuple-element.19.refs_4_.rest_0_), channel_id=1, source_target_pairs={{0,1},{1,2},{2,3},{4,5},{5,6},{6,7},{8,9},{9,10},{10,11},{12,13},{... | collective-permute-start | bytes 3538952 | tf_op jit(solution)/shard_map/ppermute | solution.py:347
  45.6 1.3 collective-permute-start.1
  46.9 5.6 %collective-permute-start.2 = (bf16[576,1024]{1,0:T(8,128)(2,1)S(1)}, bf16[576,1024]{1,0:T(8,128)(2,1)}, u32[]{:S(2)}, u32[]{:S(2)}) collective-permute-start(bf16[576,1024]{1,0:T(8,128)(2,1)S(1)} %get-tuple-element.20.refs_5_.rest_1_), channel_id=1, source_target_pairs={{0,1},{1,2},{2,3},{4,5},{5,6},{6,7},{8,9},{9,10},{10,11},{12,13},{... | collective-permute-start | bytes 3538952 | tf_op jit(solution)/shard_map/ppermute | solution.py:347
  52.5 8.1 %collective-permute-done.6.rest_3_.refs_10_ = bf16[2,128,2048]{2,1,0:T(8,128)(2,1)S(1)} collective-permute-done((bf16[2,128,2048]{2,1,0:T(8,128)(2,1)S(1)}, bf16[2,128,2048]{2,1,0:T(8,128)(2,1)S(1)}, u32[]{:S(2)}, u32[]{:S(2)}) %collective-permute-start.6) | collective-permute-done | bytes 1048608 | tf_op jit(solution)/shard_map/ppermute | solution.py:351
  60.6 1.0 copy-done.1
  61.5 1.3 collective-permute-start.3
  62.8 0.0 collective-permute-done.7.rest_4_.refs_11_
  62.8 1.0 copy-done.4
  63.8 12.0 %collective-permute-start.8 = (bf16[2,128,2048]{2,1,0:T(8,128)(2,1)}, bf16[2,128,2048]{2,1,0:T(8,128)(2,1)}, u32[]{:S(2)}, u32[]{:S(2)}) collective-permute-start(bf16[2,128,2048]{2,1,0:T(8,128)(2,1)} %get-tuple-element.26), channel_id=1, source_target_pairs={{0,12},{4,0},{8,4},{12,8},{1,13},{5,1},{9,5},{13,9},{2,14},{6,2},{... | collective-permute-start | bytes 3145736 | tf_op jit(solution)/shard_map/ppermute | solution.py:351
  75.8 0.1 pad_add_fusion.2.refs_0_
  75.9 9.5 %project.5.refs_4_ = f32[576,2048]{1,0:T(8,128)} custom-call(s32[4]{0:T(128)S(1)} %pad_add_fusion.2.refs_0_, s32[4,6]{1,0:T(4,128)S(1)} %copy-done.11, s32[32]{0:T(128)S(1)} %copy-done.13, s32[1,6]{1,0:T(1,128)S(1)} %copy-done.14, bf16[576,1024]{1,0:T(8,128)(2,1)S(1)} %get-tuple-element.19.refs_4_.rest_0_, ...), custom_call_target="tpu_custom_call" | custom-call | flops 1 | bytes 1 | tf_op jit(solution)/shard_map/project/pallas_call | solution.py:284
  85.4 3.0 %collective-permute-done.8.rest_5_.refs_12_ = bf16[2,128,2048]{2,1,0:T(8,128)(2,1)} collective-permute-done((bf16[2,128,2048]{2,1,0:T(8,128)(2,1)}, bf16[2,128,2048]{2,1,0:T(8,128)(2,1)}, u32[]{:S(2)}, u32[]{:S(2)}) %collective-permute-start.8) | collective-permute-done | bytes 1048608 | tf_op jit(solution)/shard_map/ppermute | solution.py:351
  88.5 4.7 %shrink.1 = f32[64,576]{1,0:T(8,128)S(1)} custom-call(s32[4,6]{1,0:T(4,128)S(1)} %copy-done.11, s32[32]{0:T(128)S(1)} %copy-done.13, s32[1,6]{1,0:T(1,128)S(1)} %copy-done.14, bf16[576,1024]{1,0:T(8,128)(2,1)S(1)} %get-tuple-element.19.refs_4_.rest_0_, bf16[576,1024]{1,0:T(8,128)(2,1)} %copy-done, ...), custom_call_target="tpu_custom_call" | custom-call | flops 1 | bytes 1 | tf_op jit(solution)/shard_map/shrink/pallas_call | solution.py:166
  93.2 0.0 copy-start.9
  93.2 0.7 copy-done.9
  93.9 1.7 collective-permute-start.4
  95.6 1.3 collective-permute-start.5
  96.9 0.7 collective-permute-start.9
  97.6 3.1 %collective-permute-done.3.refs_8_ = bf16[576,1024]{1,0:T(8,128)(2,1)} collective-permute-done((bf16[576,1024]{1,0:T(8,128)(2,1)S(1)}, bf16[576,1024]{1,0:T(8,128)(2,1)}, u32[]{:S(2)}, u32[]{:S(2)}) %collective-permute-start.3) | collective-permute-done | bytes 1179680 | tf_op jit(solution)/shard_map/ppermute | solution.py:347
  100.7 1.3 collective-permute-start.10
  102.0 1.1 copy.9
  103.1 6.9 %collective-permute-start.13 = (f32[64,576]{0,1:T(8,128)S(1)}, f32[64,576]{0,1:T(8,128)S(1)}, u32[]{:S(2)}, u32[]{:S(2)}) collective-permute-start(f32[64,576]{0,1:T(8,128)S(1)} %copy.9), channel_id=1, source_target_pairs={{0,1},{1,0},{2,3},{3,2},{4,5},{5,4},{6,7},{7,6},{8,9},{9,8},{10,11... | collective-permute-start | bytes 442376 | tf_op jit(solution)/shard_map/ppermute | solution.py:395
  110.0 0.1 stack.74.refs_0_
  110.1 0.1 pad_add_fusion.3.refs_0_
  110.2 14.7 %project.6.refs_4_ = f32[576,2048]{1,0:T(8,128)} custom-call(s32[8]{0:T(128)S(1)} %stack.74.refs_0_, s32[4,6]{1,0:T(4,128)S(1)} %copy-done.11, s32[32]{0:T(128)S(1)} %copy-done.13, s32[1,6]{1,0:T(1,128)S(1)} %copy-done.14, f32[576,2048]{1,0:T(8,128)} %project.5.refs_4_, bf16[576,1024]{1,0:T(8,128)(2,1)} %collective-permute-done.refs_5_, ...), custom_call_target="tpu_custom_call" | custom-call | flops 1 | bytes 1 | tf_op jit(solution)/shard_map/project/pallas_call | solution.py:284
  124.9 35.5 %collective-permute-done.13 = f32[64,576]{0,1:T(8,128)S(1)} collective-permute-done((f32[64,576]{0,1:T(8,128)S(1)}, f32[64,576]{0,1:T(8,128)S(1)}, u32[]{:S(2)}, u32[]{:S(2)}) %collective-permute-start.13) | collective-permute-done | bytes 147488 | tf_op jit(solution)/shard_map/ppermute | solution.py:395
  160.4 0.8 add.44
  161.1 0.7 collective-permute-start.11
  161.9 1.3 collective-permute-start.12
  163.2 11.7 %project.7.refs_4_ = f32[576,2048]{1,0:T(8,128)} custom-call(s32[4]{0:T(128)S(1)} %pad_add_fusion.3.refs_0_, s32[4,6]{1,0:T(4,128)S(1)} %copy-done.11, s32[32]{0:T(128)S(1)} %copy-done.13, s32[1,6]{1,0:T(1,128)S(1)} %copy-done.14, f32[576,2048]{1,0:T(8,128)} %project.6.refs_4_, bf16[576,1024]{1,0:T(8,128)(2,1)} %collective-permute-done.4.refs_5_, ...), custom_call_target="tpu_custom_call" | custom-call | flops 1 | bytes 1 | tf_op jit(solution)/shard_map/project/pallas_call | solution.py:284
  174.9 1.0 copy-done.8
  175.9 0.7 collective-permute-start.14
  176.7 1.5 collective-permute-start.15
  178.1 2.6 %collective-permute-start.16 = (f32[64,576]{0,1:T(8,128)}, f32[64,576]{0,1:T(8,128)}, u32[]{:S(2)}, u32[]{:S(2)}) collective-permute-start(f32[64,576]{0,1:T(8,128)} %add.44), channel_id=1, source_target_pairs={{0,2},{1,3},{2,0},{3,1},{4,6},{5,7},{6,4},{7,5},{8,10},{9,11},{10,... | collective-permute-start | bytes 442376 | tf_op jit(solution)/shard_map/ppermute | solution.py:395
  180.7 0.1 pad_add_fusion
  180.8 14.1 %collective-permute-done.16 = f32[64,576]{0,1:T(8,128)} collective-permute-done((f32[64,576]{0,1:T(8,128)}, f32[64,576]{0,1:T(8,128)}, u32[]{:S(2)}, u32[]{:S(2)}) %collective-permute-start.16) | collective-permute-done | bytes 147488 | tf_op jit(solution)/shard_map/ppermute | solution.py:395
  194.9 1.1 convert_bitcast_fusion.refs_8_
  196.0 3.2 %collective-permute-done.12.refs_6_ = bf16[576,1024]{1,0:T(8,128)(2,1)} collective-permute-done((bf16[576,1024]{1,0:T(8,128)(2,1)}, bf16[576,1024]{1,0:T(8,128)(2,1)}, u32[]{:S(2)}, u32[]{:S(2)}) %collective-permute-start.12) | collective-permute-done | bytes 1179680 | tf_op jit(solution)/shard_map/ppermute | solution.py:347
  199.2 8.9 %project.8.refs_4_ = f32[576,2048]{1,0:T(8,128)} custom-call(s32[2]{0:T(128)S(1)} %get-tuple-element.33.refs_0_, s32[4,6]{1,0:T(4,128)S(1)} %copy-done.11, s32[32]{0:T(128)S(1)} %copy-done.13, s32[1,6]{1,0:T(1,128)S(1)} %copy-done.14, f32[576,2048]{1,0:T(8,128)} %project.7.refs_4_, bf16[576,1024]{1,0:T(8,128)(2,1)S(1)} %collective-permute-done.11.refs_5_, ...), custom_call_target="tpu_custom_call" | custom-call | flops 1 | bytes 1 | tf_op jit(solution)/shard_map/project/pallas_call | solution.py:284
  208.1 15.6 %collective-permute-done.15.refs_6_ = bf16[576,1024]{1,0:T(8,128)(2,1)} collective-permute-done((bf16[576,1024]{1,0:T(8,128)(2,1)}, bf16[576,1024]{1,0:T(8,128)(2,1)}, u32[]{:S(2)}, u32[]{:S(2)}) %collective-permute-start.15) | collective-permute-done | bytes 1179680 | tf_op jit(solution)/shard_map/ppermute | solution.py:347
  223.7 12.7 %project.9 = bf16[768,2048]{1,0:T(8,128)(2,1)} custom-call(s32[2]{0:T(128)S(1)} %get-tuple-element.34.refs_0_, s32[4,6]{1,0:T(4,128)S(1)} %copy-done.11, s32[32]{0:T(128)S(1)} %copy-done.13, s32[1,6]{1,0:T(1,128)S(1)} %copy-done.14, f32[576,2048]{1,0:T(8,128)} %project.8.refs_4_, bf16[576,1024]{1,0:T(8,128)(2,1)S(1)} %collective-permute-done.14.refs_5_, ...), custom_call_target="tpu_custom_call" | custom-call | flops 1 | bytes 1 | tf_op jit(solution)/shard_map/project/pallas_call | solution.py:284
  (31 shorter events, 0.1 us)
Async XLA Ops:
  0.0 38.5 %copy-start.7 = (bf16[768,2048]{1,0:T(8,128)(2,1)S(1)}, bf16[768,2048]{1,0:T(8,128)(2,1)}, u32[]{:S(2)}) copy-start(bf16[768,2048]{1,0:T(8,128)(2,1)} %x.1) | copy-start | bytes 9437188
  0.0 0.8 copy-start.10
  0.8 0.8 copy-start.12
  1.6 36.8 %copy-start.14 = (s32[1,6]{1,0:T(1,128)S(1)}, s32[1,6]{1,0:T(1,128)}, u32[]{:S(2)}) copy-start(s32[1,6]{1,0:T(1,128)} %refs_3_.9) | copy-start | bytes 76
  35.4 25.2 %collective-permute-start.6 = (bf16[2,128,2048]{2,1,0:T(8,128)(2,1)S(1)}, bf16[2,128,2048]{2,1,0:T(8,128)(2,1)S(1)}, u32[]{:S(2)}, u32[]{:S(2)}) collective-permute-start(bf16[2,128,2048]{2,1,0:T(8,128)(2,1)S(1)} %get-tuple-element.24), channel_id=1, source_target_pairs={{0,4},{4,8},{8,12},{12,0},{1,5},{5,9},{9,13},{13,1},{2,6},{6,10},{... | collective-permute-start | bytes 3145736 | tf_op jit(solution)/shard_map/ppermute | solution.py:351
  35.9 40.1 %copy-start.11 = (s32[4,6]{1,0:T(4,128)S(1)}, s32[4,6]{1,0:T(4,128)}, u32[]{:S(2)}) copy-start(s32[4,6]{1,0:T(4,128)} %refs_1_.9) | copy-start | bytes 292
  35.9 40.1 %copy-start.13 = (s32[32]{0:T(128)S(1)}, s32[32]{0:T(128)}, u32[]{:S(2)}) copy-start(s32[32]{0:T(128)} %refs_2_.9) | copy-start | bytes 388
  35.9 27.0 %collective-permute-start.7 = (bf16[2,128,2048]{2,1,0:T(8,128)(2,1)S(1)}, bf16[2,128,2048]{2,1,0:T(8,128)(2,1)S(1)}, u32[]{:S(2)}, u32[]{:S(2)}) collective-permute-start(bf16[2,128,2048]{2,1,0:T(8,128)(2,1)S(1)} %get-tuple-element.25), channel_id=1, source_target_pairs={{0,8},{4,12},{8,0},{12,4},{1,9},{5,13},{9,1},{13,5},{2,10},{6,14},... | collective-permute-start | bytes 3145736 | tf_op jit(solution)/shard_map/ppermute | solution.py:351
  41.0 44.5 %copy-start = (bf16[576,1024]{1,0:T(8,128)(2,1)}, bf16[576,1024]{1,0:T(8,128)(2,1)S(1)}, u32[]{:S(2)}) copy-start(bf16[576,1024]{1,0:T(8,128)(2,1)S(1)} %get-tuple-element.20.refs_5_.rest_1_) | copy-start | bytes 3538948
  41.0 52.9 %collective-permute-start = (bf16[576,1024]{1,0:T(8,128)(2,1)S(1)}, bf16[576,1024]{1,0:T(8,128)(2,1)}, u32[]{:S(2)}, u32[]{:S(2)}) collective-permute-start(bf16[576,1024]{1,0:T(8,128)(2,1)S(1)} %get-tuple-element.19.refs_4_.rest_0_), channel_id=1, source_target_pairs={{0,1},{1,2},{2,3},{4,5},{5,6},{6,7},{8,9},{9,10},{10,11},{12,13},{... | collective-permute-start | bytes 3538952 | tf_op jit(solution)/shard_map/ppermute | solution.py:347
  45.6 50.0 %collective-permute-start.1 = (bf16[576,1024]{1,0:T(8,128)(2,1)S(1)}, bf16[576,1024]{1,0:T(8,128)(2,1)}, u32[]{:S(2)}, u32[]{:S(2)}) collective-permute-start(bf16[576,1024]{1,0:T(8,128)(2,1)S(1)} %get-tuple-element.19.refs_4_.rest_0_), channel_id=1, source_target_pairs={{1,0},{2,1},{3,2},{5,4},{6,5},{7,6},{9,8},{10,9},{11,10},{13,12},{... | collective-permute-start | bytes 3538952 | tf_op jit(solution)/shard_map/ppermute | solution.py:347
  46.9 50.0 %collective-permute-start.2 = (bf16[576,1024]{1,0:T(8,128)(2,1)S(1)}, bf16[576,1024]{1,0:T(8,128)(2,1)}, u32[]{:S(2)}, u32[]{:S(2)}) collective-permute-start(bf16[576,1024]{1,0:T(8,128)(2,1)S(1)} %get-tuple-element.20.refs_5_.rest_1_), channel_id=1, source_target_pairs={{0,1},{1,2},{2,3},{4,5},{5,6},{6,7},{8,9},{9,10},{10,11},{12,13},{... | collective-permute-start | bytes 3538952 | tf_op jit(solution)/shard_map/ppermute | solution.py:347
  60.6 1.0 copy-start.1
  61.5 39.2 %collective-permute-start.3 = (bf16[576,1024]{1,0:T(8,128)(2,1)S(1)}, bf16[576,1024]{1,0:T(8,128)(2,1)}, u32[]{:S(2)}, u32[]{:S(2)}) collective-permute-start(bf16[576,1024]{1,0:T(8,128)(2,1)S(1)} %get-tuple-element.20.refs_5_.rest_1_), channel_id=1, source_target_pairs={{1,0},{2,1},{3,2},{5,4},{6,5},{7,6},{9,8},{10,9},{11,10},{13,12},{... | collective-permute-start | bytes 3538952 | tf_op jit(solution)/shard_map/ppermute | solution.py:347
  62.8 1.0 copy-start.4
  63.8 24.7 %collective-permute-start.8 = (bf16[2,128,2048]{2,1,0:T(8,128)(2,1)}, bf16[2,128,2048]{2,1,0:T(8,128)(2,1)}, u32[]{:S(2)}, u32[]{:S(2)}) collective-permute-start(bf16[2,128,2048]{2,1,0:T(8,128)(2,1)} %get-tuple-element.26), channel_id=1, source_target_pairs={{0,12},{4,0},{8,4},{12,8},{1,13},{5,1},{9,5},{13,9},{2,14},{6,2},{... | collective-permute-start | bytes 3145736 | tf_op jit(solution)/shard_map/ppermute | solution.py:351
  75.9 12.6 %copy-start.2 = (bf16[2,128,2048]{2,1,0:T(8,128)(2,1)S(1)}, bf16[2,128,2048]{2,1,0:T(8,128)(2,1)}, u32[]{:S(2)}) copy-start(bf16[2,128,2048]{2,1,0:T(8,128)(2,1)} %copy-done.1) | copy-start | bytes 3145732
  75.9 12.6 %copy-start.5 = (bf16[2,128,2048]{2,1,0:T(8,128)(2,1)S(1)}, bf16[2,128,2048]{2,1,0:T(8,128)(2,1)}, u32[]{:S(2)}) copy-start(bf16[2,128,2048]{2,1,0:T(8,128)(2,1)} %copy-done.4) | copy-start | bytes 3145732
  93.2 0.7 copy-start.9
  93.9 67.3 %collective-permute-start.4 = (bf16[576,1024]{1,0:T(8,128)(2,1)}, bf16[576,1024]{1,0:T(8,128)(2,1)}, u32[]{:S(2)}, u32[]{:S(2)}) collective-permute-start(bf16[576,1024]{1,0:T(8,128)(2,1)} %collective-permute-done.refs_5_), channel_id=1, source_target_pairs={{1,2},{2,3},{5,6},{6,7},{9,10},{10,11},{13,14},{14,15},{17,18},{18... | collective-permute-start | bytes 3538952 | tf_op jit(solution)/shard_map/ppermute | solution.py:347
  95.6 66.3 %collective-permute-start.5 = (bf16[576,1024]{1,0:T(8,128)(2,1)}, bf16[576,1024]{1,0:T(8,128)(2,1)}, u32[]{:S(2)}, u32[]{:S(2)}) collective-permute-start(bf16[576,1024]{1,0:T(8,128)(2,1)} %collective-permute-done.1.refs_6_), channel_id=1, source_target_pairs={{1,0},{2,1},{5,4},{6,5},{9,8},{10,9},{13,12},{14,13},{17,16},{18,1... | collective-permute-start | bytes 3538952 | tf_op jit(solution)/shard_map/ppermute | solution.py:347
  96.9 66.3 %collective-permute-start.9 = (bf16[576,1024]{1,0:T(8,128)(2,1)}, bf16[576,1024]{1,0:T(8,128)(2,1)S(1)}, u32[]{:S(2)}, u32[]{:S(2)}) collective-permute-start(bf16[576,1024]{1,0:T(8,128)(2,1)} %collective-permute-done.2.refs_7_), channel_id=1, source_target_pairs={{1,2},{2,3},{5,6},{6,7},{9,10},{10,11},{13,14},{14,15},{17,18},{18... | collective-permute-start | bytes 3538952 | tf_op jit(solution)/shard_map/ppermute | solution.py:347
  100.7 62.5 %collective-permute-start.10 = (bf16[576,1024]{1,0:T(8,128)(2,1)}, bf16[576,1024]{1,0:T(8,128)(2,1)}, u32[]{:S(2)}, u32[]{:S(2)}) collective-permute-start(bf16[576,1024]{1,0:T(8,128)(2,1)} %collective-permute-done.3.refs_8_), channel_id=1, source_target_pairs={{1,0},{2,1},{5,4},{6,5},{9,8},{10,9},{13,12},{14,13},{17,16},{18,1... | collective-permute-start | bytes 3538952 | tf_op jit(solution)/shard_map/ppermute | solution.py:347
  103.1 57.3 %collective-permute-start.13 = (f32[64,576]{0,1:T(8,128)S(1)}, f32[64,576]{0,1:T(8,128)S(1)}, u32[]{:S(2)}, u32[]{:S(2)}) collective-permute-start(f32[64,576]{0,1:T(8,128)S(1)} %copy.9), channel_id=1, source_target_pairs={{0,1},{1,0},{2,3},{3,2},{4,5},{5,4},{6,7},{7,6},{8,9},{9,8},{10,11... | collective-permute-start | bytes 442376 | tf_op jit(solution)/shard_map/ppermute | solution.py:395
  161.1 34.9 %collective-permute-start.11 = (bf16[576,1024]{1,0:T(8,128)(2,1)}, bf16[576,1024]{1,0:T(8,128)(2,1)S(1)}, u32[]{:S(2)}, u32[]{:S(2)}) collective-permute-start(bf16[576,1024]{1,0:T(8,128)(2,1)} %collective-permute-done.4.refs_5_), channel_id=1, source_target_pairs={{2,3},{6,7},{10,11},{14,15},{18,19},{22,23},{26,27},{30,31}} | collective-permute-start | bytes 3538952 | tf_op jit(solution)/shard_map/ppermute | solution.py:347
  161.9 37.3 %collective-permute-start.12 = (bf16[576,1024]{1,0:T(8,128)(2,1)}, bf16[576,1024]{1,0:T(8,128)(2,1)}, u32[]{:S(2)}, u32[]{:S(2)}) collective-permute-start(bf16[576,1024]{1,0:T(8,128)(2,1)} %collective-permute-done.5.refs_6_), channel_id=1, source_target_pairs={{1,0},{5,4},{9,8},{13,12},{17,16},{21,20},{25,24},{29,28}} | collective-permute-start | bytes 3538952 | tf_op jit(solution)/shard_map/ppermute | solution.py:347
  174.9 1.0 copy-start.8
  175.9 32.2 %collective-permute-start.14 = (bf16[576,1024]{1,0:T(8,128)(2,1)}, bf16[576,1024]{1,0:T(8,128)(2,1)S(1)}, u32[]{:S(2)}, u32[]{:S(2)}) collective-permute-start(bf16[576,1024]{1,0:T(8,128)(2,1)} %copy-done.8), channel_id=1, source_target_pairs={{2,3},{6,7},{10,11},{14,15},{18,19},{22,23},{26,27},{30,31}} | collective-permute-start | bytes 3538952 | tf_op jit(solution)/shard_map/ppermute | solution.py:347
  176.7 47.0 %collective-permute-start.15 = (bf16[576,1024]{1,0:T(8,128)(2,1)}, bf16[576,1024]{1,0:T(8,128)(2,1)}, u32[]{:S(2)}, u32[]{:S(2)}) collective-permute-start(bf16[576,1024]{1,0:T(8,128)(2,1)} %collective-permute-done.10.refs_8_), channel_id=1, source_target_pairs={{1,0},{5,4},{9,8},{13,12},{17,16},{21,20},{25,24},{29,28}} | collective-permute-start | bytes 3538952 | tf_op jit(solution)/shard_map/ppermute | solution.py:347
  178.1 16.8 %collective-permute-start.16 = (f32[64,576]{0,1:T(8,128)}, f32[64,576]{0,1:T(8,128)}, u32[]{:S(2)}, u32[]{:S(2)}) collective-permute-start(f32[64,576]{0,1:T(8,128)} %add.44), channel_id=1, source_target_pairs={{0,2},{1,3},{2,0},{3,1},{4,6},{5,7},{6,4},{7,5},{8,10},{9,11},{10,... | collective-permute-start | bytes 442376 | tf_op jit(solution)/shard_map/ppermute | solution.py:395
  199.2 24.5 %copy-start.3 = (bf16[2,128,2048]{2,1,0:T(8,128)(2,1)S(1)}, bf16[2,128,2048]{2,1,0:T(8,128)(2,1)}, u32[]{:S(2)}) copy-start(bf16[2,128,2048]{2,1,0:T(8,128)(2,1)} %copy-done.1) | copy-start | bytes 3145732
  199.2 24.5 %copy-start.6 = (bf16[2,128,2048]{2,1,0:T(8,128)(2,1)S(1)}, bf16[2,128,2048]{2,1,0:T(8,128)(2,1)}, u32[]{:S(2)}) copy-start(bf16[2,128,2048]{2,1,0:T(8,128)(2,1)} %copy-done.4) | copy-start | bytes 3145732

commit v5 on v4

--- a/solution.py
+++ b/solution.py
@@ -22,7 +22,7 @@
     return pltpu.CompilerParams(vmem_limit_bytes=vmem_bytes)
 
 
-def cost(flops, moved):
+def cost():
     return pl.CostEstimate(flops=1, bytes_accessed=1, transcendentals=0)
 
 
@@ -42,32 +42,10 @@
     return (lax.broadcasted_iota(i32, shape, 1 - axis) == place).astype(f32).astype(bf16)
 
 
-def pack_kernel(live, x, *outs):
-    hot = one_hot(live, x.shape[0], 1)
-    start = 0
-    for out in outs:
-        stop = start + out.shape[1]
-        rows = jnp.dot(hot, x[:, start:stop], preferred_element_type=f32)
-        out[...] = rows.astype(bf16)
-        start = stop
-
-
-def pack(hidden, live, widths):
-    rows, width = hidden.shape
-    return pl.pallas_call(
-        pack_kernel,
-        grid=(1,),
-        in_specs=[smem, pl.BlockSpec((rows, width), lambda i: (0, 0))],
-        out_specs=[pl.BlockSpec((live_total, w), lambda i: (0, 0)) for w in widths],
-        out_shape=[jax.ShapeDtypeStruct((live_total, w), bf16) for w in widths],
-        compiler_params=params(),
-        cost_estimate=cost(2 * rows * live_total * width, (rows + live_total) * width * 2),
-        name="pack",
-    )(live, hidden)
-
-
-def choose_kernel(variants, slots, down, up, *rest, replicas, capacity, blocks):
-    outs, sems = rest[:replicas], rest[replicas]
+def prepare_kernel(
+    variants, slots, live, x, down, up, *rest, chunks, replicas, capacity, blocks
+):
+    packed, picked, sems = rest[:chunks], rest[chunks : chunks + replicas], rest[-1]
     pool, rank = down.shape[0], down.shape[1]
     me = lax.axis_index("dp")
     copies = []
@@ -83,34 +61,48 @@
                 index[m] = jnp.where(mine & (seen == m), slot - owner * pool, index[m])
             seen = seen + mine.astype(i32)
         for m in range(capacity):
-            for kind, source in enumerate((down, up)):
+            for kind, pooled in enumerate((down, up)):
                 copies.append(
                     pltpu.make_async_copy(
-                        source.at[index[m]],
-                        outs[step].at[kind, m * rank : (m + 1) * rank],
+                        pooled.at[index[m]],
+                        picked[step].at[kind, m * rank : (m + 1) * rank],
                         sems.at[len(copies)],
                     )
                 )
                 copies[-1].start()
+    hot = one_hot(live, x.shape[0], 1)
+    start = 0
+    for out in packed:
+        stop = start + out.shape[1]
+        out[...] = jnp.dot(hot, x[:, start:stop], preferred_element_type=f32).astype(bf16)
+        start = stop
     for copy in copies:
         copy.wait()
 
 
-def choose(variants, slots, down, up, replicas, capacity):
-    pool, rank, width = down.shape
-    out = jax.ShapeDtypeStruct((2, capacity * rank, width), bf16)
-    return pl.pallas_call(
+def prepare(ints, hidden, down, up, widths, replicas, capacity):
+    rows, width = hidden.shape
+    depth = capacity * down.shape[1]
+    outs = [jax.ShapeDtypeStruct((live_total, w), bf16) for w in widths]
+    outs += [jax.ShapeDtypeStruct((2, depth, width), bf16)] * replicas
+    results = pl.pallas_call(
         functools.partial(
-            choose_kernel, replicas=replicas, capacity=capacity, blocks=variants.shape[1]
+            prepare_kernel,
+            chunks=len(widths),
+            replicas=replicas,
+            capacity=capacity,
+            blocks=ints[0].shape[1],
         ),
-        in_specs=[smem, smem, hbm, hbm],
-        out_specs=[hbm] * replicas,
-        out_shape=[out] * replicas,
+        grid=(1,),
+        in_specs=[smem] * 3 + [pl.BlockSpec((rows, width), lambda i: (0, 0)), hbm, hbm],
+        out_specs=[pl.BlockSpec(o.shape, lambda i, r=len(o.shape): (0,) * r) for o in outs],
+        out_shape=outs,
         scratch_shapes=[pltpu.SemaphoreType.DMA((replicas * capacity * 2,))],
         compiler_params=params(),
-        cost_estimate=cost(0, replicas * capacity * rank * width * 8),
-        name="choose",
-    )(variants, slots, down, up)
+        cost_estimate=cost(),
+        name="prepare",
+    )(*ints, hidden, down, up)
+    return results[: len(widths)], results[len(widths) :]
 
 
 def row_groups(variants, slots, live, shape, axis, replicas, capacity, pool):
@@ -174,14 +166,12 @@
         out_specs=pl.BlockSpec((rank, live_total), lambda i: (0, 0)),
         out_shape=jax.ShapeDtypeStruct((rank, live_total), f32),
         compiler_params=params(),
-        cost_estimate=cost(
-            2 * live_total * width * depth * replicas, (live_total + depth * replicas) * width * 2
-        ),
+        cost_estimate=cost(),
         name="shrink",
     )(variants, slots, live, *xs, *factors)
 
 
-def project_kernel(*refs, groups, has_total, delta, last, replicas, capacity, pool):
+def project_kernel(*refs, groups, certain, has_total, delta, last, replicas, capacity, pool):
     refs = list(refs)
     meta, variants, slots, live = refs[:4]
     refs = refs[4:]
@@ -216,7 +206,7 @@
             x = x + other[...]
         return jnp.dot(x, ws[s][...], preferred_element_type=f32)
 
-    sure = [s for s in range(len(groups)) if not has_total or groups[s] > 1]
+    sure = [s for s in range(len(groups)) if s in certain]
     value = total[...] if has_total else None
     for s in sure:
         value = product(s) if value is None else value + product(s)
@@ -242,13 +232,12 @@
         out[...] = jnp.dot(hot[...], result, preferred_element_type=f32).astype(bf16)
 
 
-def project(meta, ints, total, xs, weight, sizes, low=None, factors=None, rows=None):
+def project(meta, ints, total, xs, weight, sizes, certain, low=None, factors=None, rows=None):
     replicas, capacity, pool = sizes
     columns = weight.shape[1]
     tile = min(column_tile, columns)
     in_specs = [smem] * 3
     args = list(ints)
-    flops, moved = 0, live_total * columns * 8
     if total is not None:
         in_specs.append(pl.BlockSpec((live_total, tile), lambda i, m: (0, i)))
         args.append(total)
@@ -256,13 +245,10 @@
         for x in group:
             in_specs.append(pl.BlockSpec(x.shape, lambda i, m: (0, 0)))
             args.append(x)
-            moved += x.size * 2
     for s, group in enumerate(xs):
         k = group[0].shape[1]
         in_specs.append(pl.BlockSpec((k, tile), lambda i, m, s=s: (m[2 * s], i)))
         args.append(weight)
-        flops += 2 * live_total * k * columns
-        moved += k * columns * 2
     scratch = []
     if low is not None:
         in_specs.append(pl.BlockSpec(low.shape, lambda i, m: (0, 0)))
@@ -271,7 +257,6 @@
         for u in factors:
             in_specs.append(pl.BlockSpec((1, depth, tile), lambda i, m: (1, 0, i)))
             args.append(u)
-            flops += 2 * live_total * depth * columns
         scratch.append(pltpu.VMEM((live_total, replicas * depth), bf16))
     if rows is None:
         out = jax.ShapeDtypeStruct((live_total, columns), f32)
@@ -280,11 +265,11 @@
         out = jax.ShapeDtypeStruct((rows, columns), bf16)
         out_spec = pl.BlockSpec((rows, tile), lambda i, m: (0, i))
         scratch += [pltpu.VMEM((live_total, tile), f32), pltpu.VMEM((rows, live_total), bf16)]
-        flops += 2 * live_total * rows * columns
     return pl.pallas_call(
         functools.partial(
             project_kernel,
             groups=tuple(len(g) for g in xs),
+            certain=certain,
             has_total=total is not None,
             delta=low is not None,
             last=rows is not None,
@@ -301,7 +286,7 @@
         ),
         out_shape=out,
         compiler_params=params(),
-        cost_estimate=cost(flops, moved),
+        cost_estimate=cost(),
         name="project",
     )(meta, *args)
 
@@ -352,7 +337,7 @@
 
     one = jnp.int32(1)
 
-    def arrivals(total, step, js, **more):
+    def arrivals(step, js):
         items, xs = [], []
         for j in js:
             if 2 * step >= tensor:
@@ -364,10 +349,15 @@
                 behind = place + step
                 items.append((jnp.minimum(behind, tensor - 1), j, (behind < tensor).astype(i32)))
                 xs.append((left[step][j],))
-        return project(meta(items), ints, total, xs, query_weight, sizes, **more)
-
-    factors = choose(*ints[:2], adapter_down, adapter_up, replicas, capacity)
-    own = pack(hidden, block_live_count, (piece,) * chunks)
+        return items, xs
+
+    def add(total, items, xs, **more):
+        certain = tuple(s for s, item in enumerate(items) if item[2] is one)
+        return project(meta(items), ints, total, xs, query_weight, sizes, certain, **more)
+
+    own, factors = prepare(
+        ints, hidden, adapter_down, adapter_up, (piece,) * chunks, replicas, capacity
+    )
     right, left = [own], [own]
 
     def pass_on(first=(), final=()):
@@ -380,32 +370,26 @@
 
     pass_on()
     got = [factors[0]] + [send(factors[step], step) for step in range(1, replicas)]
-    own_total = project(
-        meta([(place, j, one) for j in range(chunks)]),
-        ints, None, [(x,) for x in own], query_weight, sizes,
-    )
+
     partial = shrink(*ints, own, got, capacity, pool)
-    total = arrivals(own_total, 1, range(chunks))
+    shared = lax.all_gather(partial.astype(bf16), "tensor", axis=0)
+    other = (jnp.arange(tensor) != place)[:, None, None]
+    low = partial + jnp.sum(jnp.where(other, shared.astype(f32), 0.0), axis=0)
+    low = low.astype(bf16).astype(f32).T
+
+    items, xs = arrivals(1, range(chunks))
+    items = [(place, j, one) for j in range(chunks)] + items
+    total = add(None, items, [(x,) for x in own] + xs)
     first_total = total
-
-    sums = [partial]
-    gap = 1
-    while gap < tensor:
-        pairs = [(i, i ^ gap) for i in range(tensor)]
-        sums.append(sums[-1] + lax.ppermute(sums[-1], "tensor", pairs))
-        gap *= 2
-
     for step in range(2, tensor):
-        if step == tensor - 1:
-            pass_on([first_total], [sums[1], total] if step > 2 else [])
-            break
-        pass_on(*([[own_total], [partial]] if step == 2 else []))
-        total = arrivals(total, step, range(chunks))
+        pass_on(*([[first_total], [partial]] if step == tensor - 1 else []))
+        if step < tensor - 1:
+            total = add(total, *arrivals(step, range(chunks)))
     for j in range(chunks):
         more = {"rows": rows} if j == chunks - 1 else {}
-        if j == chunks - 1:
-            more.update(low=sums[-1].astype(bf16).astype(f32).T, factors=got)
-        total = arrivals(total, tensor - 1, [j], **more)
+        if j == max(chunks - 2, 0):
+            more.update(low=low, factors=got)
+        total = add(total, *arrivals(tensor - 1, [j]), **more)
     return total
 
 

time: 237 us -> 218 us (0.920)
  blocking collectives: 0 us -> 62.1 us
  Pallas kernels: 98.5 us -> 63.4 us
  waiting for transfers between devices: 82.6 us -> 59.6 us
  starting transfers between devices: 46.6 us -> 27.1 us
    all_gather x0 -> x1, blocking collectives: none -> 62.1 us  [shards(): shared = lax.all_gather(partial.astype(bf16), 'tensor', axis=0)]
    ppermute x2 -> x0, waiting for transfers between devices: 49.6 us -> none  [shards(): sums.append(sums[-1] + lax.ppermute(sums[-1], 'tensor', pairs))]
    pallas_call x2 -> x1, Pallas kernels: 36.3 us -> 6.71 us  [prepare(): pl.pallas_call(functools.partial(prepare_kernel, chunks=len(widths), repl...]
    ppermute x12, waiting for transfers between devices: 21.9 us -> 47 us  [move(): return lax.ppermute(x, 'tensor', pairs)]
    ppermute x3, starting transfers between devices: 15.1 us -> 1.88 us  [send(): return lax.ppermute(x, 'dp', pairs)]
    ppermute x2 -> x0, starting transfers between devices: 9.51 us -> none  [shards(): sums.append(sums[-1] + lax.ppermute(sums[-1], 'tensor', pairs))]
    pallas_call x5 -> x4, Pallas kernels: 57.6 us -> 51.9 us  [project(): pl.pallas_call(functools.partial(project_kernel, groups=tuple((len(g) for...]
    ppermute x12, starting transfers between devices: 22 us -> 25.2 us  [move(): return lax.ppermute(x, 'tensor', pairs)]
  transfers between devices with their start and end apart: 17 -> 15, of which waited for: 7 -> 6; matrix products, arithmetic and copies ran while one was open for 1% -> 0% of each run, Pallas kernels for 22% -> 21%
where the time goes in v5:
time: 218 us; the launch traced here: 217 us
  Pallas kernels  63.4 us (29%)
  blocking collectives  62.1 us (28%)
  waiting for transfers between devices  59.6 us (27%)
  starting transfers between devices  27.1 us (12%)
  local copies, waits for them, and re-layouts  4.42 us (2%)
    all_gather x1, blocking collectives, shards(): shared = lax.all_gather(partial.astype(bf16), 'tensor', axis=0)  62.1 us
    pallas_call x4, Pallas kernels, project(): pl.pallas_call(functools.partial(project_kernel, groups=tuple((len(g) for...  51.9 us
    ppermute x12, waiting for transfers between devices, move(): return lax.ppermute(x, 'tensor', pairs)  47 us
    ppermute x12, starting transfers between devices, move(): return lax.ppermute(x, 'tensor', pairs)  25.2 us
    ppermute x3, waiting for transfers between devices, send(): return lax.ppermute(x, 'dp', pairs)  12.6 us
    pallas_call x1, Pallas kernels, prepare(): pl.pallas_call(functools.partial(prepare_kernel, chunks=len(widths), repl...  6.71 us
    pallas_call x1, Pallas kernels, shrink(): pl.pallas_call(functools.partial(shrink_kernel, replicas=replicas, capaci...  4.8 us
  transfers between devices with their start and end apart: 15, of which 6 were waited for; matrix products, arithmetic and copies ran while one was open for 0% of the time, Pallas kernels for 21%

profile of v5, /device:TPU:0, one launch (start us, length us, event | category | flops | bytes accessed | tf_op | source)
XLA Modules:
  0.0 217.1 jit_solution(15831373945196259891)
XLA Ops:
  0.0 0.7 copy-done.4
  0.7 0.7 copy-done.6
  1.3 0.7 copy-done.8
  2.0 6.7 %prepare.1 = (bf16[576,1024]{1,0:T(8,128)(2,1)S(1)}, bf16[576,1024]{1,0:T(8,128)(2,1)}, bf16[2,128,2048]{2,1,0:T(8,128)(2,1)S(1)}, bf16[2,128,2048]{2,1,0:T(8,12...) custom-call(s32[4,6]{1,0:T(4,128)S(1)} %copy-done.4, s32[32]{0:T(128)S(1)} %copy-done.6, ...), custom_call_target="tpu_custom_call" | custom-call | flops 1 | bytes 1 | tf_op jit(solution)/shard_map/prepare/pallas_call | solution.py:88
  8.7 6.0 %collective-permute-start = (bf16[576,1024]{1,0:T(8,128)(2,1)S(1)}, bf16[576,1024]{1,0:T(8,128)(2,1)}, u32[]{:S(2)}, u32[]{:S(2)}) collective-permute-start(bf16[576,1024]{1,0:T(8,128)(2,1)S(1)} %get-tuple-element.15.refs_4_.rest_0_), channel_id=1, source_target_pairs={{0,1},{1,2},{2,3},{4,5},{5,6},{6,7},{8,9},{9,10},{10,11},{12,13},{... | collective-permute-start | bytes 3538952 | tf_op jit(solution)/shard_map/ppermute | solution.py:332
  14.7 1.3 collective-permute-start.1
  16.0 5.6 %collective-permute-start.2 = (bf16[576,1024]{1,0:T(8,128)(2,1)}, bf16[576,1024]{1,0:T(8,128)(2,1)}, u32[]{:S(2)}, u32[]{:S(2)}) collective-permute-start(bf16[576,1024]{1,0:T(8,128)(2,1)} %get-tuple-element.16.refs_5_.rest_1_), channel_id=1, source_target_pairs={{0,1},{1,2},{2,3},{4,5},{5,6},{6,7},{8,9},{9,10},{10,11},{12,13},{... | collective-permute-start | bytes 3538952 | tf_op jit(solution)/shard_map/ppermute | solution.py:332
  21.6 1.3 collective-permute-start.3
  22.9 0.1 collective-permute-start.10
  23.0 17.0 %collective-permute-done.refs_6_ = bf16[576,1024]{1,0:T(8,128)(2,1)} collective-permute-done((bf16[576,1024]{1,0:T(8,128)(2,1)S(1)}, bf16[576,1024]{1,0:T(8,128)(2,1)}, u32[]{:S(2)}, u32[]{:S(2)}) %collective-permute-start) | collective-permute-done | bytes 1179680 | tf_op jit(solution)/shard_map/ppermute | solution.py:332
  40.0 1.8 collective-permute-start.11
  41.8 3.8 %collective-permute-done.1.refs_7_ = bf16[576,1024]{1,0:T(8,128)(2,1)} collective-permute-done((bf16[576,1024]{1,0:T(8,128)(2,1)S(1)}, bf16[576,1024]{1,0:T(8,128)(2,1)}, u32[]{:S(2)}, u32[]{:S(2)}) %collective-permute-start.1) | collective-permute-done | bytes 1179680 | tf_op jit(solution)/shard_map/ppermute | solution.py:332
  45.6 1.7 collective-permute-start.4
  47.3 17.0 %collective-permute-done.2.refs_8_ = bf16[576,1024]{1,0:T(8,128)(2,1)} collective-permute-done((bf16[576,1024]{1,0:T(8,128)(2,1)}, bf16[576,1024]{1,0:T(8,128)(2,1)}, u32[]{:S(2)}, u32[]{:S(2)}) %collective-permute-start.2) | collective-permute-done | bytes 1179680 | tf_op jit(solution)/shard_map/ppermute | solution.py:332
  64.3 1.3 collective-permute-start.5
  65.6 4.4 %collective-permute-done.3.refs_9_ = bf16[576,1024]{1,0:T(8,128)(2,1)} collective-permute-done((bf16[576,1024]{1,0:T(8,128)(2,1)}, bf16[576,1024]{1,0:T(8,128)(2,1)}, u32[]{:S(2)}, u32[]{:S(2)}) %collective-permute-start.3) | collective-permute-done | bytes 1179680 | tf_op jit(solution)/shard_map/ppermute | solution.py:332
  70.0 1.7 collective-permute-start.6
  71.8 0.0 collective-permute-done.10.rest_3_.refs_10_
  71.8 1.3 collective-permute-start.7
  73.0 0.0 collective-permute-done.11.rest_4_.refs_11_
  73.1 1.0 copy-done.1
  74.0 0.0 collective-permute-start.12
  74.0 0.1 stack.73.refs_0_
  74.1 12.5 %collective-permute-done.12.rest_5_.refs_12_ = bf16[2,128,2048]{2,1,0:T(8,128)(2,1)} collective-permute-done((bf16[2,128,2048]{2,1,0:T(8,128)(2,1)}, bf16[2,128,2048]{2,1,0:T(8,128)(2,1)}, u32[]{:S(2)}, u32[]{:S(2)}) %collective-permute-start.12) | collective-permute-done | bytes 1048608 | tf_op jit(solution)/shard_map/ppermute | solution.py:336
  86.7 0.0 copy-done.9
  86.7 1.2 copy-done.2
  87.9 4.8 %shrink.1 = f32[64,576]{1,0:T(8,128)S(1)} custom-call(s32[4,6]{1,0:T(4,128)S(1)} %copy-done.5, s32[32]{0:T(128)S(1)} %copy-done.7, s32[1,6]{1,0:T(1,128)S(1)} %copy-done.9, bf16[576,1024]{1,0:T(8,128)(2,1)S(1)} %get-tuple-element.15.refs_4_.rest_0_, bf16[576,1024]{1,0:T(8,128)(2,1)} %get-tuple-element.16.refs_5_.rest_1_, ...), custom_call_target="tpu_custom_call" | custom-call | flops 1 | bytes 1 | tf_op jit(solution)/shard_map/shrink/pallas_call | solution.py:158
  92.7 18.8 %project.4.refs_4_ = f32[576,2048]{1,0:T(8,128)} custom-call(s32[12]{0:T(128)S(1)} %stack.73.refs_0_, s32[4,6]{1,0:T(4,128)S(1)} %copy-done.5, s32[32]{0:T(128)S(1)} %copy-done.7, s32[1,6]{1,0:T(1,128)S(1)} %copy-done.9, bf16[576,1024]{1,0:T(8,128)(2,1)S(1)} %get-tuple-element.15.refs_4_.rest_0_, bf16[576,1024]{1,0:T(8,128)(2,1)S(1)} %copy-done, ...), custom_call_target="tpu_custom_call" | custom-call | flops 1 | bytes 1 | tf_op jit(solution)/shard_map/project/pallas_call | solution.py:268
  111.5 0.0 collective-permute-done.4.refs_5_
  111.5 0.7 collective-permute-start.8
  112.3 0.0 collective-permute-done.5.refs_6_
  112.3 1.3 collective-permute-start.9
  113.6 0.0 collective-permute-done.6.refs_7_
  113.6 1.7 collective-permute-start.13
  115.3 4.8 %collective-permute-done.7.refs_8_ = bf16[576,1024]{1,0:T(8,128)(2,1)} collective-permute-done((bf16[576,1024]{1,0:T(8,128)(2,1)}, bf16[576,1024]{1,0:T(8,128)(2,1)}, u32[]{:S(2)}, u32[]{:S(2)}) %collective-permute-start.7) | collective-permute-done | bytes 1179680 | tf_op jit(solution)/shard_map/ppermute | solution.py:332
  120.1 1.3 collective-permute-start.14
  121.4 0.1 pad_add_fusion.2.refs_0_
  121.5 0.1 pad_add_fusion
  121.6 62.1 %all-gather = bf16[256,576]{1,0:T(8,128)(2,1)S(1)} all-gather(bf16[64,576]{1,0:T(8,128)(2,1)S(1)} %convert_element_type.6), channel_id=2, replica_groups=mesh['groups'=2,'dp'=4,'tensor'=4] {'tensor'}, dimensions={0}, use_global_device_ids=true | all-gather | bytes 368640 | tf_op jit(solution)/shard_map/all_gather | solution.py:375
  183.6 0.1 fusion
  183.8 0.1 copy.11
  184.0 12.1 %project.5.refs_4_ = f32[576,2048]{1,0:T(8,128)} custom-call(s32[4]{0:T(128)S(1)} %pad_add_fusion.2.refs_0_, s32[4,6]{1,0:T(4,128)S(1)} %copy-done.5, s32[32]{0:T(128)S(1)} %copy-done.7, s32[1,6]{1,0:T(1,128)S(1)} %copy-done.9, f32[576,2048]{1,0:T(8,128)} %project.4.refs_4_, bf16[576,1024]{1,0:T(8,128)(2,1)} %collective-permute-done.4.refs_5_, ...), custom_call_target="tpu_custom_call" | custom-call | flops 1 | bytes 1 | tf_op jit(solution)/shard_map/project/pallas_call | solution.py:268
  196.1 0.0 collective-permute-done.8.refs_5_
  196.1 0.0 collective-permute-done.9.refs_6_
  196.2 10.5 %project.6.refs_4_ = f32[576,2048]{1,0:T(8,128)} custom-call(s32[2]{0:T(128)S(1)} %get-tuple-element.25.refs_0_, s32[4,6]{1,0:T(4,128)S(1)} %copy-done.5, s32[32]{0:T(128)S(1)} %copy-done.7, s32[1,6]{1,0:T(1,128)S(1)} %copy-done.9, f32[576,2048]{1,0:T(8,128)} %project.5.refs_4_, bf16[576,1024]{1,0:T(8,128)(2,1)S(1)} %collective-permute-done.8.refs_5_, ...), custom_call_target="tpu_custom_call" | custom-call | flops 1 | bytes 1 | tf_op jit(solution)/shard_map/project/pallas_call | solution.py:268
  206.6 0.0 collective-permute-done.13.refs_5_
  206.6 0.0 collective-permute-done.14.refs_6_
  206.6 10.5 %project.7 = bf16[768,2048]{1,0:T(8,128)(2,1)} custom-call(s32[2]{0:T(128)S(1)} %get-tuple-element.26.refs_0_, s32[4,6]{1,0:T(4,128)S(1)} %copy-done.5, s32[32]{0:T(128)S(1)} %copy-done.7, s32[1,6]{1,0:T(1,128)S(1)} %copy-done.9, f32[576,2048]{1,0:T(8,128)} %project.6.refs_4_, bf16[576,1024]{1,0:T(8,128)(2,1)} %collective-permute-done.13.refs_5_, ...), custom_call_target="tpu_custom_call" | custom-call | flops 1 | bytes 1 | tf_op jit(solution)/shard_map/project/pallas_call | solution.py:268
  (18 shorter events, 0.1 us)
Async XLA Ops:
  0.0 0.7 copy-start.4
  0.7 0.7 copy-start.6
  1.3 0.7 copy-start.8
  2.0 84.7 %copy-start.5 = (s32[4,6]{1,0:T(4,128)S(1)}, s32[4,6]{1,0:T(4,128)}, u32[]{:S(2)}) copy-start(s32[4,6]{1,0:T(4,128)} %refs_1_.7) | copy-start | bytes 292
  2.0 84.7 %copy-start.7 = (s32[32]{0:T(128)S(1)}, s32[32]{0:T(128)}, u32[]{:S(2)}) copy-start(s32[32]{0:T(128)} %refs_2_.7) | copy-start | bytes 388
  2.0 84.7 %copy-start.9 = (s32[1,6]{1,0:T(1,128)S(1)}, s32[1,6]{1,0:T(1,128)}, u32[]{:S(2)}) copy-start(s32[1,6]{1,0:T(1,128)} %refs_3_.7) | copy-start | bytes 76
  8.7 31.3 %collective-permute-start = (bf16[576,1024]{1,0:T(8,128)(2,1)S(1)}, bf16[576,1024]{1,0:T(8,128)(2,1)}, u32[]{:S(2)}, u32[]{:S(2)}) collective-permute-start(bf16[576,1024]{1,0:T(8,128)(2,1)S(1)} %get-tuple-element.15.refs_4_.rest_0_), channel_id=1, source_target_pairs={{0,1},{1,2},{2,3},{4,5},{5,6},{6,7},{8,9},{9,10},{10,11},{12,13},{... | collective-permute-start | bytes 3538952 | tf_op jit(solution)/shard_map/ppermute | solution.py:332
  14.7 30.9 %collective-permute-start.1 = (bf16[576,1024]{1,0:T(8,128)(2,1)S(1)}, bf16[576,1024]{1,0:T(8,128)(2,1)}, u32[]{:S(2)}, u32[]{:S(2)}) collective-permute-start(bf16[576,1024]{1,0:T(8,128)(2,1)S(1)} %get-tuple-element.15.refs_4_.rest_0_), channel_id=1, source_target_pairs={{1,0},{2,1},{3,2},{5,4},{6,5},{7,6},{9,8},{10,9},{11,10},{13,12},{... | collective-permute-start | bytes 3538952 | tf_op jit(solution)/shard_map/ppermute | solution.py:332
  16.0 48.3 %collective-permute-start.2 = (bf16[576,1024]{1,0:T(8,128)(2,1)}, bf16[576,1024]{1,0:T(8,128)(2,1)}, u32[]{:S(2)}, u32[]{:S(2)}) collective-permute-start(bf16[576,1024]{1,0:T(8,128)(2,1)} %get-tuple-element.16.refs_5_.rest_1_), channel_id=1, source_target_pairs={{0,1},{1,2},{2,3},{4,5},{5,6},{6,7},{8,9},{9,10},{10,11},{12,13},{... | collective-permute-start | bytes 3538952 | tf_op jit(solution)/shard_map/ppermute | solution.py:332
  21.6 48.4 %collective-permute-start.3 = (bf16[576,1024]{1,0:T(8,128)(2,1)}, bf16[576,1024]{1,0:T(8,128)(2,1)}, u32[]{:S(2)}, u32[]{:S(2)}) collective-permute-start(bf16[576,1024]{1,0:T(8,128)(2,1)} %get-tuple-element.16.refs_5_.rest_1_), channel_id=1, source_target_pairs={{1,0},{2,1},{3,2},{5,4},{6,5},{7,6},{9,8},{10,9},{11,10},{13,12},{... | collective-permute-start | bytes 3538952 | tf_op jit(solution)/shard_map/ppermute | solution.py:332
  22.9 48.9 %collective-permute-start.10 = (bf16[2,128,2048]{2,1,0:T(8,128)(2,1)S(1)}, bf16[2,128,2048]{2,1,0:T(8,128)(2,1)S(1)}, u32[]{:S(2)}, u32[]{:S(2)}) collective-permute-start(bf16[2,128,2048]{2,1,0:T(8,128)(2,1)S(1)} %get-tuple-element.20), channel_id=1, source_target_pairs={{0,4},{4,8},{8,12},{12,0},{1,5},{5,9},{9,13},{13,1},{2,6},{6,10},{... | collective-permute-start | bytes 3145736 | tf_op jit(solution)/shard_map/ppermute | solution.py:336
  40.0 33.0 %collective-permute-start.11 = (bf16[2,128,2048]{2,1,0:T(8,128)(2,1)S(1)}, bf16[2,128,2048]{2,1,0:T(8,128)(2,1)S(1)}, u32[]{:S(2)}, u32[]{:S(2)}) collective-permute-start(bf16[2,128,2048]{2,1,0:T(8,128)(2,1)S(1)} %get-tuple-element.21), channel_id=1, source_target_pairs={{0,8},{4,12},{8,0},{12,4},{1,9},{5,13},{9,1},{13,5},{2,10},{6,14},... | collective-permute-start | bytes 3145736 | tf_op jit(solution)/shard_map/ppermute | solution.py:336
  45.6 65.9 %collective-permute-start.4 = (bf16[576,1024]{1,0:T(8,128)(2,1)}, bf16[576,1024]{1,0:T(8,128)(2,1)}, u32[]{:S(2)}, u32[]{:S(2)}) collective-permute-start(bf16[576,1024]{1,0:T(8,128)(2,1)} %collective-permute-done.refs_6_), channel_id=1, source_target_pairs={{1,2},{2,3},{5,6},{6,7},{9,10},{10,11},{13,14},{14,15},{17,18},{18... | collective-permute-start | bytes 3538952 | tf_op jit(solution)/shard_map/ppermute | solution.py:332
  64.3 47.9 %collective-permute-start.5 = (bf16[576,1024]{1,0:T(8,128)(2,1)}, bf16[576,1024]{1,0:T(8,128)(2,1)}, u32[]{:S(2)}, u32[]{:S(2)}) collective-permute-start(bf16[576,1024]{1,0:T(8,128)(2,1)} %collective-permute-done.1.refs_7_), channel_id=1, source_target_pairs={{1,0},{2,1},{5,4},{6,5},{9,8},{10,9},{13,12},{14,13},{17,16},{18,1... | collective-permute-start | bytes 3538952 | tf_op jit(solution)/shard_map/ppermute | solution.py:332
  70.0 43.5 %collective-permute-start.6 = (bf16[576,1024]{1,0:T(8,128)(2,1)}, bf16[576,1024]{1,0:T(8,128)(2,1)}, u32[]{:S(2)}, u32[]{:S(2)}) collective-permute-start(bf16[576,1024]{1,0:T(8,128)(2,1)} %collective-permute-done.2.refs_8_), channel_id=1, source_target_pairs={{1,2},{2,3},{5,6},{6,7},{9,10},{10,11},{13,14},{14,15},{17,18},{18... | collective-permute-start | bytes 3538952 | tf_op jit(solution)/shard_map/ppermute | solution.py:332
  71.8 48.3 %collective-permute-start.7 = (bf16[576,1024]{1,0:T(8,128)(2,1)}, bf16[576,1024]{1,0:T(8,128)(2,1)}, u32[]{:S(2)}, u32[]{:S(2)}) collective-permute-start(bf16[576,1024]{1,0:T(8,128)(2,1)} %collective-permute-done.3.refs_9_), channel_id=1, source_target_pairs={{1,0},{2,1},{5,4},{6,5},{9,8},{10,9},{13,12},{14,13},{17,16},{18,1... | collective-permute-start | bytes 3538952 | tf_op jit(solution)/shard_map/ppermute | solution.py:332
  73.1 1.0 copy-start.1
  74.0 12.6 %collective-permute-start.12 = (bf16[2,128,2048]{2,1,0:T(8,128)(2,1)}, bf16[2,128,2048]{2,1,0:T(8,128)(2,1)}, u32[]{:S(2)}, u32[]{:S(2)}) collective-permute-start(bf16[2,128,2048]{2,1,0:T(8,128)(2,1)} %get-tuple-element.22), channel_id=1, source_target_pairs={{0,12},{4,0},{8,4},{12,8},{1,13},{5,1},{9,5},{13,9},{2,14},{6,2},{... | collective-permute-start | bytes 3145736 | tf_op jit(solution)/shard_map/ppermute | solution.py:336
  86.7 1.2 copy-start.2
  87.9 4.8 %copy-start = (bf16[576,1024]{1,0:T(8,128)(2,1)S(1)}, bf16[576,1024]{1,0:T(8,128)(2,1)}, u32[]{:S(2)}) copy-start(bf16[576,1024]{1,0:T(8,128)(2,1)} %get-tuple-element.16.refs_5_.rest_1_) | copy-start | bytes 3538948
  111.5 84.6 %collective-permute-start.8 = (bf16[576,1024]{1,0:T(8,128)(2,1)}, bf16[576,1024]{1,0:T(8,128)(2,1)S(1)}, u32[]{:S(2)}, u32[]{:S(2)}) collective-permute-start(bf16[576,1024]{1,0:T(8,128)(2,1)} %collective-permute-done.4.refs_5_), channel_id=1, source_target_pairs={{2,3},{6,7},{10,11},{14,15},{18,19},{22,23},{26,27},{30,31}} | collective-permute-start | bytes 3538952 | tf_op jit(solution)/shard_map/ppermute | solution.py:332
  112.3 83.9 %collective-permute-start.9 = (bf16[576,1024]{1,0:T(8,128)(2,1)}, bf16[576,1024]{1,0:T(8,128)(2,1)}, u32[]{:S(2)}, u32[]{:S(2)}) collective-permute-start(bf16[576,1024]{1,0:T(8,128)(2,1)} %collective-permute-done.5.refs_6_), channel_id=1, source_target_pairs={{1,0},{5,4},{9,8},{13,12},{17,16},{21,20},{25,24},{29,28}} | collective-permute-start | bytes 3538952 | tf_op jit(solution)/shard_map/ppermute | solution.py:332
  113.6 93.0 %collective-permute-start.13 = (bf16[576,1024]{1,0:T(8,128)(2,1)}, bf16[576,1024]{1,0:T(8,128)(2,1)}, u32[]{:S(2)}, u32[]{:S(2)}) collective-permute-start(bf16[576,1024]{1,0:T(8,128)(2,1)} %collective-permute-done.6.refs_7_), channel_id=1, source_target_pairs={{2,3},{6,7},{10,11},{14,15},{18,19},{22,23},{26,27},{30,31}} | collective-permute-start | bytes 3538952 | tf_op jit(solution)/shard_map/ppermute | solution.py:332
  120.1 86.6 %collective-permute-start.14 = (bf16[576,1024]{1,0:T(8,128)(2,1)}, bf16[576,1024]{1,0:T(8,128)(2,1)}, u32[]{:S(2)}, u32[]{:S(2)}) collective-permute-start(bf16[576,1024]{1,0:T(8,128)(2,1)} %collective-permute-done.7.refs_8_), channel_id=1, source_target_pairs={{1,0},{5,4},{9,8},{13,12},{17,16},{21,20},{25,24},{29,28}} | collective-permute-start | bytes 3538952 | tf_op jit(solution)/shard_map/ppermute | solution.py:332
  184.0 12.2 %copy-start.3 = (bf16[2,128,2048]{2,1,0:T(8,128)(2,1)S(1)}, bf16[2,128,2048]{2,1,0:T(8,128)(2,1)}, u32[]{:S(2)}) copy-start(bf16[2,128,2048]{2,1,0:T(8,128)(2,1)} %copy-done.1) | copy-start | bytes 3145732

commit v6 on v5

--- a/solution.py
+++ b/solution.py
@@ -22,8 +22,8 @@
     return pltpu.CompilerParams(vmem_limit_bytes=vmem_bytes)
 
 
-def cost():
-    return pl.CostEstimate(flops=1, bytes_accessed=1, transcendentals=0)
+def cost(flops=1):
+    return pl.CostEstimate(flops=flops, bytes_accessed=1, transcendentals=0)
 
 
 def one_hot(live, rows, axis):
@@ -286,7 +286,7 @@
         ),
         out_shape=out,
         compiler_params=params(),
-        cost_estimate=cost(),
+        cost_estimate=cost(1 if low is None else 40_000_000_000),
         name="project",
     )(meta, *args)
 
@@ -369,27 +369,48 @@
             moved.append([move(x, w, step) for x in xs])
 
     pass_on()
-    got = [factors[0]] + [send(factors[step], step) for step in range(1, replicas)]
-
-    partial = shrink(*ints, own, got, capacity, pool)
-    shared = lax.all_gather(partial.astype(bf16), "tensor", axis=0)
-    other = (jnp.arange(tensor) != place)[:, None, None]
-    low = partial + jnp.sum(jnp.where(other, shared.astype(f32), 0.0), axis=0)
+    items = [(place, j, one) for j in range(chunks)]
+    own_total = add(None, items, [(x,) for x in own])
+
+    got = [factors[0], send(factors[1], 1)]
+    for step in range(2, replicas):
+        got.append(send(after(factors[step], got[-1]), step))
+
+    total = add(own_total, *arrivals(1, range(chunks)))
+    first_total = total
+    partial = shrink(*ints[:2], after(ints[2], total), own, got, capacity, pool)
+
+    for step in range(2, tensor - 1):
+        pass_on(*([[own_total]] if step == 2 else []))
+        total = add(total, *arrivals(step, range(chunks)))
+
+    def pick(j, *events):
+        return jnp.where(place == 1, after(left[-1][j], *events), after(right[-1][j], *events))
+
+    ends = [(tensor - 2, tensor - 1), (1, 0)]
+    source_end = jnp.where(place > 0, 0, tensor - 1)
+    first_pick = pick(0)
+
+    low = hopped = partial
+    for step in range(1, tensor):
+        pairs = [(step - 1, step), (tensor - step, tensor - step - 1)]
+        came = lax.ppermute(hopped, "tensor", pairs)
+        if step == tensor - 2:
+            came = after(came, first_pick)
+        low = low + came
+        if step < tensor - 1:
+            hopped = partial + came
     low = low.astype(bf16).astype(f32).T
 
-    items, xs = arrivals(1, range(chunks))
-    items = [(place, j, one) for j in range(chunks)] + items
-    total = add(None, items, [(x,) for x in own] + xs)
-    first_total = total
-    for step in range(2, tensor):
-        pass_on(*([[first_total], [partial]] if step == tensor - 1 else []))
-        if step < tensor - 1:
-            total = add(total, *arrivals(step, range(chunks)))
+    final = []
+    for j in range(chunks):
+        x = first_pick if j == 0 else pick(j, hopped)
+        final.append(lax.ppermute(x, "tensor", ends))
     for j in range(chunks):
         more = {"rows": rows} if j == chunks - 1 else {}
         if j == max(chunks - 2, 0):
             more.update(low=low, factors=got)
-        total = add(total, *arrivals(tensor - 1, [j]), **more)
+        total = add(total, [(source_end, j, one)], [(final[j],)], **more)
     return total
 
 

time: 218 us -> 205 us (0.940)
  blocking collectives: 62.1 us -> 0 us
  waiting for transfers between devices: 59.6 us -> 82.1 us
  starting transfers between devices: 27.1 us -> 38.1 us
  local copies, waits for them, and re-layouts: 4.42 us -> 11.1 us
  other arithmetic: 0.35 us -> 5.4 us
  Pallas kernels: 63.4 us -> 67.4 us
    all_gather x1 -> x0, blocking collectives: 62.1 us -> none  [shards(): shared = lax.all_gather(partial.astype(bf16), 'tensor', axis=0)]
    ppermute x0 -> x5, waiting for transfers between devices: none -> 34.1 us  [the longest x3 21.5 us: shards(): came = lax.ppermute(hopped, 'tensor', pairs)]
    ppermute x0 -> x5, starting transfers between devices: none -> 18.1 us  [the longest x3 15.2 us: shards(): came = lax.ppermute(hopped, 'tensor', pairs)]
    ppermute x12 -> x8, waiting for transfers between devices: 47 us -> 36.7 us  [move(): return lax.ppermute(x, 'tensor', pairs)]
    ppermute x12 -> x8, starting transfers between devices: 25.2 us -> 17.3 us  [move(): return lax.ppermute(x, 'tensor', pairs)]
    unnamed x20 -> x42, local copies, waits for them, and re-layouts: 4.2 us -> 9.25 us
    pallas_call x4 -> x5, Pallas kernels: 51.9 us -> 55.6 us  [project(): pl.pallas_call(functools.partial(project_kernel, groups=tuple((len(g) for...]
    add x1 -> x2, other arithmetic: 0.02 us -> 2.79 us  [the longest x1 1.8 us: shards(): low = low + came]
  transfers between devices with their start and end apart: 15 -> 16, of which waited for: 6 -> 7; matrix products, arithmetic and copies ran while one was open for 0% -> 4% of each run, Pallas kernels for 21% -> 25%
where the time goes in v6:
time: 205 us; the launch traced here: 204 us
  waiting for transfers between devices  82.1 us (40%)
  Pallas kernels  67.4 us (33%)
  starting transfers between devices  38.1 us (19%)
  local copies, waits for them, and re-layouts  11.1 us (5%)
  other arithmetic  5.4 us (3%)
    pallas_call x5, Pallas kernels, project(): pl.pallas_call(functools.partial(project_kernel, groups=tuple((len(g) for...  55.6 us
    ppermute x8, waiting for transfers between devices, move(): return lax.ppermute(x, 'tensor', pairs)  36.7 us
    ppermute x3, waiting for transfers between devices, shards(): came = lax.ppermute(hopped, 'tensor', pairs)  21.5 us
    ppermute x8, starting transfers between devices, move(): return lax.ppermute(x, 'tensor', pairs)  17.3 us
    ppermute x3, starting transfers between devices, shards(): came = lax.ppermute(hopped, 'tensor', pairs)  15.2 us
    ppermute x2, waiting for transfers between devices, shards(): final.append(lax.ppermute(x, 'tensor', ends))  12.7 us
    ppermute x3, waiting for transfers between devices, send(): return lax.ppermute(x, 'dp', pairs)  11.3 us
    unnamed x42, local copies, waits for them, and re-layouts  9.25 us
  transfers between devices with their start and end apart: 16, of which 7 were waited for; matrix products, arithmetic and copies ran while one was open for 4% of the time, Pallas kernels for 25%

profile of v6, /device:TPU:0, one launch (start us, length us, event | category | flops | bytes accessed | tf_op | source)
XLA Modules:
  0.0 204.5 jit_solution(1142282828699353215)
XLA Ops:
  0.0 0.7 copy-done.14
  0.7 0.7 copy-done.16
  1.3 0.7 copy-done.18
  2.0 7.1 %prepare.1 = (bf16[576,1024]{1,0:T(8,128)(2,1)S(1)}, bf16[576,1024]{1,0:T(8,128)(2,1)}, bf16[2,128,2048]{2,1,0:T(8,128)(2,1)S(1)}, bf16[2,128,2048]{2,1,0:T(8,12...) custom-call(s32[4,6]{1,0:T(4,128)S(1)} %copy-done.14, s32[32]{0:T(128)S(1)} %copy-done.16, ...), custom_call_target="tpu_custom_call" | custom-call | flops 1 | bytes 1 | tf_op jit(solution)/shard_map/prepare/pallas_call | solution.py:88
  9.1 1.0 copy-done.4
  10.1 0.4 collective-permute-start.9
  10.5 1.3 collective-permute-start.1
  11.8 6.2 %collective-permute-start = (bf16[576,1024]{1,0:T(8,128)(2,1)S(1)}, bf16[576,1024]{1,0:T(8,128)(2,1)}, u32[]{:S(2)}, u32[]{:S(2)}) collective-permute-start(bf16[576,1024]{1,0:T(8,128)(2,1)S(1)} %get-tuple-element.19.refs_4_.rest_0_), channel_id=1, source_target_pairs={{0,1},{1,2},{2,3},{4,5},{5,6},{6,7},{8,9},{9,10},{10,11},{12,13},{... | collective-permute-start | bytes 3538952 | tf_op jit(solution)/shard_map/ppermute | solution.py:332
  18.0 7.2 %collective-permute-done.9.rest_3_.refs_9_ = bf16[2,128,2048]{2,1,0:T(8,128)(2,1)S(1)} collective-permute-done((bf16[2,128,2048]{2,1,0:T(8,128)(2,1)S(1)}, bf16[2,128,2048]{2,1,0:T(8,128)(2,1)S(1)}, u32[]{:S(2)}, u32[]{:S(2)}) %collective-permute-start.9) | collective-permute-done | bytes 1048608 | tf_op jit(solution)/shard_map/ppermute | solution.py:336
  25.2 1.0 copy-done.7
  26.1 2.3 %collective-permute-start.10 = (bf16[2,128,2048]{2,1,0:T(8,128)(2,1)}, bf16[2,128,2048]{2,1,0:T(8,128)(2,1)S(1)}, u32[]{:S(2)}, u32[]{:S(2)}) collective-permute-start(bf16[2,128,2048]{2,1,0:T(8,128)(2,1)} %get-tuple-element.27), channel_id=1, source_target_pairs={{0,8},{4,12},{8,0},{12,4},{1,9},{5,13},{9,1},{13,5},{2,10},{6,14},... | collective-permute-start | bytes 3145736 | tf_op jit(solution)/shard_map/ppermute | solution.py:336
  28.5 4.5 %collective-permute-start.2 = (bf16[576,1024]{1,0:T(8,128)(2,1)}, bf16[576,1024]{1,0:T(8,128)(2,1)}, u32[]{:S(2)}, u32[]{:S(2)}) collective-permute-start(bf16[576,1024]{1,0:T(8,128)(2,1)} %get-tuple-element.20.refs_5_.rest_1_), channel_id=1, source_target_pairs={{0,1},{1,2},{2,3},{4,5},{5,6},{6,7},{8,9},{9,10},{10,11},{12,13},{... | collective-permute-start | bytes 3538952 | tf_op jit(solution)/shard_map/ppermute | solution.py:332
  32.9 1.3 collective-permute-start.3
  34.2 0.1 pad_add_fusion.2.refs_0_
  34.3 1.3 copy-done.3
  35.6 9.6 %project.5.refs_4_ = f32[576,2048]{1,0:T(8,128)} custom-call(s32[4]{0:T(128)S(1)} %pad_add_fusion.2.refs_0_, s32[4,6]{1,0:T(4,128)S(1)} %copy-done.15, s32[32]{0:T(128)S(1)} %copy-done.17, s32[1,6]{1,0:T(1,128)S(1)} %copy-done.19, bf16[576,1024]{1,0:T(8,128)(2,1)S(1)} %get-tuple-element.19.refs_4_.rest_0_, bf16[576,1024]{1,0:T(8,128)(2,1)S(1)} %copy-done.3, ...), custom_call_target="tpu_custom_call" | custom-call | flops 1 | bytes 1 | tf_op jit(solution)/shard_map/project/pallas_call | solution.py:268
  45.2 1.3 collective-permute-start.5
  46.5 0.7 collective-permute-start.4
  47.3 4.1 %collective-permute-done.10.rest_4_.refs_10_ = bf16[2,128,2048]{2,1,0:T(8,128)(2,1)S(1)} collective-permute-done((bf16[2,128,2048]{2,1,0:T(8,128)(2,1)}, bf16[2,128,2048]{2,1,0:T(8,128)(2,1)S(1)}, u32[]{:S(2)}, u32[]{:S(2)}) %collective-permute-start.10) | collective-permute-done | bytes 1048608 | tf_op jit(solution)/shard_map/ppermute | solution.py:336
  51.4 1.0 copy-done.10
  52.4 15.4 %collective-permute-done.2.refs_7_ = bf16[576,1024]{1,0:T(8,128)(2,1)} collective-permute-done((bf16[576,1024]{1,0:T(8,128)(2,1)}, bf16[576,1024]{1,0:T(8,128)(2,1)}, u32[]{:S(2)}, u32[]{:S(2)}) %collective-permute-start.2) | collective-permute-done | bytes 1179680 | tf_op jit(solution)/shard_map/ppermute | solution.py:332
  67.7 0.7 collective-permute-start.6
  68.5 1.3 collective-permute-start.7
  69.8 21.3 %collective-permute-done.5.refs_6_ = bf16[576,1024]{1,0:T(8,128)(2,1)S(1)} collective-permute-done((bf16[576,1024]{1,0:T(8,128)(2,1)}, bf16[576,1024]{1,0:T(8,128)(2,1)S(1)}, u32[]{:S(2)}, u32[]{:S(2)}) %collective-permute-start.5) | collective-permute-done | bytes 1179680 | tf_op jit(solution)/shard_map/ppermute | solution.py:332
  91.1 1.1 broadcast_select_fusion.1
  92.3 1.3 collective-permute-start.8
  93.6 0.1 stack.74.refs_0_
  93.7 15.0 %project.6.refs_4_ = f32[576,2048]{1,0:T(8,128)} custom-call(s32[8]{0:T(128)S(1)} %stack.74.refs_0_, s32[4,6]{1,0:T(4,128)S(1)} %copy-done.15, s32[32]{0:T(128)S(1)} %copy-done.17, s32[1,6]{1,0:T(1,128)S(1)} %copy-done.19, f32[576,2048]{1,0:T(8,128)} %project.5.refs_4_, bf16[576,1024]{1,0:T(8,128)(2,1)} %collective-permute-done.refs_5_, ...), custom_call_target="tpu_custom_call" | custom-call | flops 1 | bytes 1 | tf_op jit(solution)/shard_map/project/pallas_call | solution.py:268
  108.7 4.7 %shrink.1 = f32[64,576]{1,0:T(8,128)S(1)} custom-call(s32[4,6]{1,0:T(4,128)S(1)} %copy-done.15, s32[32]{0:T(128)S(1)} %copy-done.17, s32[1,6]{1,0:T(1,128)S(1)} %copy-done.19, bf16[576,1024]{1,0:T(8,128)(2,1)S(1)} %copy-done.2, bf16[576,1024]{1,0:T(8,128)(2,1)} %get-tuple-element.20.refs_5_.rest_1_, bf16[2,128,2048]{2,1,0:T(8,128)(2,1)S(1)} %copy-done.5, ...), custom_call_target="tpu_custom_call" | custom-call | flops 1 | bytes 1 | tf_op jit(solution)/shard_map/shrink/pallas_call | solution.py:158
  113.5 0.7 copy-done.13
  114.1 1.8 copy.9
  115.9 12.5 %collective-permute-start.12 = (f32[64,576]{0,1:T(8,128)}, f32[64,576]{0,1:T(8,128)}, u32[]{:S(2)}, u32[]{:S(2)}) collective-permute-start(f32[64,576]{0,1:T(8,128)} %copy.9), channel_id=1, source_target_pairs={{0,1},{3,2},{4,5},{7,6},{8,9},{11,10},{12,13},{15,14},{16,17},{19,... | collective-permute-start | bytes 442376 | tf_op jit(solution)/shard_map/ppermute | solution.py:397
  128.4 6.8 %collective-permute-done.12 = f32[64,576]{0,1:T(8,128)} collective-permute-done((f32[64,576]{0,1:T(8,128)}, f32[64,576]{0,1:T(8,128)}, u32[]{:S(2)}, u32[]{:S(2)}) %collective-permute-start.12) | collective-permute-done | bytes 147488 | tf_op jit(solution)/shard_map/ppermute | solution.py:397
  135.3 1.8 add.45
  137.1 1.4 collective-permute-start.13
  138.5 0.1 pad_add_fusion.3.refs_0_
  138.5 0.1 pad_add_fusion
  138.6 11.3 %project.7.refs_4_ = f32[576,2048]{1,0:T(8,128)} custom-call(s32[4]{0:T(128)S(1)} %pad_add_fusion.3.refs_0_, s32[4,6]{1,0:T(4,128)S(1)} %copy-done.15, s32[32]{0:T(128)S(1)} %copy-done.17, s32[1,6]{1,0:T(1,128)S(1)} %copy-done.19, f32[576,2048]{1,0:T(8,128)} %project.6.refs_4_, bf16[576,1024]{1,0:T(8,128)(2,1)S(1)} %collective-permute-done.4.refs_5_, ...), custom_call_target="tpu_custom_call" | custom-call | flops 1 | bytes 1 | tf_op jit(solution)/shard_map/project/pallas_call | solution.py:268
  149.9 1.0 add.47
  150.9 1.3 collective-permute-start.14
  152.2 0.1 broadcast_select_fusion
  152.4 1.6 collective-permute-start.15
  154.0 14.6 %collective-permute-done.14 = f32[64,576]{0,1:T(8,128)S(1)} collective-permute-done((f32[64,576]{0,1:T(8,128)S(1)}, f32[64,576]{0,1:T(8,128)S(1)}, u32[]{:S(2)}, u32[]{:S(2)}) %collective-permute-start.14) | collective-permute-done | bytes 147488 | tf_op jit(solution)/shard_map/ppermute | solution.py:397
  168.6 1.1 convert_bitcast_fusion.refs_7_
  169.8 10.5 %project.8.refs_4_ = f32[576,2048]{1,0:T(8,128)} custom-call(s32[2]{0:T(128)S(1)} %get-tuple-element.33.refs_0_, s32[4,6]{1,0:T(4,128)S(1)} %copy-done.15, s32[32]{0:T(128)S(1)} %copy-done.17, s32[1,6]{1,0:T(1,128)S(1)} %copy-done.19, f32[576,2048]{1,0:T(8,128)} %project.7.refs_4_, bf16[576,1024]{1,0:T(8,128)(2,1)} %collective-permute-done.8.refs_5_, ...), custom_call_target="tpu_custom_call" | custom-call | flops 40000000000 | bytes 1 | tf_op jit(solution)/shard_map/project/pallas_call | solution.py:268
  180.2 12.7 %collective-permute-done.15.refs_5_ = bf16[576,1024]{1,0:T(8,128)(2,1)S(1)} collective-permute-done((bf16[576,1024]{1,0:T(8,128)(2,1)S(1)}, bf16[576,1024]{1,0:T(8,128)(2,1)S(1)}, u32[]{:S(2)}, u32[]{:S(2)}) %collective-permute-start.15) | collective-permute-done | bytes 1179680 | tf_op jit(solution)/shard_map/ppermute | solution.py:408
  192.9 2.3 %copy-done = f32[576,2048]{1,0:T(8,128)S(1)} copy-done((f32[576,2048]{1,0:T(8,128)S(1)}, f32[576,2048]{1,0:T(8,128)}, u32[]{:S(2)}) %copy-start) | copy-done | bytes 4718616
  195.2 9.2 %project.9 = bf16[768,2048]{1,0:T(8,128)(2,1)} custom-call(s32[2]{0:T(128)S(1)} %get-tuple-element.34.refs_0_, s32[4,6]{1,0:T(4,128)S(1)} %copy-done.15, s32[32]{0:T(128)S(1)} %copy-done.17, s32[1,6]{1,0:T(1,128)S(1)} %copy-done.19, f32[576,2048]{1,0:T(8,128)S(1)} %copy-done, bf16[576,1024]{1,0:T(8,128)(2,1)S(1)} %collective-permute-done.15.refs_5_, ...), custom_call_target="tpu_custom_call" | custom-call | flops 1 | bytes 1 | tf_op jit(solution)/shard_map/project/pallas_call | solution.py:268
  (43 shorter events, 0.1 us)
Async XLA Ops:
  0.0 0.7 copy-start.14
  0.7 0.7 copy-start.16
  1.3 0.7 copy-start.18
  2.0 32.3 %copy-start.15 = (s32[4,6]{1,0:T(4,128)S(1)}, s32[4,6]{1,0:T(4,128)}, u32[]{:S(2)}) copy-start(s32[4,6]{1,0:T(4,128)} %refs_1_.9) | copy-start | bytes 292
  2.0 32.3 %copy-start.17 = (s32[32]{0:T(128)S(1)}, s32[32]{0:T(128)}, u32[]{:S(2)}) copy-start(s32[32]{0:T(128)} %refs_2_.9) | copy-start | bytes 388
  2.0 32.3 %copy-start.19 = (s32[1,6]{1,0:T(1,128)S(1)}, s32[1,6]{1,0:T(1,128)}, u32[]{:S(2)}) copy-start(s32[1,6]{1,0:T(1,128)} %refs_3_.9) | copy-start | bytes 76
  9.1 1.0 copy-start.4
  10.1 35.1 %copy-start.1 = (bf16[576,1024]{1,0:T(8,128)(2,1)}, bf16[576,1024]{1,0:T(8,128)(2,1)S(1)}, u32[]{:S(2)}) copy-start(bf16[576,1024]{1,0:T(8,128)(2,1)S(1)} %get-tuple-element.19.refs_4_.rest_0_) | copy-start | bytes 3538948
  10.1 15.0 %collective-permute-start.9 = (bf16[2,128,2048]{2,1,0:T(8,128)(2,1)S(1)}, bf16[2,128,2048]{2,1,0:T(8,128)(2,1)S(1)}, u32[]{:S(2)}, u32[]{:S(2)}) collective-permute-start(bf16[2,128,2048]{2,1,0:T(8,128)(2,1)S(1)} %get-tuple-element.25), channel_id=1, source_target_pairs={{0,4},{4,8},{8,12},{12,0},{1,5},{5,9},{9,13},{13,1},{2,6},{6,10},{... | collective-permute-start | bytes 3145736 | tf_op jit(solution)/shard_map/ppermute | solution.py:336
  10.5 34.7 %collective-permute-start.1 = (bf16[576,1024]{1,0:T(8,128)(2,1)S(1)}, bf16[576,1024]{1,0:T(8,128)(2,1)}, u32[]{:S(2)}, u32[]{:S(2)}) collective-permute-start(bf16[576,1024]{1,0:T(8,128)(2,1)S(1)} %get-tuple-element.19.refs_4_.rest_0_), channel_id=1, source_target_pairs={{1,0},{2,1},{3,2},{5,4},{6,5},{7,6},{9,8},{10,9},{11,10},{13,12},{... | collective-permute-start | bytes 3538952 | tf_op jit(solution)/shard_map/ppermute | solution.py:332
  11.8 34.7 %collective-permute-start = (bf16[576,1024]{1,0:T(8,128)(2,1)S(1)}, bf16[576,1024]{1,0:T(8,128)(2,1)}, u32[]{:S(2)}, u32[]{:S(2)}) collective-permute-start(bf16[576,1024]{1,0:T(8,128)(2,1)S(1)} %get-tuple-element.19.refs_4_.rest_0_), channel_id=1, source_target_pairs={{0,1},{1,2},{2,3},{4,5},{5,6},{6,7},{8,9},{9,10},{10,11},{12,13},{... | collective-permute-start | bytes 3538952 | tf_op jit(solution)/shard_map/ppermute | solution.py:332
  25.2 1.0 copy-start.7
  26.1 25.2 %collective-permute-start.10 = (bf16[2,128,2048]{2,1,0:T(8,128)(2,1)}, bf16[2,128,2048]{2,1,0:T(8,128)(2,1)S(1)}, u32[]{:S(2)}, u32[]{:S(2)}) collective-permute-start(bf16[2,128,2048]{2,1,0:T(8,128)(2,1)} %get-tuple-element.27), channel_id=1, source_target_pairs={{0,8},{4,12},{8,0},{12,4},{1,9},{5,13},{9,1},{13,5},{2,10},{6,14},... | collective-permute-start | bytes 3145736 | tf_op jit(solution)/shard_map/ppermute | solution.py:336
  28.5 39.3 %collective-permute-start.2 = (bf16[576,1024]{1,0:T(8,128)(2,1)}, bf16[576,1024]{1,0:T(8,128)(2,1)}, u32[]{:S(2)}, u32[]{:S(2)}) collective-permute-start(bf16[576,1024]{1,0:T(8,128)(2,1)} %get-tuple-element.20.refs_5_.rest_1_), channel_id=1, source_target_pairs={{0,1},{1,2},{2,3},{4,5},{5,6},{6,7},{8,9},{9,10},{10,11},{12,13},{... | collective-permute-start | bytes 3538952 | tf_op jit(solution)/shard_map/ppermute | solution.py:332
  32.9 35.5 %collective-permute-start.3 = (bf16[576,1024]{1,0:T(8,128)(2,1)}, bf16[576,1024]{1,0:T(8,128)(2,1)}, u32[]{:S(2)}, u32[]{:S(2)}) collective-permute-start(bf16[576,1024]{1,0:T(8,128)(2,1)} %get-tuple-element.20.refs_5_.rest_1_), channel_id=1, source_target_pairs={{1,0},{2,1},{3,2},{5,4},{6,5},{7,6},{9,8},{10,9},{11,10},{13,12},{... | collective-permute-start | bytes 3538952 | tf_op jit(solution)/shard_map/ppermute | solution.py:332
  34.3 1.3 copy-start.3
  45.2 45.9 %collective-permute-start.5 = (bf16[576,1024]{1,0:T(8,128)(2,1)}, bf16[576,1024]{1,0:T(8,128)(2,1)S(1)}, u32[]{:S(2)}, u32[]{:S(2)}) collective-permute-start(bf16[576,1024]{1,0:T(8,128)(2,1)} %collective-permute-done.1.refs_6_), channel_id=1, source_target_pairs={{1,0},{2,1},{5,4},{6,5},{9,8},{10,9},{13,12},{14,13},{17,16},{18,1... | collective-permute-start | bytes 3538952 | tf_op jit(solution)/shard_map/ppermute | solution.py:332
  46.5 44.6 %collective-permute-start.4 = (bf16[576,1024]{1,0:T(8,128)(2,1)}, bf16[576,1024]{1,0:T(8,128)(2,1)S(1)}, u32[]{:S(2)}, u32[]{:S(2)}) collective-permute-start(bf16[576,1024]{1,0:T(8,128)(2,1)} %collective-permute-done.refs_5_), channel_id=1, source_target_pairs={{1,2},{2,3},{5,6},{6,7},{9,10},{10,11},{13,14},{14,15},{17,18},{18... | collective-permute-start | bytes 3538952 | tf_op jit(solution)/shard_map/ppermute | solution.py:332
  51.4 1.0 copy-start.10
  52.4 56.3 %collective-permute-start.11 = (bf16[2,128,2048]{2,1,0:T(8,128)(2,1)}, bf16[2,128,2048]{2,1,0:T(8,128)(2,1)}, u32[]{:S(2)}, u32[]{:S(2)}) collective-permute-start(bf16[2,128,2048]{2,1,0:T(8,128)(2,1)} %get-tuple-element.29), channel_id=1, source_target_pairs={{0,12},{4,0},{8,4},{12,8},{1,13},{5,1},{9,5},{13,9},{2,14},{6,2},{... | collective-permute-start | bytes 3145736 | tf_op jit(solution)/shard_map/ppermute | solution.py:336
  67.7 70.9 %collective-permute-start.6 = (bf16[576,1024]{1,0:T(8,128)(2,1)}, bf16[576,1024]{1,0:T(8,128)(2,1)S(1)}, u32[]{:S(2)}, u32[]{:S(2)}) collective-permute-start(bf16[576,1024]{1,0:T(8,128)(2,1)} %collective-permute-done.2.refs_7_), channel_id=1, source_target_pairs={{1,2},{2,3},{5,6},{6,7},{9,10},{10,11},{13,14},{14,15},{17,18},{18... | collective-permute-start | bytes 3538952 | tf_op jit(solution)/shard_map/ppermute | solution.py:332
  68.5 70.2 %collective-permute-start.7 = (bf16[576,1024]{1,0:T(8,128)(2,1)}, bf16[576,1024]{1,0:T(8,128)(2,1)}, u32[]{:S(2)}, u32[]{:S(2)}) collective-permute-start(bf16[576,1024]{1,0:T(8,128)(2,1)} %collective-permute-done.3.refs_8_), channel_id=1, source_target_pairs={{1,0},{2,1},{5,4},{6,5},{9,8},{10,9},{13,12},{14,13},{17,16},{18,1... | collective-permute-start | bytes 3538952 | tf_op jit(solution)/shard_map/ppermute | solution.py:332
  92.3 77.5 %collective-permute-start.8 = (bf16[576,1024]{1,0:T(8,128)(2,1)}, bf16[576,1024]{1,0:T(8,128)(2,1)}, u32[]{:S(2)}, u32[]{:S(2)}) collective-permute-start(bf16[576,1024]{1,0:T(8,128)(2,1)} %broadcast_select_fusion.1), channel_id=1, source_target_pairs={{2,3},{1,0},{6,7},{5,4},{10,11},{9,8},{14,15},{13,12},{18,19},{17,... | collective-permute-start | bytes 3538952 | tf_op jit(solution)/shard_map/ppermute | solution.py:408
  93.6 15.0 %copy-start.2 = (bf16[576,1024]{1,0:T(8,128)(2,1)S(1)}, bf16[576,1024]{1,0:T(8,128)(2,1)}, u32[]{:S(2)}) copy-start(bf16[576,1024]{1,0:T(8,128)(2,1)} %copy-done.1) | copy-start | bytes 3538948
  93.6 15.1 %copy-start.5 = (bf16[2,128,2048]{2,1,0:T(8,128)(2,1)S(1)}, bf16[2,128,2048]{2,1,0:T(8,128)(2,1)}, u32[]{:S(2)}) copy-start(bf16[2,128,2048]{2,1,0:T(8,128)(2,1)} %copy-done.4) | copy-start | bytes 3145732
  93.6 15.1 %copy-start.8 = (bf16[2,128,2048]{2,1,0:T(8,128)(2,1)S(1)}, bf16[2,128,2048]{2,1,0:T(8,128)(2,1)}, u32[]{:S(2)}) copy-start(bf16[2,128,2048]{2,1,0:T(8,128)(2,1)} %copy-done.7) | copy-start | bytes 3145732
  93.7 15.1 %copy-start.11 = (bf16[2,128,2048]{2,1,0:T(8,128)(2,1)S(1)}, bf16[2,128,2048]{2,1,0:T(8,128)(2,1)}, u32[]{:S(2)}) copy-start(bf16[2,128,2048]{2,1,0:T(8,128)(2,1)} %copy-done.10) | copy-start | bytes 3145732
  113.5 0.7 copy-start.13
  115.9 19.4 %collective-permute-start.12 = (f32[64,576]{0,1:T(8,128)}, f32[64,576]{0,1:T(8,128)}, u32[]{:S(2)}, u32[]{:S(2)}) collective-permute-start(f32[64,576]{0,1:T(8,128)} %copy.9), channel_id=1, source_target_pairs={{0,1},{3,2},{4,5},{7,6},{8,9},{11,10},{12,13},{15,14},{16,17},{19,... | collective-permute-start | bytes 442376 | tf_op jit(solution)/shard_map/ppermute | solution.py:397
  137.1 12.8 %collective-permute-start.13 = (f32[64,576]{0,1:T(8,128)}, f32[64,576]{0,1:T(8,128)}, u32[]{:S(2)}, u32[]{:S(2)}) collective-permute-start(f32[64,576]{0,1:T(8,128)} %add.45), channel_id=1, source_target_pairs={{1,2},{2,1},{5,6},{6,5},{9,10},{10,9},{13,14},{14,13},{17,18},{18,... | collective-permute-start | bytes 442376 | tf_op jit(solution)/shard_map/ppermute | solution.py:397
  138.6 11.3 %copy-start.20 = (f32[64,576]{0,1:T(8,128)S(1)}, f32[64,576]{0,1:T(8,128)}, u32[]{:S(2)}) copy-start(f32[64,576]{0,1:T(8,128)} %copy.9) | copy-start | bytes 442372
  150.9 17.7 %collective-permute-start.14 = (f32[64,576]{0,1:T(8,128)S(1)}, f32[64,576]{0,1:T(8,128)S(1)}, u32[]{:S(2)}, u32[]{:S(2)}) collective-permute-start(f32[64,576]{0,1:T(8,128)S(1)} %add.47), channel_id=1, source_target_pairs={{2,3},{1,0},{6,7},{5,4},{10,11},{9,8},{14,15},{13,12},{18,19},{17,... | collective-permute-start | bytes 442376 | tf_op jit(solution)/shard_map/ppermute | solution.py:397
  152.2 17.5 %copy-start.9 = (bf16[2,128,2048]{2,1,0:T(8,128)(2,1)S(1)}, bf16[2,128,2048]{2,1,0:T(8,128)(2,1)}, u32[]{:S(2)}) copy-start(bf16[2,128,2048]{2,1,0:T(8,128)(2,1)} %copy-done.7) | copy-start | bytes 3145732
  152.2 17.5 %copy-start.12 = (bf16[2,128,2048]{2,1,0:T(8,128)(2,1)S(1)}, bf16[2,128,2048]{2,1,0:T(8,128)(2,1)}, u32[]{:S(2)}) copy-start(bf16[2,128,2048]{2,1,0:T(8,128)(2,1)} %copy-done.10) | copy-start | bytes 3145732
  152.4 17.4 %copy-start.6 = (bf16[2,128,2048]{2,1,0:T(8,128)(2,1)S(1)}, bf16[2,128,2048]{2,1,0:T(8,128)(2,1)}, u32[]{:S(2)}) copy-start(bf16[2,128,2048]{2,1,0:T(8,128)(2,1)} %copy-done.4) | copy-start | bytes 3145732
  152.4 40.5 %collective-permute-start.15 = (bf16[576,1024]{1,0:T(8,128)(2,1)S(1)}, bf16[576,1024]{1,0:T(8,128)(2,1)S(1)}, u32[]{:S(2)}, u32[]{:S(2)}) collective-permute-start(bf16[576,1024]{1,0:T(8,128)(2,1)S(1)} %broadcast_select_fusion), channel_id=1, source_target_pairs={{2,3},{1,0},{6,7},{5,4},{10,11},{9,8},{14,15},{13,12},{18,19},{17,... | collective-permute-start | bytes 3538952 | tf_op jit(solution)/shard_map/ppermute | solution.py:408
  192.9 2.3 %copy-start = (f32[576,2048]{1,0:T(8,128)S(1)}, f32[576,2048]{1,0:T(8,128)}, u32[]{:S(2)}) copy-start(f32[576,2048]{1,0:T(8,128)} %project.8.refs_4_) | copy-start | bytes 14155780

commit v7 on v6

--- a/solution.py
+++ b/solution.py
@@ -11,7 +11,7 @@
 live_total = 576
 chunk_width = 1024
 column_tile = 512
-vmem_bytes = 48 * 1024 * 1024
+vmem_bytes = 62 * 1024 * 1024
 bf16, f32, i32 = jnp.bfloat16, jnp.float32, jnp.int32
 
 smem = pl.BlockSpec(memory_space=pltpu.SMEM)
@@ -376,20 +376,27 @@
     for step in range(2, replicas):
         got.append(send(after(factors[step], got[-1]), step))
 
-    total = add(own_total, *arrivals(1, range(chunks)))
-    first_total = total
+    total = own_total
+    firsts = []
+    for j in range(chunks):
+        total = add(total, *arrivals(1, [j]))
+        firsts.append(total)
     partial = shrink(*ints[:2], after(ints[2], total), own, got, capacity, pool)
 
+    late = ([], [])
     for step in range(2, tensor - 1):
-        pass_on(*([[own_total]] if step == 2 else []))
-        total = add(total, *arrivals(step, range(chunks)))
+        pass_on(*([[own_total], firsts[:1]] if step == 2 else []))
+        total = add(total, *arrivals(step, range(max(chunks - 1, 1))))
+        if chunks > 1:
+            items, xs = arrivals(step, [chunks - 1])
+            late = (late[0] + items, late[1] + xs)
 
     def pick(j, *events):
         return jnp.where(place == 1, after(left[-1][j], *events), after(right[-1][j], *events))
 
     ends = [(tensor - 2, tensor - 1), (1, 0)]
     source_end = jnp.where(place > 0, 0, tensor - 1)
-    first_pick = pick(0)
+    first_pick = pick(0, partial)
 
     low = hopped = partial
     for step in range(1, tensor):
@@ -404,13 +411,15 @@
 
     final = []
     for j in range(chunks):
-        x = first_pick if j == 0 else pick(j, hopped)
+        x = first_pick if j == 0 else pick(j, hopped, total)
         final.append(lax.ppermute(x, "tensor", ends))
     for j in range(chunks):
         more = {"rows": rows} if j == chunks - 1 else {}
+        items, xs = [(source_end, j, one)], [(final[j],)]
         if j == max(chunks - 2, 0):
             more.update(low=low, factors=got)
-        total = add(total, [(source_end, j, one)], [(final[j],)], **more)
+            items, xs = late[0] + items, late[1] + xs
+        total = add(total, items, xs, **more)
     return total
 
 

time: 205 us -> 189 us (0.922)
  waiting for transfers between devices: 82.1 us -> 69.9 us
  Pallas kernels: 67.4 us -> 78.8 us
  local copies, waits for them, and re-layouts: 11.1 us -> 1.2 us
  starting transfers between devices: 38.1 us -> 30.4 us
  other arithmetic: 5.4 us -> 8.14 us
    ppermute x8, waiting for transfers between devices: 36.7 us -> 18.4 us  [move(): return lax.ppermute(x, 'tensor', pairs)]
    ppermute x3, waiting for transfers between devices: 21.5 us -> 31.7 us  [shards(): came = lax.ppermute(hopped, 'tensor', pairs)]
    pallas_call x5 -> x6, Pallas kernels: 55.6 us -> 64.9 us  [project(): pl.pallas_call(functools.partial(project_kernel, groups=tuple((len(g) for...]
    unnamed x42 -> x6, local copies, waits for them, and re-layouts: 9.25 us -> 1.05 us
    ppermute x3, starting transfers between devices: 15.2 us -> 7.54 us  [shards(): came = lax.ppermute(hopped, 'tensor', pairs)]
    another operation x3 -> x6, other arithmetic: 0.23 us -> 3.76 us  [meta(): return jnp.stack([jnp.asarray(p, i32) for p in pairs])]
    ppermute x2, waiting for transfers between devices: 12.7 us -> 9.88 us  [shards(): final.append(lax.ppermute(x, 'tensor', ends))]
    select_n x2, other arithmetic: 1.29 us -> 3.57 us  [pick(): jnp.where(place == 1, after(left[-1][j], *events), after(right[-1][j], *e...]
  transfers between devices with their start and end apart: 16 -> 16, of which waited for: 7 -> 9; matrix products, arithmetic and copies ran while one was open for 4% -> 4% of each run, Pallas kernels for 25% -> 32%
where the time goes in v7:
time: 189 us
  Pallas kernels  78.8 us (42%)
  waiting for transfers between devices  69.9 us (37%)
  starting transfers between devices  30.4 us (16%)
  other arithmetic  8.14 us (4%)
    pallas_call x6, Pallas kernels, project(): pl.pallas_call(functools.partial(project_kernel, groups=tuple((len(g) for...  64.9 us
    ppermute x3, waiting for transfers between devices, shards(): came = lax.ppermute(hopped, 'tensor', pairs)  31.7 us
    ppermute x8, waiting for transfers between devices, move(): return lax.ppermute(x, 'tensor', pairs)  18.4 us
    ppermute x8, starting transfers between devices, move(): return lax.ppermute(x, 'tensor', pairs)  17.9 us
    ppermute x3, waiting for transfers between devices, send(): return lax.ppermute(x, 'dp', pairs)  9.88 us
    ppermute x2, waiting for transfers between devices, shards(): final.append(lax.ppermute(x, 'tensor', ends))  9.88 us
    pallas_call x1, Pallas kernels, prepare(): pl.pallas_call(functools.partial(prepare_kernel, chunks=len(widths), repl...  7.63 us
    ppermute x3, starting transfers between devices, shards(): came = lax.ppermute(hopped, 'tensor', pairs)  7.54 us
  transfers between devices with their start and end apart: 16, of which 9 were waited for; matrix products, arithmetic and copies ran while one was open for 4% of the time, Pallas kernels for 32%

profile of v7, /device:TPU:0, one launch (start us, length us, event | category | flops | bytes accessed | tf_op | source)
XLA Modules:
  0.0 188.6 jit_solution(11429653177255001691)
XLA Ops:
  0.0 7.6 %prepare.1 = (bf16[576,1024]{1,0:T(8,128)(2,1)}, bf16[576,1024]{1,0:T(8,128)(2,1)}, bf16[2,128,2048]{2,1,0:T(8,128)(2,1)}, bf16[2,128,2048]{2,1,0:T(8,128)(2,1)}...) custom-call(s32[4,6]{1,0:T(4,128)} %refs_1_.11, s32[32]{0:T(128)} %refs_2_.11, s32[1,6]{1,0:T(1,128)} %refs_3_.11, ...), custom_call_target="tpu_custom_call" | custom-call | flops 1 | bytes 1 | tf_op jit(solution)/shard_map/prepare/pallas_call | solution.py:88
  7.6 0.2 collective-permute-start.8
  7.8 5.8 %collective-permute-start = (bf16[576,1024]{1,0:T(8,128)(2,1)}, bf16[576,1024]{1,0:T(8,128)(2,1)}, u32[]{:S(2)}, u32[]{:S(2)}) collective-permute-start(bf16[576,1024]{1,0:T(8,128)(2,1)} %get-tuple-element.23.refs_4_.rest_0_), channel_id=1, source_target_pairs={{0,1},{1,2},{2,3},{4,5},{5,6},{6,7},{8,9},{9,10},{10,11},{12,13},{... | collective-permute-start | bytes 3538952 | tf_op jit(solution)/shard_map/ppermute | solution.py:332
  13.7 1.3 collective-permute-start.1
  15.0 7.9 %collective-permute-done.8.rest_3_.refs_12_ = bf16[2,128,2048]{2,1,0:T(8,128)(2,1)} collective-permute-done((bf16[2,128,2048]{2,1,0:T(8,128)(2,1)}, bf16[2,128,2048]{2,1,0:T(8,128)(2,1)}, u32[]{:S(2)}, u32[]{:S(2)}) %collective-permute-start.8) | collective-permute-done | bytes 1048608 | tf_op jit(solution)/shard_map/ppermute | solution.py:336
  22.9 2.0 %collective-permute-start.9 = (bf16[2,128,2048]{2,1,0:T(8,128)(2,1)}, bf16[2,128,2048]{2,1,0:T(8,128)(2,1)}, u32[]{:S(2)}, u32[]{:S(2)}) collective-permute-start(bf16[2,128,2048]{2,1,0:T(8,128)(2,1)} %get-tuple-element.33), channel_id=1, source_target_pairs={{0,8},{4,12},{8,0},{12,4},{1,9},{5,13},{9,1},{13,5},{2,10},{6,14},... | collective-permute-start | bytes 3145736 | tf_op jit(solution)/shard_map/ppermute | solution.py:336
  24.9 4.5 %collective-permute-start.2 = (bf16[576,1024]{1,0:T(8,128)(2,1)}, bf16[576,1024]{1,0:T(8,128)(2,1)}, u32[]{:S(2)}, u32[]{:S(2)}) collective-permute-start(bf16[576,1024]{1,0:T(8,128)(2,1)} %get-tuple-element.24.refs_5_.rest_1_), channel_id=1, source_target_pairs={{0,1},{1,2},{2,3},{4,5},{5,6},{6,7},{8,9},{9,10},{10,11},{12,13},{... | collective-permute-start | bytes 3538952 | tf_op jit(solution)/shard_map/ppermute | solution.py:332
  29.4 1.3 collective-permute-start.3
  30.7 0.6 pad_add_fusion.2.refs_0_
  31.3 10.4 %project.6.refs_4_ = f32[576,2048]{1,0:T(8,128)} custom-call(s32[4]{0:T(128)} %pad_add_fusion.2.refs_0_, s32[4,6]{1,0:T(4,128)} %refs_1_.11, s32[32]{0:T(128)} %refs_2_.11, s32[1,6]{1,0:T(1,128)} %refs_3_.11, bf16[576,1024]{1,0:T(8,128)(2,1)} %get-tuple-element.23.refs_4_.rest_0_, bf16[576,1024]{1,0:T(8,128)(2,1)} %get-tuple-element.24.refs_5_.rest_1_, ...), custom_call_target="tpu_custom_call" | custom-call | flops 1 | bytes 1 | tf_op jit(solution)/shard_map/project/pallas_call | solution.py:268
  41.7 0.0 collective-permute-done.refs_5_
  41.7 0.7 collective-permute-start.4
  42.4 2.3 %collective-permute-done.1.refs_6_ = bf16[576,1024]{1,0:T(8,128)(2,1)} collective-permute-done((bf16[576,1024]{1,0:T(8,128)(2,1)}, bf16[576,1024]{1,0:T(8,128)(2,1)}, u32[]{:S(2)}, u32[]{:S(2)}) %collective-permute-start.1) | collective-permute-done | bytes 1179680 | tf_op jit(solution)/shard_map/ppermute | solution.py:332
  44.7 1.3 collective-permute-start.5
  45.9 2.0 %collective-permute-done.9.rest_4_.refs_13_ = bf16[2,128,2048]{2,1,0:T(8,128)(2,1)} collective-permute-done((bf16[2,128,2048]{2,1,0:T(8,128)(2,1)}, bf16[2,128,2048]{2,1,0:T(8,128)(2,1)}, u32[]{:S(2)}, u32[]{:S(2)}) %collective-permute-start.9) | collective-permute-done | bytes 1048608 | tf_op jit(solution)/shard_map/ppermute | solution.py:336
  47.9 0.0 collective-permute-start.10
  47.9 0.6 add_add_fusion.1.refs_0_
  48.5 10.4 %project.7.refs_4_ = f32[576,2048]{1,0:T(8,128)} custom-call(s32[4]{0:T(128)} %add_add_fusion.1.refs_0_, s32[4,6]{1,0:T(4,128)} %refs_1_.11, s32[32]{0:T(128)} %refs_2_.11, s32[1,6]{1,0:T(1,128)} %refs_3_.11, f32[576,2048]{1,0:T(8,128)} %project.6.refs_4_, bf16[576,1024]{1,0:T(8,128)(2,1)} %collective-permute-done.refs_5_, ...), custom_call_target="tpu_custom_call" | custom-call | flops 1 | bytes 1 | tf_op jit(solution)/shard_map/project/pallas_call | solution.py:268
  58.9 5.4 %collective-permute-done.2.refs_5_ = bf16[576,1024]{1,0:T(8,128)(2,1)} collective-permute-done((bf16[576,1024]{1,0:T(8,128)(2,1)}, bf16[576,1024]{1,0:T(8,128)(2,1)}, u32[]{:S(2)}, u32[]{:S(2)}) %collective-permute-start.2) | collective-permute-done | bytes 1179680 | tf_op jit(solution)/shard_map/ppermute | solution.py:332
  64.2 1.7 collective-permute-start.6
  66.0 4.0 %collective-permute-done.3.refs_6_ = bf16[576,1024]{1,0:T(8,128)(2,1)} collective-permute-done((bf16[576,1024]{1,0:T(8,128)(2,1)}, bf16[576,1024]{1,0:T(8,128)(2,1)}, u32[]{:S(2)}, u32[]{:S(2)}) %collective-permute-start.3) | collective-permute-done | bytes 1179680 | tf_op jit(solution)/shard_map/ppermute | solution.py:332
  69.9 1.3 collective-permute-start.7
  71.2 0.6 add_add_fusion.refs_0_
  71.9 10.3 %project.8.refs_4_ = f32[576,2048]{1,0:T(8,128)} custom-call(s32[4]{0:T(128)} %add_add_fusion.refs_0_, s32[4,6]{1,0:T(4,128)} %refs_1_.11, s32[32]{0:T(128)} %refs_2_.11, s32[1,6]{1,0:T(1,128)} %refs_3_.11, f32[576,2048]{1,0:T(8,128)} %project.7.refs_4_, bf16[576,1024]{1,0:T(8,128)(2,1)} %collective-permute-done.2.refs_5_, ...), custom_call_target="tpu_custom_call" | custom-call | flops 1 | bytes 1 | tf_op jit(solution)/shard_map/project/pallas_call | solution.py:268
  82.2 0.0 collective-permute-done.10.rest_5_.refs_14_
  82.2 6.2 %shrink.1 = f32[64,576]{1,0:T(8,128)} custom-call(s32[4,6]{1,0:T(4,128)} %refs_1_.11, s32[32]{0:T(128)} %refs_2_.11, s32[1,6]{1,0:T(1,128)} %refs_3_.11, bf16[576,1024]{1,0:T(8,128)(2,1)} %get-tuple-element.23.refs_4_.rest_0_, bf16[576,1024]{1,0:T(8,128)(2,1)} %get-tuple-element.24.refs_5_.rest_1_, bf16[2,128,2048]{2,1,0:T(8,128)(2,1)} %get-tuple-element.30.rest_2_.refs_11_, ...), custom_call_target="tpu_custom_call" | custom-call | flops 1 | bytes 1 | tf_op jit(solution)/shard_map/shrink/pallas_call | solution.py:158
  88.4 0.0 copy-start
  88.4 6.8 %collective-permute-done.5.refs_6_ = bf16[576,1024]{1,0:T(8,128)(2,1)} collective-permute-done((bf16[576,1024]{1,0:T(8,128)(2,1)}, bf16[576,1024]{1,0:T(8,128)(2,1)}, u32[]{:S(2)}, u32[]{:S(2)}) %collective-permute-start.5) | collective-permute-done | bytes 1179680 | tf_op jit(solution)/shard_map/ppermute | solution.py:332
  95.2 1.2 broadcast_select_fusion.1
  96.4 1.3 collective-permute-start.11
  97.7 0.1 copy.9
  97.8 5.6 %collective-permute-start.12 = (f32[64,576]{0,1:T(8,128)S(1)}, f32[64,576]{0,1:T(8,128)S(1)}, u32[]{:S(2)}, u32[]{:S(2)}) collective-permute-start(f32[64,576]{0,1:T(8,128)S(1)} %copy.9), channel_id=1, source_target_pairs={{0,1},{3,2},{4,5},{7,6},{8,9},{11,10},{12,13},{15,14},{16,17},{19,... | collective-permute-start | bytes 442376 | tf_op jit(solution)/shard_map/ppermute | solution.py:404
  103.4 0.7 pad_add_fusion.1.refs_0_
  104.1 5.7 %collective-permute-done.12 = f32[64,576]{0,1:T(8,128)S(1)} collective-permute-done((f32[64,576]{0,1:T(8,128)S(1)}, f32[64,576]{0,1:T(8,128)S(1)}, u32[]{:S(2)}, u32[]{:S(2)}) %collective-permute-start.12) | collective-permute-done | bytes 147488 | tf_op jit(solution)/shard_map/ppermute | solution.py:404
  109.8 0.7 collective-permute-start.13
  110.5 0.7 pad_add_fusion.refs_0_
  111.1 0.6 pad_add_fusion.3.refs_0_
  111.7 9.0 %project.9.refs_4_ = f32[576,2048]{1,0:T(8,128)} custom-call(s32[2]{0:T(128)} %pad_add_fusion.refs_0_, s32[4,6]{1,0:T(4,128)} %refs_1_.11, s32[32]{0:T(128)} %refs_2_.11, s32[1,6]{1,0:T(1,128)} %refs_3_.11, f32[576,2048]{1,0:T(8,128)} %project.8.refs_4_, bf16[576,1024]{1,0:T(8,128)(2,1)} %copy-done, bf16[576,1024]{1,0:T(8,128)(2,1)} %collective-permute-done.5.refs_6_, ...), custom_call_target="tpu_custom_call" | custom-call | flops 1 | bytes 1 | tf_op jit(solution)/shard_map/project/pallas_call | solution.py:268
  120.8 1.3 collective-permute-start.14
  122.1 0.0 collective-permute-done.6.refs_5_
  122.1 2.4 %broadcast_select_fusion = bf16[576,1024]{1,0:T(8,128)(2,1)} fusion(bf16[576,1024]{1,0:T(8,128)(2,1)} %collective-permute-done.7.refs_6_, bf16[576,1024]{1,0:T(8,128)(2,1)} %collective-permute-done.6.refs_5_, pred[]{:T(512)S(6)} %eq.4), kind=kLoop, calls=%fused_computation | loop fusion | flops 589824 | bytes 3538945 | tf_op jit(solution)/shard_map/jit(_where)/select_n | solution.py:395
  124.5 1.5 collective-permute-start.15
  126.0 26.0 %collective-permute-done.14 = f32[64,576]{0,1:T(8,128)S(1)} collective-permute-done((f32[64,576]{0,1:T(8,128)S(1)}, f32[64,576]{0,1:T(8,128)S(1)}, u32[]{:S(2)}, u32[]{:S(2)}) %collective-permute-start.14) | collective-permute-done | bytes 147488 | tf_op jit(solution)/shard_map/ppermute | solution.py:404
  152.0 0.8 convert_bitcast_fusion.refs_10_
  152.7 14.6 %project.10.refs_4_ = f32[576,2048]{1,0:T(8,128)} custom-call(s32[4]{0:T(128)} %pad_add_fusion.3.refs_0_, s32[4,6]{1,0:T(4,128)} %refs_1_.11, s32[32]{0:T(128)} %refs_2_.11, s32[1,6]{1,0:T(1,128)} %refs_3_.11, f32[576,2048]{1,0:T(8,128)} %project.9.refs_4_, bf16[576,1024]{1,0:T(8,128)(2,1)} %collective-permute-done.6.refs_5_, ...), custom_call_target="tpu_custom_call" | custom-call | flops 40000000000 | bytes 1 | tf_op jit(solution)/shard_map/project/pallas_call | solution.py:268
  167.4 9.9 %collective-permute-done.15.refs_5_ = bf16[576,1024]{1,0:T(8,128)(2,1)S(1)} collective-permute-done((bf16[576,1024]{1,0:T(8,128)(2,1)}, bf16[576,1024]{1,0:T(8,128)(2,1)S(1)}, u32[]{:S(2)}, u32[]{:S(2)}) %collective-permute-start.15) | collective-permute-done | bytes 1179680 | tf_op jit(solution)/shard_map/ppermute | solution.py:415
  177.3 1.0 copy-done.1
  178.3 10.3 %project.11 = bf16[768,2048]{1,0:T(8,128)(2,1)} custom-call(s32[2]{0:T(128)} %pad_add_fusion.1.refs_0_, s32[4,6]{1,0:T(4,128)} %refs_1_.11, s32[32]{0:T(128)} %refs_2_.11, s32[1,6]{1,0:T(1,128)} %refs_3_.11, f32[576,2048]{1,0:T(8,128)} %project.10.refs_4_, bf16[576,1024]{1,0:T(8,128)(2,1)} %copy-done.1, bf16[8192,2048]{1,0:T(8,128)(2,1)} %refs_6_.3), custom_call_target="tpu_custom_call" | custom-call | flops 1 | bytes 1 | tf_op jit(solution)/shard_map/project/pallas_call | solution.py:268
  (10 shorter events, 0.1 us)
Async XLA Ops:
  7.6 15.2 %collective-permute-start.8 = (bf16[2,128,2048]{2,1,0:T(8,128)(2,1)}, bf16[2,128,2048]{2,1,0:T(8,128)(2,1)}, u32[]{:S(2)}, u32[]{:S(2)}) collective-permute-start(bf16[2,128,2048]{2,1,0:T(8,128)(2,1)} %get-tuple-element.31), channel_id=1, source_target_pairs={{0,4},{4,8},{8,12},{12,0},{1,5},{5,9},{9,13},{13,1},{2,6},{6,10},{... | collective-permute-start | bytes 3145736 | tf_op jit(solution)/shard_map/ppermute | solution.py:336
  7.8 33.8 %collective-permute-start = (bf16[576,1024]{1,0:T(8,128)(2,1)}, bf16[576,1024]{1,0:T(8,128)(2,1)}, u32[]{:S(2)}, u32[]{:S(2)}) collective-permute-start(bf16[576,1024]{1,0:T(8,128)(2,1)} %get-tuple-element.23.refs_4_.rest_0_), channel_id=1, source_target_pairs={{0,1},{1,2},{2,3},{4,5},{5,6},{6,7},{8,9},{9,10},{10,11},{12,13},{... | collective-permute-start | bytes 3538952 | tf_op jit(solution)/shard_map/ppermute | solution.py:332
  13.7 31.0 %collective-permute-start.1 = (bf16[576,1024]{1,0:T(8,128)(2,1)}, bf16[576,1024]{1,0:T(8,128)(2,1)}, u32[]{:S(2)}, u32[]{:S(2)}) collective-permute-start(bf16[576,1024]{1,0:T(8,128)(2,1)} %get-tuple-element.23.refs_4_.rest_0_), channel_id=1, source_target_pairs={{1,0},{2,1},{3,2},{5,4},{6,5},{7,6},{9,8},{10,9},{11,10},{13,12},{... | collective-permute-start | bytes 3538952 | tf_op jit(solution)/shard_map/ppermute | solution.py:332
  22.9 25.0 %collective-permute-start.9 = (bf16[2,128,2048]{2,1,0:T(8,128)(2,1)}, bf16[2,128,2048]{2,1,0:T(8,128)(2,1)}, u32[]{:S(2)}, u32[]{:S(2)}) collective-permute-start(bf16[2,128,2048]{2,1,0:T(8,128)(2,1)} %get-tuple-element.33), channel_id=1, source_target_pairs={{0,8},{4,12},{8,0},{12,4},{1,9},{5,13},{9,1},{13,5},{2,10},{6,14},... | collective-permute-start | bytes 3145736 | tf_op jit(solution)/shard_map/ppermute | solution.py:336
  24.9 39.3 %collective-permute-start.2 = (bf16[576,1024]{1,0:T(8,128)(2,1)}, bf16[576,1024]{1,0:T(8,128)(2,1)}, u32[]{:S(2)}, u32[]{:S(2)}) collective-permute-start(bf16[576,1024]{1,0:T(8,128)(2,1)} %get-tuple-element.24.refs_5_.rest_1_), channel_id=1, source_target_pairs={{0,1},{1,2},{2,3},{4,5},{5,6},{6,7},{8,9},{9,10},{10,11},{12,13},{... | collective-permute-start | bytes 3538952 | tf_op jit(solution)/shard_map/ppermute | solution.py:332
  29.4 40.5 %collective-permute-start.3 = (bf16[576,1024]{1,0:T(8,128)(2,1)}, bf16[576,1024]{1,0:T(8,128)(2,1)}, u32[]{:S(2)}, u32[]{:S(2)}) collective-permute-start(bf16[576,1024]{1,0:T(8,128)(2,1)} %get-tuple-element.24.refs_5_.rest_1_), channel_id=1, source_target_pairs={{1,0},{2,1},{3,2},{5,4},{6,5},{7,6},{9,8},{10,9},{11,10},{13,12},{... | collective-permute-start | bytes 3538952 | tf_op jit(solution)/shard_map/ppermute | solution.py:332
  41.7 46.7 %collective-permute-start.4 = (bf16[576,1024]{1,0:T(8,128)(2,1)}, bf16[576,1024]{1,0:T(8,128)(2,1)S(1)}, u32[]{:S(2)}, u32[]{:S(2)}) collective-permute-start(bf16[576,1024]{1,0:T(8,128)(2,1)} %collective-permute-done.refs_5_), channel_id=1, source_target_pairs={{1,2},{2,3},{5,6},{6,7},{9,10},{10,11},{13,14},{14,15},{17,18},{18... | collective-permute-start | bytes 3538952 | tf_op jit(solution)/shard_map/ppermute | solution.py:332
  44.7 50.6 %collective-permute-start.5 = (bf16[576,1024]{1,0:T(8,128)(2,1)}, bf16[576,1024]{1,0:T(8,128)(2,1)}, u32[]{:S(2)}, u32[]{:S(2)}) collective-permute-start(bf16[576,1024]{1,0:T(8,128)(2,1)} %collective-permute-done.1.refs_6_), channel_id=1, source_target_pairs={{1,0},{2,1},{5,4},{6,5},{9,8},{10,9},{13,12},{14,13},{17,16},{18,1... | collective-permute-start | bytes 3538952 | tf_op jit(solution)/shard_map/ppermute | solution.py:332
  47.9 34.3 %collective-permute-start.10 = (bf16[2,128,2048]{2,1,0:T(8,128)(2,1)}, bf16[2,128,2048]{2,1,0:T(8,128)(2,1)}, u32[]{:S(2)}, u32[]{:S(2)}) collective-permute-start(bf16[2,128,2048]{2,1,0:T(8,128)(2,1)} %get-tuple-element.35), channel_id=1, source_target_pairs={{0,12},{4,0},{8,4},{12,8},{1,13},{5,1},{9,5},{13,9},{2,14},{6,2},{... | collective-permute-start | bytes 3145736 | tf_op jit(solution)/shard_map/ppermute | solution.py:336
  64.2 57.8 %collective-permute-start.6 = (bf16[576,1024]{1,0:T(8,128)(2,1)}, bf16[576,1024]{1,0:T(8,128)(2,1)}, u32[]{:S(2)}, u32[]{:S(2)}) collective-permute-start(bf16[576,1024]{1,0:T(8,128)(2,1)} %collective-permute-done.2.refs_5_), channel_id=1, source_target_pairs={{1,2},{2,3},{5,6},{6,7},{9,10},{10,11},{13,14},{14,15},{17,18},{18... | collective-permute-start | bytes 3538952 | tf_op jit(solution)/shard_map/ppermute | solution.py:332
  69.9 52.2 %collective-permute-start.7 = (bf16[576,1024]{1,0:T(8,128)(2,1)}, bf16[576,1024]{1,0:T(8,128)(2,1)}, u32[]{:S(2)}, u32[]{:S(2)}) collective-permute-start(bf16[576,1024]{1,0:T(8,128)(2,1)} %collective-permute-done.3.refs_6_), channel_id=1, source_target_pairs={{1,0},{2,1},{5,4},{6,5},{9,8},{10,9},{13,12},{14,13},{17,16},{18,1... | collective-permute-start | bytes 3538952 | tf_op jit(solution)/shard_map/ppermute | solution.py:332
  88.4 9.3 %copy-start.2 = (f32[64,576]{1,0:T(8,128)S(1)}, f32[64,576]{1,0:T(8,128)}, u32[]{:S(2)}) copy-start(f32[64,576]{1,0:T(8,128)} %shrink.1) | copy-start | bytes 442372
  88.4 8.0 %copy-start = (bf16[576,1024]{1,0:T(8,128)(2,1)}, bf16[576,1024]{1,0:T(8,128)(2,1)S(1)}, u32[]{:S(2)}) copy-start(bf16[576,1024]{1,0:T(8,128)(2,1)S(1)} %collective-permute-done.4.refs_5_) | copy-start | bytes 3538948
  96.4 56.4 %collective-permute-start.11 = (bf16[576,1024]{1,0:T(8,128)(2,1)}, bf16[576,1024]{1,0:T(8,128)(2,1)}, u32[]{:S(2)}, u32[]{:S(2)}) collective-permute-start(bf16[576,1024]{1,0:T(8,128)(2,1)} %broadcast_select_fusion.1), channel_id=1, source_target_pairs={{2,3},{1,0},{6,7},{5,4},{10,11},{9,8},{14,15},{13,12},{18,19},{17,... | collective-permute-start | bytes 3538952 | tf_op jit(solution)/shard_map/ppermute | solution.py:415
  97.8 11.9 %collective-permute-start.12 = (f32[64,576]{0,1:T(8,128)S(1)}, f32[64,576]{0,1:T(8,128)S(1)}, u32[]{:S(2)}, u32[]{:S(2)}) collective-permute-start(f32[64,576]{0,1:T(8,128)S(1)} %copy.9), channel_id=1, source_target_pairs={{0,1},{3,2},{4,5},{7,6},{8,9},{11,10},{12,13},{15,14},{16,17},{19,... | collective-permute-start | bytes 442376 | tf_op jit(solution)/shard_map/ppermute | solution.py:404
  109.8 11.0 %collective-permute-start.13 = (f32[64,576]{0,1:T(8,128)S(1)}, f32[64,576]{0,1:T(8,128)S(1)}, u32[]{:S(2)}, u32[]{:S(2)}) collective-permute-start(f32[64,576]{0,1:T(8,128)S(1)} %add.45), channel_id=1, source_target_pairs={{1,2},{2,1},{5,6},{6,5},{9,10},{10,9},{13,14},{14,13},{17,18},{18,... | collective-permute-start | bytes 442376 | tf_op jit(solution)/shard_map/ppermute | solution.py:404
  120.8 31.2 %collective-permute-start.14 = (f32[64,576]{0,1:T(8,128)S(1)}, f32[64,576]{0,1:T(8,128)S(1)}, u32[]{:S(2)}, u32[]{:S(2)}) collective-permute-start(f32[64,576]{0,1:T(8,128)S(1)} %add.47), channel_id=1, source_target_pairs={{2,3},{1,0},{6,7},{5,4},{10,11},{9,8},{14,15},{13,12},{18,19},{17,... | collective-permute-start | bytes 442376 | tf_op jit(solution)/shard_map/ppermute | solution.py:404
  124.5 52.7 %collective-permute-start.15 = (bf16[576,1024]{1,0:T(8,128)(2,1)}, bf16[576,1024]{1,0:T(8,128)(2,1)S(1)}, u32[]{:S(2)}, u32[]{:S(2)}) collective-permute-start(bf16[576,1024]{1,0:T(8,128)(2,1)} %broadcast_select_fusion), channel_id=1, source_target_pairs={{2,3},{1,0},{6,7},{5,4},{10,11},{9,8},{14,15},{13,12},{18,19},{17,... | collective-permute-start | bytes 3538952 | tf_op jit(solution)/shard_map/ppermute | solution.py:415
  177.3 1.0 copy-start.1

commit v8 on v5

--- a/solution.py
+++ b/solution.py
@@ -9,9 +9,8 @@
 
 adapter_scale = 2.0
 live_total = 576
-chunk_width = 1024
 column_tile = 512
-vmem_bytes = 48 * 1024 * 1024
+vmem_bytes = 62 * 1024 * 1024
 bf16, f32, i32 = jnp.bfloat16, jnp.float32, jnp.int32
 
 smem = pl.BlockSpec(memory_space=pltpu.SMEM)
@@ -22,8 +21,8 @@
     return pltpu.CompilerParams(vmem_limit_bytes=vmem_bytes)
 
 
-def cost():
-    return pl.CostEstimate(flops=1, bytes_accessed=1, transcendentals=0)
+def cost(flops=1):
+    return pl.CostEstimate(flops=flops, bytes_accessed=1, transcendentals=0)
 
 
 def one_hot(live, rows, axis):
@@ -43,13 +42,13 @@
 
 
 def prepare_kernel(
-    variants, slots, live, x, down, up, *rest, chunks, replicas, capacity, blocks
+    variants, slots, live, x, down, up, packed, *rest, steps, replicas, capacity, blocks
 ):
-    packed, picked, sems = rest[:chunks], rest[chunks : chunks + replicas], rest[-1]
+    picked, sems = rest[:-1], rest[-1]
     pool, rank = down.shape[0], down.shape[1]
     me = lax.axis_index("dp")
     copies = []
-    for step in range(replicas):
+    for step, place in zip(steps, picked):
         target = lax.rem(me + step, replicas)
         seen = jnp.int32(0)
         index = [jnp.int32(0)] * capacity
@@ -65,44 +64,41 @@
                 copies.append(
                     pltpu.make_async_copy(
                         pooled.at[index[m]],
-                        picked[step].at[kind, m * rank : (m + 1) * rank],
+                        place.at[kind, m * rank : (m + 1) * rank],
                         sems.at[len(copies)],
                     )
                 )
                 copies[-1].start()
     hot = one_hot(live, x.shape[0], 1)
-    start = 0
-    for out in packed:
-        stop = start + out.shape[1]
-        out[...] = jnp.dot(hot, x[:, start:stop], preferred_element_type=f32).astype(bf16)
-        start = stop
+    packed[...] = jnp.dot(hot, x[...], preferred_element_type=f32).astype(bf16)
     for copy in copies:
         copy.wait()
 
 
-def prepare(ints, hidden, down, up, widths, replicas, capacity):
-    rows, width = hidden.shape
+def prepare(ints, hidden, down, up, part, parts, steps, replicas, capacity):
+    rows, features = hidden.shape
+    width = features // parts
     depth = capacity * down.shape[1]
-    outs = [jax.ShapeDtypeStruct((live_total, w), bf16) for w in widths]
-    outs += [jax.ShapeDtypeStruct((2, depth, width), bf16)] * replicas
+    outs = [jax.ShapeDtypeStruct((live_total, width), bf16)]
+    outs += [jax.ShapeDtypeStruct((2, depth, features), bf16)] * len(steps)
     results = pl.pallas_call(
         functools.partial(
             prepare_kernel,
-            chunks=len(widths),
+            steps=steps,
             replicas=replicas,
             capacity=capacity,
             blocks=ints[0].shape[1],
         ),
         grid=(1,),
-        in_specs=[smem] * 3 + [pl.BlockSpec((rows, width), lambda i: (0, 0)), hbm, hbm],
+        in_specs=[smem] * 3 + [pl.BlockSpec((rows, width), lambda i: (0, part)), hbm, hbm],
         out_specs=[pl.BlockSpec(o.shape, lambda i, r=len(o.shape): (0,) * r) for o in outs],
         out_shape=outs,
-        scratch_shapes=[pltpu.SemaphoreType.DMA((replicas * capacity * 2,))],
+        scratch_shapes=[pltpu.SemaphoreType.DMA((len(steps) * capacity * 2,))],
         compiler_params=params(),
         cost_estimate=cost(),
         name="prepare",
     )(*ints, hidden, down, up)
-    return results[: len(widths)], results[len(widths) :]
+    return results[0], results[1:]
 
 
 def row_groups(variants, slots, live, shape, axis, replicas, capacity, pool):
@@ -171,7 +167,7 @@
     )(variants, slots, live, *xs, *factors)
 
 
-def project_kernel(*refs, groups, certain, has_total, delta, last, replicas, capacity, pool):
+def project_kernel(*refs, groups, has_total, delta, last, replicas, capacity, pool):
     refs = list(refs)
     meta, variants, slots, live = refs[:4]
     refs = refs[4:]
@@ -182,7 +178,7 @@
     ups = [refs.pop(0) for _ in range(replicas)] if delta else None
     out = refs.pop(0)
     spread = refs.pop(0) if delta else None
-    held, hot = (refs.pop(0), refs.pop(0)) if last else (out, None)
+    hot = refs.pop(0) if last else None
 
     if delta or last:
 
@@ -206,9 +202,8 @@
             x = x + other[...]
         return jnp.dot(x, ws[s][...], preferred_element_type=f32)
 
-    sure = [s for s in range(len(groups)) if s in certain]
     value = total[...] if has_total else None
-    for s in sure:
+    for s in range(len(groups)):
         value = product(s) if value is None else value + product(s)
     if delta:
         depth = ups[0].shape[1]
@@ -216,23 +211,12 @@
             value = value + jnp.dot(
                 spread[:, o * depth : (o + 1) * depth], ups[o][0], preferred_element_type=f32
             )
-    if len(sure) == len(groups) and last:
-        result = value.astype(bf16)
-    else:
-        held[...] = value
-        for s in range(len(groups)):
-            if s not in sure:
-
-                @pl.when(meta[2 * s + 1] > 0)
-                def _(s=s):
-                    held[...] += product(s)
-
-        result = held[...].astype(bf16) if last else None
     if last:
-        out[...] = jnp.dot(hot[...], result, preferred_element_type=f32).astype(bf16)
-
-
-def project(meta, ints, total, xs, weight, sizes, certain, low=None, factors=None, rows=None):
+        value = jnp.dot(hot[...], value.astype(bf16), preferred_element_type=f32)
+    out[...] = value.astype(out.dtype)
+
+
+def project(meta, ints, total, xs, weight, sizes, low=None, factors=None, rows=None, flops=1):
     replicas, capacity, pool = sizes
     columns = weight.shape[1]
     tile = min(column_tile, columns)
@@ -247,7 +231,7 @@
             args.append(x)
     for s, group in enumerate(xs):
         k = group[0].shape[1]
-        in_specs.append(pl.BlockSpec((k, tile), lambda i, m, s=s: (m[2 * s], i)))
+        in_specs.append(pl.BlockSpec((k, tile), lambda i, m, s=s: (m[s], i)))
         args.append(weight)
     scratch = []
     if low is not None:
@@ -264,12 +248,11 @@
     else:
         out = jax.ShapeDtypeStruct((rows, columns), bf16)
         out_spec = pl.BlockSpec((rows, tile), lambda i, m: (0, i))
-        scratch += [pltpu.VMEM((live_total, tile), f32), pltpu.VMEM((rows, live_total), bf16)]
+        scratch.append(pltpu.VMEM((rows, live_total), bf16))
     return pl.pallas_call(
         functools.partial(
             project_kernel,
             groups=tuple(len(g) for g in xs),
-            certain=certain,
             has_total=total is not None,
             delta=low is not None,
             last=rows is not None,
@@ -286,7 +269,7 @@
         ),
         out_shape=out,
         compiler_params=params(),
-        cost_estimate=cost(),
+        cost_estimate=cost(flops),
         name="project",
     )(meta, *args)
 
@@ -307,90 +290,89 @@
     blocks = block_variant_index.shape[1]
     rows, width = hidden.shape
     capacity = (blocks + replicas - 1) // replicas
-    piece = min(chunk_width, width)
-    chunks = width // piece
+    piece = width // 2
     ints = (block_variant_index, variant_pool_slot, block_live_count)
     sizes = (replicas, capacity, pool)
 
     def after(values, *events):
         return lax.optimization_barrier((values, events))[0]
 
-    def source(step):
-        return jnp.where(place >= step, place - step, jnp.minimum(place + step, tensor - 1))
-
-    def meta(items):
-        pairs = []
-        for device, j, there in items:
-            pairs += [device * chunks + j, there]
-        return jnp.stack([jnp.asarray(p, i32) for p in pairs])
-
-    def move(x, way, step):
-        if way > 0:
-            pairs = [(i, i + 1) for i in range(step - 1, tensor - 1)]
-        else:
-            pairs = [(i, i - 1) for i in range(1, tensor - step + 1)]
-        return lax.ppermute(x, "tensor", pairs)
+    def add(total, items, **more):
+        xs = [item[2] for item in items]
+        meta = [item[0] * (width // item[2][0].shape[1]) + item[1] for item in items]
+        meta = jnp.stack([jnp.asarray(m, i32) for m in meta])
+        return project(meta, ints, total, xs, query_weight, sizes, **more)
+
+    pools = (hidden, adapter_down, adapter_up)
+    own0, (next_factors,) = prepare(ints, *pools, 0, 2, (1,), replicas, capacity)
+    steps = (0,) + tuple(range(2, replicas))
+    own1, factors = prepare(ints, *pools, 1, 2, steps, replicas, capacity)
+    factors = [factors[0], next_factors, *factors[1:]]
+    own = (own0, own1)
 
     def send(x, step):
         pairs = [(i, (i + step) % replicas) for i in range(replicas)]
         return lax.ppermute(x, "dp", pairs)
 
-    one = jnp.int32(1)
-
-    def arrivals(step, js):
-        items, xs = [], []
-        for j in js:
-            if 2 * step >= tensor:
-                items.append((source(step), j, one))
-                xs.append((right[step][j], left[step][j]))
-            else:
-                items.append((jnp.maximum(place - step, 0), j, (place >= step).astype(i32)))
-                xs.append((right[step][j],))
-                behind = place + step
-                items.append((jnp.minimum(behind, tensor - 1), j, (behind < tensor).astype(i32)))
-                xs.append((left[step][j],))
-        return items, xs
-
-    def add(total, items, xs, **more):
-        certain = tuple(s for s, item in enumerate(items) if item[2] is one)
-        return project(meta(items), ints, total, xs, query_weight, sizes, certain, **more)
-
-    own, factors = prepare(
-        ints, hidden, adapter_down, adapter_up, (piece,) * chunks, replicas, capacity
-    )
-    right, left = [own], [own]
-
-    def pass_on(first=(), final=()):
-        step = len(right)
-        for w, moved in ((1, right), (-1, left)):
-            xs = list(moved[-1])
-            xs[0] = after(xs[0], *first)
-            xs[-1] = after(xs[-1], *final)
-            moved.append([move(x, w, step) for x in xs])
-
-    pass_on()
-    got = [factors[0]] + [send(factors[step], step) for step in range(1, replicas)]
-
-    partial = shrink(*ints, own, got, capacity, pool)
-    shared = lax.all_gather(partial.astype(bf16), "tensor", axis=0)
-    other = (jnp.arange(tensor) != place)[:, None, None]
-    low = partial + jnp.sum(jnp.where(other, shared.astype(f32), 0.0), axis=0)
-    low = low.astype(bf16).astype(f32).T
-
-    items, xs = arrivals(1, range(chunks))
-    items = [(place, j, one) for j in range(chunks)] + items
-    total = add(None, items, [(x,) for x in own] + xs)
-    first_total = total
-    for step in range(2, tensor):
-        pass_on(*([[first_total], [partial]] if step == tensor - 1 else []))
-        if step < tensor - 1:
-            total = add(total, *arrivals(step, range(chunks)))
-    for j in range(chunks):
-        more = {"rows": rows} if j == chunks - 1 else {}
-        if j == max(chunks - 2, 0):
-            more.update(low=low, factors=got)
-        total = add(total, *arrivals(tensor - 1, [j]), **more)
-    return total
+    own_total = add(None, [(place, j, (own[j],)) for j in range(2)])
+    got = [factors[0], send(factors[1], 1)]
+    for step in range(2, replicas):
+        events = got[-1:] if step < replicas - 1 else [got[-1], own_total]
+        got.append(send(after(factors[step], *events), step))
+
+    if tensor != 4:
+        gathered = [lax.all_gather(x, "tensor", axis=0) for x in own]
+        low = lax.psum(shrink(*ints, own, got, capacity, pool), "tensor")
+        low = low.astype(bf16).astype(f32).T
+        total = own_total
+        for step in range(1, tensor):
+            device = (place + step) % tensor
+            xs = [lax.dynamic_index_in_dim(x, device, 0, keepdims=False) for x in gathered]
+            items = [(device, j, (xs[j],)) for j in range(2)]
+            more = {"rows": rows, "low": low, "factors": got} if step == tensor - 1 else {}
+            total = add(total, items, **more)
+        return total
+
+    def pairs(x):
+        return lax.ppermute(x, "tensor", [(0, 1), (1, 0), (2, 3), (3, 2)])
+
+    def middle(x):
+        return lax.ppermute(x, "tensor", [(1, 2), (2, 1)])
+
+    def outward(x):
+        return lax.ppermute(x, "tensor", [(1, 0), (2, 3)])
+
+    near = place ^ 1
+    far = jnp.where(place < 2, 2, 1)
+    farthest = jnp.where(place < 2, 3, 0)
+
+    x1 = [pairs(x) for x in own]
+    y1 = [middle(x) for x in own]
+    near_total = add(own_total, [(near, 0, (x1[0],))])
+    total = add(near_total, [(near, 1, (x1[1],))])
+    partial = shrink(*ints[:2], after(ints[2], total), own, got, capacity, pool)
+
+    x2_0, y2_0 = outward(y1[0]), middle(x1[0])
+    x2_1, y2_1 = outward(after(y1[1], near_total)), middle(after(x1[1], near_total))
+    total = add(total, [(far, 0, (y1[0], x2_0))], flops=20_000_000_000)
+
+    inward = lax.ppermute(partial, "tensor", [(0, 1), (3, 2)])
+    across = middle(partial + inward)
+    across = after(across, y2_0)
+    hopped = partial + across
+    outer = outward(hopped)
+    low = (partial + inward + across + outer).astype(bf16).astype(f32).T
+
+    x3_0 = outward(after(y2_0, partial))
+    y2_1 = after(y2_1, hopped, total)
+    half = piece // 2
+    halves = [y2_1[:, :half], y2_1[:, half:]]
+    x3_1 = [outward(h) for h in halves]
+
+    items = [(far, 1, (y1[1], x2_1)), (farthest, 0, (y2_0, x3_0))]
+    total = add(total, items, low=low, factors=got, flops=40_000_000_000)
+    total = add(total, [(farthest, 2, (halves[0], x3_1[0]))])
+    return add(total, [(farthest, 3, (halves[1], x3_1[1]))], rows=rows)
 
 
 def solution(mesh):

time: 218 us -> 183 us (0.84)
  blocking collectives: 62.1 us -> 0 us
  Pallas kernels: 63.4 us -> 81.2 us
  waiting for transfers between devices: 59.6 us -> 68.7 us
    all_gather x1 -> x0, blocking collectives: 62.1 us -> none  [shards(): shared = lax.all_gather(partial.astype(bf16), 'tensor', axis=0)]
    pallas_call x4 -> x7, Pallas kernels: 51.9 us -> 64.8 us  [project(): pl.pallas_call(functools.partial(project_kernel, groups=tuple((len(g) for...]
    ppermute x12 -> x14, waiting for transfers between devices: 47 us -> 54.4 us  [the longest x6 51.4 us: outward(): return lax.ppermute(x, 'tensor', [(1, 0), (2, 3)])]
    unnamed x20 -> x12, local copies, waits for them, and re-layouts: 4.2 us -> 0.03 us
    pallas_call x1 -> x2, Pallas kernels: 6.71 us -> 10.2 us  [prepare(): pl.pallas_call(functools.partial(prepare_kernel, steps=steps, replicas=re...]
    ppermute x12 -> x14, starting transfers between devices: 25.2 us -> 25 us  [the longest x6 7.72 us: outward(): return lax.ppermute(x, 'tensor', [(1, 0), (2, 3)])]
  transfers between devices with their start and end apart: 15 -> 17, of which waited for: 6 -> 6; matrix products, arithmetic and copies ran while one was open for 0% -> 2% of each run, Pallas kernels for 21% -> 38%
where the time goes in v8:
time: 183 us; the launch traced here: 182 us
  Pallas kernels  81.2 us (44%)
  waiting for transfers between devices  68.7 us (38%)
  starting transfers between devices  27.8 us (15%)
  local copies, waits for them, and re-layouts  2.45 us (1%)
  other arithmetic  2.09 us (1%)
    pallas_call x7, Pallas kernels, project(): pl.pallas_call(functools.partial(project_kernel, groups=tuple((len(g) for...  64.8 us
    ppermute x6, waiting for transfers between devices, outward(): return lax.ppermute(x, 'tensor', [(1, 0), (2, 3)])  51.4 us
    ppermute x3, waiting for transfers between devices, send(): return lax.ppermute(x, 'dp', pairs)  14.4 us
    pallas_call x2, Pallas kernels, prepare(): pl.pallas_call(functools.partial(prepare_kernel, steps=steps, replicas=re...  10.2 us
    ppermute x6, starting transfers between devices, outward(): return lax.ppermute(x, 'tensor', [(1, 0), (2, 3)])  7.72 us
    ppermute x5, starting transfers between devices, middle(): return lax.ppermute(x, 'tensor', [(1, 2), (2, 1)])  7.45 us
    pallas_call x1, Pallas kernels, shrink(): pl.pallas_call(functools.partial(shrink_kernel, replicas=replicas, capaci...  6.19 us
    ppermute x1, starting transfers between devices, shards(): inward = lax.ppermute(partial, 'tensor', [(0, 1), (3, 2)])  5.58 us
  transfers between devices with their start and end apart: 17, of which 6 were waited for; matrix products, arithmetic and copies ran while one was open for 2% of the time, Pallas kernels for 38%

profile of v8, /device:TPU:0, one launch (start us, length us, event | category | flops | bytes accessed | tf_op | source)
XLA Modules:
  0.0 182.5 jit_solution(5763998687070882886)
XLA Ops:
  0.0 4.4 %prepare.2 = (bf16[576,1024]{1,0:T(8,128)(2,1)}, bf16[2,128,2048]{2,1,0:T(8,128)(2,1)}) custom-call(s32[4,6]{1,0:T(4,128)} %refs_1_.13, s32[32]{0:T(128)} %refs_2_.13, s32[1,6]{1,0:T(1,128)} %refs_3_.13, bf16[768,2048]{1,0:T(8,128)(2,1)} %x.3, bf16[8,64,2048]{2,1,0:T(8,128)(2,1)} %down.3, bf16[8,64,2048]{2,1,0:T(8,128)(2,1)} %up.3), custom_call_target="tpu_custom_call" | custom-call | flops 1 | bytes 1 | tf_op jit(solution)/shard_map/prepare/pallas_call | solution.py:84
  4.4 0.5 collective-permute-start.7
  4.9 2.6 %collective-permute-start = (bf16[576,1024]{1,0:T(8,128)(2,1)}, bf16[576,1024]{1,0:T(8,128)(2,1)}, u32[]{:S(2)}, u32[]{:S(2)}) collective-permute-start(bf16[576,1024]{1,0:T(8,128)(2,1)} %get-tuple-element.19.refs_4_.rest_0_), channel_id=1, source_target_pairs={{0,1},{1,0},{2,3},{3,2},{4,5},{5,4},{6,7},{7,6},{8,9},{9,8},{10,11... | collective-permute-start | bytes 3538952 | tf_op jit(solution)/shard_map/ppermute | solution.py:337
  7.6 1.7 collective-permute-start.2
  9.2 5.8 %prepare.3 = (bf16[576,1024]{1,0:T(8,128)(2,1)}, bf16[2,128,2048]{2,1,0:T(8,128)(2,1)}, bf16[2,128,2048]{2,1,0:T(8,128)(2,1)}, bf16[2,128,2048]{2,1,0:T(8,128)(2,1)}) custom-call(s32[4,6]{1,0:T(4,128)} %refs_1_.13, s32[32]{0:T(128)} %refs_2_.13, s32[1,6]{1,0:T(1,128)} %refs_3_.13, bf16[768,2048]{1,0:T(8,128)(2,1)} %x.3, bf16[8,64,2048]{2,1,0:T(8,128)(2,1)} %down.3, ...), custom_call_target="tpu_custom_call" | custom-call | flops 1 | bytes 1 | tf_op jit(solution)/shard_map/prepare/pallas_call | solution.py:84
  15.1 4.5 %collective-permute-done.7.rest_3_.refs_13_ = bf16[2,128,2048]{2,1,0:T(8,128)(2,1)S(1)} collective-permute-done((bf16[2,128,2048]{2,1,0:T(8,128)(2,1)}, bf16[2,128,2048]{2,1,0:T(8,128)(2,1)S(1)}, u32[]{:S(2)}, u32[]{:S(2)}) %collective-permute-start.7) | collective-permute-done | bytes 1048608 | tf_op jit(solution)/shard_map/ppermute | solution.py:315
  19.6 2.3 %collective-permute-start.8 = (bf16[2,128,2048]{2,1,0:T(8,128)(2,1)}, bf16[2,128,2048]{2,1,0:T(8,128)(2,1)}, u32[]{:S(2)}, u32[]{:S(2)}) collective-permute-start(bf16[2,128,2048]{2,1,0:T(8,128)(2,1)} %get-tuple-element.26), channel_id=1, source_target_pairs={{0,8},{4,12},{8,0},{12,4},{1,9},{5,13},{9,1},{13,5},{2,10},{6,14},... | collective-permute-start | bytes 3145736 | tf_op jit(solution)/shard_map/ppermute | solution.py:315
  21.8 1.6 collective-permute-start.1
  23.4 0.6 pad_add_fusion.1.refs_0_
  24.1 11.0 %project.7.refs_4_ = f32[576,2048]{1,0:T(8,128)} custom-call(s32[2]{0:T(128)} %pad_add_fusion.1.refs_0_, s32[4,6]{1,0:T(4,128)} %refs_1_.13, s32[32]{0:T(128)} %refs_2_.13, s32[1,6]{1,0:T(1,128)} %refs_3_.13, bf16[576,1024]{1,0:T(8,128)(2,1)} %get-tuple-element.19.refs_4_.rest_0_, bf16[576,1024]{1,0:T(8,128)(2,1)} %get-tuple-element.20.refs_5_.rest_1_, ...), custom_call_target="tpu_custom_call" | custom-call | flops 1 | bytes 1 | tf_op jit(solution)/shard_map/project/pallas_call | solution.py:252
  35.1 9.9 %collective-permute-done.8.rest_4_.refs_14_ = bf16[2,128,2048]{2,1,0:T(8,128)(2,1)} collective-permute-done((bf16[2,128,2048]{2,1,0:T(8,128)(2,1)}, bf16[2,128,2048]{2,1,0:T(8,128)(2,1)}, u32[]{:S(2)}, u32[]{:S(2)}) %collective-permute-start.8) | collective-permute-done | bytes 1048608 | tf_op jit(solution)/shard_map/ppermute | solution.py:315
  45.0 0.0 collective-permute-start.9
  45.0 1.7 collective-permute-start.4
  46.6 0.0 collective-permute-done.refs_5_
  46.6 1.7 collective-permute-start.6
  48.3 0.0 collective-permute-done.2.refs_5_
  48.3 1.3 collective-permute-start.3
  49.6 7.9 %project.8.refs_4_ = f32[576,2048]{1,0:T(8,128)} custom-call(s32[1]{0:T(128)} %bitcast.6.refs_0_, s32[4,6]{1,0:T(4,128)} %refs_1_.13, s32[32]{0:T(128)} %refs_2_.13, s32[1,6]{1,0:T(1,128)} %refs_3_.13, f32[576,2048]{1,0:T(8,128)} %project.7.refs_4_, bf16[576,1024]{1,0:T(8,128)(2,1)} %collective-permute-done.refs_5_, bf16[8192,2048]{1,0:T(8,128)(2,1)} %refs_7_.7), custom_call_target="tpu_custom_call" | custom-call | flops 1 | bytes 1 | tf_op jit(solution)/shard_map/project/pallas_call | solution.py:252
  57.5 1.5 collective-permute-done.1.refs_5_
  59.0 7.9 %project.9.refs_4_ = f32[576,2048]{1,0:T(8,128)} custom-call(s32[1]{0:T(128)} %bitcast.5.refs_0_, s32[4,6]{1,0:T(4,128)} %refs_1_.13, s32[32]{0:T(128)} %refs_2_.13, s32[1,6]{1,0:T(1,128)} %refs_3_.13, f32[576,2048]{1,0:T(8,128)} %project.8.refs_4_, bf16[576,1024]{1,0:T(8,128)(2,1)} %collective-permute-done.1.refs_5_, bf16[8192,2048]{1,0:T(8,128)(2,1)} %refs_7_.7), custom_call_target="tpu_custom_call" | custom-call | flops 1 | bytes 1 | tf_op jit(solution)/shard_map/project/pallas_call | solution.py:252
  66.9 0.0 collective-permute-done.9.rest_5_.refs_15_
  66.9 6.2 %shrink.1 = f32[64,576]{1,0:T(8,128)} custom-call(s32[4,6]{1,0:T(4,128)} %refs_1_.13, s32[32]{0:T(128)} %refs_2_.13, s32[1,6]{1,0:T(1,128)} %refs_3_.13, bf16[576,1024]{1,0:T(8,128)(2,1)} %get-tuple-element.19.refs_4_.rest_0_, bf16[576,1024]{1,0:T(8,128)(2,1)} %get-tuple-element.20.refs_5_.rest_1_, bf16[2,128,2048]{2,1,0:T(8,128)(2,1)} %get-tuple-element.23.rest_2_.refs_12_, ...), custom_call_target="tpu_custom_call" | custom-call | flops 1 | bytes 1 | tf_op jit(solution)/shard_map/shrink/pallas_call | solution.py:154
  73.1 1.1 copy.9
  74.2 5.6 %collective-permute-start.11 = (f32[64,576]{0,1:T(8,128)S(1)}, f32[64,576]{0,1:T(8,128)S(1)}, u32[]{:S(2)}, u32[]{:S(2)}) collective-permute-start(f32[64,576]{0,1:T(8,128)S(1)} %copy.9), channel_id=1, source_target_pairs={{0,1},{3,2},{4,5},{7,6},{8,9},{11,10},{12,13},{15,14},{16,17},{19,... | collective-permute-start | bytes 442376 | tf_op jit(solution)/shard_map/ppermute | solution.py:359
  79.8 0.6 pad_add_fusion.refs_0_
  80.4 0.0 collective-permute-done.4.refs_5_
  80.4 1.3 collective-permute-start.5
  81.7 1.7 collective-permute-start.14
  83.4 0.0 collective-permute-done.6.refs_7_
  83.4 1.3 collective-permute-start.10
  84.7 1.4 collective-permute-done.11
  86.1 0.7 collective-permute-start.12
  86.8 0.0 collective-permute-done.3.refs_6_
  86.8 8.3 %project.10.refs_4_ = f32[576,2048]{1,0:T(8,128)} custom-call(s32[1]{0:T(128)} %bitcast.4.refs_0_, s32[4,6]{1,0:T(4,128)} %refs_1_.13, s32[32]{0:T(128)} %refs_2_.13, s32[1,6]{1,0:T(1,128)} %refs_3_.13, f32[576,2048]{1,0:T(8,128)} %project.9.refs_4_, bf16[576,1024]{1,0:T(8,128)(2,1)} %collective-permute-done.2.refs_5_, ...), custom_call_target="tpu_custom_call" | custom-call | flops 20000000000 | bytes 1 | tf_op jit(solution)/shard_map/project/pallas_call | solution.py:252
  95.2 0.0 collective-permute-done.12
  95.2 1.3 collective-permute-start.13
  96.5 1.4 fusion
  97.9 0.0 copy-start.2
  97.9 1.3 collective-permute-start.16
  99.2 1.3 collective-permute-start.15
  100.5 42.3 %collective-permute-done.13 = f32[64,576]{0,1:T(8,128)S(1)} collective-permute-done((f32[64,576]{0,1:T(8,128)S(1)}, f32[64,576]{0,1:T(8,128)S(1)}, u32[]{:S(2)}, u32[]{:S(2)}) %collective-permute-start.13) | collective-permute-done | bytes 147488 | tf_op jit(solution)/shard_map/ppermute | solution.py:343
  142.8 0.8 convert_bitcast_fusion.refs_11_
  143.6 0.0 collective-permute-done.10.refs_8_
  143.6 14.7 %project.11.refs_4_ = f32[576,2048]{1,0:T(8,128)} custom-call(s32[2]{0:T(128)} %pad_add_fusion.refs_0_, s32[4,6]{1,0:T(4,128)} %refs_1_.13, s32[32]{0:T(128)} %refs_2_.13, s32[1,6]{1,0:T(1,128)} %refs_3_.13, f32[576,2048]{1,0:T(8,128)} %project.10.refs_4_, bf16[576,1024]{1,0:T(8,128)(2,1)} %collective-permute-done.4.refs_5_, ...), custom_call_target="tpu_custom_call" | custom-call | flops 40000000000 | bytes 1 | tf_op jit(solution)/shard_map/project/pallas_call | solution.py:252
  158.3 9.1 %collective-permute-done.15.refs_6_ = bf16[576,512]{1,0:T(8,128)(2,1)} collective-permute-done((bf16[576,512]{1,0:T(8,128)(2,1)S(1)}, bf16[576,512]{1,0:T(8,128)(2,1)}, u32[]{:S(2)}, u32[]{:S(2)}) %collective-permute-start.15) | collective-permute-done | bytes 589856 | tf_op jit(solution)/shard_map/ppermute | solution.py:343
  167.4 6.7 %project.12.refs_4_ = f32[576,2048]{1,0:T(8,128)} custom-call(s32[1]{0:T(128)} %bitcast.1.refs_0_, s32[4,6]{1,0:T(4,128)} %refs_1_.13, s32[32]{0:T(128)} %refs_2_.13, s32[1,6]{1,0:T(1,128)} %refs_3_.13, f32[576,2048]{1,0:T(8,128)} %project.11.refs_4_, bf16[576,512]{1,0:T(8,128)(2,1)} %copy-done.2, bf16[576,512]{1,0:T(8,128)(2,1)} %collective-permute-done.15.refs_6_, ...), custom_call_target="tpu_custom_call" | custom-call | flops 1 | bytes 1 | tf_op jit(solution)/shard_map/project/pallas_call | solution.py:252
  174.1 0.0 collective-permute-done.16.refs_6_
  174.1 8.4 %project.13 = bf16[768,2048]{1,0:T(8,128)(2,1)} custom-call(s32[1]{0:T(128)} %bitcast.refs_0_, s32[4,6]{1,0:T(4,128)} %refs_1_.13, s32[32]{0:T(128)} %refs_2_.13, s32[1,6]{1,0:T(1,128)} %refs_3_.13, f32[576,2048]{1,0:T(8,128)} %project.12.refs_4_, bf16[576,512]{1,0:T(8,128)(2,1)} %copy-done.1, bf16[576,512]{1,0:T(8,128)(2,1)} %collective-permute-done.16.refs_6_, ...), custom_call_target="tpu_custom_call" | custom-call | flops 1 | bytes 1 | tf_op jit(solution)/shard_map/project/pallas_call | solution.py:252
  (15 shorter events, 0.1 us)
Async XLA Ops:
  4.4 15.2 %collective-permute-start.7 = (bf16[2,128,2048]{2,1,0:T(8,128)(2,1)}, bf16[2,128,2048]{2,1,0:T(8,128)(2,1)S(1)}, u32[]{:S(2)}, u32[]{:S(2)}) collective-permute-start(bf16[2,128,2048]{2,1,0:T(8,128)(2,1)} %get-tuple-element.24), channel_id=1, source_target_pairs={{0,4},{4,8},{8,12},{12,0},{1,5},{5,9},{9,13},{13,1},{2,6},{6,10},{... | collective-permute-start | bytes 3145736 | tf_op jit(solution)/shard_map/ppermute | solution.py:315
  4.9 41.7 %collective-permute-start = (bf16[576,1024]{1,0:T(8,128)(2,1)}, bf16[576,1024]{1,0:T(8,128)(2,1)}, u32[]{:S(2)}, u32[]{:S(2)}) collective-permute-start(bf16[576,1024]{1,0:T(8,128)(2,1)} %get-tuple-element.19.refs_4_.rest_0_), channel_id=1, source_target_pairs={{0,1},{1,0},{2,3},{3,2},{4,5},{5,4},{6,7},{7,6},{8,9},{9,8},{10,11... | collective-permute-start | bytes 3538952 | tf_op jit(solution)/shard_map/ppermute | solution.py:337
  7.6 40.8 %collective-permute-start.2 = (bf16[576,1024]{1,0:T(8,128)(2,1)}, bf16[576,1024]{1,0:T(8,128)(2,1)}, u32[]{:S(2)}, u32[]{:S(2)}) collective-permute-start(bf16[576,1024]{1,0:T(8,128)(2,1)} %get-tuple-element.19.refs_4_.rest_0_), channel_id=1, source_target_pairs={{1,2},{2,1},{5,6},{6,5},{9,10},{10,9},{13,14},{14,13},{17,18},{18,... | collective-permute-start | bytes 3538952 | tf_op jit(solution)/shard_map/ppermute | solution.py:340
  19.6 3.9 %copy-start.5 = (bf16[2,128,2048]{2,1,0:T(8,128)(2,1)}, bf16[2,128,2048]{2,1,0:T(8,128)(2,1)S(1)}, u32[]{:S(2)}) copy-start(bf16[2,128,2048]{2,1,0:T(8,128)(2,1)S(1)} %collective-permute-done.7.rest_3_.refs_13_) | copy-start | bytes 3145732
  19.6 25.4 %collective-permute-start.8 = (bf16[2,128,2048]{2,1,0:T(8,128)(2,1)}, bf16[2,128,2048]{2,1,0:T(8,128)(2,1)}, u32[]{:S(2)}, u32[]{:S(2)}) collective-permute-start(bf16[2,128,2048]{2,1,0:T(8,128)(2,1)} %get-tuple-element.26), channel_id=1, source_target_pairs={{0,8},{4,12},{8,0},{12,4},{1,9},{5,13},{9,1},{13,5},{2,10},{6,14},... | collective-permute-start | bytes 3145736 | tf_op jit(solution)/shard_map/ppermute | solution.py:315
  21.8 37.2 %collective-permute-start.1 = (bf16[576,1024]{1,0:T(8,128)(2,1)}, bf16[576,1024]{1,0:T(8,128)(2,1)}, u32[]{:S(2)}, u32[]{:S(2)}) collective-permute-start(bf16[576,1024]{1,0:T(8,128)(2,1)} %get-tuple-element.20.refs_5_.rest_1_), channel_id=1, source_target_pairs={{0,1},{1,0},{2,3},{3,2},{4,5},{5,4},{6,7},{7,6},{8,9},{9,8},{10,11... | collective-permute-start | bytes 3538952 | tf_op jit(solution)/shard_map/ppermute | solution.py:337
  24.1 20.9 %copy-start = (bf16[576,1024]{1,0:T(8,128)(2,1)S(1)}, bf16[576,1024]{1,0:T(8,128)(2,1)}, u32[]{:S(2)}) copy-start(bf16[576,1024]{1,0:T(8,128)(2,1)} %get-tuple-element.20.refs_5_.rest_1_) | copy-start | bytes 3538948
  45.0 22.0 %collective-permute-start.9 = (bf16[2,128,2048]{2,1,0:T(8,128)(2,1)}, bf16[2,128,2048]{2,1,0:T(8,128)(2,1)}, u32[]{:S(2)}, u32[]{:S(2)}) collective-permute-start(bf16[2,128,2048]{2,1,0:T(8,128)(2,1)} %get-tuple-element.28), channel_id=1, source_target_pairs={{0,12},{4,0},{8,4},{12,8},{1,13},{5,1},{9,5},{13,9},{2,14},{6,2},{... | collective-permute-start | bytes 3145736 | tf_op jit(solution)/shard_map/ppermute | solution.py:315
  45.0 35.4 %collective-permute-start.4 = (bf16[576,1024]{1,0:T(8,128)(2,1)S(1)}, bf16[576,1024]{1,0:T(8,128)(2,1)}, u32[]{:S(2)}, u32[]{:S(2)}) collective-permute-start(bf16[576,1024]{1,0:T(8,128)(2,1)S(1)} %copy-done), channel_id=1, source_target_pairs={{1,2},{2,1},{5,6},{6,5},{9,10},{10,9},{13,14},{14,13},{17,18},{18,... | collective-permute-start | bytes 3538952 | tf_op jit(solution)/shard_map/ppermute | solution.py:340
  46.6 36.8 %collective-permute-start.6 = (bf16[576,1024]{1,0:T(8,128)(2,1)}, bf16[576,1024]{1,0:T(8,128)(2,1)}, u32[]{:S(2)}, u32[]{:S(2)}) collective-permute-start(bf16[576,1024]{1,0:T(8,128)(2,1)} %collective-permute-done.refs_5_), channel_id=1, source_target_pairs={{1,2},{2,1},{5,6},{6,5},{9,10},{10,9},{13,14},{14,13},{17,18},{18,... | collective-permute-start | bytes 3538952 | tf_op jit(solution)/shard_map/ppermute | solution.py:340
  48.3 38.5 %collective-permute-start.3 = (bf16[576,1024]{1,0:T(8,128)(2,1)}, bf16[576,1024]{1,0:T(8,128)(2,1)}, u32[]{:S(2)}, u32[]{:S(2)}) collective-permute-start(bf16[576,1024]{1,0:T(8,128)(2,1)} %collective-permute-done.2.refs_5_), channel_id=1, source_target_pairs={{1,0},{2,3},{5,4},{6,7},{9,8},{10,11},{13,12},{14,15},{17,16},{18,... | collective-permute-start | bytes 3538952 | tf_op jit(solution)/shard_map/ppermute | solution.py:343
  74.2 11.9 %collective-permute-start.11 = (f32[64,576]{0,1:T(8,128)S(1)}, f32[64,576]{0,1:T(8,128)S(1)}, u32[]{:S(2)}, u32[]{:S(2)}) collective-permute-start(f32[64,576]{0,1:T(8,128)S(1)} %copy.9), channel_id=1, source_target_pairs={{0,1},{3,2},{4,5},{7,6},{8,9},{11,10},{12,13},{15,14},{16,17},{19,... | collective-permute-start | bytes 442376 | tf_op jit(solution)/shard_map/ppermute | solution.py:359
  80.4 63.2 %collective-permute-start.5 = (bf16[576,1024]{1,0:T(8,128)(2,1)}, bf16[576,1024]{1,0:T(8,128)(2,1)}, u32[]{:S(2)}, u32[]{:S(2)}) collective-permute-start(bf16[576,1024]{1,0:T(8,128)(2,1)} %collective-permute-done.4.refs_5_), channel_id=1, source_target_pairs={{1,0},{2,3},{5,4},{6,7},{9,8},{10,11},{13,12},{14,15},{17,16},{18,... | collective-permute-start | bytes 3538952 | tf_op jit(solution)/shard_map/ppermute | solution.py:343
  81.7 14.9 %collective-permute-start.14 = (bf16[576,1024]{1,0:T(8,128)(2,1)}, bf16[576,1024]{1,0:T(8,128)(2,1)}, u32[]{:S(2)}, u32[]{:S(2)}) collective-permute-start(bf16[576,1024]{1,0:T(8,128)(2,1)} %collective-permute-done.1.refs_5_), channel_id=1, source_target_pairs={{1,2},{2,1},{5,6},{6,5},{9,10},{10,9},{13,14},{14,13},{17,18},{18,... | collective-permute-start | bytes 3538952 | tf_op jit(solution)/shard_map/ppermute | solution.py:340
  83.4 60.2 %collective-permute-start.10 = (bf16[576,1024]{1,0:T(8,128)(2,1)}, bf16[576,1024]{1,0:T(8,128)(2,1)}, u32[]{:S(2)}, u32[]{:S(2)}) collective-permute-start(bf16[576,1024]{1,0:T(8,128)(2,1)} %collective-permute-done.6.refs_7_), channel_id=1, source_target_pairs={{1,0},{2,3},{5,4},{6,7},{9,8},{10,11},{13,12},{14,15},{17,16},{18,... | collective-permute-start | bytes 3538952 | tf_op jit(solution)/shard_map/ppermute | solution.py:343
  86.1 9.0 %collective-permute-start.12 = (f32[64,576]{0,1:T(8,128)S(1)}, f32[64,576]{0,1:T(8,128)S(1)}, u32[]{:S(2)}, u32[]{:S(2)}) collective-permute-start(f32[64,576]{0,1:T(8,128)S(1)} %add.33), channel_id=1, source_target_pairs={{1,2},{2,1},{5,6},{6,5},{9,10},{10,9},{13,14},{14,13},{17,18},{18,... | collective-permute-start | bytes 442376 | tf_op jit(solution)/shard_map/ppermute | solution.py:340
  95.2 1.3 copy-start.3
  95.2 47.6 %collective-permute-start.13 = (f32[64,576]{0,1:T(8,128)S(1)}, f32[64,576]{0,1:T(8,128)S(1)}, u32[]{:S(2)}, u32[]{:S(2)}) collective-permute-start(f32[64,576]{0,1:T(8,128)S(1)} %add.35), channel_id=1, source_target_pairs={{1,0},{2,3},{5,4},{6,7},{9,8},{10,11},{13,12},{14,15},{17,16},{18,... | collective-permute-start | bytes 442376 | tf_op jit(solution)/shard_map/ppermute | solution.py:343
  96.5 46.3 %copy-start.4 = (f32[64,576]{0,1:T(8,128)S(1)}, f32[64,576]{0,1:T(8,128)}, u32[]{:S(2)}) copy-start(f32[64,576]{0,1:T(8,128)} %copy-done.3) | copy-start | bytes 442372
  97.9 60.4 %copy-start.1 = (bf16[576,512]{1,0:T(8,128)(2,1)}, bf16[576,512]{1,0:T(8,128)(2,1)S(1)}, u32[]{:S(2)}) copy-start(bf16[576,512]{1,0:T(8,128)(2,1)S(1)} %get-tuple-element.33.refs_5_) | copy-start | bytes 1769476
  97.9 60.4 %copy-start.2 = (bf16[576,512]{1,0:T(8,128)(2,1)}, bf16[576,512]{1,0:T(8,128)(2,1)S(1)}, u32[]{:S(2)}) copy-start(bf16[576,512]{1,0:T(8,128)(2,1)S(1)} %get-tuple-element.34.refs_5_) | copy-start | bytes 1769476
  97.9 76.2 %collective-permute-start.16 = (bf16[576,512]{1,0:T(8,128)(2,1)S(1)}, bf16[576,512]{1,0:T(8,128)(2,1)}, u32[]{:S(2)}, u32[]{:S(2)}) collective-permute-start(bf16[576,512]{1,0:T(8,128)(2,1)S(1)} %get-tuple-element.33.refs_5_), channel_id=1, source_target_pairs={{1,0},{2,3},{5,4},{6,7},{9,8},{10,11},{13,12},{14,15},{17,16},{18,... | collective-permute-start | bytes 1769480 | tf_op jit(solution)/shard_map/ppermute | solution.py:343
  99.2 68.2 %collective-permute-start.15 = (bf16[576,512]{1,0:T(8,128)(2,1)S(1)}, bf16[576,512]{1,0:T(8,128)(2,1)}, u32[]{:S(2)}, u32[]{:S(2)}) collective-permute-start(bf16[576,512]{1,0:T(8,128)(2,1)S(1)} %get-tuple-element.34.refs_5_), channel_id=1, source_target_pairs={{1,0},{2,3},{5,4},{6,7},{9,8},{10,11},{13,12},{14,15},{17,16},{18,... | collective-permute-start | bytes 1769480 | tf_op jit(solution)/shard_map/ppermute | solution.py:343

commit v9 on v8

--- a/solution.py
+++ b/solution.py
@@ -354,7 +354,7 @@
 
     x2_0, y2_0 = outward(y1[0]), middle(x1[0])
     x2_1, y2_1 = outward(after(y1[1], near_total)), middle(after(x1[1], near_total))
-    total = add(total, [(far, 0, (y1[0], x2_0))], flops=20_000_000_000)
+    total = add(total, [(far, 0, (y1[0], x2_0))], flops=3_450_000_000)
 
     inward = lax.ppermute(partial, "tensor", [(0, 1), (3, 2)])
     across = middle(partial + inward)
@@ -370,8 +370,8 @@
     x3_1 = [outward(h) for h in halves]
 
     items = [(far, 1, (y1[1], x2_1)), (farthest, 0, (y2_0, x3_0))]
-    total = add(total, items, low=low, factors=got, flops=40_000_000_000)
-    total = add(total, [(farthest, 2, (halves[0], x3_1[0]))])
+    total = add(total, items, low=low, factors=got, flops=2_300_000_000)
+    total = add(total, [(farthest, 2, (halves[0], x3_1[0]))], flops=1_150_000_000)
     return add(total, [(farthest, 3, (halves[1], x3_1[1]))], rows=rows)
 
 

time: 183 us -> 176 us (0.962)
  waiting for transfers between devices: 68.7 us -> 49 us
  starting transfers between devices: 27.8 us -> 39.4 us
    ppermute x6, waiting for transfers between devices: 51.4 us -> 26.9 us  [outward(): return lax.ppermute(x, 'tensor', [(1, 0), (2, 3)])]
    ppermute x1, starting transfers between devices: 5.58 us -> 15.6 us  [shards(): inward = lax.ppermute(partial, 'tensor', [(0, 1), (3, 2)])]
    ppermute x3, waiting for transfers between devices: 14.4 us -> 4.45 us  [send(): return lax.ppermute(x, 'dp', pairs)]
    ppermute x2, waiting for transfers between devices: 1.5 us -> 10.4 us  [pairs(): return lax.ppermute(x, 'tensor', [(0, 1), (1, 0), (2, 3), (3, 2)])]
    ppermute x1, waiting for transfers between devices: 1.41 us -> 7.24 us  [shards(): inward = lax.ppermute(partial, 'tensor', [(0, 1), (3, 2)])]
  transfers between devices with their start and end apart: 17 -> 17, of which waited for: 6 -> 6; matrix products, arithmetic and copies ran while one was open for 2% -> 3% of each run, Pallas kernels for 38% -> 39%
where the time goes in v9:
time: 176 us; the launch traced here: 175 us
  Pallas kernels  80.7 us (46%)
  waiting for transfers between devices  49 us (28%)
  starting transfers between devices  39.4 us (22%)
  local copies, waits for them, and re-layouts  3.36 us (2%)
  other arithmetic  2.12 us (1%)
    pallas_call x7, Pallas kernels, project(): pl.pallas_call(functools.partial(project_kernel, groups=tuple((len(g) for...  64.3 us
    ppermute x6, waiting for transfers between devices, outward(): return lax.ppermute(x, 'tensor', [(1, 0), (2, 3)])  26.9 us
    ppermute x1, starting transfers between devices, shards(): inward = lax.ppermute(partial, 'tensor', [(0, 1), (3, 2)])  15.6 us
    ppermute x2, waiting for transfers between devices, pairs(): return lax.ppermute(x, 'tensor', [(0, 1), (1, 0), (2, 3), (3, 2)])  10.4 us
    pallas_call x2, Pallas kernels, prepare(): pl.pallas_call(functools.partial(prepare_kernel, steps=steps, replicas=re...  10.2 us
    ppermute x6, starting transfers between devices, outward(): return lax.ppermute(x, 'tensor', [(1, 0), (2, 3)])  7.72 us
    ppermute x5, starting transfers between devices, middle(): return lax.ppermute(x, 'tensor', [(1, 2), (2, 1)])  7.48 us
    ppermute x1, waiting for transfers between devices, shards(): inward = lax.ppermute(partial, 'tensor', [(0, 1), (3, 2)])  7.24 us
  transfers between devices with their start and end apart: 17, of which 6 were waited for; matrix products, arithmetic and copies ran while one was open for 3% of the time, Pallas kernels for 39%

profile of v9, /device:TPU:0, one launch (start us, length us, event | category | flops | bytes accessed | tf_op | source)
XLA Modules:
  0.0 174.8 jit_solution(2808495751848223194)
XLA Ops:
  0.0 4.4 %prepare.2 = (bf16[576,1024]{1,0:T(8,128)(2,1)}, bf16[2,128,2048]{2,1,0:T(8,128)(2,1)}) custom-call(s32[4,6]{1,0:T(4,128)} %refs_1_.13, s32[32]{0:T(128)} %refs_2_.13, s32[1,6]{1,0:T(1,128)} %refs_3_.13, bf16[768,2048]{1,0:T(8,128)(2,1)} %x.3, bf16[8,64,2048]{2,1,0:T(8,128)(2,1)} %down.3, bf16[8,64,2048]{2,1,0:T(8,128)(2,1)} %up.3), custom_call_target="tpu_custom_call" | custom-call | flops 1 | bytes 1 | tf_op jit(solution)/shard_map/prepare/pallas_call | solution.py:84
  4.4 0.5 collective-permute-start.7
  4.9 2.6 %collective-permute-start = (bf16[576,1024]{1,0:T(8,128)(2,1)}, bf16[576,1024]{1,0:T(8,128)(2,1)}, u32[]{:S(2)}, u32[]{:S(2)}) collective-permute-start(bf16[576,1024]{1,0:T(8,128)(2,1)} %get-tuple-element.19.refs_4_.rest_0_), channel_id=1, source_target_pairs={{0,1},{1,0},{2,3},{3,2},{4,5},{5,4},{6,7},{7,6},{8,9},{9,8},{10,11... | collective-permute-start | bytes 3538952 | tf_op jit(solution)/shard_map/ppermute | solution.py:337
  7.6 1.7 collective-permute-start.2
  9.3 5.9 %prepare.3 = (bf16[576,1024]{1,0:T(8,128)(2,1)}, bf16[2,128,2048]{2,1,0:T(8,128)(2,1)}, bf16[2,128,2048]{2,1,0:T(8,128)(2,1)}, bf16[2,128,2048]{2,1,0:T(8,128)(2,1)}) custom-call(s32[4,6]{1,0:T(4,128)} %refs_1_.13, s32[32]{0:T(128)} %refs_2_.13, s32[1,6]{1,0:T(1,128)} %refs_3_.13, bf16[768,2048]{1,0:T(8,128)(2,1)} %x.3, bf16[8,64,2048]{2,1,0:T(8,128)(2,1)} %down.3, ...), custom_call_target="tpu_custom_call" | custom-call | flops 1 | bytes 1 | tf_op jit(solution)/shard_map/prepare/pallas_call | solution.py:84
  15.1 4.4 %collective-permute-done.7.rest_3_.refs_13_ = bf16[2,128,2048]{2,1,0:T(8,128)(2,1)S(1)} collective-permute-done((bf16[2,128,2048]{2,1,0:T(8,128)(2,1)}, bf16[2,128,2048]{2,1,0:T(8,128)(2,1)S(1)}, u32[]{:S(2)}, u32[]{:S(2)}) %collective-permute-start.7) | collective-permute-done | bytes 1048608 | tf_op jit(solution)/shard_map/ppermute | solution.py:315
  19.6 2.2 %collective-permute-start.8 = (bf16[2,128,2048]{2,1,0:T(8,128)(2,1)}, bf16[2,128,2048]{2,1,0:T(8,128)(2,1)}, u32[]{:S(2)}, u32[]{:S(2)}) collective-permute-start(bf16[2,128,2048]{2,1,0:T(8,128)(2,1)} %get-tuple-element.26), channel_id=1, source_target_pairs={{0,8},{4,12},{8,0},{12,4},{1,9},{5,13},{9,1},{13,5},{2,10},{6,14},... | collective-permute-start | bytes 3145736 | tf_op jit(solution)/shard_map/ppermute | solution.py:315
  21.8 1.6 collective-permute-start.1
  23.4 1.7 collective-permute-start.4
  25.1 8.6 %collective-permute-done.refs_5_ = bf16[576,1024]{1,0:T(8,128)(2,1)} collective-permute-done((bf16[576,1024]{1,0:T(8,128)(2,1)}, bf16[576,1024]{1,0:T(8,128)(2,1)}, u32[]{:S(2)}, u32[]{:S(2)}) %collective-permute-start) | collective-permute-done | bytes 1179680 | tf_op jit(solution)/shard_map/ppermute | solution.py:337
  33.7 1.7 collective-permute-start.6
  35.4 0.6 pad_add_fusion.1.refs_0_
  36.1 10.4 %project.7.refs_4_ = f32[576,2048]{1,0:T(8,128)} custom-call(s32[2]{0:T(128)} %pad_add_fusion.1.refs_0_, s32[4,6]{1,0:T(4,128)} %refs_1_.13, s32[32]{0:T(128)} %refs_2_.13, s32[1,6]{1,0:T(1,128)} %refs_3_.13, bf16[576,1024]{1,0:T(8,128)(2,1)} %get-tuple-element.19.refs_4_.rest_0_, bf16[576,1024]{1,0:T(8,128)(2,1)} %get-tuple-element.20.refs_5_.rest_1_, ...), custom_call_target="tpu_custom_call" | custom-call | flops 1 | bytes 1 | tf_op jit(solution)/shard_map/project/pallas_call | solution.py:252
  46.5 0.0 collective-permute-done.8.rest_4_.refs_14_
  46.5 1.6 collective-permute-start.9
  48.1 0.0 collective-permute-done.2.refs_5_
  48.1 1.3 collective-permute-start.3
  49.4 7.9 %project.8.refs_4_ = f32[576,2048]{1,0:T(8,128)} custom-call(s32[1]{0:T(128)} %bitcast.6.refs_0_, s32[4,6]{1,0:T(4,128)} %refs_1_.13, s32[32]{0:T(128)} %refs_2_.13, s32[1,6]{1,0:T(1,128)} %refs_3_.13, f32[576,2048]{1,0:T(8,128)} %project.7.refs_4_, bf16[576,1024]{1,0:T(8,128)(2,1)} %collective-permute-done.refs_5_, bf16[8192,2048]{1,0:T(8,128)(2,1)} %refs_7_.7), custom_call_target="tpu_custom_call" | custom-call | flops 1 | bytes 1 | tf_op jit(solution)/shard_map/project/pallas_call | solution.py:252
  57.3 1.8 %collective-permute-done.1.refs_5_ = bf16[576,1024]{1,0:T(8,128)(2,1)} collective-permute-done((bf16[576,1024]{1,0:T(8,128)(2,1)}, bf16[576,1024]{1,0:T(8,128)(2,1)}, u32[]{:S(2)}, u32[]{:S(2)}) %collective-permute-start.1) | collective-permute-done | bytes 1179680 | tf_op jit(solution)/shard_map/ppermute | solution.py:337
  59.0 1.7 collective-permute-start.14
  60.7 0.0 collective-permute-done.4.refs_5_
  60.7 1.3 collective-permute-start.5
  62.0 8.0 %project.9.refs_4_ = f32[576,2048]{1,0:T(8,128)} custom-call(s32[1]{0:T(128)} %bitcast.5.refs_0_, s32[4,6]{1,0:T(4,128)} %refs_1_.13, s32[32]{0:T(128)} %refs_2_.13, s32[1,6]{1,0:T(1,128)} %refs_3_.13, f32[576,2048]{1,0:T(8,128)} %project.8.refs_4_, bf16[576,1024]{1,0:T(8,128)(2,1)} %collective-permute-done.1.refs_5_, bf16[8192,2048]{1,0:T(8,128)(2,1)} %refs_7_.7), custom_call_target="tpu_custom_call" | custom-call | flops 1 | bytes 1 | tf_op jit(solution)/shard_map/project/pallas_call | solution.py:252
  70.0 0.0 collective-permute-done.9.rest_5_.refs_15_
  70.0 1.0 copy-done.1
  70.9 6.2 %shrink.1 = f32[64,576]{1,0:T(8,128)} custom-call(s32[4,6]{1,0:T(4,128)} %refs_1_.13, s32[32]{0:T(128)} %refs_2_.13, s32[1,6]{1,0:T(1,128)} %refs_3_.13, bf16[576,1024]{1,0:T(8,128)(2,1)} %get-tuple-element.19.refs_4_.rest_0_, bf16[576,1024]{1,0:T(8,128)(2,1)} %get-tuple-element.20.refs_5_.rest_1_, bf16[2,128,2048]{2,1,0:T(8,128)(2,1)} %get-tuple-element.23.rest_2_.refs_12_, ...), custom_call_target="tpu_custom_call" | custom-call | flops 1 | bytes 1 | tf_op jit(solution)/shard_map/shrink/pallas_call | solution.py:154
  77.1 0.0 collective-permute-done.6.refs_7_
  77.1 1.3 collective-permute-start.10
  78.4 1.1 copy.9
  79.5 15.6 %collective-permute-start.11 = (f32[64,576]{0,1:T(8,128)S(1)}, f32[64,576]{0,1:T(8,128)S(1)}, u32[]{:S(2)}, u32[]{:S(2)}) collective-permute-start(f32[64,576]{0,1:T(8,128)S(1)} %copy.9), channel_id=1, source_target_pairs={{0,1},{3,2},{4,5},{7,6},{8,9},{11,10},{12,13},{15,14},{16,17},{19,... | collective-permute-start | bytes 442376 | tf_op jit(solution)/shard_map/ppermute | solution.py:359
  95.1 7.2 %collective-permute-done.11 = f32[64,576]{0,1:T(8,128)S(1)} collective-permute-done((f32[64,576]{0,1:T(8,128)S(1)}, f32[64,576]{0,1:T(8,128)S(1)}, u32[]{:S(2)}, u32[]{:S(2)}) %collective-permute-start.11) | collective-permute-done | bytes 147488 | tf_op jit(solution)/shard_map/ppermute | solution.py:359
  102.4 0.7 collective-permute-start.12
  103.1 0.0 collective-permute-done.3.refs_6_
  103.1 8.3 %project.10.refs_4_ = f32[576,2048]{1,0:T(8,128)} custom-call(s32[1]{0:T(128)} %bitcast.4.refs_0_, s32[4,6]{1,0:T(4,128)} %refs_1_.13, s32[32]{0:T(128)} %refs_2_.13, s32[1,6]{1,0:T(1,128)} %refs_3_.13, f32[576,2048]{1,0:T(8,128)} %project.9.refs_4_, bf16[576,1024]{1,0:T(8,128)(2,1)} %collective-permute-done.2.refs_5_, ...), custom_call_target="tpu_custom_call" | custom-call | flops 3449999872 | bytes 1 | tf_op jit(solution)/shard_map/project/pallas_call | solution.py:252
  111.4 0.0 collective-permute-done.12
  111.4 1.3 collective-permute-start.13
  112.7 1.3 fusion
  114.1 0.0 copy-start.3
  114.1 1.3 collective-permute-start.15
  115.4 1.3 collective-permute-start.16
  116.7 0.7 pad_add_fusion.refs_0_
  117.3 23.7 %collective-permute-done.13 = f32[64,576]{0,1:T(8,128)S(1)} collective-permute-done((f32[64,576]{0,1:T(8,128)S(1)}, f32[64,576]{0,1:T(8,128)S(1)}, u32[]{:S(2)}, u32[]{:S(2)}) %collective-permute-start.13) | collective-permute-done | bytes 147488 | tf_op jit(solution)/shard_map/ppermute | solution.py:343
  141.0 0.7 convert_bitcast_fusion.refs_11_
  141.8 14.7 %project.11.refs_4_ = f32[576,2048]{1,0:T(8,128)} custom-call(s32[2]{0:T(128)} %pad_add_fusion.refs_0_, s32[4,6]{1,0:T(4,128)} %refs_1_.13, s32[32]{0:T(128)} %refs_2_.13, s32[1,6]{1,0:T(1,128)} %refs_3_.13, f32[576,2048]{1,0:T(8,128)} %project.10.refs_4_, bf16[576,1024]{1,0:T(8,128)(2,1)} %collective-permute-done.4.refs_5_, ...), custom_call_target="tpu_custom_call" | custom-call | flops 2300000000 | bytes 1 | tf_op jit(solution)/shard_map/project/pallas_call | solution.py:252
  156.5 0.0 collective-permute-done.15.refs_6_
  156.5 6.6 %project.12.refs_4_ = f32[576,2048]{1,0:T(8,128)} custom-call(s32[1]{0:T(128)} %bitcast.1.refs_0_, s32[4,6]{1,0:T(4,128)} %refs_1_.13, s32[32]{0:T(128)} %refs_2_.13, s32[1,6]{1,0:T(1,128)} %refs_3_.13, f32[576,2048]{1,0:T(8,128)} %project.11.refs_4_, bf16[576,512]{1,0:T(8,128)(2,1)} %copy-done.3, bf16[576,512]{1,0:T(8,128)(2,1)} %collective-permute-done.15.refs_6_, ...), custom_call_target="tpu_custom_call" | custom-call | flops 1150000000 | bytes 1 | tf_op jit(solution)/shard_map/project/pallas_call | solution.py:252
  163.2 3.2 %collective-permute-done.16.refs_6_ = bf16[576,512]{1,0:T(8,128)(2,1)} collective-permute-done((bf16[576,512]{1,0:T(8,128)(2,1)S(1)}, bf16[576,512]{1,0:T(8,128)(2,1)}, u32[]{:S(2)}, u32[]{:S(2)}) %collective-permute-start.16) | collective-permute-done | bytes 589856 | tf_op jit(solution)/shard_map/ppermute | solution.py:343
  166.4 8.3 %project.13 = bf16[768,2048]{1,0:T(8,128)(2,1)} custom-call(s32[1]{0:T(128)} %bitcast.refs_0_, s32[4,6]{1,0:T(4,128)} %refs_1_.13, s32[32]{0:T(128)} %refs_2_.13, s32[1,6]{1,0:T(1,128)} %refs_3_.13, f32[576,2048]{1,0:T(8,128)} %project.12.refs_4_, bf16[576,512]{1,0:T(8,128)(2,1)} %copy-done.2, bf16[576,512]{1,0:T(8,128)(2,1)} %collective-permute-done.16.refs_6_, ...), custom_call_target="tpu_custom_call" | custom-call | flops 1 | bytes 1 | tf_op jit(solution)/shard_map/project/pallas_call | solution.py:252
  (11 shorter events, 0.1 us)
Async XLA Ops:
  4.4 15.2 %collective-permute-start.7 = (bf16[2,128,2048]{2,1,0:T(8,128)(2,1)}, bf16[2,128,2048]{2,1,0:T(8,128)(2,1)S(1)}, u32[]{:S(2)}, u32[]{:S(2)}) collective-permute-start(bf16[2,128,2048]{2,1,0:T(8,128)(2,1)} %get-tuple-element.24), channel_id=1, source_target_pairs={{0,4},{4,8},{8,12},{12,0},{1,5},{5,9},{9,13},{13,1},{2,6},{6,10},{... | collective-permute-start | bytes 3145736 | tf_op jit(solution)/shard_map/ppermute | solution.py:315
  4.9 28.8 %collective-permute-start = (bf16[576,1024]{1,0:T(8,128)(2,1)}, bf16[576,1024]{1,0:T(8,128)(2,1)}, u32[]{:S(2)}, u32[]{:S(2)}) collective-permute-start(bf16[576,1024]{1,0:T(8,128)(2,1)} %get-tuple-element.19.refs_4_.rest_0_), channel_id=1, source_target_pairs={{0,1},{1,0},{2,3},{3,2},{4,5},{5,4},{6,7},{7,6},{8,9},{9,8},{10,11... | collective-permute-start | bytes 3538952 | tf_op jit(solution)/shard_map/ppermute | solution.py:337
  7.6 40.5 %collective-permute-start.2 = (bf16[576,1024]{1,0:T(8,128)(2,1)}, bf16[576,1024]{1,0:T(8,128)(2,1)}, u32[]{:S(2)}, u32[]{:S(2)}) collective-permute-start(bf16[576,1024]{1,0:T(8,128)(2,1)} %get-tuple-element.19.refs_4_.rest_0_), channel_id=1, source_target_pairs={{1,2},{2,1},{5,6},{6,5},{9,10},{10,9},{13,14},{14,13},{17,18},{18,... | collective-permute-start | bytes 3538952 | tf_op jit(solution)/shard_map/ppermute | solution.py:340
  19.6 26.9 %copy-start = (bf16[2,128,2048]{2,1,0:T(8,128)(2,1)}, bf16[2,128,2048]{2,1,0:T(8,128)(2,1)S(1)}, u32[]{:S(2)}) copy-start(bf16[2,128,2048]{2,1,0:T(8,128)(2,1)S(1)} %collective-permute-done.7.rest_3_.refs_13_) | copy-start | bytes 3145732
  19.6 26.9 %collective-permute-start.8 = (bf16[2,128,2048]{2,1,0:T(8,128)(2,1)}, bf16[2,128,2048]{2,1,0:T(8,128)(2,1)}, u32[]{:S(2)}, u32[]{:S(2)}) collective-permute-start(bf16[2,128,2048]{2,1,0:T(8,128)(2,1)} %get-tuple-element.26), channel_id=1, source_target_pairs={{0,8},{4,12},{8,0},{12,4},{1,9},{5,13},{9,1},{13,5},{2,10},{6,14},... | collective-permute-start | bytes 3145736 | tf_op jit(solution)/shard_map/ppermute | solution.py:315
  21.8 37.2 %collective-permute-start.1 = (bf16[576,1024]{1,0:T(8,128)(2,1)}, bf16[576,1024]{1,0:T(8,128)(2,1)}, u32[]{:S(2)}, u32[]{:S(2)}) collective-permute-start(bf16[576,1024]{1,0:T(8,128)(2,1)} %get-tuple-element.20.refs_5_.rest_1_), channel_id=1, source_target_pairs={{0,1},{1,0},{2,3},{3,2},{4,5},{5,4},{6,7},{7,6},{8,9},{9,8},{10,11... | collective-permute-start | bytes 3538952 | tf_op jit(solution)/shard_map/ppermute | solution.py:337
  23.4 37.3 %collective-permute-start.4 = (bf16[576,1024]{1,0:T(8,128)(2,1)}, bf16[576,1024]{1,0:T(8,128)(2,1)}, u32[]{:S(2)}, u32[]{:S(2)}) collective-permute-start(bf16[576,1024]{1,0:T(8,128)(2,1)} %get-tuple-element.20.refs_5_.rest_1_), channel_id=1, source_target_pairs={{1,2},{2,1},{5,6},{6,5},{9,10},{10,9},{13,14},{14,13},{17,18},{18,... | collective-permute-start | bytes 3538952 | tf_op jit(solution)/shard_map/ppermute | solution.py:340
  33.7 43.4 %collective-permute-start.6 = (bf16[576,1024]{1,0:T(8,128)(2,1)}, bf16[576,1024]{1,0:T(8,128)(2,1)}, u32[]{:S(2)}, u32[]{:S(2)}) collective-permute-start(bf16[576,1024]{1,0:T(8,128)(2,1)} %collective-permute-done.refs_5_), channel_id=1, source_target_pairs={{1,2},{2,1},{5,6},{6,5},{9,10},{10,9},{13,14},{14,13},{17,18},{18,... | collective-permute-start | bytes 3538952 | tf_op jit(solution)/shard_map/ppermute | solution.py:340
  46.5 23.5 %collective-permute-start.9 = (bf16[2,128,2048]{2,1,0:T(8,128)(2,1)}, bf16[2,128,2048]{2,1,0:T(8,128)(2,1)S(1)}, u32[]{:S(2)}, u32[]{:S(2)}) collective-permute-start(bf16[2,128,2048]{2,1,0:T(8,128)(2,1)} %get-tuple-element.28), channel_id=1, source_target_pairs={{0,12},{4,0},{8,4},{12,8},{1,13},{5,1},{9,5},{13,9},{2,14},{6,2},{... | collective-permute-start | bytes 3145736 | tf_op jit(solution)/shard_map/ppermute | solution.py:315
  48.1 55.0 %collective-permute-start.3 = (bf16[576,1024]{1,0:T(8,128)(2,1)}, bf16[576,1024]{1,0:T(8,128)(2,1)}, u32[]{:S(2)}, u32[]{:S(2)}) collective-permute-start(bf16[576,1024]{1,0:T(8,128)(2,1)} %collective-permute-done.2.refs_5_), channel_id=1, source_target_pairs={{1,0},{2,3},{5,4},{6,7},{9,8},{10,11},{13,12},{14,15},{17,16},{18,... | collective-permute-start | bytes 3538952 | tf_op jit(solution)/shard_map/ppermute | solution.py:343
  59.0 53.7 %collective-permute-start.14 = (bf16[576,1024]{1,0:T(8,128)(2,1)}, bf16[576,1024]{1,0:T(8,128)(2,1)}, u32[]{:S(2)}, u32[]{:S(2)}) collective-permute-start(bf16[576,1024]{1,0:T(8,128)(2,1)} %collective-permute-done.1.refs_5_), channel_id=1, source_target_pairs={{1,2},{2,1},{5,6},{6,5},{9,10},{10,9},{13,14},{14,13},{17,18},{18,... | collective-permute-start | bytes 3538952 | tf_op jit(solution)/shard_map/ppermute | solution.py:340
  60.7 81.1 %collective-permute-start.5 = (bf16[576,1024]{1,0:T(8,128)(2,1)}, bf16[576,1024]{1,0:T(8,128)(2,1)}, u32[]{:S(2)}, u32[]{:S(2)}) collective-permute-start(bf16[576,1024]{1,0:T(8,128)(2,1)} %collective-permute-done.4.refs_5_), channel_id=1, source_target_pairs={{1,0},{2,3},{5,4},{6,7},{9,8},{10,11},{13,12},{14,15},{17,16},{18,... | collective-permute-start | bytes 3538952 | tf_op jit(solution)/shard_map/ppermute | solution.py:343
  70.0 1.0 copy-start.1
  77.1 64.6 %collective-permute-start.10 = (bf16[576,1024]{1,0:T(8,128)(2,1)}, bf16[576,1024]{1,0:T(8,128)(2,1)}, u32[]{:S(2)}, u32[]{:S(2)}) collective-permute-start(bf16[576,1024]{1,0:T(8,128)(2,1)} %collective-permute-done.6.refs_7_), channel_id=1, source_target_pairs={{1,0},{2,3},{5,4},{6,7},{9,8},{10,11},{13,12},{14,15},{17,16},{18,... | collective-permute-start | bytes 3538952 | tf_op jit(solution)/shard_map/ppermute | solution.py:343
  79.5 22.9 %collective-permute-start.11 = (f32[64,576]{0,1:T(8,128)S(1)}, f32[64,576]{0,1:T(8,128)S(1)}, u32[]{:S(2)}, u32[]{:S(2)}) collective-permute-start(f32[64,576]{0,1:T(8,128)S(1)} %copy.9), channel_id=1, source_target_pairs={{0,1},{3,2},{4,5},{7,6},{8,9},{11,10},{12,13},{15,14},{16,17},{19,... | collective-permute-start | bytes 442376 | tf_op jit(solution)/shard_map/ppermute | solution.py:359
  102.4 9.0 %collective-permute-start.12 = (f32[64,576]{0,1:T(8,128)S(1)}, f32[64,576]{0,1:T(8,128)S(1)}, u32[]{:S(2)}, u32[]{:S(2)}) collective-permute-start(f32[64,576]{0,1:T(8,128)S(1)} %add.33), channel_id=1, source_target_pairs={{1,2},{2,1},{5,6},{6,5},{9,10},{10,9},{13,14},{14,13},{17,18},{18,... | collective-permute-start | bytes 442376 | tf_op jit(solution)/shard_map/ppermute | solution.py:340
  111.4 29.6 %collective-permute-start.13 = (f32[64,576]{0,1:T(8,128)S(1)}, f32[64,576]{0,1:T(8,128)S(1)}, u32[]{:S(2)}, u32[]{:S(2)}) collective-permute-start(f32[64,576]{0,1:T(8,128)S(1)} %add.35), channel_id=1, source_target_pairs={{1,0},{2,3},{5,4},{6,7},{9,8},{10,11},{13,12},{14,15},{17,16},{18,... | collective-permute-start | bytes 442376 | tf_op jit(solution)/shard_map/ppermute | solution.py:343
  114.0 42.5 %copy-start.2 = (bf16[576,512]{1,0:T(8,128)(2,1)}, bf16[576,512]{1,0:T(8,128)(2,1)S(1)}, u32[]{:S(2)}) copy-start(bf16[576,512]{1,0:T(8,128)(2,1)S(1)} %get-tuple-element.33.refs_5_) | copy-start | bytes 1769476
  114.1 42.4 %copy-start.3 = (bf16[576,512]{1,0:T(8,128)(2,1)}, bf16[576,512]{1,0:T(8,128)(2,1)S(1)}, u32[]{:S(2)}) copy-start(bf16[576,512]{1,0:T(8,128)(2,1)S(1)} %get-tuple-element.34.refs_5_) | copy-start | bytes 1769476
  114.1 42.4 %collective-permute-start.15 = (bf16[576,512]{1,0:T(8,128)(2,1)S(1)}, bf16[576,512]{1,0:T(8,128)(2,1)}, u32[]{:S(2)}, u32[]{:S(2)}) collective-permute-start(bf16[576,512]{1,0:T(8,128)(2,1)S(1)} %get-tuple-element.34.refs_5_), channel_id=1, source_target_pairs={{1,0},{2,3},{5,4},{6,7},{9,8},{10,11},{13,12},{14,15},{17,16},{18,... | collective-permute-start | bytes 1769480 | tf_op jit(solution)/shard_map/ppermute | solution.py:343
  115.4 51.0 %collective-permute-start.16 = (bf16[576,512]{1,0:T(8,128)(2,1)S(1)}, bf16[576,512]{1,0:T(8,128)(2,1)}, u32[]{:S(2)}, u32[]{:S(2)}) collective-permute-start(bf16[576,512]{1,0:T(8,128)(2,1)S(1)} %get-tuple-element.33.refs_5_), channel_id=1, source_target_pairs={{1,0},{2,3},{5,4},{6,7},{9,8},{10,11},{13,12},{14,15},{17,16},{18,... | collective-permute-start | bytes 1769480 | tf_op jit(solution)/shard_map/ppermute | solution.py:343

commit v10 on v9

--- a/solution.py
+++ b/solution.py
@@ -10,6 +10,8 @@
 adapter_scale = 2.0
 live_total = 576
 column_tile = 512
+strip_width = 256
+pack_strip = 512
 vmem_bytes = 62 * 1024 * 1024
 bf16, f32, i32 = jnp.bfloat16, jnp.float32, jnp.int32
 
@@ -44,40 +46,53 @@
 def prepare_kernel(
     variants, slots, live, x, down, up, packed, *rest, steps, replicas, capacity, blocks
 ):
-    picked, sems = rest[:-1], rest[-1]
+    picked, hot, sems = rest[:-2], rest[-2], rest[-1]
     pool, rank = down.shape[0], down.shape[1]
-    me = lax.axis_index("dp")
-    copies = []
-    for step, place in zip(steps, picked):
-        target = lax.rem(me + step, replicas)
-        seen = jnp.int32(0)
-        index = [jnp.int32(0)] * capacity
-        for b in range(blocks):
-            slot = slots[variants[target, b]]
-            owner = lax.div(slot, pool)
-            mine = owner == me
+
+    def copies():
+        me = lax.axis_index("dp")
+        made = []
+        for step, place in zip(steps, picked):
+            target = lax.rem(me + step, replicas)
+            seen = jnp.int32(0)
+            index = [jnp.int32(0)] * capacity
+            for b in range(blocks):
+                slot = slots[variants[target, b]]
+                owner = lax.div(slot, pool)
+                mine = owner == me
+                for m in range(capacity):
+                    index[m] = jnp.where(mine & (seen == m), slot - owner * pool, index[m])
+                seen = seen + mine.astype(i32)
             for m in range(capacity):
-                index[m] = jnp.where(mine & (seen == m), slot - owner * pool, index[m])
-            seen = seen + mine.astype(i32)
-        for m in range(capacity):
-            for kind, pooled in enumerate((down, up)):
-                copies.append(
-                    pltpu.make_async_copy(
-                        pooled.at[index[m]],
-                        place.at[kind, m * rank : (m + 1) * rank],
-                        sems.at[len(copies)],
+                for kind, pooled in enumerate((down, up)):
+                    made.append(
+                        pltpu.make_async_copy(
+                            pooled.at[index[m]],
+                            place.at[kind, m * rank : (m + 1) * rank],
+                            sems.at[len(made)],
+                        )
                     )
-                )
-                copies[-1].start()
-    hot = one_hot(live, x.shape[0], 1)
-    packed[...] = jnp.dot(hot, x[...], preferred_element_type=f32).astype(bf16)
-    for copy in copies:
-        copy.wait()
+        return made
+
+    @pl.when(pl.program_id(0) == 0)
+    def _():
+        for copy in copies():
+            copy.start()
+        hot[...] = one_hot(live, x.shape[0], 1)
+
+    packed[...] = jnp.dot(hot[...], x[...], preferred_element_type=f32).astype(bf16)
+
+    @pl.when(pl.program_id(0) == pl.num_programs(0) - 1)
+    def _():
+        for copy in copies():
+            copy.wait()
 
 
 def prepare(ints, hidden, down, up, part, parts, steps, replicas, capacity):
     rows, features = hidden.shape
     width = features // parts
+    strip = min(pack_strip, width)
+    strips = width // strip
     depth = capacity * down.shape[1]
     outs = [jax.ShapeDtypeStruct((live_total, width), bf16)]
     outs += [jax.ShapeDtypeStruct((2, depth, features), bf16)] * len(steps)
@@ -89,11 +104,15 @@
             capacity=capacity,
             blocks=ints[0].shape[1],
         ),
-        grid=(1,),
-        in_specs=[smem] * 3 + [pl.BlockSpec((rows, width), lambda i: (0, part)), hbm, hbm],
-        out_specs=[pl.BlockSpec(o.shape, lambda i, r=len(o.shape): (0,) * r) for o in outs],
+        grid=(strips,),
+        in_specs=[smem] * 3 + [pl.BlockSpec((rows, strip), lambda i: (0, part * strips + i)), hbm, hbm],
+        out_specs=[pl.BlockSpec((live_total, strip), lambda i: (0, i))]
+        + [pl.BlockSpec(o.shape, lambda i: (0, 0, 0)) for o in outs[1:]],
         out_shape=outs,
-        scratch_shapes=[pltpu.SemaphoreType.DMA((len(steps) * capacity * 2,))],
+        scratch_shapes=[
+            pltpu.VMEM((live_total, rows), bf16),
+            pltpu.SemaphoreType.DMA((len(steps) * capacity * 2,)),
+        ],
         compiler_params=params(),
         cost_estimate=cost(),
         name="prepare",
@@ -196,24 +215,32 @@
                     mine = jnp.where(group == o * capacity + nth, wide, 0.0)
                     spread[:, o * depth : (o + 1) * depth] = mine.astype(bf16)
 
-    def product(s):
+    def product(s, columns):
         x = xs[s][0][...]
         for other in xs[s][1:]:
             x = x + other[...]
-        return jnp.dot(x, ws[s][...], preferred_element_type=f32)
-
-    value = total[...] if has_total else None
-    for s in range(len(groups)):
-        value = product(s) if value is None else value + product(s)
-    if delta:
-        depth = ups[0].shape[1]
-        for o in range(replicas):
-            value = value + jnp.dot(
-                spread[:, o * depth : (o + 1) * depth], ups[o][0], preferred_element_type=f32
-            )
-    if last:
-        value = jnp.dot(hot[...], value.astype(bf16), preferred_element_type=f32)
-    out[...] = value.astype(out.dtype)
+        return jnp.dot(x, ws[s][:, columns], preferred_element_type=f32)
+
+    def work(columns):
+        value = total[:, columns] if has_total else None
+        for s in range(len(groups)):
+            value = product(s, columns) if value is None else value + product(s, columns)
+        if delta:
+            depth = ups[0].shape[1]
+            for o in range(replicas):
+                value = value + jnp.dot(
+                    spread[:, o * depth : (o + 1) * depth],
+                    ups[o][0, :, columns],
+                    preferred_element_type=f32,
+                )
+        if last:
+            value = jnp.dot(hot[...], value.astype(bf16), preferred_element_type=f32)
+        out[:, columns] = value.astype(out.dtype)
+
+    width = out.shape[1]
+    strip = min(strip_width, width) if last else width
+    for start in range(0, width, strip):
+        work(slice(start, start + strip))
 
 
 def project(meta, ints, total, xs, weight, sizes, low=None, factors=None, rows=None, flops=1):

time: 176 us -> 176 us (level)
  no operation moved by 1% of the time
where the time goes in v10:
time: 176 us; the launch traced here: 174 us
  Pallas kernels  80 us (45%)
  waiting for transfers between devices  49.3 us (28%)
  starting transfers between devices  39.4 us (22%)
  local copies, waits for them, and re-layouts  3.36 us (2%)
  other arithmetic  2.12 us (1%)
    pallas_call x7, Pallas kernels, project(): pl.pallas_call(functools.partial(project_kernel, groups=tuple((len(g) for...  64.4 us
    ppermute x6, waiting for transfers between devices, outward(): return lax.ppermute(x, 'tensor', [(1, 0), (2, 3)])  26.9 us
    ppermute x1, starting transfers between devices, shards(): inward = lax.ppermute(partial, 'tensor', [(0, 1), (3, 2)])  15.6 us
    ppermute x2, waiting for transfers between devices, pairs(): return lax.ppermute(x, 'tensor', [(0, 1), (1, 0), (2, 3), (3, 2)])  10.4 us
    pallas_call x2, Pallas kernels, prepare(): pl.pallas_call(functools.partial(prepare_kernel, steps=steps, replicas=re...  9.38 us
    ppermute x6, starting transfers between devices, outward(): return lax.ppermute(x, 'tensor', [(1, 0), (2, 3)])  7.72 us
    ppermute x5, starting transfers between devices, middle(): return lax.ppermute(x, 'tensor', [(1, 2), (2, 1)])  7.48 us
    ppermute x1, waiting for transfers between devices, shards(): inward = lax.ppermute(partial, 'tensor', [(0, 1), (3, 2)])  7.23 us
  transfers between devices with their start and end apart: 17, of which 6 were waited for; matrix products, arithmetic and copies ran while one was open for 3% of the time, Pallas kernels for 39%

profile of v10, /device:TPU:0, one launch (start us, length us, event | category | flops | bytes accessed | tf_op | source)
XLA Modules:
  0.0 174.4 jit_solution(15520981886227378111)
XLA Ops:
  0.0 3.9 %prepare.2 = (bf16[576,1024]{1,0:T(8,128)(2,1)}, bf16[2,128,2048]{2,1,0:T(8,128)(2,1)}) custom-call(s32[4,6]{1,0:T(4,128)} %refs_1_.13, s32[32]{0:T(128)} %refs_2_.13, s32[1,6]{1,0:T(1,128)} %refs_3_.13, bf16[768,2048]{1,0:T(8,128)(2,1)} %x.3, bf16[8,64,2048]{2,1,0:T(8,128)(2,1)} %down.3, bf16[8,64,2048]{2,1,0:T(8,128)(2,1)} %up.3), custom_call_target="tpu_custom_call" | custom-call | flops 1 | bytes 1 | tf_op jit(solution)/shard_map/prepare/pallas_call | solution.py:99
  3.9 0.5 collective-permute-start.7
  4.4 2.6 %collective-permute-start = (bf16[576,1024]{1,0:T(8,128)(2,1)}, bf16[576,1024]{1,0:T(8,128)(2,1)}, u32[]{:S(2)}, u32[]{:S(2)}) collective-permute-start(bf16[576,1024]{1,0:T(8,128)(2,1)} %get-tuple-element.19.refs_4_.rest_0_), channel_id=1, source_target_pairs={{0,1},{1,0},{2,3},{3,2},{4,5},{5,4},{6,7},{7,6},{8,9},{9,8},{10,11... | collective-permute-start | bytes 3538952 | tf_op jit(solution)/shard_map/ppermute | solution.py:364
  7.0 1.7 collective-permute-start.2
  8.7 5.5 %prepare.3 = (bf16[576,1024]{1,0:T(8,128)(2,1)}, bf16[2,128,2048]{2,1,0:T(8,128)(2,1)}, bf16[2,128,2048]{2,1,0:T(8,128)(2,1)}, bf16[2,128,2048]{2,1,0:T(8,128)(2,1)}) custom-call(s32[4,6]{1,0:T(4,128)} %refs_1_.13, s32[32]{0:T(128)} %refs_2_.13, s32[1,6]{1,0:T(1,128)} %refs_3_.13, bf16[768,2048]{1,0:T(8,128)(2,1)} %x.3, bf16[8,64,2048]{2,1,0:T(8,128)(2,1)} %down.3, ...), custom_call_target="tpu_custom_call" | custom-call | flops 1 | bytes 1 | tf_op jit(solution)/shard_map/prepare/pallas_call | solution.py:99
  14.3 4.7 %collective-permute-done.7.rest_3_.refs_13_ = bf16[2,128,2048]{2,1,0:T(8,128)(2,1)S(1)} collective-permute-done((bf16[2,128,2048]{2,1,0:T(8,128)(2,1)}, bf16[2,128,2048]{2,1,0:T(8,128)(2,1)S(1)}, u32[]{:S(2)}, u32[]{:S(2)}) %collective-permute-start.7) | collective-permute-done | bytes 1048608 | tf_op jit(solution)/shard_map/ppermute | solution.py:342
  19.0 2.3 %collective-permute-start.8 = (bf16[2,128,2048]{2,1,0:T(8,128)(2,1)}, bf16[2,128,2048]{2,1,0:T(8,128)(2,1)}, u32[]{:S(2)}, u32[]{:S(2)}) collective-permute-start(bf16[2,128,2048]{2,1,0:T(8,128)(2,1)} %get-tuple-element.26), channel_id=1, source_target_pairs={{0,8},{4,12},{8,0},{12,4},{1,9},{5,13},{9,1},{13,5},{2,10},{6,14},... | collective-permute-start | bytes 3145736 | tf_op jit(solution)/shard_map/ppermute | solution.py:342
  21.3 1.6 collective-permute-start.1
  22.9 1.7 collective-permute-start.4
  24.6 8.6 %collective-permute-done.refs_5_ = bf16[576,1024]{1,0:T(8,128)(2,1)} collective-permute-done((bf16[576,1024]{1,0:T(8,128)(2,1)}, bf16[576,1024]{1,0:T(8,128)(2,1)}, u32[]{:S(2)}, u32[]{:S(2)}) %collective-permute-start) | collective-permute-done | bytes 1179680 | tf_op jit(solution)/shard_map/ppermute | solution.py:364
  33.2 1.7 collective-permute-start.6
  34.9 0.6 pad_add_fusion.1.refs_0_
  35.5 10.4 %project.7.refs_4_ = f32[576,2048]{1,0:T(8,128)} custom-call(s32[2]{0:T(128)} %pad_add_fusion.1.refs_0_, s32[4,6]{1,0:T(4,128)} %refs_1_.13, s32[32]{0:T(128)} %refs_2_.13, s32[1,6]{1,0:T(1,128)} %refs_3_.13, bf16[576,1024]{1,0:T(8,128)(2,1)} %get-tuple-element.19.refs_4_.rest_0_, bf16[576,1024]{1,0:T(8,128)(2,1)} %get-tuple-element.20.refs_5_.rest_1_, ...), custom_call_target="tpu_custom_call" | custom-call | flops 1 | bytes 1 | tf_op jit(solution)/shard_map/project/pallas_call | solution.py:279
  45.9 0.0 collective-permute-done.8.rest_4_.refs_14_
  46.0 1.6 collective-permute-start.9
  47.5 0.0 collective-permute-done.2.refs_5_
  47.5 1.3 collective-permute-start.3
  48.8 7.9 %project.8.refs_4_ = f32[576,2048]{1,0:T(8,128)} custom-call(s32[1]{0:T(128)} %bitcast.6.refs_0_, s32[4,6]{1,0:T(4,128)} %refs_1_.13, s32[32]{0:T(128)} %refs_2_.13, s32[1,6]{1,0:T(1,128)} %refs_3_.13, f32[576,2048]{1,0:T(8,128)} %project.7.refs_4_, bf16[576,1024]{1,0:T(8,128)(2,1)} %collective-permute-done.refs_5_, bf16[8192,2048]{1,0:T(8,128)(2,1)} %refs_7_.7), custom_call_target="tpu_custom_call" | custom-call | flops 1 | bytes 1 | tf_op jit(solution)/shard_map/project/pallas_call | solution.py:279
  56.7 1.7 %collective-permute-done.1.refs_5_ = bf16[576,1024]{1,0:T(8,128)(2,1)} collective-permute-done((bf16[576,1024]{1,0:T(8,128)(2,1)}, bf16[576,1024]{1,0:T(8,128)(2,1)}, u32[]{:S(2)}, u32[]{:S(2)}) %collective-permute-start.1) | collective-permute-done | bytes 1179680 | tf_op jit(solution)/shard_map/ppermute | solution.py:364
  58.5 1.7 collective-permute-start.14
  60.2 0.0 collective-permute-done.4.refs_5_
  60.2 1.3 collective-permute-start.5
  61.5 8.0 %project.9.refs_4_ = f32[576,2048]{1,0:T(8,128)} custom-call(s32[1]{0:T(128)} %bitcast.5.refs_0_, s32[4,6]{1,0:T(4,128)} %refs_1_.13, s32[32]{0:T(128)} %refs_2_.13, s32[1,6]{1,0:T(1,128)} %refs_3_.13, f32[576,2048]{1,0:T(8,128)} %project.8.refs_4_, bf16[576,1024]{1,0:T(8,128)(2,1)} %collective-permute-done.1.refs_5_, bf16[8192,2048]{1,0:T(8,128)(2,1)} %refs_7_.7), custom_call_target="tpu_custom_call" | custom-call | flops 1 | bytes 1 | tf_op jit(solution)/shard_map/project/pallas_call | solution.py:279
  69.4 1.0 copy-done.1
  70.4 6.2 %shrink.1 = f32[64,576]{1,0:T(8,128)} custom-call(s32[4,6]{1,0:T(4,128)} %refs_1_.13, s32[32]{0:T(128)} %refs_2_.13, s32[1,6]{1,0:T(1,128)} %refs_3_.13, bf16[576,1024]{1,0:T(8,128)(2,1)} %get-tuple-element.19.refs_4_.rest_0_, bf16[576,1024]{1,0:T(8,128)(2,1)} %get-tuple-element.20.refs_5_.rest_1_, bf16[2,128,2048]{2,1,0:T(8,128)(2,1)} %get-tuple-element.23.rest_2_.refs_12_, ...), custom_call_target="tpu_custom_call" | custom-call | flops 1 | bytes 1 | tf_op jit(solution)/shard_map/shrink/pallas_call | solution.py:173
  76.6 0.0 collective-permute-done.6.refs_7_
  76.6 1.3 collective-permute-start.10
  77.9 1.1 copy.9
  78.9 15.6 %collective-permute-start.11 = (f32[64,576]{0,1:T(8,128)S(1)}, f32[64,576]{0,1:T(8,128)S(1)}, u32[]{:S(2)}, u32[]{:S(2)}) collective-permute-start(f32[64,576]{0,1:T(8,128)S(1)} %copy.9), channel_id=1, source_target_pairs={{0,1},{3,2},{4,5},{7,6},{8,9},{11,10},{12,13},{15,14},{16,17},{19,... | collective-permute-start | bytes 442376 | tf_op jit(solution)/shard_map/ppermute | solution.py:386
  94.6 7.2 %collective-permute-done.11 = f32[64,576]{0,1:T(8,128)S(1)} collective-permute-done((f32[64,576]{0,1:T(8,128)S(1)}, f32[64,576]{0,1:T(8,128)S(1)}, u32[]{:S(2)}, u32[]{:S(2)}) %collective-permute-start.11) | collective-permute-done | bytes 147488 | tf_op jit(solution)/shard_map/ppermute | solution.py:386
  101.8 0.7 collective-permute-start.12
  102.5 0.0 collective-permute-done.3.refs_6_
  102.5 8.3 %project.10.refs_4_ = f32[576,2048]{1,0:T(8,128)} custom-call(s32[1]{0:T(128)} %bitcast.4.refs_0_, s32[4,6]{1,0:T(4,128)} %refs_1_.13, s32[32]{0:T(128)} %refs_2_.13, s32[1,6]{1,0:T(1,128)} %refs_3_.13, f32[576,2048]{1,0:T(8,128)} %project.9.refs_4_, bf16[576,1024]{1,0:T(8,128)(2,1)} %collective-permute-done.2.refs_5_, ...), custom_call_target="tpu_custom_call" | custom-call | flops 3449999872 | bytes 1 | tf_op jit(solution)/shard_map/project/pallas_call | solution.py:279
  110.8 0.0 collective-permute-done.12
  110.9 1.3 collective-permute-start.13
  112.2 0.0 collective-permute-done.14
  112.2 1.3 fusion
  113.5 0.0 copy-start.3
  113.5 1.3 collective-permute-start.15
  114.8 1.3 collective-permute-start.16
  116.1 0.7 pad_add_fusion.refs_0_
  116.8 23.7 %collective-permute-done.13 = f32[64,576]{0,1:T(8,128)S(1)} collective-permute-done((f32[64,576]{0,1:T(8,128)S(1)}, f32[64,576]{0,1:T(8,128)S(1)}, u32[]{:S(2)}, u32[]{:S(2)}) %collective-permute-start.13) | collective-permute-done | bytes 147488 | tf_op jit(solution)/shard_map/ppermute | solution.py:370
  140.5 0.7 convert_bitcast_fusion.refs_11_
  141.2 14.7 %project.11.refs_4_ = f32[576,2048]{1,0:T(8,128)} custom-call(s32[2]{0:T(128)} %pad_add_fusion.refs_0_, s32[4,6]{1,0:T(4,128)} %refs_1_.13, s32[32]{0:T(128)} %refs_2_.13, s32[1,6]{1,0:T(1,128)} %refs_3_.13, f32[576,2048]{1,0:T(8,128)} %project.10.refs_4_, bf16[576,1024]{1,0:T(8,128)(2,1)} %collective-permute-done.4.refs_5_, ...), custom_call_target="tpu_custom_call" | custom-call | flops 2300000000 | bytes 1 | tf_op jit(solution)/shard_map/project/pallas_call | solution.py:279
  156.0 0.0 collective-permute-done.15.refs_6_
  156.0 6.6 %project.12.refs_4_ = f32[576,2048]{1,0:T(8,128)} custom-call(s32[1]{0:T(128)} %bitcast.1.refs_0_, s32[4,6]{1,0:T(4,128)} %refs_1_.13, s32[32]{0:T(128)} %refs_2_.13, s32[1,6]{1,0:T(1,128)} %refs_3_.13, f32[576,2048]{1,0:T(8,128)} %project.11.refs_4_, bf16[576,512]{1,0:T(8,128)(2,1)} %copy-done.3, bf16[576,512]{1,0:T(8,128)(2,1)} %collective-permute-done.15.refs_6_, ...), custom_call_target="tpu_custom_call" | custom-call | flops 1150000000 | bytes 1 | tf_op jit(solution)/shard_map/project/pallas_call | solution.py:279
  162.6 3.2 %collective-permute-done.16.refs_6_ = bf16[576,512]{1,0:T(8,128)(2,1)} collective-permute-done((bf16[576,512]{1,0:T(8,128)(2,1)S(1)}, bf16[576,512]{1,0:T(8,128)(2,1)}, u32[]{:S(2)}, u32[]{:S(2)}) %collective-permute-start.16) | collective-permute-done | bytes 589856 | tf_op jit(solution)/shard_map/ppermute | solution.py:370
  165.9 8.5 %project.13 = bf16[768,2048]{1,0:T(8,128)(2,1)} custom-call(s32[1]{0:T(128)} %bitcast.refs_0_, s32[4,6]{1,0:T(4,128)} %refs_1_.13, s32[32]{0:T(128)} %refs_2_.13, s32[1,6]{1,0:T(1,128)} %refs_3_.13, f32[576,2048]{1,0:T(8,128)} %project.12.refs_4_, bf16[576,512]{1,0:T(8,128)(2,1)} %copy-done.2, bf16[576,512]{1,0:T(8,128)(2,1)} %collective-permute-done.16.refs_6_, ...), custom_call_target="tpu_custom_call" | custom-call | flops 1 | bytes 1 | tf_op jit(solution)/shard_map/project/pallas_call | solution.py:279
  (11 shorter events, 0.1 us)
Async XLA Ops:
  3.9 15.1 %collective-permute-start.7 = (bf16[2,128,2048]{2,1,0:T(8,128)(2,1)}, bf16[2,128,2048]{2,1,0:T(8,128)(2,1)S(1)}, u32[]{:S(2)}, u32[]{:S(2)}) collective-permute-start(bf16[2,128,2048]{2,1,0:T(8,128)(2,1)} %get-tuple-element.24), channel_id=1, source_target_pairs={{0,4},{4,8},{8,12},{12,0},{1,5},{5,9},{9,13},{13,1},{2,6},{6,10},{... | collective-permute-start | bytes 3145736 | tf_op jit(solution)/shard_map/ppermute | solution.py:342
  4.4 28.8 %collective-permute-start = (bf16[576,1024]{1,0:T(8,128)(2,1)}, bf16[576,1024]{1,0:T(8,128)(2,1)}, u32[]{:S(2)}, u32[]{:S(2)}) collective-permute-start(bf16[576,1024]{1,0:T(8,128)(2,1)} %get-tuple-element.19.refs_4_.rest_0_), channel_id=1, source_target_pairs={{0,1},{1,0},{2,3},{3,2},{4,5},{5,4},{6,7},{7,6},{8,9},{9,8},{10,11... | collective-permute-start | bytes 3538952 | tf_op jit(solution)/shard_map/ppermute | solution.py:364
  7.0 40.5 %collective-permute-start.2 = (bf16[576,1024]{1,0:T(8,128)(2,1)}, bf16[576,1024]{1,0:T(8,128)(2,1)}, u32[]{:S(2)}, u32[]{:S(2)}) collective-permute-start(bf16[576,1024]{1,0:T(8,128)(2,1)} %get-tuple-element.19.refs_4_.rest_0_), channel_id=1, source_target_pairs={{1,2},{2,1},{5,6},{6,5},{9,10},{10,9},{13,14},{14,13},{17,18},{18,... | collective-permute-start | bytes 3538952 | tf_op jit(solution)/shard_map/ppermute | solution.py:367
  19.0 27.0 %copy-start = (bf16[2,128,2048]{2,1,0:T(8,128)(2,1)}, bf16[2,128,2048]{2,1,0:T(8,128)(2,1)S(1)}, u32[]{:S(2)}) copy-start(bf16[2,128,2048]{2,1,0:T(8,128)(2,1)S(1)} %collective-permute-done.7.rest_3_.refs_13_) | copy-start | bytes 3145732
  19.0 27.0 %collective-permute-start.8 = (bf16[2,128,2048]{2,1,0:T(8,128)(2,1)}, bf16[2,128,2048]{2,1,0:T(8,128)(2,1)}, u32[]{:S(2)}, u32[]{:S(2)}) collective-permute-start(bf16[2,128,2048]{2,1,0:T(8,128)(2,1)} %get-tuple-element.26), channel_id=1, source_target_pairs={{0,8},{4,12},{8,0},{12,4},{1,9},{5,13},{9,1},{13,5},{2,10},{6,14},... | collective-permute-start | bytes 3145736 | tf_op jit(solution)/shard_map/ppermute | solution.py:342
  21.3 37.2 %collective-permute-start.1 = (bf16[576,1024]{1,0:T(8,128)(2,1)}, bf16[576,1024]{1,0:T(8,128)(2,1)}, u32[]{:S(2)}, u32[]{:S(2)}) collective-permute-start(bf16[576,1024]{1,0:T(8,128)(2,1)} %get-tuple-element.20.refs_5_.rest_1_), channel_id=1, source_target_pairs={{0,1},{1,0},{2,3},{3,2},{4,5},{5,4},{6,7},{7,6},{8,9},{9,8},{10,11... | collective-permute-start | bytes 3538952 | tf_op jit(solution)/shard_map/ppermute | solution.py:364
  22.9 37.3 %collective-permute-start.4 = (bf16[576,1024]{1,0:T(8,128)(2,1)}, bf16[576,1024]{1,0:T(8,128)(2,1)}, u32[]{:S(2)}, u32[]{:S(2)}) collective-permute-start(bf16[576,1024]{1,0:T(8,128)(2,1)} %get-tuple-element.20.refs_5_.rest_1_), channel_id=1, source_target_pairs={{1,2},{2,1},{5,6},{6,5},{9,10},{10,9},{13,14},{14,13},{17,18},{18,... | collective-permute-start | bytes 3538952 | tf_op jit(solution)/shard_map/ppermute | solution.py:367
  33.2 43.4 %collective-permute-start.6 = (bf16[576,1024]{1,0:T(8,128)(2,1)}, bf16[576,1024]{1,0:T(8,128)(2,1)}, u32[]{:S(2)}, u32[]{:S(2)}) collective-permute-start(bf16[576,1024]{1,0:T(8,128)(2,1)} %collective-permute-done.refs_5_), channel_id=1, source_target_pairs={{1,2},{2,1},{5,6},{6,5},{9,10},{10,9},{13,14},{14,13},{17,18},{18,... | collective-permute-start | bytes 3538952 | tf_op jit(solution)/shard_map/ppermute | solution.py:367
  46.0 23.5 %collective-permute-start.9 = (bf16[2,128,2048]{2,1,0:T(8,128)(2,1)}, bf16[2,128,2048]{2,1,0:T(8,128)(2,1)S(1)}, u32[]{:S(2)}, u32[]{:S(2)}) collective-permute-start(bf16[2,128,2048]{2,1,0:T(8,128)(2,1)} %get-tuple-element.28), channel_id=1, source_target_pairs={{0,12},{4,0},{8,4},{12,8},{1,13},{5,1},{9,5},{13,9},{2,14},{6,2},{... | collective-permute-start | bytes 3145736 | tf_op jit(solution)/shard_map/ppermute | solution.py:342
  47.5 55.0 %collective-permute-start.3 = (bf16[576,1024]{1,0:T(8,128)(2,1)}, bf16[576,1024]{1,0:T(8,128)(2,1)}, u32[]{:S(2)}, u32[]{:S(2)}) collective-permute-start(bf16[576,1024]{1,0:T(8,128)(2,1)} %collective-permute-done.2.refs_5_), channel_id=1, source_target_pairs={{1,0},{2,3},{5,4},{6,7},{9,8},{10,11},{13,12},{14,15},{17,16},{18,... | collective-permute-start | bytes 3538952 | tf_op jit(solution)/shard_map/ppermute | solution.py:370
  58.5 53.7 %collective-permute-start.14 = (bf16[576,1024]{1,0:T(8,128)(2,1)}, bf16[576,1024]{1,0:T(8,128)(2,1)}, u32[]{:S(2)}, u32[]{:S(2)}) collective-permute-start(bf16[576,1024]{1,0:T(8,128)(2,1)} %collective-permute-done.1.refs_5_), channel_id=1, source_target_pairs={{1,2},{2,1},{5,6},{6,5},{9,10},{10,9},{13,14},{14,13},{17,18},{18,... | collective-permute-start | bytes 3538952 | tf_op jit(solution)/shard_map/ppermute | solution.py:367
  60.2 81.1 %collective-permute-start.5 = (bf16[576,1024]{1,0:T(8,128)(2,1)}, bf16[576,1024]{1,0:T(8,128)(2,1)}, u32[]{:S(2)}, u32[]{:S(2)}) collective-permute-start(bf16[576,1024]{1,0:T(8,128)(2,1)} %collective-permute-done.4.refs_5_), channel_id=1, source_target_pairs={{1,0},{2,3},{5,4},{6,7},{9,8},{10,11},{13,12},{14,15},{17,16},{18,... | collective-permute-start | bytes 3538952 | tf_op jit(solution)/shard_map/ppermute | solution.py:370
  69.4 1.0 copy-start.1
  76.6 64.6 %collective-permute-start.10 = (bf16[576,1024]{1,0:T(8,128)(2,1)}, bf16[576,1024]{1,0:T(8,128)(2,1)}, u32[]{:S(2)}, u32[]{:S(2)}) collective-permute-start(bf16[576,1024]{1,0:T(8,128)(2,1)} %collective-permute-done.6.refs_7_), channel_id=1, source_target_pairs={{1,0},{2,3},{5,4},{6,7},{9,8},{10,11},{13,12},{14,15},{17,16},{18,... | collective-permute-start | bytes 3538952 | tf_op jit(solution)/shard_map/ppermute | solution.py:370
  78.9 22.8 %collective-permute-start.11 = (f32[64,576]{0,1:T(8,128)S(1)}, f32[64,576]{0,1:T(8,128)S(1)}, u32[]{:S(2)}, u32[]{:S(2)}) collective-permute-start(f32[64,576]{0,1:T(8,128)S(1)} %copy.9), channel_id=1, source_target_pairs={{0,1},{3,2},{4,5},{7,6},{8,9},{11,10},{12,13},{15,14},{16,17},{19,... | collective-permute-start | bytes 442376 | tf_op jit(solution)/shard_map/ppermute | solution.py:386
  101.8 9.0 %collective-permute-start.12 = (f32[64,576]{0,1:T(8,128)S(1)}, f32[64,576]{0,1:T(8,128)S(1)}, u32[]{:S(2)}, u32[]{:S(2)}) collective-permute-start(f32[64,576]{0,1:T(8,128)S(1)} %add.33), channel_id=1, source_target_pairs={{1,2},{2,1},{5,6},{6,5},{9,10},{10,9},{13,14},{14,13},{17,18},{18,... | collective-permute-start | bytes 442376 | tf_op jit(solution)/shard_map/ppermute | solution.py:367
  110.9 29.6 %collective-permute-start.13 = (f32[64,576]{0,1:T(8,128)S(1)}, f32[64,576]{0,1:T(8,128)S(1)}, u32[]{:S(2)}, u32[]{:S(2)}) collective-permute-start(f32[64,576]{0,1:T(8,128)S(1)} %add.35), channel_id=1, source_target_pairs={{1,0},{2,3},{5,4},{6,7},{9,8},{10,11},{13,12},{14,15},{17,16},{18,... | collective-permute-start | bytes 442376 | tf_op jit(solution)/shard_map/ppermute | solution.py:370
  113.5 42.5 %copy-start.2 = (bf16[576,512]{1,0:T(8,128)(2,1)}, bf16[576,512]{1,0:T(8,128)(2,1)S(1)}, u32[]{:S(2)}) copy-start(bf16[576,512]{1,0:T(8,128)(2,1)S(1)} %get-tuple-element.33.refs_5_) | copy-start | bytes 1769476
  113.5 42.5 %copy-start.3 = (bf16[576,512]{1,0:T(8,128)(2,1)}, bf16[576,512]{1,0:T(8,128)(2,1)S(1)}, u32[]{:S(2)}) copy-start(bf16[576,512]{1,0:T(8,128)(2,1)S(1)} %get-tuple-element.34.refs_5_) | copy-start | bytes 1769476
  113.5 42.5 %collective-permute-start.15 = (bf16[576,512]{1,0:T(8,128)(2,1)S(1)}, bf16[576,512]{1,0:T(8,128)(2,1)}, u32[]{:S(2)}, u32[]{:S(2)}) collective-permute-start(bf16[576,512]{1,0:T(8,128)(2,1)S(1)} %get-tuple-element.34.refs_5_), channel_id=1, source_target_pairs={{1,0},{2,3},{5,4},{6,7},{9,8},{10,11},{13,12},{14,15},{17,16},{18,... | collective-permute-start | bytes 1769480 | tf_op jit(solution)/shard_map/ppermute | solution.py:370
  114.8 51.0 %collective-permute-start.16 = (bf16[576,512]{1,0:T(8,128)(2,1)S(1)}, bf16[576,512]{1,0:T(8,128)(2,1)}, u32[]{:S(2)}, u32[]{:S(2)}) collective-permute-start(bf16[576,512]{1,0:T(8,128)(2,1)S(1)} %get-tuple-element.33.refs_5_), channel_id=1, source_target_pairs={{1,0},{2,3},{5,4},{6,7},{9,8},{10,11},{13,12},{14,15},{17,16},{18,... | collective-permute-start | bytes 1769480 | tf_op jit(solution)/shard_map/ppermute | solution.py:370

commit v11 on v10

--- a/solution.py
+++ b/solution.py
@@ -10,17 +10,15 @@
 adapter_scale = 2.0
 live_total = 576
 column_tile = 512
-strip_width = 256
 pack_strip = 512
-vmem_bytes = 62 * 1024 * 1024
 bf16, f32, i32 = jnp.bfloat16, jnp.float32, jnp.int32
 
 smem = pl.BlockSpec(memory_space=pltpu.SMEM)
 hbm = pl.BlockSpec(memory_space=pl.ANY)
 
 
-def params():
-    return pltpu.CompilerParams(vmem_limit_bytes=vmem_bytes)
+def params(limit=62):
+    return pltpu.CompilerParams(vmem_limit_bytes=limit * 1024 * 1024)
 
 
 def cost(flops=1):
@@ -186,7 +184,7 @@
     )(variants, slots, live, *xs, *factors)
 
 
-def project_kernel(*refs, groups, has_total, delta, last, replicas, capacity, pool):
+def project_kernel(*refs, groups, widths, has_total, delta, last, replicas, capacity, pool):
     refs = list(refs)
     meta, variants, slots, live = refs[:4]
     refs = refs[4:]
@@ -210,15 +208,21 @@
                 shape = (live_total, depth)
                 group = row_groups(variants, slots, live, shape, 0, replicas, capacity, pool)
                 nth = lax.broadcasted_iota(i32, shape, 1) // (depth // capacity)
-                wide = jnp.concatenate([low[...]] * capacity, axis=1) * adapter_scale
+                mine = low[...]
+                rank = mine.shape[1]
+                riding = xs[0][-1]
+                for k in range(widths[0], riding.shape[1], rank):
+                    mine = mine + riding[:, k : k + rank].astype(f32)
+                mine = mine.astype(bf16).astype(f32)
+                wide = jnp.concatenate([mine] * capacity, axis=1) * adapter_scale
                 for o in range(replicas):
                     mine = jnp.where(group == o * capacity + nth, wide, 0.0)
                     spread[:, o * depth : (o + 1) * depth] = mine.astype(bf16)
 
     def product(s, columns):
-        x = xs[s][0][...]
+        x = xs[s][0][:, : widths[s]]
         for other in xs[s][1:]:
-            x = x + other[...]
+            x = x + other[:, : widths[s]]
         return jnp.dot(x, ws[s][:, columns], preferred_element_type=f32)
 
     def work(columns):
@@ -237,13 +241,10 @@
             value = jnp.dot(hot[...], value.astype(bf16), preferred_element_type=f32)
         out[:, columns] = value.astype(out.dtype)
 
-    width = out.shape[1]
-    strip = min(strip_width, width) if last else width
-    for start in range(0, width, strip):
-        work(slice(start, start + strip))
-
-
-def project(meta, ints, total, xs, weight, sizes, low=None, factors=None, rows=None, flops=1):
+    work(slice(0, out.shape[1]))
+
+
+def project(meta, ints, total, xs, widths, weight, sizes, low=None, factors=None, rows=None, flops=1, limit=62):
     replicas, capacity, pool = sizes
     columns = weight.shape[1]
     tile = min(column_tile, columns)
@@ -257,7 +258,7 @@
             in_specs.append(pl.BlockSpec(x.shape, lambda i, m: (0, 0)))
             args.append(x)
     for s, group in enumerate(xs):
-        k = group[0].shape[1]
+        k = widths[s]
         in_specs.append(pl.BlockSpec((k, tile), lambda i, m, s=s: (m[s], i)))
         args.append(weight)
     scratch = []
@@ -280,6 +281,7 @@
         functools.partial(
             project_kernel,
             groups=tuple(len(g) for g in xs),
+            widths=widths,
             has_total=total is not None,
             delta=low is not None,
             last=rows is not None,
@@ -295,7 +297,7 @@
             scratch_shapes=scratch,
         ),
         out_shape=out,
-        compiler_params=params(),
+        compiler_params=params(limit),
         cost_estimate=cost(flops),
         name="project",
     )(meta, *args)
@@ -326,9 +328,10 @@
 
     def add(total, items, **more):
         xs = [item[2] for item in items]
-        meta = [item[0] * (width // item[2][0].shape[1]) + item[1] for item in items]
+        widths = tuple(width // item[3] for item in items)
+        meta = [item[0] * item[3] + item[1] for item in items]
         meta = jnp.stack([jnp.asarray(m, i32) for m in meta])
-        return project(meta, ints, total, xs, query_weight, sizes, **more)
+        return project(meta, ints, total, xs, widths, query_weight, sizes, **more)
 
     pools = (hidden, adapter_down, adapter_up)
     own0, (next_factors,) = prepare(ints, *pools, 0, 2, (1,), replicas, capacity)
@@ -341,7 +344,7 @@
         pairs = [(i, (i + step) % replicas) for i in range(replicas)]
         return lax.ppermute(x, "dp", pairs)
 
-    own_total = add(None, [(place, j, (own[j],)) for j in range(2)])
+    own_total = add(None, [(place, j, (own[j],), 2) for j in range(2)])
     got = [factors[0], send(factors[1], 1)]
     for step in range(2, replicas):
         events = got[-1:] if step < replicas - 1 else [got[-1], own_total]
@@ -350,12 +353,12 @@
     if tensor != 4:
         gathered = [lax.all_gather(x, "tensor", axis=0) for x in own]
         low = lax.psum(shrink(*ints, own, got, capacity, pool), "tensor")
-        low = low.astype(bf16).astype(f32).T
+        low = low.T
         total = own_total
         for step in range(1, tensor):
             device = (place + step) % tensor
             xs = [lax.dynamic_index_in_dim(x, device, 0, keepdims=False) for x in gathered]
-            items = [(device, j, (xs[j],)) for j in range(2)]
+            items = [(device, j, (xs[j],), 2) for j in range(2)]
             more = {"rows": rows, "low": low, "factors": got} if step == tensor - 1 else {}
             total = add(total, items, **more)
         return total
@@ -375,31 +378,34 @@
 
     x1 = [pairs(x) for x in own]
     y1 = [middle(x) for x in own]
-    near_total = add(own_total, [(near, 0, (x1[0],))])
-    total = add(near_total, [(near, 1, (x1[1],))])
-    partial = shrink(*ints[:2], after(ints[2], total), own, got, capacity, pool)
+    near_total = add(own_total, [(near, 0, (x1[0],), 2)])
+    total = add(near_total, [(near, 1, (x1[1],), 2)])
+    partial = shrink(*ints[:2], after(ints[2], total, y1[1]), own, got, capacity, pool)
 
     x2_0, y2_0 = outward(y1[0]), middle(x1[0])
     x2_1, y2_1 = outward(after(y1[1], near_total)), middle(after(x1[1], near_total))
-    total = add(total, [(far, 0, (y1[0], x2_0))], flops=3_450_000_000)
+    total = add(total, [(far, 0, (y1[0], x2_0), 2)], flops=3_450_000_000)
 
     inward = lax.ppermute(partial, "tensor", [(0, 1), (3, 2)])
     across = middle(partial + inward)
     across = after(across, y2_0)
-    hopped = partial + across
-    outer = outward(hopped)
-    low = (partial + inward + across + outer).astype(bf16).astype(f32).T
+    hopped = (partial + across).T
+    low = (partial + inward + across).T
 
     x3_0 = outward(after(y2_0, partial))
     y2_1 = after(y2_1, hopped, total)
     half = piece // 2
-    halves = [y2_1[:, :half], y2_1[:, half:]]
+    upper = hopped.astype(bf16)
+    rest = (hopped - upper.astype(f32)).astype(bf16)
+    first_half = jnp.concatenate([y2_1[:, :half], upper, rest], axis=1)
+    halves = [first_half, after(y2_1, first_half)[:, half:]]
     x3_1 = [outward(h) for h in halves]
 
-    items = [(far, 1, (y1[1], x2_1)), (farthest, 0, (y2_0, x3_0))]
-    total = add(total, items, low=low, factors=got, flops=2_300_000_000)
-    total = add(total, [(farthest, 2, (halves[0], x3_1[0]))], flops=1_150_000_000)
-    return add(total, [(farthest, 3, (halves[1], x3_1[1]))], rows=rows)
+    items = [(far, 1, (y1[1], x2_1), 2), (farthest, 0, (y2_0, x3_0), 2)]
+    total = add(total, items, flops=5_750_000_000)
+    items = [(farthest, 2, (halves[0], x3_1[0]), 4)]
+    total = add(total, items, low=low, factors=got, flops=1_150_000_000, limit=24)
+    return add(total, [(farthest, 3, (halves[1], x3_1[1]), 4)], rows=rows, limit=24)
 
 
 def solution(mesh):

time: 176 us -> 173 us (0.983)
  local copies, waits for them, and re-layouts: 3.36 us -> 10.8 us
  waiting for transfers between devices: 49.3 us -> 42.3 us
  Pallas kernels: 80 us -> 76.7 us
    ppermute x6 -> x5, waiting for transfers between devices: 26.9 us -> 20.4 us  [outward(): return lax.ppermute(x, 'tensor', [(1, 0), (2, 3)])]
    unnamed x8 -> x20, local copies, waits for them, and re-layouts: 0.98 us -> 6.72 us
    pallas_call x7, Pallas kernels: 64.4 us -> 61.3 us  [project(): pl.pallas_call(functools.partial(project_kernel, groups=tuple((len(g) for...]
    ppermute x6 -> x5, starting transfers between devices: 7.72 us -> 6.42 us  [outward(): return lax.ppermute(x, 'tensor', [(1, 0), (2, 3)])]
  transfers between devices with their start and end apart: 17 -> 16, of which waited for: 6 -> 6; matrix products, arithmetic and copies ran while one was open for 3% -> 4% of each run, Pallas kernels for 39% -> 38%
where the time goes in v11:
time: 173 us; the launch traced here: 170 us
  Pallas kernels  76.7 us (44%)
  waiting for transfers between devices  42.3 us (24%)
  starting transfers between devices  38.2 us (22%)
  local copies, waits for them, and re-layouts  10.8 us (6%)
  other arithmetic  2.2 us (1%)
    pallas_call x7, Pallas kernels, project(): pl.pallas_call(functools.partial(project_kernel, groups=tuple((len(g) for...  61.3 us
    ppermute x5, waiting for transfers between devices, outward(): return lax.ppermute(x, 'tensor', [(1, 0), (2, 3)])  20.4 us
    ppermute x1, starting transfers between devices, shards(): inward = lax.ppermute(partial, 'tensor', [(0, 1), (3, 2)])  15.7 us
    ppermute x2, waiting for transfers between devices, pairs(): return lax.ppermute(x, 'tensor', [(0, 1), (1, 0), (2, 3), (3, 2)])  10.4 us
    pallas_call x2, Pallas kernels, prepare(): pl.pallas_call(functools.partial(prepare_kernel, steps=steps, replicas=re...  9.17 us
    ppermute x5, starting transfers between devices, middle(): return lax.ppermute(x, 'tensor', [(1, 2), (2, 1)])  7.46 us
    unnamed x20, local copies, waits for them, and re-layouts  6.72 us
    ppermute x1, waiting for transfers between devices, shards(): inward = lax.ppermute(partial, 'tensor', [(0, 1), (3, 2)])  6.57 us
  transfers between devices with their start and end apart: 16, of which 6 were waited for; matrix products, arithmetic and copies ran while one was open for 4% of the time, Pallas kernels for 38%

profile of v11, /device:TPU:0, one launch (start us, length us, event | category | flops | bytes accessed | tf_op | source)
XLA Modules:
  0.0 170.4 jit_solution(18336185168268415496)
XLA Ops:
  0.0 3.8 %prepare.2 = (bf16[576,1024]{1,0:T(8,128)(2,1)}, bf16[2,128,2048]{2,1,0:T(8,128)(2,1)}) custom-call(s32[4,6]{1,0:T(4,128)} %refs_1_.13, s32[32]{0:T(128)} %refs_2_.13, s32[1,6]{1,0:T(1,128)} %refs_3_.13, bf16[768,2048]{1,0:T(8,128)(2,1)} %x.3, bf16[8,64,2048]{2,1,0:T(8,128)(2,1)} %down.3, bf16[8,64,2048]{2,1,0:T(8,128)(2,1)} %up.3), custom_call_target="tpu_custom_call" | custom-call | flops 1 | bytes 1 | tf_op jit(solution)/shard_map/prepare/pallas_call | solution.py:97
  3.8 0.5 collective-permute-start.7
  4.3 2.6 %collective-permute-start = (bf16[576,1024]{1,0:T(8,128)(2,1)}, bf16[576,1024]{1,0:T(8,128)(2,1)}, u32[]{:S(2)}, u32[]{:S(2)}) collective-permute-start(bf16[576,1024]{1,0:T(8,128)(2,1)} %get-tuple-element.20.refs_4_.rest_0_), channel_id=1, source_target_pairs={{0,1},{1,0},{2,3},{3,2},{4,5},{5,4},{6,7},{7,6},{8,9},{9,8},{10,11... | collective-permute-start | bytes 3538952 | tf_op jit(solution)/shard_map/ppermute | solution.py:367
  7.0 1.7 %collective-permute-start.2 = (bf16[576,1024]{1,0:T(8,128)(2,1)}, bf16[576,1024]{1,0:T(8,128)(2,1)}, u32[]{:S(2)}, u32[]{:S(2)}) collective-permute-start(bf16[576,1024]{1,0:T(8,128)(2,1)} %get-tuple-element.20.refs_4_.rest_0_), channel_id=1, source_target_pairs={{1,2},{2,1},{5,6},{6,5},{9,10},{10,9},{13,14},{14,13},{17,18},{18,... | collective-permute-start | bytes 3538952 | tf_op jit(solution)/shard_map/ppermute | solution.py:370
  8.7 5.3 %prepare.3 = (bf16[576,1024]{1,0:T(8,128)(2,1)}, bf16[2,128,2048]{2,1,0:T(8,128)(2,1)}, bf16[2,128,2048]{2,1,0:T(8,128)(2,1)}, bf16[2,128,2048]{2,1,0:T(8,128)(2,1)}) custom-call(s32[4,6]{1,0:T(4,128)} %refs_1_.13, s32[32]{0:T(128)} %refs_2_.13, s32[1,6]{1,0:T(1,128)} %refs_3_.13, bf16[768,2048]{1,0:T(8,128)(2,1)} %x.3, bf16[8,64,2048]{2,1,0:T(8,128)(2,1)} %down.3, ...), custom_call_target="tpu_custom_call" | custom-call | flops 1 | bytes 1 | tf_op jit(solution)/shard_map/prepare/pallas_call | solution.py:97
  14.1 4.9 %collective-permute-done.7.rest_3_.refs_10_ = bf16[2,128,2048]{2,1,0:T(8,128)(2,1)S(1)} collective-permute-done((bf16[2,128,2048]{2,1,0:T(8,128)(2,1)}, bf16[2,128,2048]{2,1,0:T(8,128)(2,1)S(1)}, u32[]{:S(2)}, u32[]{:S(2)}) %collective-permute-start.7) | collective-permute-done | bytes 1048608 | tf_op jit(solution)/shard_map/ppermute | solution.py:345
  19.0 2.3 %collective-permute-start.8 = (bf16[2,128,2048]{2,1,0:T(8,128)(2,1)}, bf16[2,128,2048]{2,1,0:T(8,128)(2,1)}, u32[]{:S(2)}, u32[]{:S(2)}) collective-permute-start(bf16[2,128,2048]{2,1,0:T(8,128)(2,1)} %get-tuple-element.27), channel_id=1, source_target_pairs={{0,8},{4,12},{8,0},{12,4},{1,9},{5,13},{9,1},{13,5},{2,10},{6,14},... | collective-permute-start | bytes 3145736 | tf_op jit(solution)/shard_map/ppermute | solution.py:345
  21.3 1.6 collective-permute-start.1
  22.8 1.7 collective-permute-start.4
  24.5 8.6 %collective-permute-done.refs_5_ = bf16[576,1024]{1,0:T(8,128)(2,1)} collective-permute-done((bf16[576,1024]{1,0:T(8,128)(2,1)}, bf16[576,1024]{1,0:T(8,128)(2,1)}, u32[]{:S(2)}, u32[]{:S(2)}) %collective-permute-start) | collective-permute-done | bytes 1179680 | tf_op jit(solution)/shard_map/ppermute | solution.py:367
  33.2 1.7 collective-permute-start.6
  34.9 0.6 pad_add_fusion.1.refs_0_
  35.4 10.4 %project.7.refs_4_ = f32[576,2048]{1,0:T(8,128)} custom-call(s32[2]{0:T(128)} %pad_add_fusion.1.refs_0_, s32[4,6]{1,0:T(4,128)} %refs_1_.13, s32[32]{0:T(128)} %refs_2_.13, s32[1,6]{1,0:T(1,128)} %refs_3_.13, bf16[576,1024]{1,0:T(8,128)(2,1)} %get-tuple-element.20.refs_4_.rest_0_, bf16[576,1024]{1,0:T(8,128)(2,1)} %get-tuple-element.21.refs_5_.rest_1_, ...), custom_call_target="tpu_custom_call" | custom-call | flops 1 | bytes 1 | tf_op jit(solution)/shard_map/project/pallas_call | solution.py:280
  45.8 1.6 collective-permute-start.9
  47.4 0.0 collective-permute-done.2.refs_5_
  47.4 1.3 collective-permute-start.3
  48.7 8.0 %project.8.refs_4_ = f32[576,2048]{1,0:T(8,128)} custom-call(s32[1]{0:T(128)} %bitcast.6.refs_0_, s32[4,6]{1,0:T(4,128)} %refs_1_.13, s32[32]{0:T(128)} %refs_2_.13, s32[1,6]{1,0:T(1,128)} %refs_3_.13, f32[576,2048]{1,0:T(8,128)} %project.7.refs_4_, bf16[576,1024]{1,0:T(8,128)(2,1)} %collective-permute-done.refs_5_, bf16[8192,2048]{1,0:T(8,128)(2,1)} %refs_7_.7), custom_call_target="tpu_custom_call" | custom-call | flops 1 | bytes 1 | tf_op jit(solution)/shard_map/project/pallas_call | solution.py:280
  56.7 1.8 %collective-permute-done.1.refs_5_ = bf16[576,1024]{1,0:T(8,128)(2,1)} collective-permute-done((bf16[576,1024]{1,0:T(8,128)(2,1)}, bf16[576,1024]{1,0:T(8,128)(2,1)}, u32[]{:S(2)}, u32[]{:S(2)}) %collective-permute-start.1) | collective-permute-done | bytes 1179680 | tf_op jit(solution)/shard_map/ppermute | solution.py:367
  58.5 1.7 collective-permute-start.11
  60.1 1.3 collective-permute-start.5
  61.4 7.9 %project.9.refs_4_ = f32[576,2048]{1,0:T(8,128)} custom-call(s32[1]{0:T(128)} %bitcast.5.refs_0_, s32[4,6]{1,0:T(4,128)} %refs_1_.13, s32[32]{0:T(128)} %refs_2_.13, s32[1,6]{1,0:T(1,128)} %refs_3_.13, f32[576,2048]{1,0:T(8,128)} %project.8.refs_4_, bf16[576,1024]{1,0:T(8,128)(2,1)} %collective-permute-done.1.refs_5_, bf16[8192,2048]{1,0:T(8,128)(2,1)} %refs_7_.7), custom_call_target="tpu_custom_call" | custom-call | flops 1 | bytes 1 | tf_op jit(solution)/shard_map/project/pallas_call | solution.py:280
  69.3 0.0 collective-permute-done.9.rest_5_.refs_12_
  69.3 1.0 copy-done.4
  70.3 6.2 %shrink.1 = f32[64,576]{1,0:T(8,128)} custom-call(s32[4,6]{1,0:T(4,128)} %refs_1_.13, s32[32]{0:T(128)} %refs_2_.13, s32[1,6]{1,0:T(1,128)} %refs_3_.13, bf16[576,1024]{1,0:T(8,128)(2,1)} %get-tuple-element.20.refs_4_.rest_0_, bf16[576,1024]{1,0:T(8,128)(2,1)} %get-tuple-element.21.refs_5_.rest_1_, bf16[2,128,2048]{2,1,0:T(8,128)(2,1)} %get-tuple-element.24.rest_2_.refs_9_, ...), custom_call_target="tpu_custom_call" | custom-call | flops 1 | bytes 1 | tf_op jit(solution)/shard_map/shrink/pallas_call | solution.py:171
  76.5 1.3 collective-permute-start.10
  77.8 1.1 copy.10
  78.9 15.7 %collective-permute-start.12 = (f32[64,576]{0,1:T(8,128)S(1)}, f32[64,576]{0,1:T(8,128)S(1)}, u32[]{:S(2)}, u32[]{:S(2)}) collective-permute-start(f32[64,576]{0,1:T(8,128)S(1)} %copy.10), channel_id=1, source_target_pairs={{0,1},{3,2},{4,5},{7,6},{8,9},{11,10},{12,13},{15,14},{16,17},{19,... | collective-permute-start | bytes 442376 | tf_op jit(solution)/shard_map/ppermute | solution.py:389
  94.6 0.7 pad_add_fusion.refs_0_
  95.2 6.6 %collective-permute-done.12 = f32[64,576]{0,1:T(8,128)S(1)} collective-permute-done((f32[64,576]{0,1:T(8,128)S(1)}, f32[64,576]{0,1:T(8,128)S(1)}, u32[]{:S(2)}, u32[]{:S(2)}) %collective-permute-start.12) | collective-permute-done | bytes 147488 | tf_op jit(solution)/shard_map/ppermute | solution.py:389
  101.8 0.7 collective-permute-start.13
  102.5 0.0 collective-permute-done.3.refs_6_
  102.5 8.3 %project.10.refs_4_ = f32[576,2048]{1,0:T(8,128)} custom-call(s32[1]{0:T(128)} %bitcast.4.refs_0_, s32[4,6]{1,0:T(4,128)} %refs_1_.13, s32[32]{0:T(128)} %refs_2_.13, s32[1,6]{1,0:T(1,128)} %refs_3_.13, f32[576,2048]{1,0:T(8,128)} %project.9.refs_4_, bf16[576,1024]{1,0:T(8,128)(2,1)} %collective-permute-done.2.refs_5_, ...), custom_call_target="tpu_custom_call" | custom-call | flops 3449999872 | bytes 1 | tf_op jit(solution)/shard_map/project/pallas_call | solution.py:280
  110.9 1.1 slice.6
  112.0 0.1 pad_maximum_fusion.refs_5_
  112.2 1.3 collective-permute-start.14
  113.5 1.9 %slice.7.refs_5_ = bf16[576,512]{1,0:T(8,128)(2,1)} slice(bf16[576,1024]{1,0:T(8,128)(2,1)} %collective-permute-done.11), slice={[0:576], [512:1024]} | slice | bytes 1179648 | tf_op jit(solution)/shard_map/slice | solution.py:401
  115.4 1.3 collective-permute-start.15
  116.7 0.7 add_bitcast_fusion.refs_8_
  117.5 0.0 collective-permute-done.5.refs_6_
  117.5 16.8 %collective-permute-done.10.refs_8_ = bf16[576,1024]{1,0:T(8,128)(2,1)} collective-permute-done((bf16[576,1024]{1,0:T(8,128)(2,1)}, bf16[576,1024]{1,0:T(8,128)(2,1)}, u32[]{:S(2)}, u32[]{:S(2)}) %collective-permute-start.10) | collective-permute-done | bytes 1179680 | tf_op jit(solution)/shard_map/ppermute | solution.py:373
  134.2 12.2 %project.11.refs_4_ = f32[576,2048]{1,0:T(8,128)} custom-call(s32[2]{0:T(128)} %pad_add_fusion.refs_0_, s32[4,6]{1,0:T(4,128)} %refs_1_.13, s32[32]{0:T(128)} %refs_2_.13, s32[1,6]{1,0:T(1,128)} %refs_3_.13, f32[576,2048]{1,0:T(8,128)} %project.10.refs_4_, bf16[576,1024]{1,0:T(8,128)(2,1)} %collective-permute-done.4.refs_5_, ...), custom_call_target="tpu_custom_call" | custom-call | flops 5750000128 | bytes 1 | tf_op jit(solution)/shard_map/project/pallas_call | solution.py:280
  146.4 3.6 %collective-permute-done.14.refs_6_ = bf16[576,640]{1,0:T(8,128)(2,1)} collective-permute-done((bf16[576,640]{1,0:T(8,128)(2,1)S(1)}, bf16[576,640]{1,0:T(8,128)(2,1)}, u32[]{:S(2)}, u32[]{:S(2)}) %collective-permute-start.14) | collective-permute-done | bytes 737312 | tf_op jit(solution)/shard_map/ppermute | solution.py:373
  150.1 2.3 %copy-done = f32[576,2048]{1,0:T(8,128)S(1)} copy-done((f32[576,2048]{1,0:T(8,128)S(1)}, f32[576,2048]{1,0:T(8,128)}, u32[]{:S(2)}) %copy-start) | copy-done | bytes 4718616
  152.4 1.2 copy-done.3
  153.6 1.2 copy-done.5
  154.9 1.0 copy-done.6
  155.8 6.9 %project.12.refs_4_ = f32[576,2048]{1,0:T(8,128)S(1)} custom-call(s32[1]{0:T(128)} %bitcast.1.refs_0_, s32[4,6]{1,0:T(4,128)S(1)} %copy-done.7, s32[32]{0:T(128)S(1)} %copy-done.8, s32[1,6]{1,0:T(1,128)S(1)} %copy-done.9, f32[576,2048]{1,0:T(8,128)S(1)} %copy-done, bf16[576,640]{1,0:T(8,128)(2,1)S(1)} %pad_maximum_fusion.refs_5_, ...), custom_call_target="tpu_custom_call" | custom-call | flops 1150000000 | bytes 1 | tf_op jit(solution)/shard_map/project/pallas_call | solution.py:280
  162.7 7.7 %project.13 = bf16[768,2048]{1,0:T(8,128)(2,1)} custom-call(s32[1]{0:T(128)} %bitcast.refs_0_, s32[4,6]{1,0:T(4,128)S(1)} %copy-done.7, s32[32]{0:T(128)S(1)} %copy-done.8, s32[1,6]{1,0:T(1,128)S(1)} %copy-done.9, f32[576,2048]{1,0:T(8,128)S(1)} %project.12.refs_4_, bf16[576,512]{1,0:T(8,128)(2,1)} %slice.7.refs_5_, ...), custom_call_target="tpu_custom_call" | custom-call | flops 1 | bytes 1 | tf_op jit(solution)/shard_map/project/pallas_call | solution.py:280
  (23 shorter events, 0.1 us)
Async XLA Ops:
  3.8 15.1 %collective-permute-start.7 = (bf16[2,128,2048]{2,1,0:T(8,128)(2,1)}, bf16[2,128,2048]{2,1,0:T(8,128)(2,1)S(1)}, u32[]{:S(2)}, u32[]{:S(2)}) collective-permute-start(bf16[2,128,2048]{2,1,0:T(8,128)(2,1)} %get-tuple-element.25), channel_id=1, source_target_pairs={{0,4},{4,8},{8,12},{12,0},{1,5},{5,9},{9,13},{13,1},{2,6},{6,10},{... | collective-permute-start | bytes 3145736 | tf_op jit(solution)/shard_map/ppermute | solution.py:345
  4.3 28.8 %collective-permute-start = (bf16[576,1024]{1,0:T(8,128)(2,1)}, bf16[576,1024]{1,0:T(8,128)(2,1)}, u32[]{:S(2)}, u32[]{:S(2)}) collective-permute-start(bf16[576,1024]{1,0:T(8,128)(2,1)} %get-tuple-element.20.refs_4_.rest_0_), channel_id=1, source_target_pairs={{0,1},{1,0},{2,3},{3,2},{4,5},{5,4},{6,7},{7,6},{8,9},{9,8},{10,11... | collective-permute-start | bytes 3538952 | tf_op jit(solution)/shard_map/ppermute | solution.py:367
  7.0 40.4 %collective-permute-start.2 = (bf16[576,1024]{1,0:T(8,128)(2,1)}, bf16[576,1024]{1,0:T(8,128)(2,1)}, u32[]{:S(2)}, u32[]{:S(2)}) collective-permute-start(bf16[576,1024]{1,0:T(8,128)(2,1)} %get-tuple-element.20.refs_4_.rest_0_), channel_id=1, source_target_pairs={{1,2},{2,1},{5,6},{6,5},{9,10},{10,9},{13,14},{14,13},{17,18},{18,... | collective-permute-start | bytes 3538952 | tf_op jit(solution)/shard_map/ppermute | solution.py:370
  19.0 26.8 %copy-start.1 = (bf16[2,128,2048]{2,1,0:T(8,128)(2,1)}, bf16[2,128,2048]{2,1,0:T(8,128)(2,1)S(1)}, u32[]{:S(2)}) copy-start(bf16[2,128,2048]{2,1,0:T(8,128)(2,1)S(1)} %collective-permute-done.7.rest_3_.refs_10_) | copy-start | bytes 3145732
  19.0 26.9 %collective-permute-start.8 = (bf16[2,128,2048]{2,1,0:T(8,128)(2,1)}, bf16[2,128,2048]{2,1,0:T(8,128)(2,1)}, u32[]{:S(2)}, u32[]{:S(2)}) collective-permute-start(bf16[2,128,2048]{2,1,0:T(8,128)(2,1)} %get-tuple-element.27), channel_id=1, source_target_pairs={{0,8},{4,12},{8,0},{12,4},{1,9},{5,13},{9,1},{13,5},{2,10},{6,14},... | collective-permute-start | bytes 3145736 | tf_op jit(solution)/shard_map/ppermute | solution.py:345
  21.3 37.2 %collective-permute-start.1 = (bf16[576,1024]{1,0:T(8,128)(2,1)}, bf16[576,1024]{1,0:T(8,128)(2,1)}, u32[]{:S(2)}, u32[]{:S(2)}) collective-permute-start(bf16[576,1024]{1,0:T(8,128)(2,1)} %get-tuple-element.21.refs_5_.rest_1_), channel_id=1, source_target_pairs={{0,1},{1,0},{2,3},{3,2},{4,5},{5,4},{6,7},{7,6},{8,9},{9,8},{10,11... | collective-permute-start | bytes 3538952 | tf_op jit(solution)/shard_map/ppermute | solution.py:367
  22.8 37.3 %collective-permute-start.4 = (bf16[576,1024]{1,0:T(8,128)(2,1)}, bf16[576,1024]{1,0:T(8,128)(2,1)}, u32[]{:S(2)}, u32[]{:S(2)}) collective-permute-start(bf16[576,1024]{1,0:T(8,128)(2,1)} %get-tuple-element.21.refs_5_.rest_1_), channel_id=1, source_target_pairs={{1,2},{2,1},{5,6},{6,5},{9,10},{10,9},{13,14},{14,13},{17,18},{18,... | collective-permute-start | bytes 3538952 | tf_op jit(solution)/shard_map/ppermute | solution.py:370
  33.2 43.3 %collective-permute-start.6 = (bf16[576,1024]{1,0:T(8,128)(2,1)}, bf16[576,1024]{1,0:T(8,128)(2,1)}, u32[]{:S(2)}, u32[]{:S(2)}) collective-permute-start(bf16[576,1024]{1,0:T(8,128)(2,1)} %collective-permute-done.refs_5_), channel_id=1, source_target_pairs={{1,2},{2,1},{5,6},{6,5},{9,10},{10,9},{13,14},{14,13},{17,18},{18,... | collective-permute-start | bytes 3538952 | tf_op jit(solution)/shard_map/ppermute | solution.py:370
  45.8 23.5 %collective-permute-start.9 = (bf16[2,128,2048]{2,1,0:T(8,128)(2,1)}, bf16[2,128,2048]{2,1,0:T(8,128)(2,1)S(1)}, u32[]{:S(2)}, u32[]{:S(2)}) collective-permute-start(bf16[2,128,2048]{2,1,0:T(8,128)(2,1)} %get-tuple-element.29), channel_id=1, source_target_pairs={{0,12},{4,0},{8,4},{12,8},{1,13},{5,1},{9,5},{13,9},{2,14},{6,2},{... | collective-permute-start | bytes 3145736 | tf_op jit(solution)/shard_map/ppermute | solution.py:345
  47.4 55.1 %collective-permute-start.3 = (bf16[576,1024]{1,0:T(8,128)(2,1)}, bf16[576,1024]{1,0:T(8,128)(2,1)}, u32[]{:S(2)}, u32[]{:S(2)}) collective-permute-start(bf16[576,1024]{1,0:T(8,128)(2,1)} %collective-permute-done.2.refs_5_), channel_id=1, source_target_pairs={{1,0},{2,3},{5,4},{6,7},{9,8},{10,11},{13,12},{14,15},{17,16},{18,... | collective-permute-start | bytes 3538952 | tf_op jit(solution)/shard_map/ppermute | solution.py:373
  58.5 52.5 %collective-permute-start.11 = (bf16[576,1024]{1,0:T(8,128)(2,1)}, bf16[576,1024]{1,0:T(8,128)(2,1)}, u32[]{:S(2)}, u32[]{:S(2)}) collective-permute-start(bf16[576,1024]{1,0:T(8,128)(2,1)} %collective-permute-done.1.refs_5_), channel_id=1, source_target_pairs={{1,2},{2,1},{5,6},{6,5},{9,10},{10,9},{13,14},{14,13},{17,18},{18,... | collective-permute-start | bytes 3538952 | tf_op jit(solution)/shard_map/ppermute | solution.py:370
  60.1 57.3 %collective-permute-start.5 = (bf16[576,1024]{1,0:T(8,128)(2,1)}, bf16[576,1024]{1,0:T(8,128)(2,1)}, u32[]{:S(2)}, u32[]{:S(2)}) collective-permute-start(bf16[576,1024]{1,0:T(8,128)(2,1)} %collective-permute-done.4.refs_5_), channel_id=1, source_target_pairs={{1,0},{2,3},{5,4},{6,7},{9,8},{10,11},{13,12},{14,15},{17,16},{18,... | collective-permute-start | bytes 3538952 | tf_op jit(solution)/shard_map/ppermute | solution.py:373
  69.3 1.0 copy-start.4
  76.5 57.7 %collective-permute-start.10 = (bf16[576,1024]{1,0:T(8,128)(2,1)}, bf16[576,1024]{1,0:T(8,128)(2,1)}, u32[]{:S(2)}, u32[]{:S(2)}) collective-permute-start(bf16[576,1024]{1,0:T(8,128)(2,1)} %collective-permute-done.6.refs_7_), channel_id=1, source_target_pairs={{1,0},{2,3},{5,4},{6,7},{9,8},{10,11},{13,12},{14,15},{17,16},{18,... | collective-permute-start | bytes 3538952 | tf_op jit(solution)/shard_map/ppermute | solution.py:373
  78.9 22.9 %collective-permute-start.12 = (f32[64,576]{0,1:T(8,128)S(1)}, f32[64,576]{0,1:T(8,128)S(1)}, u32[]{:S(2)}, u32[]{:S(2)}) collective-permute-start(f32[64,576]{0,1:T(8,128)S(1)} %copy.10), channel_id=1, source_target_pairs={{0,1},{3,2},{4,5},{7,6},{8,9},{11,10},{12,13},{15,14},{16,17},{19,... | collective-permute-start | bytes 442376 | tf_op jit(solution)/shard_map/ppermute | solution.py:389
  101.8 9.0 %collective-permute-start.13 = (f32[64,576]{0,1:T(8,128)S(1)}, f32[64,576]{0,1:T(8,128)S(1)}, u32[]{:S(2)}, u32[]{:S(2)}) collective-permute-start(f32[64,576]{0,1:T(8,128)S(1)} %add.30), channel_id=1, source_target_pairs={{1,2},{2,1},{5,6},{6,5},{9,10},{10,9},{13,14},{14,13},{17,18},{18,... | collective-permute-start | bytes 442376 | tf_op jit(solution)/shard_map/ppermute | solution.py:370
  112.2 37.9 %collective-permute-start.14 = (bf16[576,640]{1,0:T(8,128)(2,1)S(1)}, bf16[576,640]{1,0:T(8,128)(2,1)}, u32[]{:S(2)}, u32[]{:S(2)}) collective-permute-start(bf16[576,640]{1,0:T(8,128)(2,1)S(1)} %pad_maximum_fusion.refs_5_), channel_id=1, source_target_pairs={{1,0},{2,3},{5,4},{6,7},{9,8},{10,11},{13,12},{14,15},{17,16},{18,... | collective-permute-start | bytes 2211848 | tf_op jit(solution)/shard_map/ppermute | solution.py:373
  115.4 47.3 %collective-permute-start.15 = (bf16[576,512]{1,0:T(8,128)(2,1)}, bf16[576,512]{1,0:T(8,128)(2,1)}, u32[]{:S(2)}, u32[]{:S(2)}) collective-permute-start(bf16[576,512]{1,0:T(8,128)(2,1)} %slice.7.refs_5_), channel_id=1, source_target_pairs={{1,0},{2,3},{5,4},{6,7},{9,8},{10,11},{13,12},{14,15},{17,16},{18,... | collective-permute-start | bytes 1769480 | tf_op jit(solution)/shard_map/ppermute | solution.py:373
  117.4 32.6 %copy-start.2 = (bf16[2,128,2048]{2,1,0:T(8,128)(2,1)S(1)}, bf16[2,128,2048]{2,1,0:T(8,128)(2,1)}, u32[]{:S(2)}) copy-start(bf16[2,128,2048]{2,1,0:T(8,128)(2,1)} %copy-done.1) | copy-start | bytes 3145732
  117.4 32.6 %copy-start.7 = (s32[4,6]{1,0:T(4,128)S(1)}, s32[4,6]{1,0:T(4,128)}, u32[]{:S(2)}) copy-start(s32[4,6]{1,0:T(4,128)} %refs_1_.13) | copy-start | bytes 292
  117.4 32.6 %copy-start.8 = (s32[32]{0:T(128)S(1)}, s32[32]{0:T(128)}, u32[]{:S(2)}) copy-start(s32[32]{0:T(128)} %refs_2_.13) | copy-start | bytes 388
  117.4 32.6 %copy-start.9 = (s32[1,6]{1,0:T(1,128)S(1)}, s32[1,6]{1,0:T(1,128)}, u32[]{:S(2)}) copy-start(s32[1,6]{1,0:T(1,128)} %refs_3_.13) | copy-start | bytes 76
  150.1 2.3 %copy-start = (f32[576,2048]{1,0:T(8,128)S(1)}, f32[576,2048]{1,0:T(8,128)}, u32[]{:S(2)}) copy-start(f32[576,2048]{1,0:T(8,128)} %project.11.refs_4_) | copy-start | bytes 14155780
  152.4 1.2 copy-start.3
  153.6 1.2 copy-start.5
  154.9 1.0 copy-start.6

commit v12 on v11

--- a/solution.py
+++ b/solution.py
@@ -395,14 +395,14 @@
     x3_0 = outward(after(y2_0, partial))
     y2_1 = after(y2_1, hopped, total)
     half = piece // 2
-    upper = hopped.astype(bf16)
+    upper = lax.optimization_barrier(hopped.astype(bf16))
     rest = (hopped - upper.astype(f32)).astype(bf16)
     first_half = jnp.concatenate([y2_1[:, :half], upper, rest], axis=1)
     halves = [first_half, after(y2_1, first_half)[:, half:]]
     x3_1 = [outward(h) for h in halves]
 
     items = [(far, 1, (y1[1], x2_1), 2), (farthest, 0, (y2_0, x3_0), 2)]
-    total = add(total, items, flops=5_750_000_000)
+    total = add(total, items, flops=10_350_000_000)
     items = [(farthest, 2, (halves[0], x3_1[0]), 4)]
     total = add(total, items, low=low, factors=got, flops=1_150_000_000, limit=24)
     return add(total, [(farthest, 3, (halves[1], x3_1[1]), 4)], rows=rows, limit=24)

time: 173 us -> 173 us (level)
  no operation moved by 1% of the time
where the time goes in v12:
time: 173 us; the launch traced here: 170 us
  Pallas kernels  76.7 us (44%)
  waiting for transfers between devices  42.1 us (24%)
  starting transfers between devices  38.3 us (22%)
  local copies, waits for them, and re-layouts  10.8 us (6%)
  other arithmetic  2.21 us (1%)
    pallas_call x7, Pallas kernels, project(): pl.pallas_call(functools.partial(project_kernel, groups=tuple((len(g) for...  61.3 us
    ppermute x5, waiting for transfers between devices, outward(): return lax.ppermute(x, 'tensor', [(1, 0), (2, 3)])  20.3 us
    ppermute x1, starting transfers between devices, shards(): inward = lax.ppermute(partial, 'tensor', [(0, 1), (3, 2)])  15.7 us
    ppermute x2, waiting for transfers between devices, pairs(): return lax.ppermute(x, 'tensor', [(0, 1), (1, 0), (2, 3), (3, 2)])  10.4 us
    pallas_call x2, Pallas kernels, prepare(): pl.pallas_call(functools.partial(prepare_kernel, steps=steps, replicas=re...  9.18 us
    ppermute x5, starting transfers between devices, middle(): return lax.ppermute(x, 'tensor', [(1, 2), (2, 1)])  7.46 us
    unnamed x20, local copies, waits for them, and re-layouts  6.72 us
    ppermute x1, waiting for transfers between devices, shards(): inward = lax.ppermute(partial, 'tensor', [(0, 1), (3, 2)])  6.57 us
  transfers between devices with their start and end apart: 16, of which 6 were waited for; matrix products, arithmetic and copies ran while one was open for 4% of the time, Pallas kernels for 38%

profile of v12, /device:TPU:0, one launch (start us, length us, event | category | flops | bytes accessed | tf_op | source)
XLA Modules:
  0.0 170.4 jit_solution(11107052936184287327)
XLA Ops:
  0.0 3.8 %prepare.2 = (bf16[576,1024]{1,0:T(8,128)(2,1)}, bf16[2,128,2048]{2,1,0:T(8,128)(2,1)}) custom-call(s32[4,6]{1,0:T(4,128)} %refs_1_.13, s32[32]{0:T(128)} %refs_2_.13, s32[1,6]{1,0:T(1,128)} %refs_3_.13, bf16[768,2048]{1,0:T(8,128)(2,1)} %x.3, bf16[8,64,2048]{2,1,0:T(8,128)(2,1)} %down.3, bf16[8,64,2048]{2,1,0:T(8,128)(2,1)} %up.3), custom_call_target="tpu_custom_call" | custom-call | flops 1 | bytes 1 | tf_op jit(solution)/shard_map/prepare/pallas_call | solution.py:97
  3.8 0.5 collective-permute-start.7
  4.3 2.6 %collective-permute-start = (bf16[576,1024]{1,0:T(8,128)(2,1)}, bf16[576,1024]{1,0:T(8,128)(2,1)}, u32[]{:S(2)}, u32[]{:S(2)}) collective-permute-start(bf16[576,1024]{1,0:T(8,128)(2,1)} %get-tuple-element.20.refs_4_.rest_0_), channel_id=1, source_target_pairs={{0,1},{1,0},{2,3},{3,2},{4,5},{5,4},{6,7},{7,6},{8,9},{9,8},{10,11... | collective-permute-start | bytes 3538952 | tf_op jit(solution)/shard_map/ppermute | solution.py:367
  7.0 1.7 %collective-permute-start.2 = (bf16[576,1024]{1,0:T(8,128)(2,1)}, bf16[576,1024]{1,0:T(8,128)(2,1)}, u32[]{:S(2)}, u32[]{:S(2)}) collective-permute-start(bf16[576,1024]{1,0:T(8,128)(2,1)} %get-tuple-element.20.refs_4_.rest_0_), channel_id=1, source_target_pairs={{1,2},{2,1},{5,6},{6,5},{9,10},{10,9},{13,14},{14,13},{17,18},{18,... | collective-permute-start | bytes 3538952 | tf_op jit(solution)/shard_map/ppermute | solution.py:370
  8.7 5.4 %prepare.3 = (bf16[576,1024]{1,0:T(8,128)(2,1)}, bf16[2,128,2048]{2,1,0:T(8,128)(2,1)}, bf16[2,128,2048]{2,1,0:T(8,128)(2,1)}, bf16[2,128,2048]{2,1,0:T(8,128)(2,1)}) custom-call(s32[4,6]{1,0:T(4,128)} %refs_1_.13, s32[32]{0:T(128)} %refs_2_.13, s32[1,6]{1,0:T(1,128)} %refs_3_.13, bf16[768,2048]{1,0:T(8,128)(2,1)} %x.3, bf16[8,64,2048]{2,1,0:T(8,128)(2,1)} %down.3, ...), custom_call_target="tpu_custom_call" | custom-call | flops 1 | bytes 1 | tf_op jit(solution)/shard_map/prepare/pallas_call | solution.py:97
  14.1 4.9 %collective-permute-done.7.rest_3_.refs_10_ = bf16[2,128,2048]{2,1,0:T(8,128)(2,1)S(1)} collective-permute-done((bf16[2,128,2048]{2,1,0:T(8,128)(2,1)}, bf16[2,128,2048]{2,1,0:T(8,128)(2,1)S(1)}, u32[]{:S(2)}, u32[]{:S(2)}) %collective-permute-start.7) | collective-permute-done | bytes 1048608 | tf_op jit(solution)/shard_map/ppermute | solution.py:345
  19.0 2.3 %collective-permute-start.8 = (bf16[2,128,2048]{2,1,0:T(8,128)(2,1)}, bf16[2,128,2048]{2,1,0:T(8,128)(2,1)}, u32[]{:S(2)}, u32[]{:S(2)}) collective-permute-start(bf16[2,128,2048]{2,1,0:T(8,128)(2,1)} %get-tuple-element.27), channel_id=1, source_target_pairs={{0,8},{4,12},{8,0},{12,4},{1,9},{5,13},{9,1},{13,5},{2,10},{6,14},... | collective-permute-start | bytes 3145736 | tf_op jit(solution)/shard_map/ppermute | solution.py:345
  21.3 1.6 collective-permute-start.1
  22.8 1.7 collective-permute-start.4
  24.5 8.6 %collective-permute-done.refs_5_ = bf16[576,1024]{1,0:T(8,128)(2,1)} collective-permute-done((bf16[576,1024]{1,0:T(8,128)(2,1)}, bf16[576,1024]{1,0:T(8,128)(2,1)}, u32[]{:S(2)}, u32[]{:S(2)}) %collective-permute-start) | collective-permute-done | bytes 1179680 | tf_op jit(solution)/shard_map/ppermute | solution.py:367
  33.2 1.7 collective-permute-start.6
  34.9 0.6 pad_add_fusion.1.refs_0_
  35.4 10.4 %project.7.refs_4_ = f32[576,2048]{1,0:T(8,128)} custom-call(s32[2]{0:T(128)} %pad_add_fusion.1.refs_0_, s32[4,6]{1,0:T(4,128)} %refs_1_.13, s32[32]{0:T(128)} %refs_2_.13, s32[1,6]{1,0:T(1,128)} %refs_3_.13, bf16[576,1024]{1,0:T(8,128)(2,1)} %get-tuple-element.20.refs_4_.rest_0_, bf16[576,1024]{1,0:T(8,128)(2,1)} %get-tuple-element.21.refs_5_.rest_1_, ...), custom_call_target="tpu_custom_call" | custom-call | flops 1 | bytes 1 | tf_op jit(solution)/shard_map/project/pallas_call | solution.py:280
  45.8 1.6 collective-permute-start.9
  47.4 0.0 collective-permute-done.2.refs_5_
  47.4 1.3 collective-permute-start.3
  48.7 8.0 %project.8.refs_4_ = f32[576,2048]{1,0:T(8,128)} custom-call(s32[1]{0:T(128)} %bitcast.6.refs_0_, s32[4,6]{1,0:T(4,128)} %refs_1_.13, s32[32]{0:T(128)} %refs_2_.13, s32[1,6]{1,0:T(1,128)} %refs_3_.13, f32[576,2048]{1,0:T(8,128)} %project.7.refs_4_, bf16[576,1024]{1,0:T(8,128)(2,1)} %collective-permute-done.refs_5_, bf16[8192,2048]{1,0:T(8,128)(2,1)} %refs_7_.7), custom_call_target="tpu_custom_call" | custom-call | flops 1 | bytes 1 | tf_op jit(solution)/shard_map/project/pallas_call | solution.py:280
  56.7 1.8 %collective-permute-done.1.refs_5_ = bf16[576,1024]{1,0:T(8,128)(2,1)} collective-permute-done((bf16[576,1024]{1,0:T(8,128)(2,1)}, bf16[576,1024]{1,0:T(8,128)(2,1)}, u32[]{:S(2)}, u32[]{:S(2)}) %collective-permute-start.1) | collective-permute-done | bytes 1179680 | tf_op jit(solution)/shard_map/ppermute | solution.py:367
  58.5 1.7 collective-permute-start.11
  60.1 1.3 collective-permute-start.5
  61.4 7.9 %project.9.refs_4_ = f32[576,2048]{1,0:T(8,128)} custom-call(s32[1]{0:T(128)} %bitcast.5.refs_0_, s32[4,6]{1,0:T(4,128)} %refs_1_.13, s32[32]{0:T(128)} %refs_2_.13, s32[1,6]{1,0:T(1,128)} %refs_3_.13, f32[576,2048]{1,0:T(8,128)} %project.8.refs_4_, bf16[576,1024]{1,0:T(8,128)(2,1)} %collective-permute-done.1.refs_5_, bf16[8192,2048]{1,0:T(8,128)(2,1)} %refs_7_.7), custom_call_target="tpu_custom_call" | custom-call | flops 1 | bytes 1 | tf_op jit(solution)/shard_map/project/pallas_call | solution.py:280
  69.3 0.0 collective-permute-done.9.rest_5_.refs_12_
  69.3 1.0 copy-done.4
  70.3 6.2 %shrink.1 = f32[64,576]{1,0:T(8,128)} custom-call(s32[4,6]{1,0:T(4,128)} %refs_1_.13, s32[32]{0:T(128)} %refs_2_.13, s32[1,6]{1,0:T(1,128)} %refs_3_.13, bf16[576,1024]{1,0:T(8,128)(2,1)} %get-tuple-element.20.refs_4_.rest_0_, bf16[576,1024]{1,0:T(8,128)(2,1)} %get-tuple-element.21.refs_5_.rest_1_, bf16[2,128,2048]{2,1,0:T(8,128)(2,1)} %get-tuple-element.24.rest_2_.refs_9_, ...), custom_call_target="tpu_custom_call" | custom-call | flops 1 | bytes 1 | tf_op jit(solution)/shard_map/shrink/pallas_call | solution.py:171
  76.5 1.3 collective-permute-start.10
  77.8 1.1 copy.10
  78.9 15.7 %collective-permute-start.12 = (f32[64,576]{0,1:T(8,128)S(1)}, f32[64,576]{0,1:T(8,128)S(1)}, u32[]{:S(2)}, u32[]{:S(2)}) collective-permute-start(f32[64,576]{0,1:T(8,128)S(1)} %copy.10), channel_id=1, source_target_pairs={{0,1},{3,2},{4,5},{7,6},{8,9},{11,10},{12,13},{15,14},{16,17},{19,... | collective-permute-start | bytes 442376 | tf_op jit(solution)/shard_map/ppermute | solution.py:389
  94.6 0.7 pad_add_fusion.refs_0_
  95.2 6.6 %collective-permute-done.12 = f32[64,576]{0,1:T(8,128)S(1)} collective-permute-done((f32[64,576]{0,1:T(8,128)S(1)}, f32[64,576]{0,1:T(8,128)S(1)}, u32[]{:S(2)}, u32[]{:S(2)}) %collective-permute-start.12) | collective-permute-done | bytes 147488 | tf_op jit(solution)/shard_map/ppermute | solution.py:389
  101.8 0.7 collective-permute-start.13
  102.5 0.0 collective-permute-done.3.refs_6_
  102.5 8.3 %project.10.refs_4_ = f32[576,2048]{1,0:T(8,128)} custom-call(s32[1]{0:T(128)} %bitcast.4.refs_0_, s32[4,6]{1,0:T(4,128)} %refs_1_.13, s32[32]{0:T(128)} %refs_2_.13, s32[1,6]{1,0:T(1,128)} %refs_3_.13, f32[576,2048]{1,0:T(8,128)} %project.9.refs_4_, bf16[576,1024]{1,0:T(8,128)(2,1)} %collective-permute-done.2.refs_5_, ...), custom_call_target="tpu_custom_call" | custom-call | flops 3449999872 | bytes 1 | tf_op jit(solution)/shard_map/project/pallas_call | solution.py:280
  110.9 0.8 fusion
  111.6 1.1 slice.6
  112.8 0.1 pad_maximum_fusion.refs_5_
  112.9 1.3 collective-permute-start.14
  114.2 1.9 %slice.7.refs_5_ = bf16[576,512]{1,0:T(8,128)(2,1)} slice(bf16[576,1024]{1,0:T(8,128)(2,1)} %collective-permute-done.11), slice={[0:576], [512:1024]} | slice | bytes 1179648 | tf_op jit(solution)/shard_map/slice | solution.py:401
  116.2 1.4 collective-permute-start.15
  117.6 0.0 collective-permute-done.5.refs_6_
  117.6 16.6 %collective-permute-done.10.refs_8_ = bf16[576,1024]{1,0:T(8,128)(2,1)} collective-permute-done((bf16[576,1024]{1,0:T(8,128)(2,1)}, bf16[576,1024]{1,0:T(8,128)(2,1)}, u32[]{:S(2)}, u32[]{:S(2)}) %collective-permute-start.10) | collective-permute-done | bytes 1179680 | tf_op jit(solution)/shard_map/ppermute | solution.py:373
  134.2 12.2 %project.11.refs_4_ = f32[576,2048]{1,0:T(8,128)} custom-call(s32[2]{0:T(128)} %pad_add_fusion.refs_0_, s32[4,6]{1,0:T(4,128)} %refs_1_.13, s32[32]{0:T(128)} %refs_2_.13, s32[1,6]{1,0:T(1,128)} %refs_3_.13, f32[576,2048]{1,0:T(8,128)} %project.10.refs_4_, bf16[576,1024]{1,0:T(8,128)(2,1)} %collective-permute-done.4.refs_5_, ...), custom_call_target="tpu_custom_call" | custom-call | flops 10350000128 | bytes 1 | tf_op jit(solution)/shard_map/project/pallas_call | solution.py:280
  146.4 3.6 %collective-permute-done.14.refs_6_ = bf16[576,640]{1,0:T(8,128)(2,1)} collective-permute-done((bf16[576,640]{1,0:T(8,128)(2,1)S(1)}, bf16[576,640]{1,0:T(8,128)(2,1)}, u32[]{:S(2)}, u32[]{:S(2)}) %collective-permute-start.14) | collective-permute-done | bytes 737312 | tf_op jit(solution)/shard_map/ppermute | solution.py:373
  150.1 2.3 %copy-done = f32[576,2048]{1,0:T(8,128)S(1)} copy-done((f32[576,2048]{1,0:T(8,128)S(1)}, f32[576,2048]{1,0:T(8,128)}, u32[]{:S(2)}) %copy-start) | copy-done | bytes 4718616
  152.4 1.2 copy-done.3
  153.6 1.2 copy-done.5
  154.9 1.0 copy-done.6
  155.8 6.9 %project.12.refs_4_ = f32[576,2048]{1,0:T(8,128)S(1)} custom-call(s32[1]{0:T(128)} %bitcast.1.refs_0_, s32[4,6]{1,0:T(4,128)S(1)} %copy-done.7, s32[32]{0:T(128)S(1)} %copy-done.8, s32[1,6]{1,0:T(1,128)S(1)} %copy-done.9, f32[576,2048]{1,0:T(8,128)S(1)} %copy-done, bf16[576,640]{1,0:T(8,128)(2,1)S(1)} %pad_maximum_fusion.refs_5_, ...), custom_call_target="tpu_custom_call" | custom-call | flops 1150000000 | bytes 1 | tf_op jit(solution)/shard_map/project/pallas_call | solution.py:280
  162.7 7.7 %project.13 = bf16[768,2048]{1,0:T(8,128)(2,1)} custom-call(s32[1]{0:T(128)} %bitcast.refs_0_, s32[4,6]{1,0:T(4,128)S(1)} %copy-done.7, s32[32]{0:T(128)S(1)} %copy-done.8, s32[1,6]{1,0:T(1,128)S(1)} %copy-done.9, f32[576,2048]{1,0:T(8,128)S(1)} %project.12.refs_4_, bf16[576,512]{1,0:T(8,128)(2,1)} %slice.7.refs_5_, ...), custom_call_target="tpu_custom_call" | custom-call | flops 1 | bytes 1 | tf_op jit(solution)/shard_map/project/pallas_call | solution.py:280
  (23 shorter events, 0.1 us)
Async XLA Ops:
  3.8 15.1 %collective-permute-start.7 = (bf16[2,128,2048]{2,1,0:T(8,128)(2,1)}, bf16[2,128,2048]{2,1,0:T(8,128)(2,1)S(1)}, u32[]{:S(2)}, u32[]{:S(2)}) collective-permute-start(bf16[2,128,2048]{2,1,0:T(8,128)(2,1)} %get-tuple-element.25), channel_id=1, source_target_pairs={{0,4},{4,8},{8,12},{12,0},{1,5},{5,9},{9,13},{13,1},{2,6},{6,10},{... | collective-permute-start | bytes 3145736 | tf_op jit(solution)/shard_map/ppermute | solution.py:345
  4.3 28.8 %collective-permute-start = (bf16[576,1024]{1,0:T(8,128)(2,1)}, bf16[576,1024]{1,0:T(8,128)(2,1)}, u32[]{:S(2)}, u32[]{:S(2)}) collective-permute-start(bf16[576,1024]{1,0:T(8,128)(2,1)} %get-tuple-element.20.refs_4_.rest_0_), channel_id=1, source_target_pairs={{0,1},{1,0},{2,3},{3,2},{4,5},{5,4},{6,7},{7,6},{8,9},{9,8},{10,11... | collective-permute-start | bytes 3538952 | tf_op jit(solution)/shard_map/ppermute | solution.py:367
  7.0 40.4 %collective-permute-start.2 = (bf16[576,1024]{1,0:T(8,128)(2,1)}, bf16[576,1024]{1,0:T(8,128)(2,1)}, u32[]{:S(2)}, u32[]{:S(2)}) collective-permute-start(bf16[576,1024]{1,0:T(8,128)(2,1)} %get-tuple-element.20.refs_4_.rest_0_), channel_id=1, source_target_pairs={{1,2},{2,1},{5,6},{6,5},{9,10},{10,9},{13,14},{14,13},{17,18},{18,... | collective-permute-start | bytes 3538952 | tf_op jit(solution)/shard_map/ppermute | solution.py:370
  19.0 26.8 %copy-start.1 = (bf16[2,128,2048]{2,1,0:T(8,128)(2,1)}, bf16[2,128,2048]{2,1,0:T(8,128)(2,1)S(1)}, u32[]{:S(2)}) copy-start(bf16[2,128,2048]{2,1,0:T(8,128)(2,1)S(1)} %collective-permute-done.7.rest_3_.refs_10_) | copy-start | bytes 3145732
  19.0 26.9 %collective-permute-start.8 = (bf16[2,128,2048]{2,1,0:T(8,128)(2,1)}, bf16[2,128,2048]{2,1,0:T(8,128)(2,1)}, u32[]{:S(2)}, u32[]{:S(2)}) collective-permute-start(bf16[2,128,2048]{2,1,0:T(8,128)(2,1)} %get-tuple-element.27), channel_id=1, source_target_pairs={{0,8},{4,12},{8,0},{12,4},{1,9},{5,13},{9,1},{13,5},{2,10},{6,14},... | collective-permute-start | bytes 3145736 | tf_op jit(solution)/shard_map/ppermute | solution.py:345
  21.3 37.2 %collective-permute-start.1 = (bf16[576,1024]{1,0:T(8,128)(2,1)}, bf16[576,1024]{1,0:T(8,128)(2,1)}, u32[]{:S(2)}, u32[]{:S(2)}) collective-permute-start(bf16[576,1024]{1,0:T(8,128)(2,1)} %get-tuple-element.21.refs_5_.rest_1_), channel_id=1, source_target_pairs={{0,1},{1,0},{2,3},{3,2},{4,5},{5,4},{6,7},{7,6},{8,9},{9,8},{10,11... | collective-permute-start | bytes 3538952 | tf_op jit(solution)/shard_map/ppermute | solution.py:367
  22.8 37.3 %collective-permute-start.4 = (bf16[576,1024]{1,0:T(8,128)(2,1)}, bf16[576,1024]{1,0:T(8,128)(2,1)}, u32[]{:S(2)}, u32[]{:S(2)}) collective-permute-start(bf16[576,1024]{1,0:T(8,128)(2,1)} %get-tuple-element.21.refs_5_.rest_1_), channel_id=1, source_target_pairs={{1,2},{2,1},{5,6},{6,5},{9,10},{10,9},{13,14},{14,13},{17,18},{18,... | collective-permute-start | bytes 3538952 | tf_op jit(solution)/shard_map/ppermute | solution.py:370
  33.2 43.3 %collective-permute-start.6 = (bf16[576,1024]{1,0:T(8,128)(2,1)}, bf16[576,1024]{1,0:T(8,128)(2,1)}, u32[]{:S(2)}, u32[]{:S(2)}) collective-permute-start(bf16[576,1024]{1,0:T(8,128)(2,1)} %collective-permute-done.refs_5_), channel_id=1, source_target_pairs={{1,2},{2,1},{5,6},{6,5},{9,10},{10,9},{13,14},{14,13},{17,18},{18,... | collective-permute-start | bytes 3538952 | tf_op jit(solution)/shard_map/ppermute | solution.py:370
  45.8 23.5 %collective-permute-start.9 = (bf16[2,128,2048]{2,1,0:T(8,128)(2,1)}, bf16[2,128,2048]{2,1,0:T(8,128)(2,1)S(1)}, u32[]{:S(2)}, u32[]{:S(2)}) collective-permute-start(bf16[2,128,2048]{2,1,0:T(8,128)(2,1)} %get-tuple-element.29), channel_id=1, source_target_pairs={{0,12},{4,0},{8,4},{12,8},{1,13},{5,1},{9,5},{13,9},{2,14},{6,2},{... | collective-permute-start | bytes 3145736 | tf_op jit(solution)/shard_map/ppermute | solution.py:345
  47.4 55.1 %collective-permute-start.3 = (bf16[576,1024]{1,0:T(8,128)(2,1)}, bf16[576,1024]{1,0:T(8,128)(2,1)}, u32[]{:S(2)}, u32[]{:S(2)}) collective-permute-start(bf16[576,1024]{1,0:T(8,128)(2,1)} %collective-permute-done.2.refs_5_), channel_id=1, source_target_pairs={{1,0},{2,3},{5,4},{6,7},{9,8},{10,11},{13,12},{14,15},{17,16},{18,... | collective-permute-start | bytes 3538952 | tf_op jit(solution)/shard_map/ppermute | solution.py:373
  58.5 53.2 %collective-permute-start.11 = (bf16[576,1024]{1,0:T(8,128)(2,1)}, bf16[576,1024]{1,0:T(8,128)(2,1)}, u32[]{:S(2)}, u32[]{:S(2)}) collective-permute-start(bf16[576,1024]{1,0:T(8,128)(2,1)} %collective-permute-done.1.refs_5_), channel_id=1, source_target_pairs={{1,2},{2,1},{5,6},{6,5},{9,10},{10,9},{13,14},{14,13},{17,18},{18,... | collective-permute-start | bytes 3538952 | tf_op jit(solution)/shard_map/ppermute | solution.py:370
  60.1 57.5 %collective-permute-start.5 = (bf16[576,1024]{1,0:T(8,128)(2,1)}, bf16[576,1024]{1,0:T(8,128)(2,1)}, u32[]{:S(2)}, u32[]{:S(2)}) collective-permute-start(bf16[576,1024]{1,0:T(8,128)(2,1)} %collective-permute-done.4.refs_5_), channel_id=1, source_target_pairs={{1,0},{2,3},{5,4},{6,7},{9,8},{10,11},{13,12},{14,15},{17,16},{18,... | collective-permute-start | bytes 3538952 | tf_op jit(solution)/shard_map/ppermute | solution.py:373
  69.3 1.0 copy-start.4
  76.5 57.7 %collective-permute-start.10 = (bf16[576,1024]{1,0:T(8,128)(2,1)}, bf16[576,1024]{1,0:T(8,128)(2,1)}, u32[]{:S(2)}, u32[]{:S(2)}) collective-permute-start(bf16[576,1024]{1,0:T(8,128)(2,1)} %collective-permute-done.6.refs_7_), channel_id=1, source_target_pairs={{1,0},{2,3},{5,4},{6,7},{9,8},{10,11},{13,12},{14,15},{17,16},{18,... | collective-permute-start | bytes 3538952 | tf_op jit(solution)/shard_map/ppermute | solution.py:373
  78.9 22.9 %collective-permute-start.12 = (f32[64,576]{0,1:T(8,128)S(1)}, f32[64,576]{0,1:T(8,128)S(1)}, u32[]{:S(2)}, u32[]{:S(2)}) collective-permute-start(f32[64,576]{0,1:T(8,128)S(1)} %copy.10), channel_id=1, source_target_pairs={{0,1},{3,2},{4,5},{7,6},{8,9},{11,10},{12,13},{15,14},{16,17},{19,... | collective-permute-start | bytes 442376 | tf_op jit(solution)/shard_map/ppermute | solution.py:389
  101.8 9.0 %collective-permute-start.13 = (f32[64,576]{0,1:T(8,128)S(1)}, f32[64,576]{0,1:T(8,128)S(1)}, u32[]{:S(2)}, u32[]{:S(2)}) collective-permute-start(f32[64,576]{0,1:T(8,128)S(1)} %add.30), channel_id=1, source_target_pairs={{1,2},{2,1},{5,6},{6,5},{9,10},{10,9},{13,14},{14,13},{17,18},{18,... | collective-permute-start | bytes 442376 | tf_op jit(solution)/shard_map/ppermute | solution.py:370
  112.9 37.1 %collective-permute-start.14 = (bf16[576,640]{1,0:T(8,128)(2,1)S(1)}, bf16[576,640]{1,0:T(8,128)(2,1)}, u32[]{:S(2)}, u32[]{:S(2)}) collective-permute-start(bf16[576,640]{1,0:T(8,128)(2,1)S(1)} %pad_maximum_fusion.refs_5_), channel_id=1, source_target_pairs={{1,0},{2,3},{5,4},{6,7},{9,8},{10,11},{13,12},{14,15},{17,16},{18,... | collective-permute-start | bytes 2211848 | tf_op jit(solution)/shard_map/ppermute | solution.py:373
  116.2 33.9 %copy-start.2 = (bf16[2,128,2048]{2,1,0:T(8,128)(2,1)S(1)}, bf16[2,128,2048]{2,1,0:T(8,128)(2,1)}, u32[]{:S(2)}) copy-start(bf16[2,128,2048]{2,1,0:T(8,128)(2,1)} %copy-done.1) | copy-start | bytes 3145732
  116.2 33.9 %copy-start.7 = (s32[4,6]{1,0:T(4,128)S(1)}, s32[4,6]{1,0:T(4,128)}, u32[]{:S(2)}) copy-start(s32[4,6]{1,0:T(4,128)} %refs_1_.13) | copy-start | bytes 292
  116.2 33.9 %copy-start.8 = (s32[32]{0:T(128)S(1)}, s32[32]{0:T(128)}, u32[]{:S(2)}) copy-start(s32[32]{0:T(128)} %refs_2_.13) | copy-start | bytes 388
  116.2 33.9 %copy-start.9 = (s32[1,6]{1,0:T(1,128)S(1)}, s32[1,6]{1,0:T(1,128)}, u32[]{:S(2)}) copy-start(s32[1,6]{1,0:T(1,128)} %refs_3_.13) | copy-start | bytes 76
  116.2 46.6 %collective-permute-start.15 = (bf16[576,512]{1,0:T(8,128)(2,1)}, bf16[576,512]{1,0:T(8,128)(2,1)}, u32[]{:S(2)}, u32[]{:S(2)}) collective-permute-start(bf16[576,512]{1,0:T(8,128)(2,1)} %slice.7.refs_5_), channel_id=1, source_target_pairs={{1,0},{2,3},{5,4},{6,7},{9,8},{10,11},{13,12},{14,15},{17,16},{18,... | collective-permute-start | bytes 1769480 | tf_op jit(solution)/shard_map/ppermute | solution.py:373
  150.1 2.3 %copy-start = (f32[576,2048]{1,0:T(8,128)S(1)}, f32[576,2048]{1,0:T(8,128)}, u32[]{:S(2)}) copy-start(f32[576,2048]{1,0:T(8,128)} %project.11.refs_4_) | copy-start | bytes 14155780
  152.4 1.2 copy-start.3
  153.6 1.2 copy-start.5
  154.9 1.0 copy-start.6
